TPU v7x, 32 devices: a whole 2x2x4 slice. The times are simulated.
32 devices in a mesh: dp: 4 (over z), seq: 4 (over y, x), heads: 2 (over core).
Axes of the slice: x: 2, y: 2, z: 4, core: 2. Of those that a mesh axis runs over, the one named last changes fastest.
Arguments:
- hidden_in: bfloat16 [4, 3072, 2048], P('dp', ('seq', 'heads')), may hold values from -6 to 6
- out_cotangent: bfloat16 [4, 3072, 2048], P('dp', ('seq', 'heads')), may hold values from -6 to 6
- lengths: int32 [4, 2], P('dp'), may hold values from 1024 to 2048, as said below
- norm_gain: float32 [2048], replicated, may hold values from 0.5 to 1.5
- q_weight: bfloat16 [2048, 2048], P(None, 'heads'), may hold values from -0.125 to 0.125
- k_weight: bfloat16 [2048, 2048], P(None, 'heads'), may hold values from -0.125 to 0.125
- v_weight: bfloat16 [2048, 4096], P(None, 'heads'), may hold values from -0.125 to 0.125
- gate_weight: bfloat16 [2048, 4096], P(None, 'heads'), may hold values from -0.125 to 0.125
- decay_weight: bfloat16 [2048, 16], P(None, 'heads'), may hold values from -0.125 to 0.125
- beta_weight: bfloat16 [2048, 16], P(None, 'heads'), may hold values from -0.125 to 0.125
- conv_q: float32 [4, 2048], P(None, 'heads'), may hold values from -3 to 3
- conv_k: float32 [4, 2048], P(None, 'heads'), may hold values from -3 to 3
- conv_v: float32 [4, 4096], P(None, 'heads'), may hold values from -3 to 3
- decay_log: float32 [16], P('heads'), may hold values from -7 to -3.5
- decay_bias: float32 [16], P('heads'), may hold values from -1 to 1
- out_gain: float32 [256], replicated, may hold values from 0.5 to 1.5
- out_weight: bfloat16 [4096, 2048], P('heads'), may hold values from -0.1875 to 0.1875
- ffn_gain: float32 [2048], replicated, may hold values from 0.5 to 1.5
- ffn_gate: bfloat16 [2048, 5632], P(None, 'heads'), may hold values from -0.125 to 0.125
- ffn_up: bfloat16 [2048, 5632], P(None, 'heads'), may hold values from -0.125 to 0.125
- ffn_down: bfloat16 [5632, 2048], P('heads'), may hold values from -0.15625 to 0.15625
Outputs:
- output: bfloat16 [4, 3072, 2048], P('dp', ('seq', 'heads'))
- input_grad: float32 [4, 3072, 2048], P('dp', ('seq', 'heads'))
- norm_gain_grad: float32 [2048], replicated
- q_weight_grad: float32 [2048, 2048], P(('dp', 'seq'), 'heads')
- k_weight_grad: float32 [2048, 2048], P(('dp', 'seq'), 'heads')
- v_weight_grad: float32 [2048, 4096], P(('dp', 'seq'), 'heads')
- gate_weight_grad: float32 [2048, 4096], P(('dp', 'seq'), 'heads')
- decay_weight_grad: float32 [2048, 16], P(('dp', 'seq'), 'heads')
- beta_weight_grad: float32 [2048, 16], P(('dp', 'seq'), 'heads')
- conv_q_grad: float32 [4, 2048], replicated
- conv_k_grad: float32 [4, 2048], replicated
- conv_v_grad: float32 [4, 4096], replicated
- decay_log_grad: float32 [16], replicated
- decay_bias_grad: float32 [16], replicated
- out_gain_grad: float32 [256], replicated
- out_weight_grad: float32 [4096, 2048], P('heads', ('dp', 'seq'))
- ffn_gain_grad: float32 [2048], replicated
- ffn_gate_grad: float32 [2048, 5632], P(('dp', 'seq'), 'heads')
- ffn_up_grad: float32 [2048, 5632], P(('dp', 'seq'), 'heads')
- ffn_down_grad: float32 [5632, 2048], P('heads', ('dp', 'seq'))
Inputs may be any that keep to these rules, and one draw needn't show every extreme that they name: Row b holds the lengths of batch index b's two sequences in order: one of 1024 tokens and one of 2048 tokens, in either order.
All inputs are finite; a program needn't handle non-finite values.
Results may differ from a plain program's by a relative error of at most 0.02.
Values may be sent and summed in bfloat16 or wider, within the bound.
A program may use at most 448 MiB of HBM per device.

v0:
```python
import jax
import jax.numpy as jnp
from jax import lax
from jax.sharding import PartitionSpec as P

HEADS = 16
DK = 128
DV = 256
GROUP = 64


EPS = 1e-06
PRECISE_MODE = lax.Precision.HIGHEST


def shifted(value, axis, steps):
    count = lax.axis_size(axis)
    leading, last = (max(0, -steps), min(count, count - steps))
    return lax.ppermute(value, axis, [(source, source + steps) for source in range(leading, last)])


def prefix(array, axis, combine, identity):
    size, mine = (lax.axis_size(axis), lax.axis_index(axis))
    everything = jax.tree.map(lambda part: lax.all_gather(part, axis), array)
    start = jax.tree.map(
        lambda part, zero: jnp.broadcast_to(jnp.asarray(zero, part.dtype), part.shape),
        array,
        identity,
    )

    def hop(k, before):
        reached = k < mine
        new = combine(before, jax.tree.map(lambda part: part[k], everything))
        return jax.tree.map(lambda a, b: jnp.where(reached, a, b), new, before)

    return lax.fori_loop(0, size, hop, start)


def prefix_2(array, axis, join, neutral):
    count = lax.axis_size(axis)
    place = lax.axis_index(axis)
    ahead = count - 1 - place
    gathered = jax.tree.map(
        lambda a, kind: lax.all_gather(a.astype(kind), axis),
        array,
        jax.tree.map(lambda a: jnp.bfloat16 if a.dtype == jnp.float32 else a.dtype, array),
    )
    state = jax.tree.map(lambda a, e: jnp.zeros_like(a) + jnp.asarray(e, a.dtype), array, neutral)

    def one(hop, state):
        source = count - 1 - hop
        return join(
            state,
            jax.tree.map(
                lambda a, own: lax.dynamic_index_in_dim(a, source, 0, False).astype(own.dtype),
                gathered,
                array,
            ),
        )

    return lax.fori_loop(0, ahead, one, state)


def rms_scale(values, gain):
    return values * lax.rsqrt(jnp.mean(values * values, axis=-1, keepdims=True) + EPS) * gain


def unit_rows(values):
    return values * lax.rsqrt(jnp.sum(values * values, axis=-1, keepdims=True) + EPS)


def short_conv(padded, weight, valid):
    taps = weight.shape[0]
    count = padded.shape[0] - taps + 1
    total = padded[0:count] * weight[0] * valid[:, 0:1]
    for tap in range(1, taps):
        total = total + padded[tap : tap + count] * weight[tap] * valid[:, tap : tap + 1]
    return jax.nn.silu(total)


def prepare(
    q_ext, k_ext, v_ext, decay_proj, beta_proj, conv_q, conv_k, conv_v, decay_log, decay_bias, valid
):
    count = decay_proj.shape[0]
    heads = decay_proj.shape[1]
    query_vector = unit_rows(short_conv(q_ext, conv_q, valid).reshape(count, heads, -1))
    query_vector = query_vector * query_vector.shape[-1] ** (-0.5)
    key_vector = unit_rows(short_conv(k_ext, conv_k, valid).reshape(count, heads, -1))
    value = short_conv(v_ext, conv_v, valid).reshape(count, heads, -1)
    log_decay = -jnp.exp(decay_log) * jax.nn.softplus(decay_proj + decay_bias)
    beta = jax.nn.sigmoid(beta_proj)
    return (query_vector, key_vector, value, log_decay, beta)


def group_local(query_vector, key_vector, value, log_decay, beta):
    size = log_decay.shape[-1]
    cumul = jnp.cumsum(log_decay, axis=-1)
    order = jnp.arange(size)
    below = (order[:, None] > order[None, :]).astype(log_decay.dtype)
    within = (order[:, None] >= order[None, :]).astype(log_decay.dtype)
    spread = jnp.exp((cumul[..., :, None] - cumul[..., None, :]) * within) * within
    keys = jnp.einsum("nhik,nhjk->nhij", key_vector, key_vector, precision=PRECISE_MODE)
    unit = jnp.eye(size, dtype=log_decay.dtype) + beta[..., :, None] * keys * spread * below
    growth_factor = jnp.exp(cumul)
    right = jnp.concatenate(
        [beta[..., None] * value, (beta * growth_factor)[..., None] * key_vector], axis=-1
    )
    solved_system = jax.scipy.linalg.solve_triangular(unit, right, lower=True, unit_diagonal=True)
    value_width = value.shape[-1]
    scores = (
        jnp.einsum("nhik,nhjk->nhij", query_vector, key_vector, precision=PRECISE_MODE) * spread
    )
    tail_tokens = jnp.exp(cumul[..., -1:] - cumul)
    return (
        solved_system[..., :value_width],
        solved_system[..., value_width:],
        scores,
        growth_factor[..., None] * query_vector,
        tail_tokens[..., None] * key_vector,
        jnp.exp(cumul[..., -1]),
    )


def group_state(memory_state, u_part, w_part, scores, grown_query, tail_key, last_growth, keep):
    memory_state = memory_state * keep
    delta_update = u_part - jnp.einsum("lwo,loq->lwq", w_part, memory_state, precision=PRECISE_MODE)
    output_rows = jnp.einsum("lwo,loq->lwq", grown_query, memory_state, precision=PRECISE_MODE)
    output_rows = output_rows + jnp.einsum(
        "hij,hjv->hiv", scores, delta_update, precision=PRECISE_MODE
    )
    updated_state = last_growth[:, None, None] * memory_state
    updated_state = updated_state + jnp.einsum(
        "biw,bir->bwr", tail_key, delta_update, precision=PRECISE_MODE
    )
    return (updated_state, output_rows)


def run_span(memory_state, query_vector, key_vector, value, log_decay, beta, keep):
    count, heads = log_decay.shape
    blocks = keep.shape[0]
    size = count // blocks

    def split(values):
        shaped = values.reshape((blocks, size, heads) + values.shape[2:])
        return jnp.swapaxes(shaped, 1, 2)

    local = group_local(
        split(query_vector), split(key_vector), split(value), split(log_decay), split(beta)
    )
    step_fn = jax.checkpoint(group_state)

    def advance(carry, items):
        return step_fn(carry, *items)

    final, outs = lax.scan(advance, memory_state, local + (keep,))
    outs = jnp.swapaxes(outs, 1, 2).reshape(count, heads, -1)
    return (final, outs)


def gate_piece(mixed, gate_proj, out_gain):
    count, heads, width = mixed.shape
    gates = jax.nn.silu(gate_proj.reshape(count, heads, width))
    return (rms_scale(mixed, out_gain) * gates).reshape(count, heads * width)


def swish_product(gate_ffn, up_ffn):
    return jax.nn.silu(gate_ffn) * up_ffn


def compose(early, late):
    first_map = jnp.einsum("hij,hjk->hik", late[0], early[0], precision=PRECISE_MODE)
    second_map = jnp.einsum("hij,hjv->hiv", late[0], early[1], precision=PRECISE_MODE) + late[1]
    return (first_map, second_map)


def project(rows, weight):
    return jnp.dot(rows, weight, preferred_element_type=jnp.float32)


def rows_product(left, right):
    return jnp.dot(left, right, preferred_element_type=jnp.float32)


def rows_back(left, weight):
    return jnp.einsum("tc,dc->td", left, weight, preferred_element_type=jnp.float32)


def weight_grad(rows, grads):
    return jnp.einsum("td,tc->dc", rows, grads, preferred_element_type=jnp.float32)


def body(
    hidden_in,
    out_cotangent,
    lengths,
    norm_gain,
    q_weight,
    k_weight,
    v_weight,
    gate_weight,
    decay_weight,
    beta_weight,
    conv_q,
    conv_k,
    conv_v,
    decay_log,
    decay_bias,
    out_gain,
    out_weight,
    ffn_gain,
    ffn_gate,
    ffn_up,
    ffn_down,
):
    resid = hidden_in[0].astype(jnp.float32)
    normed_own = rms_scale(resid, norm_gain).astype(jnp.bfloat16)
    normed, cotangent = (
        lax.all_gather(normed_own, "heads", axis=0, tiled=True),
        lax.all_gather(out_cotangent[0], "heads", axis=0, tiled=True),
    )
    span = normed.shape[0]
    taps = conv_q.shape[0]
    halo = taps - 1
    q_proj = project(normed, q_weight)
    k_proj = project(normed, k_weight)
    v_proj = project(normed, v_weight)
    gate_proj = project(normed, gate_weight)
    decay_proj = project(normed, decay_weight)
    beta_proj = project(normed, beta_weight)
    seq_index = lax.axis_index("seq")
    first = lengths[0, 0]
    index = seq_index * span + jnp.arange(span, dtype=jnp.int32)
    place = index - jnp.where(index >= first, first, 0)
    valid = jnp.stack([place >= taps - 1 - tap for tap in range(taps)], axis=1).astype(jnp.float32)
    starts = seq_index * span + jnp.arange(span // GROUP, dtype=jnp.int32) * GROUP
    keep = ((starts != 0) & (starts != first)).astype(jnp.float32)
    rim = shifted((q_proj[span - halo :], k_proj[span - halo :], v_proj[span - halo :]), "seq", 1)
    q_ext = jnp.concatenate([rim[0], q_proj], axis=0)
    k_ext = jnp.concatenate([rim[1], k_proj], axis=0)
    v_ext = jnp.concatenate([rim[2], v_proj], axis=0)

    def features(
        q_in, k_in, v_in, decay_in, beta_in, conv_qin, conv_kin, conv_vin, log_in, bias_in
    ):
        return prepare(
            q_in,
            k_in,
            v_in,
            decay_in,
            beta_in,
            conv_qin,
            conv_kin,
            conv_vin,
            log_in,
            bias_in,
            valid,
        )

    feats, feat_pull = jax.vjp(
        features,
        q_ext,
        k_ext,
        v_ext,
        decay_proj,
        beta_proj,
        conv_q,
        conv_k,
        conv_v,
        decay_log,
        decay_bias,
    )
    query_vector, key_vector, value, log_decay, beta = feats
    heads = log_decay.shape[1]
    width_k = key_vector.shape[2]
    value_width = value.shape[2]
    identity = jnp.broadcast_to(jnp.eye(width_k, dtype=jnp.float32), (heads, width_k, width_k))
    empty = jnp.zeros((heads, width_k, value_width), jnp.float32)
    transfer, _ = run_span(
        identity, query_vector, key_vector, jnp.zeros_like(query_vector), log_decay, beta, keep
    )
    offset, _ = run_span(empty, query_vector, key_vector, value, log_decay, beta, keep)
    earlier = prefix((transfer, offset), "seq", compose, (identity, empty))
    start_state = earlier[1]

    def span_fn(state_in, query_in, key_in, value_in, decay_in, beta_in):
        return run_span(state_in, query_in, key_in, value_in, decay_in, beta_in, keep)

    (end_state, mixed), span_pull = jax.vjp(
        span_fn, start_state, query_vector, key_vector, value, log_decay, beta
    )
    gated, gate_pull = jax.vjp(gate_piece, mixed, gate_proj, out_gain)
    gated_low = gated.astype(jnp.bfloat16)
    mixer = lax.psum_scatter(
        rows_product(gated_low, out_weight), "heads", scatter_dimension=0, tiled=True
    )
    resid_mid = resid + mixer
    ffn_own = rms_scale(resid_mid, ffn_gain).astype(jnp.bfloat16)
    ffn_in = lax.all_gather(ffn_own, "heads", axis=0, tiled=True)
    gate_ffn = project(ffn_in, ffn_gate)
    up_ffn = project(ffn_in, ffn_up)
    act, act_pull = jax.vjp(swish_product, gate_ffn, up_ffn)
    act_low = act.astype(jnp.bfloat16)
    ffn_out = lax.psum_scatter(
        rows_product(act_low, ffn_down).astype(jnp.bfloat16),
        "heads",
        scatter_dimension=0,
        tiled=True,
    ).astype(jnp.float32)
    output = (resid_mid + ffn_out).astype(jnp.bfloat16)
    d_act = jnp.einsum("td,fd->tf", cotangent, ffn_down, preferred_element_type=jnp.float32)
    d_gate_ffn, d_up_ffn = act_pull(d_act)
    d_gate_low = d_gate_ffn.astype(jnp.bfloat16)
    d_up_low = d_up_ffn.astype(jnp.bfloat16)
    grad_down = jnp.einsum("tf,td->fd", act_low, cotangent, preferred_element_type=jnp.float32)
    grad_gate = weight_grad(ffn_in, d_gate_low)
    grad_up = weight_grad(ffn_in, d_up_low)
    d_ffn = lax.psum_scatter(
        rows_back(d_gate_low, ffn_gate) + rows_back(d_up_low, ffn_up),
        "heads",
        scatter_dimension=0,
        tiled=True,
    )
    _, ffn_norm_pull = jax.vjp(rms_scale, resid_mid, ffn_gain)
    d_mid_norm, d_ffn_gain = ffn_norm_pull(d_ffn)
    d_mid = out_cotangent[0].astype(jnp.float32) + d_mid_norm
    d_mid_all = lax.all_gather(d_mid.astype(jnp.bfloat16), "heads", axis=0, tiled=True)
    grad_out = weight_grad(gated_low, d_mid_all)
    d_gated = jnp.einsum("td,cd->tc", d_mid_all, out_weight, preferred_element_type=jnp.float32)
    d_mixed, d_gate_proj, d_out_gain = gate_pull(d_gated)
    local_back = span_pull((jnp.zeros_like(end_state), d_mixed))[0]
    flipped = jnp.swapaxes(transfer, 1, 2)
    later = prefix_2((flipped, local_back), "seq", compose, (identity, empty))
    span_grads = span_pull((later[1], d_mixed))
    ext_grads = feat_pull(span_grads[1:])
    passed = shifted((ext_grads[0][:halo], ext_grads[1][:halo], ext_grads[2][:halo]), "seq", -1)
    d_q_low = ext_grads[0][halo:].at[span - halo :].add(passed[0]).astype(jnp.bfloat16)
    d_k_low = ext_grads[1][halo:].at[span - halo :].add(passed[1]).astype(jnp.bfloat16)
    d_v_low = ext_grads[2][halo:].at[span - halo :].add(passed[2]).astype(jnp.bfloat16)
    d_decay_low = ext_grads[3].astype(jnp.bfloat16)
    d_beta_low = ext_grads[4].astype(jnp.bfloat16)
    d_gate_low_mix = d_gate_proj.astype(jnp.bfloat16)
    grad_q = weight_grad(normed, d_q_low)
    grad_k = weight_grad(normed, d_k_low)
    grad_v = weight_grad(normed, d_v_low)
    grad_gate_mix = weight_grad(normed, d_gate_low_mix)
    grad_decay = weight_grad(normed, d_decay_low)
    grad_beta = weight_grad(normed, d_beta_low)
    total = rows_back(d_q_low, q_weight) + rows_back(d_k_low, k_weight)
    total = total + rows_back(d_v_low, v_weight) + rows_back(d_gate_low_mix, gate_weight)
    total = total + rows_back(d_decay_low, decay_weight) + rows_back(d_beta_low, beta_weight)
    d_normed = lax.psum_scatter(
        total.astype(jnp.bfloat16), "heads", scatter_dimension=0, tiled=True
    ).astype(jnp.float32)
    _, in_norm_pull = jax.vjp(rms_scale, resid, norm_gain)
    d_in_norm, d_norm_gain = in_norm_pull(d_normed)
    input_grad = d_mid + d_in_norm
    head_index = lax.axis_index("heads")

    def widen(part, total):
        full = jnp.zeros(part.shape[:-1] + (total,), jnp.float32)
        return lax.dynamic_update_slice_in_dim(
            full, part, head_index * part.shape[-1], part.ndim - 1
        )

    small = lax.psum(
        (
            d_norm_gain,
            d_ffn_gain,
            d_out_gain,
            widen(ext_grads[8], HEADS),
            widen(ext_grads[9], HEADS),
            widen(ext_grads[5], HEADS * DK),
            widen(ext_grads[6], HEADS * DK),
            widen(ext_grads[7], HEADS * DV),
        ),
        ("dp", "seq", "heads"),
    )
    mixer_sums = (
        lax.psum_scatter(
            grad_q.astype(jnp.bfloat16), ("dp", "seq"), scatter_dimension=0, tiled=True
        ).astype(jnp.float32),
        lax.psum_scatter(
            grad_k.astype(jnp.bfloat16), ("dp", "seq"), scatter_dimension=0, tiled=True
        ).astype(jnp.float32),
        lax.psum_scatter(
            grad_v.astype(jnp.bfloat16), ("dp", "seq"), scatter_dimension=0, tiled=True
        ).astype(jnp.float32),
        lax.psum_scatter(
            grad_gate_mix.astype(jnp.bfloat16), ("dp", "seq"), scatter_dimension=0, tiled=True
        ).astype(jnp.float32),
        lax.psum_scatter(
            grad_decay.astype(jnp.bfloat16), ("dp", "seq"), scatter_dimension=0, tiled=True
        ).astype(jnp.float32),
        lax.psum_scatter(
            grad_beta.astype(jnp.bfloat16), ("dp", "seq"), scatter_dimension=0, tiled=True
        ).astype(jnp.float32),
        lax.psum_scatter(
            grad_out.astype(jnp.bfloat16), ("dp", "seq"), scatter_dimension=1, tiled=True
        ).astype(jnp.float32),
    )
    return (
        output[None],
        input_grad[None],
        small[0],
        mixer_sums[0],
        mixer_sums[1],
        mixer_sums[2],
        mixer_sums[3],
        mixer_sums[4],
        mixer_sums[5],
        small[5],
        small[6],
        small[7],
        small[3],
        small[4],
        small[2],
        mixer_sums[6],
        small[1],
        lax.psum_scatter(
            grad_gate.astype(jnp.bfloat16), ("dp", "seq"), scatter_dimension=0, tiled=True
        ).astype(jnp.float32),
        lax.psum_scatter(
            grad_up.astype(jnp.bfloat16), ("dp", "seq"), scatter_dimension=0, tiled=True
        ).astype(jnp.float32),
        lax.psum_scatter(
            grad_down.astype(jnp.bfloat16), ("dp", "seq"), scatter_dimension=1, tiled=True
        ).astype(jnp.float32),
    )


def solution(mesh):
    in_specs = (
        P("dp", ("seq", "heads"), None),
        P("dp", ("seq", "heads"), None),
        P("dp", None),
        P(),
        P(None, "heads"),
        P(None, "heads"),
        P(None, "heads"),
        P(None, "heads"),
        P(None, "heads"),
        P(None, "heads"),
        P(None, "heads"),
        P(None, "heads"),
        P(None, "heads"),
        P("heads"),
        P("heads"),
        P(),
        P("heads", None),
        P(),
        P(None, "heads"),
        P(None, "heads"),
        P("heads", None),
    )
    out_specs = (
        P("dp", ("seq", "heads"), None),
        P("dp", ("seq", "heads"), None),
        P(),
        P(("dp", "seq"), "heads"),
        P(("dp", "seq"), "heads"),
        P(("dp", "seq"), "heads"),
        P(("dp", "seq"), "heads"),
        P(("dp", "seq"), "heads"),
        P(("dp", "seq"), "heads"),
        P(),
        P(),
        P(),
        P(),
        P(),
        P(),
        P("heads", ("dp", "seq")),
        P(),
        P(("dp", "seq"), "heads"),
        P(("dp", "seq"), "heads"),
        P("heads", ("dp", "seq")),
    )
    return jax.shard_map(body, mesh=mesh, in_specs=in_specs, out_specs=out_specs, check_vma=False)
```

profile of v0, /device:TPU:0, one launch (start us, length us, event | category | flops | bytes accessed | tf_op | source)
XLA Modules:
  0.0 3724.0 jit_solution(17242227405739200975)
XLA Ops:
  125.0 473.3 %custom-call.13 = f32[12,8,1,64,64]{3,4,2,1,0:T(8,128)} custom-call(f32[12,8,1,64,64]{4,3,2,1,0:T(8,128)} %get-tuple-element.1404), custom_call_target="InvertDiagBlocksLowerTriangular" | custom-call | tf_op jit(solution)/shard_map/jit(_solve_triangular)/vmap(vmap())/triangular_solve | solution.py:108
  616.6 75.5 %while.107 = (s32[]{:T(128)}, f32[8,128,128]{2,1,0:T(8,128)S(1)}, f32[12,8]{1,0:T(8,128)}, f32[12]{0:T(128)S(1)}, f32[12,8,64,128]{3,2,1,0:T(8,128)}, /*index=5*...) while((s32[]{:T(128)}, f32[8,128,128]{2,1,0:T(8,128)S(1)}, f32[12,8]{1,0:T(8,128)}, ...), condition=%wide.region_4.5_spmd, body=%wide.region_3.4_spmd.sunk | while | flops 201916416 | bytes 2886341 | solution.py:155
  693.0 17.8 fusion.91
  737.5 80.9 %while.111 = (s32[]{:T(128)}, f32[8,128,256]{2,1,0:T(8,128)S(1)}, f32[12,8]{1,0:T(8,128)}, f32[12]{0:T(128)S(1)}, f32[12,8,64,128]{3,2,1,0:T(8,128)}, /*index=5*...) while((s32[]{:T(128)}, f32[8,128,256]{2,1,0:T(8,128)S(1)}, ...), condition=%wide.region_6.8_spmd.clone, body=%wide.region_5.7_spmd.clone.sunk | while | flops 404357120 | bytes 5245656 | solution.py:155
  824.6 46.7 %all-gather.22.cloned.1.call-done = f32[32,128,256]{2,1,0:T(8,128)} async-done(((f32[8,128,256]{2,1,0:T(8,128)}), f32[32,128,256]{2,1,0:T(8,128)}) %all-gather.22.cloned.1.call-update) | async-done | bytes 4194320 | tf_op jit(solution)/shard_map/all_gather | solution.py:24
  885.4 150.3 %while.108 = (s32[]{:T(128)}, f32[8,128,256]{2,1,0:T(8,128)S(1)}, f32[12,8,64,256]{3,2,1,0:T(8,128)}, f32[12,8,128,256]{3,2,1,0:T(8,128)}, f32[12,8]{1,0:T(8,128...) while((s32[]{:T(128)}, f32[8,128,256]{2,1,0:T(8,128)S(1)}, ...), condition=%wide.region_11.13_spmd, body=%wide.region_10.12_spmd.sunk | while | flops 706215936 | bytes 11015397 | solution.py:155
  1080.9 14.6 reduce-scatter.23.cloned.1.call-done
  1113.6 17.2 fusion.225
  1130.8 14.8 fusion.226
  1145.6 23.1 multiply_convert_fusion
  1196.3 15.8 reduce-scatter.27.cloned.1.call-done
  1231.8 18.4 fusion.85
  1266.8 115.8 %while.113 = (s32[]{:T(128)}, f32[8,128,256]{2,1,0:T(8,128)S(1)}, f32[12,8,64,128]{3,2,1,0:T(8,128)}, f32[12,8,64,64]{2,3,1,0:T(8,128)}, f32[12,8,64,128]{3,2,1,...) while((s32[]{:T(128)}, f32[8,128,256]{2,1,0:T(8,128)S(1)}, ...), condition=%wide.region_20.22_spmd.clone, body=%wide.region_19.21_spmd.clone.sunk | while | flops 706215936 | bytes 14287119 | solution.py:155
  1383.6 36.6 all-gather.28.cloned.1.call-done
  1437.8 271.4 %while.110 = (s32[]{:T(128)}, f32[8,128,256]{2,1,0:T(8,128)S(1)}, f32[12,8,64,256]{3,2,1,0:T(8,128)}, f32[12,8,64,128]{3,2,1,0:T(8,128)}, f32[12,8,64,64]{3,2,1,...) while((s32[]{:T(128)}, f32[8,128,256]{2,1,0:T(8,128)S(1)}, ...), condition=%wide.region_25.27_spmd, body=%wide.region_23.26_spmd.sunk | while | flops 1613758464 | bytes 27133384 | solution.py:155
  1720.9 17.5 fusion.76
  1791.4 14.5 convolution_convert_fusion
  1805.9 15.5 copy.238
  1821.5 14.7 convolution_convert_fusion.2
  1836.7 14.7 convolution_convert_fusion.1
  2038.9 20.1 add_convert_fusion
  2139.4 40.7 %reduce-scatter.49.cloned.1.call-done = bf16[128,2816]{1,0:T(8,128)(2,1)} async-done(((bf16[2048,2816]{1,0:T(8,128)(2,1)}), bf16[128,2816]{1,0:T(8,128)(2,1)}) %reduce-scatter.49.cloned.1.call-update) | async-done | bytes 720912
  2182.8 245.1 %reduce-scatter.39.cloned.1.call-done = bf16[128,2816]{1,0:T(8,128)(2,1)} async-done(((bf16[2048,2816]{1,0:T(8,128)(2,1)}), bf16[128,2816]{1,0:T(8,128)(2,1)}) %reduce-scatter.39.cloned.1.call-update) | async-done | bytes 720912 | tf_op jit(solution)/shard_map/reduce_scatter | solution.py:419
  2430.2 245.4 %reduce-scatter.41.cloned.1.call-done = bf16[128,2816]{1,0:T(8,128)(2,1)} async-done(((bf16[2048,2816]{1,0:T(8,128)(2,1)}), bf16[128,2816]{1,0:T(8,128)(2,1)}) %reduce-scatter.41.cloned.1.call-update) | async-done | bytes 720912 | tf_op jit(solution)/shard_map/reduce_scatter | solution.py:422
  2677.9 15.9 reduce-scatter.29.cloned.1.call-done
  2714.1 92.4 %reduce-scatter.33.cloned.1.call-done = bf16[128,1024]{1,0:T(8,128)(2,1)} async-done(((bf16[2048,1024]{1,0:T(8,128)(2,1)}), bf16[128,1024]{1,0:T(8,128)(2,1)}) %reduce-scatter.33.cloned.1.call-update) | async-done | bytes 262160 | tf_op jit(solution)/shard_map/reduce_scatter | solution.py:382
  2808.3 95.3 %reduce-scatter.31.cloned.1.call-done = bf16[128,1024]{1,0:T(8,128)(2,1)} async-done(((bf16[2048,1024]{1,0:T(8,128)(2,1)}), bf16[128,1024]{1,0:T(8,128)(2,1)}) %reduce-scatter.31.cloned.1.call-update) | async-done | bytes 262160 | tf_op jit(solution)/shard_map/reduce_scatter | solution.py:379
  2905.4 177.8 %reduce-scatter.47.cloned.1.call-done = bf16[128,2048]{1,0:T(8,128)(2,1)} async-done(((bf16[2048,2048]{1,0:T(8,128)(2,1)}), bf16[128,2048]{1,0:T(8,128)(2,1)}) %reduce-scatter.47.cloned.1.call-update) | async-done | bytes 524304
  3085.6 180.2 %reduce-scatter.37.cloned.1.call-done = bf16[128,2048]{1,0:T(8,128)(2,1)} async-done(((bf16[2048,2048]{1,0:T(8,128)(2,1)}), bf16[128,2048]{1,0:T(8,128)(2,1)}) %reduce-scatter.37.cloned.1.call-update) | async-done | bytes 524304 | tf_op jit(solution)/shard_map/reduce_scatter | solution.py:388
  3267.9 180.4 %reduce-scatter.35.cloned.1.call-done = bf16[128,2048]{1,0:T(8,128)(2,1)} async-done(((bf16[2048,2048]{1,0:T(8,128)(2,1)}), bf16[128,2048]{1,0:T(8,128)(2,1)}) %reduce-scatter.35.cloned.1.call-update) | async-done | bytes 524304 | tf_op jit(solution)/shard_map/reduce_scatter | solution.py:385
  3450.5 124.0 %all-reduce.32.cloned.1.call-done = f32[4,4096]{1,0:T(4,128)} async-done(((f32[4,4096]{1,0:T(4,128)}), f32[4,4096]{1,0:T(4,128)}) %all-reduce.32.cloned.1.call-update) | async-done | bytes 65552 | tf_op jit(solution)/shard_map/psum | solution.py:365
  3574.4 132.3 %all-reduce.34.cloned.1.call-done = (f32[2048]{0:T(1024)}, f32[4,2048]{1,0:T(4,128)}, f32[4,2048]{1,0:T(4,128)}, f32[16]{0:T(128)}, f32[16]{0:T(128)}, /*index=5*/f32[256]{0:T(256)}, f32[2048]{0:T(1024)}) async-done(((f32[2048]{0:T(1024)}, f32[4,2048]{1,0:T(4,128)}, f32[4,2048]{1,0:T(4,128)}, f32[16]{0:T(128)}, f32[16]{0:T(128)}, /*index=5*/f32[256]{0:T(256)}, f32[2048]{0:T(1024)}), (f32[2048]{0:T(1024)}, ...) | async-done | bytes 83088 | tf_op jit(solution)/shard_map/psum | solution.py:365
  (1273 shorter events, 1414.5 us)
Async XLA Ops:
  7.3 21.0 all-gather.14.cloned.1.call-start
  13.3 811.3 %all-gather.20.cloned.1.call-start = ((), (), s32[]{:S(2)}) async-start(), calls=%async_computation.28 | async-start | bytes 2621440 | tf_op jit(solution)/shard_map/all_gather | solution.py:24
  42.1 31.8 collective-permute-start
  51.6 37.7 %collective-permute-start.2 = (f32[3,1024]{1,0:T(4,128)}, f32[3,1024]{1,0:T(4,128)}, u32[]{:S(2)}, u32[]{:S(2)}) collective-permute-start(f32[3,1024]{1,0:T(4,128)} %slice.277), channel_id=1, source_target_pairs={{0,2},{2,4},{4,6},{1,3},{3,5},{5,7},{8,10},{10,12},{12,14},{9,11},... | collective-permute-start | bytes 36872 | tf_op jit(solution)/shard_map/ppermute | solution.py:19
  69.5 623.5 %collective-permute-start.1 = (f32[3,2048]{1,0:T(4,128)}, f32[3,2048]{1,0:T(4,128)}, u32[]{:S(2)}, u32[]{:S(2)}) collective-permute-start(f32[3,2048]{1,0:T(4,128)} %slice.270), channel_id=1, source_target_pairs={{0,2},{2,4},{4,6},{1,3},{3,5},{5,7},{8,10},{10,12},{12,14},{9,11},... | collective-permute-start | bytes 73736 | tf_op jit(solution)/shard_map/ppermute | solution.py:19
  73.1 746.3 %copy-start.90 = (f32[12,8,64]{2,1,0:T(8,128)}, f32[12,8,64]{2,1,0:T(8,128)S(1)}, u32[]{:S(2)}) copy-start(f32[12,8,64]{2,1,0:T(8,128)S(1)} %get-tuple-element.1406) | copy-start | bytes 73732
  106.5 712.9 %copy-start.78 = (f32[12,64,8]{1,2,0:T(8,128)}, f32[12,64,8]{1,2,0:T(8,128)S(1)}, u32[]{:S(2)}) copy-start(f32[12,64,8]{1,2,0:T(8,128)S(1)} %copy.183) | copy-start | bytes 73732
  692.9 178.4 %all-gather.22.cloned.1.call-start = ((), (), s32[]{:S(2)}) async-start(), calls=%async_computation.29 | async-start | bytes 5242880 | tf_op jit(solution)/shard_map/all_gather | solution.py:24
  819.3 276.2 %reduce-scatter.23.cloned.1.call-start = ((), (), s32[]{:S(2)}) async-start(), calls=%async_computation.15 | async-start | bytes 9437184 | tf_op jit(solution)/shard_map/reduce_scatter | solution.py:293
  1080.9 32.8 all-gather.16.cloned.1.call-start
  1100.2 45.4 %all-gather.24.cloned.1.call-start = ((), (), s32[]{:S(2)}) async-start(), calls=%async_computation.30 | async-start | bytes 4718592 | tf_op jit(solution)/shard_map/all_gather | solution.py:219
  1100.8 111.3 %reduce-scatter.27.cloned.1.call-start = ((), (), s32[]{:S(2)}) async-start(), calls=%async_computation.18 | async-start | bytes 9437184 | tf_op jit(solution)/shard_map/reduce_scatter | solution.py:317
  1196.3 35.5 all-gather.18.cloned.1.call-start
  1218.4 165.2 %all-gather.26.cloned.1.call-start = ((), (), s32[]{:S(2)}) async-start(), calls=%async_computation.31 | async-start | bytes 1310720 | tf_op jit(solution)/shard_map/all_gather | solution.py:44
  1222.9 197.2 %all-gather.28.cloned.1.call-start = ((), (), s32[]{:S(2)}) async-start(), calls=%async_computation.32 | async-start | bytes 2621440 | tf_op jit(solution)/shard_map/all_gather | solution.py:44
  1383.5 753.1 %reduce-scatter.43.cloned.1.call-start = ((), (), s32[]{:S(2)}) async-start(), calls=%async_computation.33 | async-start | bytes 557056
  1787.7 350.3 %reduce-scatter.45.cloned.1.call-start = ((), (), s32[]{:S(2)}) async-start(), calls=%async_computation.34 | async-start | bytes 557056
  1791.4 388.7 %reduce-scatter.49.cloned.1.call-start = ((), (), s32[]{:S(2)}) async-start(), calls=%async_computation.36 | async-start | bytes 12255232
  1821.4 606.4 %reduce-scatter.39.cloned.1.call-start = ((), (), s32[]{:S(2)}) async-start(), calls=%async_computation.26 | async-start | bytes 12255232 | tf_op jit(solution)/shard_map/reduce_scatter | solution.py:419
  1836.2 839.4 %reduce-scatter.41.cloned.1.call-start = ((), (), s32[]{:S(2)}) async-start(), calls=%async_computation.27 | async-start | bytes 12255232 | tf_op jit(solution)/shard_map/reduce_scatter | solution.py:422
  1851.4 842.4 %reduce-scatter.29.cloned.1.call-start = ((), (), s32[]{:S(2)}) async-start(), calls=%async_computation.20 | async-start | bytes 4718592 | tf_op jit(solution)/shard_map/reduce_scatter | solution.py:351
  1954.1 60.0 %collective-permute-start.4 = (f32[3,1024]{1,0:T(4,128)S(1)}, f32[3,1024]{1,0:T(4,128)S(1)}, u32[]{:S(2)}, u32[]{:S(2)}) collective-permute-start(f32[3,1024]{1,0:T(4,128)S(1)} %pad_add_fusion.7), channel_id=1, source_target_pairs={{2,0},{4,2},{6,4},{3,1},{5,3},{7,5},{10,8},{12,10},{14,12},{11,9},... | collective-permute-start | bytes 36872 | tf_op jit(solution)/shard_map/ppermute | solution.py:19
  2004.7 32.1 collective-permute-start.5
  2010.9 6.7 collective-permute-start.3
  2059.1 649.0 %reduce-scatter.25.cloned.1.call-start = ((), (), s32[]{:S(2)}) async-start(), calls=%async_computation.17 | async-start | bytes 4718592 | tf_op jit(solution)/shard_map/reduce_scatter | solution.py:303
  2073.6 732.9 %reduce-scatter.33.cloned.1.call-start = ((), (), s32[]{:S(2)}) async-start(), calls=%async_computation.22 | async-start | bytes 4456448 | tf_op jit(solution)/shard_map/reduce_scatter | solution.py:382
  2081.9 821.7 %reduce-scatter.31.cloned.1.call-start = ((), (), s32[]{:S(2)}) async-start(), calls=%async_computation.21 | async-start | bytes 4456448 | tf_op jit(solution)/shard_map/reduce_scatter | solution.py:379
  2088.6 994.6 %reduce-scatter.47.cloned.1.call-start = ((), (), s32[]{:S(2)}) async-start(), calls=%async_computation.35 | async-start | bytes 8912896
  2112.4 1153.4 %reduce-scatter.37.cloned.1.call-start = ((), (), s32[]{:S(2)}) async-start(), calls=%async_computation.24 | async-start | bytes 8912896 | tf_op jit(solution)/shard_map/reduce_scatter | solution.py:388
  2123.4 1325.0 %reduce-scatter.35.cloned.1.call-start = ((), (), s32[]{:S(2)}) async-start(), calls=%async_computation.23 | async-start | bytes 8912896 | tf_op jit(solution)/shard_map/reduce_scatter | solution.py:385
  2134.6 1439.8 %all-reduce.32.cloned.1.call-start = ((), (), s32[]{:S(2)}) async-start(), calls=%async_computation.25 | async-start | bytes 131072 | tf_op jit(solution)/shard_map/psum | solution.py:365
  2135.9 1570.8 %all-reduce.34.cloned.1.call-start = ((), (), s32[]{:S(2)}) async-start(), calls=%async_computation.37 | async-start | bytes 167936 | tf_op jit(solution)/shard_map/psum | solution.py:365
  (216 other events, 10128.0 us)
Sparse Core Ops, SparseCore 0:
  13.4 14.8 all-gather.13
  693.0 34.3 all-gather.19
  819.5 51.7 all-gather.21
  1081.0 14.4 reduce-scatter.22
  1100.3 13.2 all-gather.15
  1115.1 13.2 all-gather.23
  1196.4 15.6 reduce-scatter.26
  1218.5 13.2 all-gather.17
  1234.2 27.7 all-gather.25
  1383.6 36.4 all-gather.27
  1787.8 75.6 reduce-scatter.42
  1866.2 72.8 reduce-scatter.44
  1941.4 238.6 reduce-scatter.48
  2182.2 245.5 reduce-scatter.38
  2430.0 245.5 reduce-scatter.40
  2678.2 15.5 reduce-scatter.28
  2696.0 12.0 reduce-scatter.24
  2710.3 96.2 reduce-scatter.32
  2808.8 94.7 reduce-scatter.30
  2905.8 177.3 reduce-scatter.46
  3085.5 180.2 reduce-scatter.36
  3268.1 180.2 reduce-scatter.34
  3454.5 119.8 all-reduce.31
  3582.4 124.2 all-reduce.33
where the time goes:
time: 3740 us; the launch traced here: 3720 us
  waiting for transfers between devices  1680 us (45%)
  matrix products  904 us (24%)
  other arithmetic  689 us (18%)
  local copies, waits for them, and re-layouts  413 us (11%)
    another operation x4, other arithmetic, group_local(): jax.scipy.linalg.solve_triangular(unit, right, lower=True, unit_diagonal=...  475 us
    psum x2, waiting for transfers between devices, body(): lax.psum((d_norm_gain, d_ffn_gain, d_out_gain, widen(ext_grads[8], HEADS)...  256 us
    reduce_scatter x1, waiting for transfers between devices, body(): lax.psum_scatter(grad_up.astype(jnp.bfloat16), ('dp', 'seq'), scatter_dim...  245 us
    reduce_scatter x1, waiting for transfers between devices, body(): lax.psum_scatter(grad_gate.astype(jnp.bfloat16), ('dp', 'seq'), scatter_d...  245 us
    unnamed x28, waiting for transfers between devices  219 us
    reduce_scatter x1, waiting for transfers between devices, body(): lax.psum_scatter(grad_v.astype(jnp.bfloat16), ('dp', 'seq'), scatter_dime...  180 us
    reduce_scatter x1, waiting for transfers between devices, body(): lax.psum_scatter(grad_gate_mix.astype(jnp.bfloat16), ('dp', 'seq'), scatt...  180 us
    dot_general x84, matrix products, group_state(): jnp.einsum('lwo,loq->lwq', w_part, memory_state, precision=PRECISE_MODE)  176 us
  transfers between devices with their start and end apart: 30, of which 20 were waited for; matrix products, arithmetic and copies ran while one was open for 35% of the time, Pallas kernels for 0%

commit v1 on v0

--- a/solution.py
+++ b/solution.py
@@ -1,5 +1,6 @@
 import jax
 import jax.numpy as jnp
+import numpy as np
 from jax import lax
 from jax.sharding import PartitionSpec as P
 
@@ -187,6 +188,84 @@
 
 def weight_grad(rows, grads):
     return jnp.einsum("td,tc->dc", rows, grads, preferred_element_type=jnp.float32)
+
+
+STAGES = {"x": ("seq", 0, 1), "y": ("seq", 1, 2), "l": ("dp", 0, 4), "h": ("dp", 1, 8)}
+
+
+def trade(value, stage):
+    axis, bit, _ = STAGES[stage]
+    count = lax.axis_size(axis)
+    return lax.ppermute(value, axis, [(place, place ^ (1 << bit)) for place in range(count)])
+
+
+def relative_order(rows, order):
+    own = lax.axis_index("dp") * lax.axis_size("seq") + lax.axis_index("seq")
+    width = rows.shape[1] // 16
+    parts = []
+    for place in range(16):
+        mask = sum(STAGES[stage][2] for k, stage in enumerate(order) if place >> (3 - k) & 1)
+        parts.append(lax.dynamic_slice_in_dim(rows, (own ^ mask) * width, width, 1))
+    return jnp.concatenate(parts, axis=1)
+
+
+def low(value):
+    return value.astype(jnp.bfloat16)
+
+
+def high(value):
+    return value.astype(jnp.float32)
+
+
+def scattered_grad(rows, grads, order):
+    width = rows.shape[1] // 16
+    first = trade(low(weight_grad(rows[:, 8 * width :], grads)), order[0])
+    second = trade(
+        low(weight_grad(rows[:, 4 * width : 8 * width], grads) + high(first[4 * width :])), order[1]
+    )
+    rest = weight_grad(rows[:, : 4 * width], grads) + high(first[: 4 * width])
+    third = trade(low(rest[2 * width :] + high(second[2 * width :])), order[2])
+    rest = rest[: 2 * width] + high(second[: 2 * width])
+    fourth = trade(low(rest[width:] + high(third[width:])), order[3])
+    return rest[:width] + high(third[:width]) + high(fourth)
+
+
+def sum_all(value):
+    for stage in "xylh":
+        value = value + trade(value, stage)
+    return value
+
+
+def heads_gather(rows):
+    count = lax.axis_size("heads")
+    own = lax.axis_index("heads")
+    step = 1
+    while step < count:
+        other = lax.ppermute(rows, "heads", [(place, place ^ step) for place in range(count)])
+        size = rows.shape[0]
+        upper = lax.rem(own // step, 2)
+        both = jnp.zeros((2 * size,) + rows.shape[1:], rows.dtype)
+        both = lax.dynamic_update_slice_in_dim(both, rows, upper * size, 0)
+        rows = lax.dynamic_update_slice_in_dim(both, other, (1 - upper) * size, 0)
+        step *= 2
+    return rows
+
+
+def heads_sum(compute, count, kind):
+    if lax.axis_size("heads") != 2:
+        whole = compute(lambda rows: rows).astype(kind)
+        return high(lax.psum_scatter(whole, "heads", scatter_dimension=0, tiled=True))
+    own = lax.axis_index("heads")
+    half = count // 2
+
+    def part(which):
+        return compute(lambda rows: lax.dynamic_slice_in_dim(rows, which * half, half, 0))
+
+    got = lax.ppermute(part(1 - own).astype(kind), "heads", [(0, 1), (1, 0)])
+    return part(own) + high(got)
+
+
+ORDERS = ("xylh", "ylxh", "lxyh")
 
 
 def body(
@@ -215,8 +294,8 @@
     resid = hidden_in[0].astype(jnp.float32)
     normed_own = rms_scale(resid, norm_gain).astype(jnp.bfloat16)
     normed, cotangent = (
-        lax.all_gather(normed_own, "heads", axis=0, tiled=True),
-        lax.all_gather(out_cotangent[0], "heads", axis=0, tiled=True),
+        heads_gather(normed_own),
+        heads_gather(out_cotangent[0]),
     )
     span = normed.shape[0]
     taps = conv_q.shape[0]
@@ -290,41 +369,37 @@
     )
     gated, gate_pull = jax.vjp(gate_piece, mixed, gate_proj, out_gain)
     gated_low = gated.astype(jnp.bfloat16)
-    mixer = lax.psum_scatter(
-        rows_product(gated_low, out_weight), "heads", scatter_dimension=0, tiled=True
+    mixer = heads_sum(
+        lambda pick: rows_product(pick(gated_low), out_weight), span, jnp.float32
     )
     resid_mid = resid + mixer
     ffn_own = rms_scale(resid_mid, ffn_gain).astype(jnp.bfloat16)
-    ffn_in = lax.all_gather(ffn_own, "heads", axis=0, tiled=True)
+    ffn_in = heads_gather(ffn_own)
     gate_ffn = project(ffn_in, ffn_gate)
     up_ffn = project(ffn_in, ffn_up)
     act, act_pull = jax.vjp(swish_product, gate_ffn, up_ffn)
     act_low = act.astype(jnp.bfloat16)
-    ffn_out = lax.psum_scatter(
-        rows_product(act_low, ffn_down).astype(jnp.bfloat16),
-        "heads",
-        scatter_dimension=0,
-        tiled=True,
-    ).astype(jnp.float32)
+    ffn_out = heads_sum(lambda pick: rows_product(pick(act_low), ffn_down), span, jnp.bfloat16)
     output = (resid_mid + ffn_out).astype(jnp.bfloat16)
     d_act = jnp.einsum("td,fd->tf", cotangent, ffn_down, preferred_element_type=jnp.float32)
     d_gate_ffn, d_up_ffn = act_pull(d_act)
     d_gate_low = d_gate_ffn.astype(jnp.bfloat16)
     d_up_low = d_up_ffn.astype(jnp.bfloat16)
-    grad_down = jnp.einsum("tf,td->fd", act_low, cotangent, preferred_element_type=jnp.float32)
-    grad_gate = weight_grad(ffn_in, d_gate_low)
-    grad_up = weight_grad(ffn_in, d_up_low)
-    d_ffn = lax.psum_scatter(
-        rows_back(d_gate_low, ffn_gate) + rows_back(d_up_low, ffn_up),
-        "heads",
-        scatter_dimension=0,
-        tiled=True,
+    ffn_rel = {order: relative_order(ffn_in, order) for order in ORDERS[:2]}
+    cotangent_rel = relative_order(cotangent, ORDERS[2])
+    grad_gate = scattered_grad(ffn_rel[ORDERS[0]], d_gate_low, ORDERS[0])
+    grad_up = scattered_grad(ffn_rel[ORDERS[1]], d_up_low, ORDERS[1])
+    grad_down = scattered_grad(cotangent_rel, act_low, ORDERS[2]).T
+    d_ffn = heads_sum(
+        lambda pick: rows_back(pick(d_gate_low), ffn_gate) + rows_back(pick(d_up_low), ffn_up),
+        span,
+        jnp.float32,
     )
     _, ffn_norm_pull = jax.vjp(rms_scale, resid_mid, ffn_gain)
     d_mid_norm, d_ffn_gain = ffn_norm_pull(d_ffn)
     d_mid = out_cotangent[0].astype(jnp.float32) + d_mid_norm
-    d_mid_all = lax.all_gather(d_mid.astype(jnp.bfloat16), "heads", axis=0, tiled=True)
-    grad_out = weight_grad(gated_low, d_mid_all)
+    d_mid_all = heads_gather(low(d_mid))
+    grad_out = scattered_grad(relative_order(d_mid_all, ORDERS[2]), gated_low, ORDERS[2]).T
     d_gated = jnp.einsum("td,cd->tc", d_mid_all, out_weight, preferred_element_type=jnp.float32)
     d_mixed, d_gate_proj, d_out_gain = gate_pull(d_gated)
     local_back = span_pull((jnp.zeros_like(end_state), d_mixed))[0]
@@ -339,92 +414,82 @@
     d_decay_low = ext_grads[3].astype(jnp.bfloat16)
     d_beta_low = ext_grads[4].astype(jnp.bfloat16)
     d_gate_low_mix = d_gate_proj.astype(jnp.bfloat16)
-    grad_q = weight_grad(normed, d_q_low)
-    grad_k = weight_grad(normed, d_k_low)
-    grad_v = weight_grad(normed, d_v_low)
-    grad_gate_mix = weight_grad(normed, d_gate_low_mix)
-    grad_decay = weight_grad(normed, d_decay_low)
-    grad_beta = weight_grad(normed, d_beta_low)
-    total = rows_back(d_q_low, q_weight) + rows_back(d_k_low, k_weight)
-    total = total + rows_back(d_v_low, v_weight) + rows_back(d_gate_low_mix, gate_weight)
-    total = total + rows_back(d_decay_low, decay_weight) + rows_back(d_beta_low, beta_weight)
-    d_normed = lax.psum_scatter(
-        total.astype(jnp.bfloat16), "heads", scatter_dimension=0, tiled=True
-    ).astype(jnp.float32)
+    normed_rel = {order: relative_order(normed, order) for order in ORDERS}
+    grad_gate_mix = jnp.concatenate(
+        [
+            scattered_grad(normed_rel[ORDERS[0]], d_gate_low_mix[:, : d_gate_low_mix.shape[1] // 2], ORDERS[0]),
+            scattered_grad(normed_rel[ORDERS[1]], d_gate_low_mix[:, d_gate_low_mix.shape[1] // 2 :], ORDERS[1]),
+        ],
+        axis=1,
+    )
+    mix_low = jnp.concatenate([d_q_low, d_k_low, d_v_low, d_decay_low, d_beta_low], axis=1)
+    width_q = d_q_low.shape[1]
+    width_v = d_v_low.shape[1]
+    cuts = (0, 4 * width_q // 3 // 128 * 128, 8 * width_q // 3 // 128 * 128, mix_low.shape[1])
+    grad_mix = jnp.concatenate(
+        [
+            scattered_grad(normed_rel[order], mix_low[:, cuts[k] : cuts[k + 1]], order)
+            for k, order in enumerate(ORDERS)
+        ],
+        axis=1,
+    )
+    heads_here = d_decay_low.shape[1]
+    ends = (width_q, 2 * width_q, 2 * width_q + width_v, 2 * width_q + width_v + heads_here)
+    grad_q, grad_k, grad_v, grad_decay, grad_beta = jnp.split(grad_mix, ends, axis=1)
+    pairs = (
+        (d_q_low, q_weight),
+        (d_k_low, k_weight),
+        (d_v_low, v_weight),
+        (d_gate_low_mix, gate_weight),
+        (d_decay_low, decay_weight),
+        (d_beta_low, beta_weight),
+    )
+    d_normed = heads_sum(
+        lambda pick: sum(rows_back(pick(rows), weight) for rows, weight in pairs),
+        span,
+        jnp.bfloat16,
+    )
     _, in_norm_pull = jax.vjp(rms_scale, resid, norm_gain)
     d_in_norm, d_norm_gain = in_norm_pull(d_normed)
     input_grad = d_mid + d_in_norm
-    head_index = lax.axis_index("heads")
-
-    def widen(part, total):
-        full = jnp.zeros(part.shape[:-1] + (total,), jnp.float32)
-        return lax.dynamic_update_slice_in_dim(
-            full, part, head_index * part.shape[-1], part.ndim - 1
+    shared = (d_norm_gain, d_ffn_gain, d_out_gain)
+    owned = (
+        ext_grads[8],
+        ext_grads[9],
+        ext_grads[5].reshape(-1),
+        ext_grads[6].reshape(-1),
+        ext_grads[7].reshape(-1),
+    )
+    flat = sum_all(jnp.concatenate(shared + owned))
+    everyone = heads_gather(flat[None])
+    marks = np.cumsum([part.size for part in shared + owned])
+    pieces = jnp.split(everyone, marks[:-1], axis=1)
+    small = [piece.sum(0) for piece in pieces[:3]] + [pieces[3].reshape(-1), pieces[4].reshape(-1)]
+    for piece in pieces[5:]:
+        small.append(
+            jnp.swapaxes(piece.reshape(piece.shape[0], taps, -1), 0, 1).reshape(taps, -1)
         )
-
-    small = lax.psum(
-        (
-            d_norm_gain,
-            d_ffn_gain,
-            d_out_gain,
-            widen(ext_grads[8], HEADS),
-            widen(ext_grads[9], HEADS),
-            widen(ext_grads[5], HEADS * DK),
-            widen(ext_grads[6], HEADS * DK),
-            widen(ext_grads[7], HEADS * DV),
-        ),
-        ("dp", "seq", "heads"),
-    )
-    mixer_sums = (
-        lax.psum_scatter(
-            grad_q.astype(jnp.bfloat16), ("dp", "seq"), scatter_dimension=0, tiled=True
-        ).astype(jnp.float32),
-        lax.psum_scatter(
-            grad_k.astype(jnp.bfloat16), ("dp", "seq"), scatter_dimension=0, tiled=True
-        ).astype(jnp.float32),
-        lax.psum_scatter(
-            grad_v.astype(jnp.bfloat16), ("dp", "seq"), scatter_dimension=0, tiled=True
-        ).astype(jnp.float32),
-        lax.psum_scatter(
-            grad_gate_mix.astype(jnp.bfloat16), ("dp", "seq"), scatter_dimension=0, tiled=True
-        ).astype(jnp.float32),
-        lax.psum_scatter(
-            grad_decay.astype(jnp.bfloat16), ("dp", "seq"), scatter_dimension=0, tiled=True
-        ).astype(jnp.float32),
-        lax.psum_scatter(
-            grad_beta.astype(jnp.bfloat16), ("dp", "seq"), scatter_dimension=0, tiled=True
-        ).astype(jnp.float32),
-        lax.psum_scatter(
-            grad_out.astype(jnp.bfloat16), ("dp", "seq"), scatter_dimension=1, tiled=True
-        ).astype(jnp.float32),
-    )
     return (
         output[None],
         input_grad[None],
         small[0],
-        mixer_sums[0],
-        mixer_sums[1],
-        mixer_sums[2],
-        mixer_sums[3],
-        mixer_sums[4],
-        mixer_sums[5],
+        grad_q,
+        grad_k,
+        grad_v,
+        grad_gate_mix,
+        grad_decay,
+        grad_beta,
         small[5],
         small[6],
         small[7],
         small[3],
         small[4],
         small[2],
-        mixer_sums[6],
+        grad_out,
         small[1],
-        lax.psum_scatter(
-            grad_gate.astype(jnp.bfloat16), ("dp", "seq"), scatter_dimension=0, tiled=True
-        ).astype(jnp.float32),
-        lax.psum_scatter(
-            grad_up.astype(jnp.bfloat16), ("dp", "seq"), scatter_dimension=0, tiled=True
-        ).astype(jnp.float32),
-        lax.psum_scatter(
-            grad_down.astype(jnp.bfloat16), ("dp", "seq"), scatter_dimension=1, tiled=True
-        ).astype(jnp.float32),
+        grad_gate,
+        grad_up,
+        grad_down,
     )
 
 

time: 3740 us -> 2660 us (0.71)
  waiting for transfers between devices: 1680 us -> 425 us
  matrix products: 904 us -> 978 us
  starting transfers between devices: 17.3 us -> 67.9 us
    reduce_scatter x10 -> x0, waiting for transfers between devices: 1100 us -> none  [the longest x1 245 us: body(): lax.psum_scatter(grad_up.astype(jnp.bfloat16), ('dp', 'seq'), scatter_dim...]
    ppermute x0 -> x49, waiting for transfers between devices: none -> 378 us  [the longest x40 378 us: trade(): lax.ppermute(value, axis, [(place, place ^ 1 << bit) for place in range(c...]
    psum x2 -> x0, waiting for transfers between devices: 256 us -> none  [body(): lax.psum((d_norm_gain, d_ffn_gain, d_out_gain, widen(ext_grads[8], HEADS)...]
    unnamed x28 -> x4, waiting for transfers between devices: 219 us -> 0.07 us
    dot_general x9 -> x27, matrix products: 80.6 us -> 141 us  [weight_grad(): jnp.einsum('td,tc->dc', rows, grads, preferred_element_type=jnp.float32)]
    ppermute x0 -> x49, starting transfers between devices: none -> 51.1 us  [the longest x40 49.4 us: trade(): lax.ppermute(value, axis, [(place, place ^ 1 << bit) for place in range(c...]
    dot_general x8 -> x16, matrix products: 84.2 us -> 121 us  [rows_back(): jnp.einsum('tc,dc->td', left, weight, preferred_element_type=jnp.float32)]
    unnamed x463 -> x786, local copies, waits for them, and re-layouts: 122 us -> 104 us
  transfers between devices with their start and end apart: 30 -> 59, of which waited for: 20 -> 17; matrix products, arithmetic and copies ran while one was open for 35% -> 78% of each run, Pallas kernels for 0% -> 0%
where the time goes in v1:
time: 2660 us; the launch traced here: 2640 us
  matrix products  978 us (37%)
  other arithmetic  724 us (27%)
  waiting for transfers between devices  425 us (16%)
  local copies, waits for them, and re-layouts  420 us (16%)
  starting transfers between devices  67.9 us (3%)
    another operation x4, other arithmetic, group_local(): jax.scipy.linalg.solve_triangular(unit, right, lower=True, unit_diagonal=...  475 us
    ppermute x40, waiting for transfers between devices, trade(): lax.ppermute(value, axis, [(place, place ^ 1 << bit) for place in range(c...  378 us
    dot_general x84, matrix products, group_state(): jnp.einsum('lwo,loq->lwq', w_part, memory_state, precision=PRECISE_MODE)  176 us
    dot_general x72, matrix products, group_state(): jnp.einsum('biw,bir->bwr', tail_key, delta_update, precision=PRECISE_MODE)  152 us
    dot_general x27, matrix products, weight_grad(): jnp.einsum('td,tc->dc', rows, grads, preferred_element_type=jnp.float32)  141 us
    squeeze x132, local copies, waits for them, and re-layouts, run_span(): final, outs = lax.scan(advance, memory_state, local + (keep,))  134 us
    dot_general x16, matrix products, rows_back(): jnp.einsum('tc,dc->td', left, weight, preferred_element_type=jnp.float32)  121 us
    unnamed x786, local copies, waits for them, and re-layouts  104 us
  transfers between devices with their start and end apart: 59, of which 17 were waited for; matrix products, arithmetic and copies ran while one was open for 78% of the time, Pallas kernels for 0%

profile of v1, /device:TPU:0, one launch (start us, length us, event | category | flops | bytes accessed | tf_op | source)
XLA Modules:
  0.0 2638.3 jit_solution(3994095644160900655)
XLA Ops:
  114.5 473.3 %custom-call.13 = f32[12,8,1,64,64]{3,4,2,1,0:T(8,128)} custom-call(f32[12,8,1,64,64]{4,3,2,1,0:T(8,128)} %get-tuple-element.1593), custom_call_target="InvertDiagBlocksLowerTriangular" | custom-call | tf_op jit(solution)/shard_map/jit(_solve_triangular)/vmap(vmap())/triangular_solve | solution.py:109
  606.3 75.5 %while.107 = (s32[]{:T(128)}, f32[8,128,128]{2,1,0:T(8,128)S(1)}, f32[12,8]{1,0:T(8,128)}, f32[12]{0:T(128)S(1)}, f32[12,8,64,128]{3,2,1,0:T(8,128)}, /*index=5*...) while((s32[]{:T(128)}, f32[8,128,128]{2,1,0:T(8,128)S(1)}, f32[12,8]{1,0:T(8,128)}, ...), condition=%wide.region_4.5_spmd, body=%wide.region_3.4_spmd.sunk | while | flops 201916416 | bytes 2886341 | solution.py:156
  682.8 17.6 fusion.91
  709.0 10.7 fusion.68
  727.3 80.9 %while.111 = (s32[]{:T(128)}, f32[8,128,256]{2,1,0:T(8,128)S(1)}, f32[12,8]{1,0:T(8,128)}, f32[12]{0:T(128)S(1)}, f32[12,8,64,128]{3,2,1,0:T(8,128)}, /*index=5*...) while((s32[]{:T(128)}, f32[8,128,256]{2,1,0:T(8,128)S(1)}, ...), condition=%wide.region_6.8_spmd.clone, body=%wide.region_5.7_spmd.clone.sunk | while | flops 404357120 | bytes 5245656 | solution.py:156
  814.5 46.9 %all-gather.11.cloned.1.call-done = f32[32,128,256]{2,1,0:T(8,128)} async-done(((f32[8,128,256]{2,1,0:T(8,128)}), f32[32,128,256]{2,1,0:T(8,128)}) %all-gather.11.cloned.1.call-update) | async-done | bytes 4194320 | tf_op jit(solution)/shard_map/all_gather | solution.py:25
  861.4 10.6 while.112
  875.5 150.2 %while.108 = (s32[]{:T(128)}, f32[8,128,256]{2,1,0:T(8,128)S(1)}, f32[12,8,64,256]{3,2,1,0:T(8,128)}, f32[12,8,128,256]{3,2,1,0:T(8,128)}, f32[12,8]{1,0:T(8,128...) while((s32[]{:T(128)}, f32[8,128,256]{2,1,0:T(8,128)S(1)}, ...), condition=%wide.region_11.13_spmd, body=%wide.region_10.12_spmd.sunk | while | flops 706215936 | bytes 11015397 | solution.py:156
  1042.0 14.1 multiply_convert_fusion.2
  1114.1 14.9 fusion.382
  1129.0 11.3 fusion.383
  1140.3 23.2 multiply_convert_fusion
  1163.6 10.1 convolution_convert_fusion
  1175.2 11.3 fusion.148
  1186.5 13.9 convolution_add_fusion.18
  1230.0 14.1 multiply_reduce_fusion.16
  1267.4 18.4 fusion.85
  1310.7 115.8 %while.113 = (s32[]{:T(128)}, f32[8,128,256]{2,1,0:T(8,128)S(1)}, f32[12,8,64,128]{3,2,1,0:T(8,128)}, f32[12,8,64,64]{2,3,1,0:T(8,128)}, f32[12,8,64,128]{3,2,1,...) while((s32[]{:T(128)}, f32[8,128,256]{2,1,0:T(8,128)S(1)}, ...), condition=%wide.region_17.19_spmd.clone, body=%wide.region_16.18_spmd.clone.sunk | while | flops 706215936 | bytes 14287119 | solution.py:156
  1529.7 271.1 %while.110 = (s32[]{:T(128)}, f32[8,128,256]{2,1,0:T(8,128)S(1)}, f32[12,8,64,256]{3,2,1,0:T(8,128)}, f32[12,8,64,128]{3,2,1,0:T(8,128)}, f32[12,8,64,64]{3,2,1,...) while((s32[]{:T(128)}, f32[8,128,256]{2,1,0:T(8,128)S(1)}, ...), condition=%wide.region_22.24_spmd, body=%wide.region_20.23_spmd.sunk | while | flops 1613758464 | bytes 27133384 | solution.py:156
  1800.8 11.3 fusion.77
  1857.9 14.0 fusion.76
  1894.2 11.8 add_bitcast_fusion
  2062.9 13.5 add_convert_fusion.4
  2114.5 136.8 %collective-permute-done.34 = bf16[128,1024]{1,0:T(8,128)(2,1)S(1)} collective-permute-done((bf16[128,1024]{1,0:T(8,128)(2,1)S(1)}, bf16[128,1024]{1,0:T(8,128)(2,1)S(1)}, u32[]{:S(2)}, u32[]{:S(2)}) %collective-permute-start.34) | collective-permute-done | bytes 262176 | tf_op jit(solution)/shard_map/ppermute | solution.py:199
  2269.2 14.6 fusion.95
  2296.7 65.6 %collective-permute-done.15 = f32[20752]{0:T(1024)S(1)} collective-permute-done((f32[20752]{0:T(1024)S(1)}, f32[20752]{0:T(1024)S(1)}, u32[]{:S(2)}, u32[]{:S(2)}) %collective-permute-start.15) | collective-permute-done | bytes 83040 | tf_op jit(solution)/shard_map/ppermute | solution.py:199
  2390.6 23.4 collective-permute-done.49
  2450.6 36.4 %collective-permute-done.54 = bf16[128,2816]{1,0:T(8,128)(2,1)S(1)} collective-permute-done((bf16[128,2816]{1,0:T(8,128)(2,1)S(1)}, bf16[128,2816]{1,0:T(8,128)(2,1)S(1)}, u32[]{:S(2)}, u32[]{:S(2)}) %collective-permute-start.54) | collective-permute-done | bytes 720928 | tf_op jit(solution)/shard_map/ppermute | solution.py:199
  2489.5 13.1 collective-permute-done.50
  2532.7 26.3 collective-permute-done.24
  2578.7 12.4 collective-permute-done.22
  2599.3 21.4 collective-permute-done.26
  (1725 shorter events, 1541.6 us)
Async XLA Ops:
  7.2 807.3 %all-gather.9.cloned.1.call-start = ((), (), s32[]{:S(2)}) async-start(), calls=%async_computation | async-start | bytes 2621440 | tf_op jit(solution)/shard_map/all_gather | solution.py:25
  36.5 646.2 %collective-permute-start.2 = (f32[3,2048]{1,0:T(4,128)}, f32[3,2048]{1,0:T(4,128)}, u32[]{:S(2)}, u32[]{:S(2)}) collective-permute-start(f32[3,2048]{1,0:T(4,128)} %slice.703), channel_id=1, source_target_pairs={{0,2},{2,4},{4,6},{1,3},{3,5},{5,7},{8,10},{10,12},{12,14},{9,11},... | collective-permute-start | bytes 73736 | tf_op jit(solution)/shard_map/ppermute | solution.py:20
  682.6 178.8 %all-gather.11.cloned.1.call-start = ((), (), s32[]{:S(2)}) async-start(), calls=%async_computation.1 | async-start | bytes 5242880 | tf_op jit(solution)/shard_map/all_gather | solution.py:25
  809.2 702.4 %all-gather.13.cloned.1.call-start = ((), (), s32[]{:S(2)}) async-start(), calls=%async_computation.2 | async-start | bytes 1310720 | tf_op jit(solution)/shard_map/all_gather | solution.py:45
  809.2 258.5 %collective-permute-start.7 = (bf16[384,2048]{1,0:T(8,128)(2,1)}, bf16[384,2048]{1,0:T(8,128)(2,1)}, u32[]{:S(2)}, u32[]{:S(2)}) collective-permute-start(bf16[384,2048]{1,0:T(8,128)(2,1)} %bitcast.63), channel_id=1, source_target_pairs={{0,1},{1,0},{2,3},{3,2},{4,5},{5,4},{6,7},{7,6},{8,9},{9,8},{10,11... | collective-permute-start | bytes 4718600 | tf_op jit(solution)/shard_map/ppermute | solution.py:244
  1102.4 409.2 %all-gather.15.cloned.1.call-start = ((), (), s32[]{:S(2)}) async-start(), calls=%async_computation.3 | async-start | bytes 2621440 | tf_op jit(solution)/shard_map/all_gather | solution.py:45
  1173.7 279.8 %collective-permute-start.51 = (bf16[1024,2816]{1,0:T(8,128)(2,1)}, bf16[1024,2816]{1,0:T(8,128)(2,1)}, u32[]{:S(2)}, u32[]{:S(2)}) collective-permute-start(bf16[1024,2816]{1,0:T(8,128)(2,1)} %convolution_convert_fusion), channel_id=1, source_target_pairs={{0,8},{8,0},{16,24},{24,16},{1,9},{9,1},{17,25},{25,17},{2,10},{10... | collective-permute-start | bytes 17301512 | tf_op jit(solution)/shard_map/ppermute | solution.py:199
  1212.7 248.2 %collective-permute-start.47 = (bf16[1024,2816]{1,0:T(8,128)(2,1)}, bf16[1024,2816]{1,0:T(8,128)(2,1)}, u32[]{:S(2)}, u32[]{:S(2)}) collective-permute-start(bf16[1024,2816]{1,0:T(8,128)(2,1)} %convolution_convert_fusion.1), channel_id=1, source_target_pairs={{0,4},{2,6},{4,0},{6,2},{1,5},{3,7},{5,1},{7,3},{8,12},{10,14},{12... | collective-permute-start | bytes 17301512 | tf_op jit(solution)/shard_map/ppermute | solution.py:199
  1258.5 208.9 %collective-permute-start.43 = (bf16[1024,2816]{1,0:T(8,128)(2,1)}, bf16[1024,2816]{1,0:T(8,128)(2,1)}, u32[]{:S(2)}, u32[]{:S(2)}) collective-permute-start(bf16[1024,2816]{1,0:T(8,128)(2,1)} %convolution_convert_fusion.2), channel_id=1, source_target_pairs={{0,2},{2,0},{4,6},{6,4},{1,3},{3,1},{5,7},{7,5},{8,10},{10,8},{12,... | collective-permute-start | bytes 17301512 | tf_op jit(solution)/shard_map/ppermute | solution.py:199
  1290.5 204.5 %collective-permute-start.31 = (bf16[1024,1024]{1,0:T(8,128)(2,1)}, bf16[1024,1024]{1,0:T(8,128)(2,1)}, u32[]{:S(2)}, u32[]{:S(2)}) collective-permute-start(bf16[1024,1024]{1,0:T(8,128)(2,1)} %convolution_convert_fusion.9), channel_id=1, source_target_pairs={{0,2},{2,0},{4,6},{6,4},{1,3},{3,1},{5,7},{7,5},{8,10},{10,8},{12,... | collective-permute-start | bytes 6291464 | tf_op jit(solution)/shard_map/ppermute | solution.py:199
  1296.6 203.0 %collective-permute-start.35 = (bf16[1024,1024]{1,0:T(8,128)(2,1)}, bf16[1024,1024]{1,0:T(8,128)(2,1)}, u32[]{:S(2)}, u32[]{:S(2)}) collective-permute-start(bf16[1024,1024]{1,0:T(8,128)(2,1)} %convolution_convert_fusion.8), channel_id=1, source_target_pairs={{0,4},{2,6},{4,0},{6,2},{1,5},{3,7},{5,1},{7,3},{8,12},{10,14},{12... | collective-permute-start | bytes 6291464 | tf_op jit(solution)/shard_map/ppermute | solution.py:199
  1459.6 637.9 %collective-permute-start.52 = (bf16[512,2816]{1,0:T(8,128)(2,1)}, bf16[512,2816]{1,0:T(8,128)(2,1)}, u32[]{:S(2)}, u32[]{:S(2)}) collective-permute-start(bf16[512,2816]{1,0:T(8,128)(2,1)} %add_convert_fusion), channel_id=1, source_target_pairs={{0,2},{2,0},{4,6},{6,4},{1,3},{3,1},{5,7},{7,5},{8,10},{10,8},{12,... | collective-permute-start | bytes 8650760 | tf_op jit(solution)/shard_map/ppermute | solution.py:199
  1466.9 635.9 %collective-permute-start.48 = (bf16[512,2816]{1,0:T(8,128)(2,1)}, bf16[512,2816]{1,0:T(8,128)(2,1)}, u32[]{:S(2)}, u32[]{:S(2)}) collective-permute-start(bf16[512,2816]{1,0:T(8,128)(2,1)} %add_convert_fusion.1), channel_id=1, source_target_pairs={{0,8},{8,0},{16,24},{24,16},{1,9},{9,1},{17,25},{25,17},{2,10},{10... | collective-permute-start | bytes 8650760 | tf_op jit(solution)/shard_map/ppermute | solution.py:199
  1473.6 633.9 %collective-permute-start.44 = (bf16[512,2816]{1,0:T(8,128)(2,1)}, bf16[512,2816]{1,0:T(8,128)(2,1)}, u32[]{:S(2)}, u32[]{:S(2)}) collective-permute-start(bf16[512,2816]{1,0:T(8,128)(2,1)} %add_convert_fusion.2), channel_id=1, source_target_pairs={{0,4},{2,6},{4,0},{6,2},{1,5},{3,7},{5,1},{7,3},{8,12},{10,14},{12... | collective-permute-start | bytes 8650760 | tf_op jit(solution)/shard_map/ppermute | solution.py:199
  1498.4 476.8 %collective-permute-start.32 = (bf16[512,1024]{1,0:T(8,128)(2,1)}, bf16[512,1024]{1,0:T(8,128)(2,1)}, u32[]{:S(2)}, u32[]{:S(2)}) collective-permute-start(bf16[512,1024]{1,0:T(8,128)(2,1)} %add_convert_fusion.7), channel_id=1, source_target_pairs={{0,4},{2,6},{4,0},{6,2},{1,5},{3,7},{5,1},{7,3},{8,12},{10,14},{12... | collective-permute-start | bytes 3145736 | tf_op jit(solution)/shard_map/ppermute | solution.py:199
  1502.9 507.5 %collective-permute-start.36 = (bf16[512,1024]{1,0:T(8,128)(2,1)}, bf16[512,1024]{1,0:T(8,128)(2,1)}, u32[]{:S(2)}, u32[]{:S(2)}) collective-permute-start(bf16[512,1024]{1,0:T(8,128)(2,1)} %add_convert_fusion.6), channel_id=1, source_target_pairs={{0,8},{8,0},{16,24},{24,16},{1,9},{9,1},{17,25},{25,17},{2,10},{10... | collective-permute-start | bytes 3145736 | tf_op jit(solution)/shard_map/ppermute | solution.py:199
  1977.9 115.7 %collective-permute-start.33 = (bf16[256,1024]{1,0:T(8,128)(2,1)}, bf16[256,1024]{1,0:T(8,128)(2,1)}, u32[]{:S(2)}, u32[]{:S(2)}) collective-permute-start(bf16[256,1024]{1,0:T(8,128)(2,1)} %get-tuple-element.1558), channel_id=1, source_target_pairs={{0,8},{8,0},{16,24},{24,16},{1,9},{9,1},{17,25},{25,17},{2,10},{10... | collective-permute-start | bytes 1572872 | tf_op jit(solution)/shard_map/ppermute | solution.py:199
  2093.7 194.8 %collective-permute-start.39 = (bf16[1024,2048]{1,0:T(8,128)(2,1)}, bf16[1024,2048]{1,0:T(8,128)(2,1)}, u32[]{:S(2)}, u32[]{:S(2)}) collective-permute-start(bf16[1024,2048]{1,0:T(8,128)(2,1)} %convolution_convert_fusion.6), channel_id=1, source_target_pairs={{0,8},{8,0},{16,24},{24,16},{1,9},{9,1},{17,25},{25,17},{2,10},{10... | collective-permute-start | bytes 12582920 | tf_op jit(solution)/shard_map/ppermute | solution.py:199
  2096.4 325.9 %collective-permute-start.19 = (bf16[1024,1280]{1,0:T(8,128)(2,1)}, bf16[1024,1280]{1,0:T(8,128)(2,1)}, u32[]{:S(2)}, u32[]{:S(2)}) collective-permute-start(bf16[1024,1280]{1,0:T(8,128)(2,1)} %convolution_convert_fusion.5), channel_id=1, source_target_pairs={{0,2},{2,0},{4,6},{6,4},{1,3},{3,1},{5,7},{7,5},{8,10},{10,8},{12,... | collective-permute-start | bytes 7864328 | tf_op jit(solution)/shard_map/ppermute | solution.py:199
  2097.5 342.6 %collective-permute-start.27 = (bf16[1024,1424]{0,1:T(8,128)(2,1)}, bf16[1024,1424]{0,1:T(8,128)(2,1)}, u32[]{:S(2)}, u32[]{:S(2)}) collective-permute-start(bf16[1024,1424]{0,1:T(8,128)(2,1)} %convolution_convert_fusion.3), channel_id=1, source_target_pairs={{0,8},{8,0},{16,24},{24,16},{1,9},{9,1},{17,25},{25,17},{2,10},{10... | collective-permute-start | bytes 8749064 | tf_op jit(solution)/shard_map/ppermute | solution.py:199
  2102.8 166.3 %collective-permute-start.13 = (bf16[384,2048]{1,0:T(8,128)(2,1)S(1)}, bf16[384,2048]{1,0:T(8,128)(2,1)}, u32[]{:S(2)}, u32[]{:S(2)}) collective-permute-start(bf16[384,2048]{1,0:T(8,128)(2,1)S(1)} %copy-done.306), channel_id=1, source_target_pairs={{0,1},{1,0},{2,3},{3,2},{4,5},{5,4},{6,7},{7,6},{8,9},{9,8},{10,11... | collective-permute-start | bytes 4718600 | tf_op jit(solution)/shard_map/ppermute | solution.py:264
  2107.6 143.7 %collective-permute-start.34 = (bf16[128,1024]{1,0:T(8,128)(2,1)S(1)}, bf16[128,1024]{1,0:T(8,128)(2,1)S(1)}, u32[]{:S(2)}, u32[]{:S(2)}) collective-permute-start(bf16[128,1024]{1,0:T(8,128)(2,1)S(1)} %fusion.295), channel_id=1, source_target_pairs={{0,16},{8,24},{16,0},{24,8},{1,17},{9,25},{17,1},{25,9},{2,18},{10... | collective-permute-start | bytes 786440 | tf_op jit(solution)/shard_map/ppermute | solution.py:199
  2264.9 167.4 %collective-permute-start.23 = (bf16[1024,1408]{1,0:T(8,128)(2,1)}, bf16[1024,1408]{1,0:T(8,128)(2,1)}, u32[]{:S(2)}, u32[]{:S(2)}) collective-permute-start(bf16[1024,1408]{1,0:T(8,128)(2,1)} %convolution_convert_fusion.4), channel_id=1, source_target_pairs={{0,4},{2,6},{4,0},{6,2},{1,5},{3,7},{5,1},{7,3},{8,12},{10,14},{12... | collective-permute-start | bytes 8650760 | tf_op jit(solution)/shard_map/ppermute | solution.py:199
  2288.4 98.8 %collective-permute-start.53 = (bf16[256,2816]{1,0:T(8,128)(2,1)}, bf16[256,2816]{1,0:T(8,128)(2,1)}, u32[]{:S(2)}, u32[]{:S(2)}) collective-permute-start(bf16[256,2816]{1,0:T(8,128)(2,1)} %get-tuple-element.1500), channel_id=1, source_target_pairs={{0,4},{2,6},{4,0},{6,2},{1,5},{3,7},{5,1},{7,3},{8,12},{10,14},{12... | collective-permute-start | bytes 4325384 | tf_op jit(solution)/shard_map/ppermute | solution.py:199
  2288.5 73.8 %collective-permute-start.15 = (f32[20752]{0:T(1024)S(1)}, f32[20752]{0:T(1024)S(1)}, u32[]{:S(2)}, u32[]{:S(2)}) collective-permute-start(f32[20752]{0:T(1024)S(1)} %add.901), channel_id=1, source_target_pairs={{0,4},{2,6},{4,0},{6,2},{1,5},{3,7},{5,1},{7,3},{8,12},{10,14},{12... | collective-permute-start | bytes 249032 | tf_op jit(solution)/shard_map/ppermute | solution.py:199
  2414.0 92.0 %collective-permute-start.40 = (bf16[512,2048]{1,0:T(8,128)(2,1)}, bf16[512,2048]{1,0:T(8,128)(2,1)S(1)}, u32[]{:S(2)}, u32[]{:S(2)}) collective-permute-start(bf16[512,2048]{1,0:T(8,128)(2,1)} %add_convert_fusion.3), channel_id=1, source_target_pairs={{0,2},{2,0},{4,6},{6,4},{1,3},{3,1},{5,7},{7,5},{8,10},{10,8},{12,... | collective-permute-start | bytes 6291464 | tf_op jit(solution)/shard_map/ppermute | solution.py:199
  2421.1 65.9 %collective-permute-start.54 = (bf16[128,2816]{1,0:T(8,128)(2,1)S(1)}, bf16[128,2816]{1,0:T(8,128)(2,1)S(1)}, u32[]{:S(2)}, u32[]{:S(2)}) collective-permute-start(bf16[128,2816]{1,0:T(8,128)(2,1)S(1)} %fusion.193), channel_id=1, source_target_pairs={{0,16},{8,24},{16,0},{24,8},{1,17},{9,25},{17,1},{25,9},{2,18},{10... | collective-permute-start | bytes 2162696 | tf_op jit(solution)/shard_map/ppermute | solution.py:199
  2422.3 80.3 %collective-permute-start.50 = (bf16[128,2816]{1,0:T(8,128)(2,1)S(1)}, bf16[128,2816]{1,0:T(8,128)(2,1)S(1)}, u32[]{:S(2)}, u32[]{:S(2)}) collective-permute-start(bf16[128,2816]{1,0:T(8,128)(2,1)S(1)} %fusion.196), channel_id=1, source_target_pairs={{0,16},{8,24},{16,0},{24,8},{1,17},{9,25},{17,1},{25,9},{2,18},{10... | collective-permute-start | bytes 2162696 | tf_op jit(solution)/shard_map/ppermute | solution.py:199
  2432.2 84.5 %collective-permute-start.46 = (bf16[128,2816]{1,0:T(8,128)(2,1)S(1)}, bf16[128,2816]{1,0:T(8,128)(2,1)S(1)}, u32[]{:S(2)}, u32[]{:S(2)}) collective-permute-start(bf16[128,2816]{1,0:T(8,128)(2,1)S(1)} %fusion.198), channel_id=1, source_target_pairs={{0,16},{8,24},{16,0},{24,8},{1,17},{9,25},{17,1},{25,9},{2,18},{10... | collective-permute-start | bytes 2162696 | tf_op jit(solution)/shard_map/ppermute | solution.py:199
  2440.2 80.8 %collective-permute-start.20 = (bf16[512,1280]{1,0:T(8,128)(2,1)}, bf16[512,1280]{1,0:T(8,128)(2,1)}, u32[]{:S(2)}, u32[]{:S(2)}) collective-permute-start(bf16[512,1280]{1,0:T(8,128)(2,1)} %fusion.139), channel_id=1, source_target_pairs={{0,4},{2,6},{4,0},{6,2},{1,5},{3,7},{5,1},{7,3},{8,12},{10,14},{12... | collective-permute-start | bytes 3932168 | tf_op jit(solution)/shard_map/ppermute | solution.py:199
  2487.0 72.0 %collective-permute-start.24 = (bf16[512,1408]{1,0:T(8,128)(2,1)}, bf16[512,1408]{1,0:T(8,128)(2,1)}, u32[]{:S(2)}, u32[]{:S(2)}) collective-permute-start(bf16[512,1408]{1,0:T(8,128)(2,1)} %fusion.138), channel_id=1, source_target_pairs={{0,8},{8,0},{16,24},{24,16},{1,9},{9,1},{17,25},{25,17},{2,10},{10... | collective-permute-start | bytes 4325384 | tf_op jit(solution)/shard_map/ppermute | solution.py:199
  2502.6 60.5 %collective-permute-start.28 = (bf16[512,1424]{0,1:T(8,128)(2,1)}, bf16[512,1424]{0,1:T(8,128)(2,1)}, u32[]{:S(2)}, u32[]{:S(2)}) collective-permute-start(bf16[512,1424]{0,1:T(8,128)(2,1)} %fusion.137), channel_id=1, source_target_pairs={{0,2},{2,0},{4,6},{6,4},{1,3},{3,1},{5,7},{7,5},{8,10},{10,8},{12,... | collective-permute-start | bytes 4374536 | tf_op jit(solution)/shard_map/ppermute | solution.py:199
  (392 other events, 10230.9 us)
Sparse Core Ops, SparseCore 0:
  682.7 34.6 all-gather.8
  809.3 52.0 all-gather.10
  1102.6 26.6 all-gather.12
  1427.5 34.3 all-gather.14

commit v2 on v1

v2 whole, which is shorter than its diff:
```python
import functools

import jax
import jax.numpy as jnp
import numpy as np
from jax import lax
from jax.experimental import pallas as pl
from jax.experimental.pallas import tpu as pltpu
from jax.sharding import PartitionSpec as P

HEADS = 16
DK = 128
DV = 256
GROUP = 64
EPS = 1e-06
PAIR = 2 * GROUP
RIM = 8
VMEM_BYTES = 56 * 1024 * 1024


def mm(left, right):
    return lax.dot_general(
        left, right, (((1,), (0,)), ((), ())), preferred_element_type=jnp.float32
    )


def mm_nt(left, right):
    return lax.dot_general(
        left, right, (((1,), (1,)), ((), ())), preferred_element_type=jnp.float32
    )


def mm_tn(left, right):
    return lax.dot_general(
        left, right, (((0,), (0,)), ((), ())), preferred_element_type=jnp.float32
    )


def low(value):
    return value.astype(jnp.bfloat16)


def high(value):
    return value.astype(jnp.float32)


def grid_masks():
    row = lax.broadcasted_iota(jnp.int32, (PAIR, PAIR), 0)
    col = lax.broadcasted_iota(jnp.int32, (PAIR, PAIR), 1)
    same = (row // GROUP) == (col // GROUP)
    return row, col, same & (row >= col), same & (row > col)


def unit_inverse(lower, row, col):
    inverse = jnp.where(row == col, 1.0, 0.0)
    size = 1
    while size < GROUP:
        here = ((row // (2 * size)) == (col // (2 * size))) & ((row // size) > (col // size))
        part = jnp.where(here, lower, 0.0)
        if size == 1:
            inverse = inverse - part
        else:
            inv_low = low(inverse)
            inverse = inverse - mm(inv_low, low(mm(low(part), inv_low)))
        size *= 2
    return inverse


def ranges(base, first, count):
    token = base + lax.broadcasted_iota(jnp.int32, (count, 1), 0)
    return token - jnp.where(token >= first, first, 0)


def conv_sum(ext, width, weight, place, taps):
    count = place.shape[0]
    total = None
    for tap in range(taps):
        rows = ext[RIM - taps + 1 + tap : RIM - taps + 1 + tap + count, :width]
        if tap < taps - 1:
            rows = jnp.where(place >= taps - 1 - tap, rows, 0.0)
        term = rows * weight[tap : tap + 1, :]
        total = term if total is None else total + term
    return total


def silu(value):
    return value * jax.nn.sigmoid(value)


def unit_scale(value):
    return lax.rsqrt(jnp.sum(value * value, axis=-1, keepdims=True) + EPS)


def column(table, head):
    lane = lax.broadcasted_iota(jnp.int32, table.shape, 1)
    return jnp.sum(jnp.where(lane == head, table, 0.0), axis=1, keepdims=True)


def fill_ext(ext, rim, body, width):
    ext[0:RIM, :width] = rim
    ext[RIM : RIM + body.shape[0], :width] = body


def decay_tables(decay_ref, beta_ref, log_ref, bias_ref, cum_ref, rate_ref):
    count = decay_ref.shape[0]
    shifted_in = decay_ref[...] + bias_ref[...]
    soft = jnp.maximum(shifted_in, 0.0) + jnp.log1p(jnp.exp(-jnp.abs(shifted_in)))
    log_decay = -jnp.exp(log_ref[...]) * soft
    _, _, within, _ = grid_masks()
    ones = jnp.where(within, 1.0, 0.0)
    for pair in range(count // PAIR):
        rows = slice(pair * PAIR, (pair + 1) * PAIR)
        cum_ref[rows, :] = lax.dot_general(
            ones,
            log_decay[rows, :],
            (((1,), (0,)), ((), ())),
            precision=lax.Precision.HIGHEST,
            preferred_element_type=jnp.float32,
        )
    rate_ref[...] = jax.nn.sigmoid(beta_ref[...])
    return log_decay, shifted_in


def state_kernel(
    taps,
    per_step,
    spot,
    q_ref,
    k_ref,
    v_ref,
    q_rim,
    k_rim,
    v_rim,
    conv_q,
    conv_k,
    conv_v,
    decay_ref,
    beta_ref,
    log_ref,
    bias_ref,
    mixed_ref,
    reach_ref,
    map_ref,
    add_ref,
    inverse_ref,
    cum_ref,
    rate_ref,
    ext,
    query,
    key,
    value,
    cum,
    rate,
    u_part,
    w_part,
    score,
    tail,
    delta,
    states,
):
    step = pl.program_id(0)
    count = q_ref.shape[0]
    pairs = count // PAIR
    blocks = count // GROUP
    first, base = spot[0], spot[1]

    @pl.when(step == 0)
    def _():
        decay_tables(decay_ref, beta_ref, log_ref, bias_ref, cum_ref, rate_ref)

    place = ranges(base, first, count)
    for j in range(per_step):
        cols = slice(j * DK, (j + 1) * DK)
        wide = slice(j * DV, (j + 1) * DV)
        fill_ext(ext, q_rim[:, cols], q_ref[:, cols], DK)
        c = silu(conv_sum(ext, DK, conv_q[:, cols], place, taps))
        query[j] = c * (unit_scale(c) * DK**-0.5)
        fill_ext(ext, k_rim[:, cols], k_ref[:, cols], DK)
        c = silu(conv_sum(ext, DK, conv_k[:, cols], place, taps))
        key[j] = c * unit_scale(c)
        fill_ext(ext, v_rim[:, wide], v_ref[:, wide], DV)
        value[j] = silu(conv_sum(ext, DV, conv_v[:, wide], place, taps))
        head = step * per_step + j
        cum[j] = jnp.broadcast_to(column(cum_ref[...], head), (count, DK))
        rate[j] = jnp.broadcast_to(column(rate_ref[...], head), (count, DK))

    row, col, within, below = grid_masks()

    def local(pair, carry):
        at = pl.ds(pl.multiple_of(pair * PAIR, PAIR), PAIR)
        for j in range(per_step):
            g = cum[j, at, :]
            b = rate[j, at, :]
            k = key[j, at, :]
            k_low = low(k)
            spread = jnp.where(within, jnp.exp(jnp.where(within, g - g.T, 0.0)), 0.0)
            keys = mm_nt(k_low, k_low)
            inverse = low(unit_inverse(jnp.where(below, b * keys * spread, 0.0), row, col))
            inverse_ref[j, at, :] = inverse
            score[j, at, :] = low(mm_nt(low(query[j, at, :]), k_low) * spread)
            grown = jnp.exp(g)
            v = value[j, at, :]
            u_part[j, at, :] = mm(inverse, low(jnp.concatenate([b, b], axis=1) * v))
            w_part[j, at, :] = low(mm(inverse, low(b * grown * k)))
            ends = jnp.concatenate(
                [
                    jnp.broadcast_to(g[GROUP - 1 : GROUP], (GROUP, DK)),
                    jnp.broadcast_to(g[PAIR - 1 : PAIR], (GROUP, DK)),
                ],
                axis=0,
            )
            tail[j, at, :] = low(jnp.exp(ends - g) * k)
            query[j, at, :] = grown * query[j, at, :]
        return carry

    lax.fori_loop(0, pairs, local, 0, unroll=2)

    for j in range(per_step):
        states[j] = jnp.concatenate(
            [jnp.where(row == col, 1.0, 0.0), jnp.zeros((DK, DV), jnp.float32)], axis=1
        )

    def advance(block, carry):
        at = pl.ds(pl.multiple_of(block * GROUP, GROUP), GROUP)
        start = base + block * GROUP
        keep = jnp.where((start != 0) & (start != first), 1.0, 0.0)
        for j in range(per_step):
            state = states[j] * keep
            state_low = low(state)
            moved = mm(w_part[j, at, :], state_low)
            change = jnp.concatenate([-moved[:, :DK], u_part[j, at, :] - moved[:, DK:]], axis=1)
            change_low = low(change)
            delta[j, at, :] = change_low
            last = jnp.exp(cum[j, pl.ds(block * GROUP + GROUP - 1, 1), :])
            last = jnp.concatenate([last] * 3, axis=1)
            states[j] = last * state + mm_tn(tail[j, at, :], change_low)
            out = mm(low(query[j, at, :]), state_low)
            reach_ref[at, j * DK : (j + 1) * DK] = low(out[:, :DK])
            mixed_ref[at, j * DV : (j + 1) * DV] = out[:, DK:]
        return carry

    lax.fori_loop(0, blocks, advance, 0)

    def finish(pair, carry):
        at = pl.ds(pl.multiple_of(pair * PAIR, PAIR), PAIR)
        for j in range(per_step):
            out = mm(score[j, at, :], delta[j, at, :])
            cols = slice(j * DK, (j + 1) * DK)
            wide = slice(j * DV, (j + 1) * DV)
            reach_ref[at, cols] = low(high(reach_ref[at, cols]) + out[:, :DK])
            mixed_ref[at, wide] = mixed_ref[at, wide] + out[:, DK:]
        return carry

    lax.fori_loop(0, pairs, finish, 0, unroll=2)
    for j in range(per_step):
        map_ref[j] = low(states[j, :, :DK])
        add_ref[j] = low(states[j, :, DK:])


def spec(shape, index):
    return pl.BlockSpec(shape, index)


def state_forward(q, k, v, rims, convs, decay, beta, decay_log, decay_bias, spot, per_step):
    count = q.shape[0]
    heads = decay.shape[1]
    taps = convs[0].shape[0]
    n = per_step
    along = lambda i: (0, i)
    fixed = lambda i: (0, 0)
    lead = lambda i: (i, 0, 0)
    f32, bf16 = jnp.float32, jnp.bfloat16
    return pl.pallas_call(
        functools.partial(state_kernel, taps, n),
        grid=(heads // n,),
        in_specs=[
            pl.BlockSpec(memory_space=pltpu.SMEM),
            spec((count, n * DK), along),
            spec((count, n * DK), along),
            spec((count, n * DV), along),
            spec((RIM, n * DK), along),
            spec((RIM, n * DK), along),
            spec((RIM, n * DV), along),
            spec((taps, n * DK), along),
            spec((taps, n * DK), along),
            spec((taps, n * DV), along),
            spec((count, heads), fixed),
            spec((count, heads), fixed),
            spec((1, heads), fixed),
            spec((1, heads), fixed),
        ],
        out_specs=[
            spec((count, n * DV), along),
            spec((count, n * DK), along),
            spec((n, DK, DK), lead),
            spec((n, DK, DV), lead),
            spec((n, count, PAIR), lead),
            spec((count, heads), fixed),
            spec((count, heads), fixed),
        ],
        out_shape=[
            jax.ShapeDtypeStruct((count, heads * DV), f32),
            jax.ShapeDtypeStruct((count, heads * DK), bf16),
            jax.ShapeDtypeStruct((heads, DK, DK), bf16),
            jax.ShapeDtypeStruct((heads, DK, DV), bf16),
            jax.ShapeDtypeStruct((heads, count, PAIR), bf16),
            jax.ShapeDtypeStruct((count, heads), f32),
            jax.ShapeDtypeStruct((count, heads), f32),
        ],
        scratch_shapes=[
            pltpu.VMEM((count + RIM, DV), f32),
            pltpu.VMEM((n, count, DK), f32),
            pltpu.VMEM((n, count, DK), f32),
            pltpu.VMEM((n, count, DV), f32),
            pltpu.VMEM((n, count, DK), f32),
            pltpu.VMEM((n, count, DK), f32),
            pltpu.VMEM((n, count, DV), f32),
            pltpu.VMEM((n, count, DK), bf16),
            pltpu.VMEM((n, count, PAIR), bf16),
            pltpu.VMEM((n, count, DK), bf16),
            pltpu.VMEM((n, count, DK + DV), bf16),
            pltpu.VMEM((n, DK, DK + DV), f32),
        ],
        compiler_params=pltpu.CompilerParams(
            dimension_semantics=("arbitrary",), vmem_limit_bytes=VMEM_BYTES
        ),
        cost_estimate=pl.CostEstimate(
            flops=heads * count * 2 * 128 * 2600, bytes_accessed=count * heads * 4000, transcendentals=0
        ),
    )(spot, q, k, v, *rims, *convs, decay, beta, decay_log, decay_bias)


def gate_kernel(per_step, mixed_ref, reach_ref, map_ref, add_ref, far_ref, gate_ref, gain_ref, gated_ref, kept_ref, start_ref):
    for j in range(per_step):
        cols = slice(j * DK, (j + 1) * DK)
        wide = slice(j * DV, (j + 1) * DV)
        start = low(high(add_ref[j]) + mm(map_ref[j], far_ref[j]))
        start_ref[j] = start
        mixed = mixed_ref[:, wide] + mm(reach_ref[:, cols], start)
        kept_ref[:, wide] = low(mixed)
        scale = lax.rsqrt(jnp.mean(mixed * mixed, axis=-1, keepdims=True) + EPS)
        gated_ref[:, wide] = low(mixed * scale * gain_ref[...] * silu(gate_ref[:, wide]))


def gate_forward(mixed, reach, near_map, near_add, far_add, gate, gain, per_step):
    count = mixed.shape[0]
    heads = near_map.shape[0]
    n = per_step
    along = lambda i: (0, i)
    lead = lambda i: (i, 0, 0)
    bf16 = jnp.bfloat16
    return pl.pallas_call(
        functools.partial(gate_kernel, n),
        grid=(heads // n,),
        in_specs=[
            spec((count, n * DV), along),
            spec((count, n * DK), along),
            spec((n, DK, DK), lead),
            spec((n, DK, DV), lead),
            spec((n, DK, DV), lead),
            spec((count, n * DV), along),
            spec((1, DV), lambda i: (0, 0)),
        ],
        out_specs=[
            spec((count, n * DV), along),
            spec((count, n * DV), along),
            spec((n, DK, DV), lead),
        ],
        out_shape=[
            jax.ShapeDtypeStruct((count, heads * DV), bf16),
            jax.ShapeDtypeStruct((count, heads * DV), bf16),
            jax.ShapeDtypeStruct((heads, DK, DV), bf16),
        ],
        compiler_params=pltpu.CompilerParams(
            dimension_semantics=("arbitrary",), vmem_limit_bytes=VMEM_BYTES
        ),
    )(mixed, reach, near_map, near_add, far_add, gate, gain)


def gate_back_kernel(per_step, d_gated_ref, kept_ref, reach_ref, gate_ref, gain_ref, d_mixed_ref, d_gate_ref, d_start_ref, d_gain_ref):
    @pl.when(pl.program_id(0) == 0)
    def _():
        d_gain_ref[...] = jnp.zeros_like(d_gain_ref)

    for j in range(per_step):
        cols = slice(j * DK, (j + 1) * DK)
        wide = slice(j * DV, (j + 1) * DV)
        mixed = high(kept_ref[:, wide])
        scale = lax.rsqrt(jnp.mean(mixed * mixed, axis=-1, keepdims=True) + EPS)
        normal = mixed * scale
        gate = gate_ref[:, wide]
        sig = jax.nn.sigmoid(gate)
        d_gated = d_gated_ref[:, wide]
        d_scaled = d_gated * (gate * sig)
        d_gain_ref[...] += jnp.sum(d_scaled * normal, axis=0, keepdims=True)
        d_gate_ref[:, wide] = low(
            d_gated * (normal * gain_ref[...]) * (sig * (1.0 + gate * (1.0 - sig)))
        )
        d_normal = d_scaled * gain_ref[...]
        d_mixed = low(scale * (d_normal - normal * jnp.mean(d_normal * normal, axis=-1, keepdims=True)))
        d_mixed_ref[:, wide] = d_mixed
        d_start_ref[j] = low(mm_tn(reach_ref[:, cols], d_mixed))


def gate_backward(d_gated, kept, reach, gate, gain, per_step):
    count = kept.shape[0]
    heads = kept.shape[1] // DV
    n = per_step
    along = lambda i: (0, i)
    lead = lambda i: (i, 0, 0)
    bf16 = jnp.bfloat16
    return pl.pallas_call(
        functools.partial(gate_back_kernel, n),
        grid=(heads // n,),
        in_specs=[
            spec((count, n * DV), along),
            spec((count, n * DV), along),
            spec((count, n * DK), along),
            spec((count, n * DV), along),
            spec((1, DV), lambda i: (0, 0)),
        ],
        out_specs=[
            spec((count, n * DV), along),
            spec((count, n * DV), along),
            spec((n, DK, DV), lead),
            spec((1, DV), lambda i: (0, 0)),
        ],
        out_shape=[
            jax.ShapeDtypeStruct((count, heads * DV), bf16),
            jax.ShapeDtypeStruct((count, heads * DV), bf16),
            jax.ShapeDtypeStruct((heads, DK, DV), bf16),
            jax.ShapeDtypeStruct((1, DV), jnp.float32),
        ],
        compiler_params=pltpu.CompilerParams(
            dimension_semantics=("arbitrary",), vmem_limit_bytes=VMEM_BYTES
        ),
    )(d_gated, kept, reach, gate, gain)


def state_back_kernel(
    taps,
    per_step,
    spot,
    q_ref,
    k_ref,
    v_ref,
    q_rim,
    k_rim,
    v_rim,
    conv_q,
    conv_k,
    conv_v,
    decay_ref,
    log_ref,
    bias_ref,
    cum_ref,
    rate_ref,
    inverse_ref,
    start_ref,
    d_mixed_ref,
    near_ref,
    map_ref,
    far_ref,
    dq_ref,
    dk_ref,
    dv_ref,
    dq_rim,
    dk_rim,
    dv_rim,
    dq_end,
    dk_end,
    dv_end,
    d_conv_q,
    d_conv_k,
    d_conv_v,
    d_decay_ref,
    d_beta_ref,
    d_log_ref,
    d_bias_ref,
    ext,
    d_ext,
    query,
    key,
    value,
    cum,
    rate,
    u_part,
    w_part,
    score,
    tail,
    grown_q,
    grown_k,
    pull,
    local_r,
    delta,
    starts,
    ends,
    states,
    d_rhs,
    d_cum,
    d_rate,
):
    step = pl.program_id(0)
    count = q_ref.shape[0]
    pairs = count // PAIR
    blocks = count // GROUP
    first, base = spot[0], spot[1]
    place = ranges(base, first, count)

    @pl.when(step == 0)
    def _():
        d_cum[...] = jnp.zeros_like(d_cum)
        d_rate[...] = jnp.zeros_like(d_rate)

    for j in range(per_step):
        cols = slice(j * DK, (j + 1) * DK)
        wide = slice(j * DV, (j + 1) * DV)
        fill_ext(ext, q_rim[:, cols], q_ref[:, cols], DK)
        c = silu(conv_sum(ext, DK, conv_q[:, cols], place, taps))
        query[j] = c * (unit_scale(c) * DK**-0.5)
        fill_ext(ext, k_rim[:, cols], k_ref[:, cols], DK)
        c = silu(conv_sum(ext, DK, conv_k[:, cols], place, taps))
        key[j] = c * unit_scale(c)
        fill_ext(ext, v_rim[:, wide], v_ref[:, wide], DV)
        value[j] = silu(conv_sum(ext, DV, conv_v[:, wide], place, taps))
        head = step * per_step + j
        cum[j] = jnp.broadcast_to(column(cum_ref[...], head), (count, DK))
        rate[j] = jnp.broadcast_to(column(rate_ref[...], head), (count, DK))

    row, col, within, below = grid_masks()

    def block_ends(g):
        return jnp.concatenate(
            [
                jnp.broadcast_to(g[GROUP - 1 : GROUP], (GROUP, DK)),
                jnp.broadcast_to(g[PAIR - 1 : PAIR], (GROUP, DK)),
            ],
            axis=0,
        )

    def local(pair, carry):
        at = pl.ds(pl.multiple_of(pair * PAIR, PAIR), PAIR)
        for j in range(per_step):
            g = cum[j, at, :]
            b = rate[j, at, :]
            k = key[j, at, :]
            q = query[j, at, :]
            spread = jnp.where(within, jnp.exp(jnp.where(within, g - g.T, 0.0)), 0.0)
            inverse = inverse_ref[j, at, :]
            scored = low(mm_nt(low(q), low(k)) * spread)
            grown = jnp.exp(g)
            v = value[j, at, :]
            kb = low(b * grown * k)
            grown_k[j, at, :] = kb
            u_part[j, at, :] = mm(inverse, low(jnp.concatenate([b, b], axis=1) * v))
            w_part[j, at, :] = low(mm(inverse, kb))
            t = low(jnp.exp(block_ends(g) - g) * k)
            tail[j, at, :] = t
            grown_q[j, at, :] = low(grown * q)
            pull[j, at, :] = low(mm_tn(inverse, t))
            d_out = d_mixed_ref[at, j * DV : (j + 1) * DV]
            local_r[j, at, :] = mm_tn(inverse, low(mm_tn(scored, d_out)))
        return carry

    lax.fori_loop(0, pairs, local, 0, unroll=2)

    for j in range(per_step):
        states[j] = high(start_ref[j])

    def advance(block, carry):
        at = pl.ds(pl.multiple_of(block * GROUP, GROUP), GROUP)
        begin = base + block * GROUP
        keep = jnp.where((begin != 0) & (begin != first), 1.0, 0.0)
        for j in range(per_step):
            state = states[j] * keep
            state_low = low(state)
            starts[j, block] = state_low
            change_low = low(u_part[j, at, :] - mm(w_part[j, at, :], state_low))
            delta[j, at, :] = change_low
            last = jnp.exp(cum[j, pl.ds(block * GROUP + GROUP - 1, 1), :])
            last = jnp.concatenate([last, last], axis=1)
            states[j] = last * state + mm_tn(tail[j, at, :], change_low)
        return carry

    lax.fori_loop(0, blocks, advance, 0)

    for j in range(per_step):
        states[j] = high(near_ref[j]) + mm_tn(map_ref[j], far_ref[j])

    def retreat(reverse, carry):
        block = blocks - 1 - reverse
        at = pl.ds(pl.multiple_of(block * GROUP, GROUP), GROUP)
        begin = base + block * GROUP
        keep = jnp.where((begin != 0) & (begin != first), 1.0, 0.0)
        for j in range(per_step):
            d_state = states[j]
            d_low = low(d_state)
            ends[j, block] = d_low
            change = low(local_r[j, at, :] + mm(pull[j, at, :], d_low))
            d_rhs[j, at, :] = change
            last = jnp.exp(cum[j, pl.ds(block * GROUP + GROUP - 1, 1), :])
            last = jnp.concatenate([last, last], axis=1)
            d_out = d_mixed_ref[at, j * DV : (j + 1) * DV]
            states[j] = keep * (
                last * d_state
                + mm_tn(grown_q[j, at, :], d_out)
                - mm_tn(grown_k[j, at, :], change)
            )
        return carry

    lax.fori_loop(0, blocks, retreat, 0)

    lane = lax.broadcasted_iota(jnp.int32, (PAIR, d_cum.shape[1]), 1)
    tall = lax.broadcasted_iota(jnp.int32, (PAIR, 1), 0)

    def assemble(pair, carry):
        at = pl.ds(pl.multiple_of(pair * PAIR, PAIR), PAIR)
        for j in range(per_step):
            g = cum[j, at, :]
            b = rate[j, at, :]
            k = key[j, at, :]
            q = query[j, at, :]
            v = value[j, at, :]
            k_low, q_low = low(k), low(q)
            spread = jnp.where(within, jnp.exp(jnp.where(within, g - g.T, 0.0)), 0.0)
            d_out = d_mixed_ref[at, j * DV : (j + 1) * DV]
            change = delta[j, at, :]
            rhs = d_rhs[j, at, :]
            d_lower = jnp.where(below, -mm_nt(rhs, change), 0.0)
            d_score = mm_nt(d_out, change) * spread
            d_gk, d_gq, d_tail = [], [], []
            bonus = []
            for half in range(2):
                block = 2 * pair + half
                part = slice(half * GROUP, (half + 1) * GROUP)
                state, d_end = starts[j, block], ends[j, block]
                d_gk.append(-mm_nt(rhs[part], state))
                d_gq.append(mm_nt(d_out[part], state))
                d_tail.append(mm_nt(change[part], d_end))
                bonus.append(jnp.sum(high(state) * high(d_end)))
            d_gk = jnp.concatenate(d_gk, axis=0)
            d_gq = jnp.concatenate(d_gq, axis=0)
            d_tail = jnp.concatenate(d_tail, axis=0)
            grown = jnp.exp(g)
            fall = jnp.exp(block_ends(g) - g)
            shape = mm_nt(k_low, k_low) * spread
            d_a = d_lower * shape
            cross = d_a * b + d_score * mm_nt(q_low, k_low)
            gk_k = d_gk * k
            rate_col = jnp.sum(d_a + grown * gk_k, axis=-1, keepdims=True) + jnp.sum(
                high(rhs) * v, axis=-1, keepdims=True
            )
            tail_sum = jnp.sum(d_tail * (fall * k), axis=-1, keepdims=True)
            cum_col = (
                jnp.sum(
                    cross - cross.T + b * grown * gk_k + d_gq * (grown * q), axis=-1, keepdims=True
                )
                - tail_sum
            )
            for half in range(2):
                part = slice(half * GROUP, (half + 1) * GROUP)
                at_end = half * GROUP + GROUP - 1
                extra = jnp.sum(tail_sum[part], axis=0, keepdims=True) + bonus[half] * grown[
                    at_end : at_end + 1, :1
                ]
                cum_col = cum_col + jnp.where(tall == at_end, extra, 0.0)
            head = step * per_step + j
            d_cum[at, :] = d_cum[at, :] + jnp.where(lane == head, cum_col, 0.0)
            d_rate[at, :] = d_rate[at, :] + jnp.where(lane == head, rate_col, 0.0)
            d_keys = d_lower * spread * b
            d_keys = low(d_keys + d_keys.T)
            d_score_low = low(d_score)
            d_query = grown * d_gq + mm(d_score_low, k_low)
            d_key = b * grown * d_gk + fall * d_tail + mm(d_keys, k_low) + mm_tn(d_score_low, q_low)
            query[j, at, :] = d_query
            key[j, at, :] = d_key
            value[j, at, :] = jnp.concatenate([b, b], axis=1) * high(rhs)
        return carry

    lax.fori_loop(0, pairs, assemble, 0)

    def conv_back(width, weight, d_total, out_ref, rim_ref, end_ref, d_weight_ref, cols):
        d_ext[:, :width] = jnp.zeros((count + 2 * RIM, width), jnp.float32)
        grads = []
        for tap in range(taps):
            offset = RIM - taps + 1 + tap
            part = d_total
            if tap < taps - 1:
                part = jnp.where(place >= taps - 1 - tap, part, 0.0)
            grads.append(
                jnp.sum(part * ext[offset : offset + count, :width], axis=0, keepdims=True)
            )
            d_ext[offset : offset + count, :width] += part * weight[tap : tap + 1, :]
        d_weight_ref[:, cols] = jnp.concatenate(grads, axis=0)
        rim_ref[:, cols] = d_ext[0:RIM, :width]
        out_ref[:, cols] = low(d_ext[RIM : RIM + count, :width])
        end_ref[:, cols] = d_ext[count : count + RIM, :width]

    for j in range(per_step):
        cols = slice(j * DK, (j + 1) * DK)
        wide = slice(j * DV, (j + 1) * DV)

        def unit_back(rim, body, weight, d_unit, factor):
            fill_ext(ext, rim, body, DK)
            total = conv_sum(ext, DK, weight, place, taps)
            sig = jax.nn.sigmoid(total)
            c = total * sig
            scale = unit_scale(c)
            unit = c * scale
            d_unit = d_unit * factor
            d_c = scale * (d_unit - unit * jnp.sum(d_unit * unit, axis=-1, keepdims=True))
            return d_c * (sig * (1.0 + total * (1.0 - sig)))

        d_total = unit_back(q_rim[:, cols], q_ref[:, cols], conv_q[:, cols], query[j], DK**-0.5)
        conv_back(DK, conv_q[:, cols], d_total, dq_ref, dq_rim, dq_end, d_conv_q, cols)
        d_total = unit_back(k_rim[:, cols], k_ref[:, cols], conv_k[:, cols], key[j], 1.0)
        conv_back(DK, conv_k[:, cols], d_total, dk_ref, dk_rim, dk_end, d_conv_k, cols)
        fill_ext(ext, v_rim[:, wide], v_ref[:, wide], DV)
        total = conv_sum(ext, DV, conv_v[:, wide], place, taps)
        sig = jax.nn.sigmoid(total)
        d_total = value[j] * (sig * (1.0 + total * (1.0 - sig)))
        conv_back(DV, conv_v[:, wide], d_total, dv_ref, dv_rim, dv_end, d_conv_v, wide)

    @pl.when(step == pl.num_programs(0) - 1)
    def _():
        shifted_in = decay_ref[...] + bias_ref[...]
        soft = jnp.maximum(shifted_in, 0.0) + jnp.log1p(jnp.exp(-jnp.abs(shifted_in)))
        speed = -jnp.exp(log_ref[...])
        after = jnp.where(within, 1.0, 0.0)
        d_log = jnp.zeros_like(d_log_ref)
        d_bias = jnp.zeros_like(d_bias_ref)
        for pair in range(pairs):
            rows = slice(pair * PAIR, (pair + 1) * PAIR)
            d_decay = lax.dot_general(
                after,
                d_cum[rows, :],
                (((0,), (0,)), ((), ())),
                precision=lax.Precision.HIGHEST,
                preferred_element_type=jnp.float32,
            )
            d_log = d_log + jnp.sum(d_decay * (speed * soft[rows]), axis=0, keepdims=True)
            d_in = d_decay * speed * jax.nn.sigmoid(shifted_in[rows])
            d_bias = d_bias + jnp.sum(d_in, axis=0, keepdims=True)
            d_decay_ref[rows, :] = d_in
        d_log_ref[...] = d_log
        d_bias_ref[...] = d_bias
        rates = rate_ref[...]
        d_beta_ref[...] = d_rate[...] * rates * (1.0 - rates)


def state_backward(
    q, k, v, rims, convs, decay, decay_log, decay_bias, cum, rate, inverse, start, d_mixed, near, near_map, far, spot, per_step
):
    count = q.shape[0]
    heads = decay.shape[1]
    taps = convs[0].shape[0]
    n = per_step
    along = lambda i: (0, i)
    fixed = lambda i: (0, 0)
    lead = lambda i: (i, 0, 0)
    f32, bf16 = jnp.float32, jnp.bfloat16
    shape = jax.ShapeDtypeStruct
    vm = pltpu.VMEM
    return pl.pallas_call(
        functools.partial(state_back_kernel, taps, n),
        grid=(heads // n,),
        in_specs=[
            pl.BlockSpec(memory_space=pltpu.SMEM),
            spec((count, n * DK), along),
            spec((count, n * DK), along),
            spec((count, n * DV), along),
            spec((RIM, n * DK), along),
            spec((RIM, n * DK), along),
            spec((RIM, n * DV), along),
            spec((taps, n * DK), along),
            spec((taps, n * DK), along),
            spec((taps, n * DV), along),
            spec((count, heads), fixed),
            spec((1, heads), fixed),
            spec((1, heads), fixed),
            spec((count, heads), fixed),
            spec((count, heads), fixed),
            spec((n, count, PAIR), lead),
            spec((n, DK, DV), lead),
            spec((count, n * DV), along),
            spec((n, DK, DV), lead),
            spec((n, DK, DK), lead),
            spec((n, DK, DV), lead),
        ],
        out_specs=[
            spec((count, n * DK), along),
            spec((count, n * DK), along),
            spec((count, n * DV), along),
            spec((RIM, n * DK), along),
            spec((RIM, n * DK), along),
            spec((RIM, n * DV), along),
            spec((RIM, n * DK), along),
            spec((RIM, n * DK), along),
            spec((RIM, n * DV), along),
            spec((taps, n * DK), along),
            spec((taps, n * DK), along),
            spec((taps, n * DV), along),
            spec((count, heads), fixed),
            spec((count, heads), fixed),
            spec((1, heads), fixed),
            spec((1, heads), fixed),
        ],
        out_shape=[
            shape((count, heads * DK), bf16),
            shape((count, heads * DK), bf16),
            shape((count, heads * DV), bf16),
            shape((RIM, heads * DK), f32),
            shape((RIM, heads * DK), f32),
            shape((RIM, heads * DV), f32),
            shape((RIM, heads * DK), f32),
            shape((RIM, heads * DK), f32),
            shape((RIM, heads * DV), f32),
            shape((taps, heads * DK), f32),
            shape((taps, heads * DK), f32),
            shape((taps, heads * DV), f32),
            shape((count, heads), f32),
            shape((count, heads), f32),
            shape((1, heads), f32),
            shape((1, heads), f32),
        ],
        scratch_shapes=[
            vm((count + RIM, DV), f32),
            vm((count + 2 * RIM, DV), f32),
            vm((n, count, DK), f32),
            vm((n, count, DK), f32),
            vm((n, count, DV), f32),
            vm((n, count, DK), f32),
            vm((n, count, DK), f32),
            vm((n, count, DV), f32),
            vm((n, count, DK), bf16),
            vm((n, 16, PAIR), bf16),
            vm((n, count, DK), bf16),
            vm((n, count, DK), bf16),
            vm((n, count, DK), bf16),
            vm((n, count, DK), bf16),
            vm((n, count, DV), f32),
            vm((n, count, DV), bf16),
            vm((n, count // GROUP, DK, DV), bf16),
            vm((n, count // GROUP, DK, DV), bf16),
            vm((n, DK, DV), f32),
            vm((n, count, DV), bf16),
            vm((count, heads), f32),
            vm((count, heads), f32),
        ],
        compiler_params=pltpu.CompilerParams(
            dimension_semantics=("arbitrary",), vmem_limit_bytes=VMEM_BYTES
        ),
        cost_estimate=pl.CostEstimate(
            flops=heads * count * 2 * 128 * 5000, bytes_accessed=count * heads * 6000, transcendentals=0
        ),
    )(spot, q, k, v, *rims, *convs, decay, decay_log, decay_bias, cum, rate, inverse, start, d_mixed, near, near_map, far)


def shifted(value, axis, steps):
    count = lax.axis_size(axis)
    leading, last = (max(0, -steps), min(count, count - steps))
    return lax.ppermute(value, axis, [(source, source + steps) for source in range(leading, last)])


def rms_scale(values, gain):
    return values * lax.rsqrt(jnp.mean(values * values, axis=-1, keepdims=True) + EPS) * gain


def swish_product(gate_ffn, up_ffn):
    return jax.nn.silu(gate_ffn) * up_ffn


def project(rows, weight):
    return jnp.dot(rows, weight, preferred_element_type=jnp.float32)


def rows_product(left, right):
    return jnp.dot(left, right, preferred_element_type=jnp.float32)


def rows_back(left, weight):
    return jnp.einsum("tc,dc->td", left, weight, preferred_element_type=jnp.float32)


def weight_grad(rows, grads):
    return jnp.einsum("td,tc->dc", rows, grads, preferred_element_type=jnp.float32)


STAGES = {"x": ("seq", 0, 1), "y": ("seq", 1, 2), "l": ("dp", 0, 4), "h": ("dp", 1, 8)}


def trade(value, stage):
    axis, bit, _ = STAGES[stage]
    count = lax.axis_size(axis)
    return lax.ppermute(value, axis, [(place, place ^ (1 << bit)) for place in range(count)])


def relative_order(rows, order):
    own = lax.axis_index("dp") * lax.axis_size("seq") + lax.axis_index("seq")
    width = rows.shape[1] // 16
    parts = []
    for place in range(16):
        mask = sum(STAGES[stage][2] for k, stage in enumerate(order) if place >> (3 - k) & 1)
        parts.append(lax.dynamic_slice_in_dim(rows, (own ^ mask) * width, width, 1))
    return jnp.concatenate(parts, axis=1)


def scattered_grad(rows, grads, order):
    width = rows.shape[1] // 16
    first = trade(low(weight_grad(rows[:, 8 * width :], grads)), order[0])
    second = trade(
        low(weight_grad(rows[:, 4 * width : 8 * width], grads) + high(first[4 * width :])), order[1]
    )
    rest = weight_grad(rows[:, : 4 * width], grads) + high(first[: 4 * width])
    third = trade(low(rest[2 * width :] + high(second[2 * width :])), order[2])
    rest = rest[: 2 * width] + high(second[: 2 * width])
    fourth = trade(low(rest[width:] + high(third[width:])), order[3])
    return rest[:width] + high(third[:width]) + high(fourth)


def sum_all(value):
    for stage in "xylh":
        value = value + trade(value, stage)
    return value


def heads_gather(rows):
    count = lax.axis_size("heads")
    own = lax.axis_index("heads")
    step = 1
    while step < count:
        other = lax.ppermute(rows, "heads", [(place, place ^ step) for place in range(count)])
        size = rows.shape[0]
        upper = lax.rem(own // step, 2)
        both = jnp.zeros((2 * size,) + rows.shape[1:], rows.dtype)
        both = lax.dynamic_update_slice_in_dim(both, rows, upper * size, 0)
        rows = lax.dynamic_update_slice_in_dim(both, other, (1 - upper) * size, 0)
        step *= 2
    return rows


def heads_sum(compute, count, kind):
    if lax.axis_size("heads") != 2:
        whole = compute(lambda rows: rows).astype(kind)
        return high(lax.psum_scatter(whole, "heads", scatter_dimension=0, tiled=True))
    own = lax.axis_index("heads")
    half = count // 2

    def part(which):
        return compute(lambda rows: lax.dynamic_slice_in_dim(rows, which * half, half, 0))

    got = lax.ppermute(part(1 - own).astype(kind), "heads", [(0, 1), (1, 0)])
    return part(own) + high(got)


ORDERS = ("xylh", "ylxh", "lxyh")


def body(
    hidden_in,
    out_cotangent,
    lengths,
    norm_gain,
    q_weight,
    k_weight,
    v_weight,
    gate_weight,
    decay_weight,
    beta_weight,
    conv_q,
    conv_k,
    conv_v,
    decay_log,
    decay_bias,
    out_gain,
    out_weight,
    ffn_gain,
    ffn_gate,
    ffn_up,
    ffn_down,
):
    resid = hidden_in[0].astype(jnp.float32)
    normed_own = rms_scale(resid, norm_gain).astype(jnp.bfloat16)
    normed, cotangent = (
        heads_gather(normed_own),
        heads_gather(out_cotangent[0]),
    )
    span = normed.shape[0]
    taps = conv_q.shape[0]
    q_proj = project(normed, q_weight)
    k_proj = project(normed, k_weight)
    v_proj = project(normed, v_weight)
    gate_proj = project(normed, gate_weight)
    heads = decay_weight.shape[1]
    per_step = min(2, heads)
    narrow = project(normed, jnp.concatenate([decay_weight, beta_weight], axis=1))
    decay_proj, beta_proj = narrow[:, :heads], narrow[:, heads:]
    seq_index = lax.axis_index("seq")
    spot = jnp.stack([lengths[0, 0], seq_index * span]).astype(jnp.int32)
    rims = shifted((q_proj[span - RIM :], k_proj[span - RIM :], v_proj[span - RIM :]), "seq", 1)
    convs = (conv_q, conv_k, conv_v)
    log_row, bias_row, gain_row = decay_log[None], decay_bias[None], out_gain[None]
    mixed_local, reach, span_map, span_add, inverse, cum, rate = state_forward(
        q_proj, k_proj, v_proj, rims, convs, decay_proj, beta_proj, log_row, bias_row, spot, per_step
    )
    near_map, near_add = shifted((span_map, span_add), "seq", 1)
    far_add = shifted(span_add, "seq", 2)
    next_map = shifted(span_map, "seq", -1)
    gated_low, mixed_low, start_state = gate_forward(
        mixed_local, reach, near_map, near_add, far_add, gate_proj, gain_row, per_step
    )
    mixer = heads_sum(
        lambda pick: rows_product(pick(gated_low), out_weight), span, jnp.float32
    )
    resid_mid = resid + mixer
    ffn_own = rms_scale(resid_mid, ffn_gain).astype(jnp.bfloat16)
    ffn_in = heads_gather(ffn_own)
    gate_ffn = project(ffn_in, ffn_gate)
    up_ffn = project(ffn_in, ffn_up)
    act, act_pull = jax.vjp(swish_product, gate_ffn, up_ffn)
    act_low = act.astype(jnp.bfloat16)
    ffn_out = heads_sum(lambda pick: rows_product(pick(act_low), ffn_down), span, jnp.bfloat16)
    output = (resid_mid + ffn_out).astype(jnp.bfloat16)
    d_act = jnp.einsum("td,fd->tf", cotangent, ffn_down, preferred_element_type=jnp.float32)
    d_gate_ffn, d_up_ffn = act_pull(d_act)
    d_gate_low = d_gate_ffn.astype(jnp.bfloat16)
    d_up_low = d_up_ffn.astype(jnp.bfloat16)
    ffn_rel = {order: relative_order(ffn_in, order) for order in ORDERS[:2]}
    cotangent_rel = relative_order(cotangent, ORDERS[2])
    grad_gate = scattered_grad(ffn_rel[ORDERS[0]], d_gate_low, ORDERS[0])
    grad_up = scattered_grad(ffn_rel[ORDERS[1]], d_up_low, ORDERS[1])
    grad_down = scattered_grad(cotangent_rel, act_low, ORDERS[2]).T
    d_ffn = heads_sum(
        lambda pick: rows_back(pick(d_gate_low), ffn_gate) + rows_back(pick(d_up_low), ffn_up),
        span,
        jnp.float32,
    )
    _, ffn_norm_pull = jax.vjp(rms_scale, resid_mid, ffn_gain)
    d_mid_norm, d_ffn_gain = ffn_norm_pull(d_ffn)
    d_mid = out_cotangent[0].astype(jnp.float32) + d_mid_norm
    d_mid_all = heads_gather(low(d_mid))
    grad_out = scattered_grad(relative_order(d_mid_all, ORDERS[2]), gated_low, ORDERS[2]).T
    d_gated = jnp.einsum("td,cd->tc", d_mid_all, out_weight, preferred_element_type=jnp.float32)
    d_mixed, d_gate_low_mix, d_start, d_out_gain = gate_backward(
        d_gated, mixed_low, reach, gate_proj, gain_row, per_step
    )
    next_start = shifted(d_start, "seq", -1)
    beyond_start = shifted(d_start, "seq", -2)
    back = state_backward(
        q_proj,
        k_proj,
        v_proj,
        rims,
        convs,
        decay_proj,
        log_row,
        bias_row,
        cum,
        rate,
        inverse,
        start_state,
        d_mixed,
        next_start,
        next_map,
        beyond_start,
        spot,
        per_step,
    )
    passed = shifted(tuple(back[3:6]), "seq", -1)
    d_q_low, d_k_low, d_v_low = (
        lax.dynamic_update_slice_in_dim(whole, low(end + more), span - RIM, 0)
        for whole, end, more in zip(back[0:3], back[6:9], passed)
    )
    conv_grads = back[9:12]
    d_decay_low, d_beta_low = low(back[12]), low(back[13])
    d_log, d_bias = back[14][0], back[15][0]
    normed_rel = {order: relative_order(normed, order) for order in ORDERS}
    grad_gate_mix = jnp.concatenate(
        [
            scattered_grad(normed_rel[ORDERS[0]], d_gate_low_mix[:, : d_gate_low_mix.shape[1] // 2], ORDERS[0]),
            scattered_grad(normed_rel[ORDERS[1]], d_gate_low_mix[:, d_gate_low_mix.shape[1] // 2 :], ORDERS[1]),
        ],
        axis=1,
    )
    mix_low = jnp.concatenate([d_q_low, d_k_low, d_v_low, d_decay_low, d_beta_low], axis=1)
    width_q = d_q_low.shape[1]
    width_v = d_v_low.shape[1]
    cuts = (0, 4 * width_q // 3 // 128 * 128, 8 * width_q // 3 // 128 * 128, mix_low.shape[1])
    grad_mix = jnp.concatenate(
        [
            scattered_grad(normed_rel[order], mix_low[:, cuts[k] : cuts[k + 1]], order)
            for k, order in enumerate(ORDERS)
        ],
        axis=1,
    )
    heads_here = d_decay_low.shape[1]
    ends = (width_q, 2 * width_q, 2 * width_q + width_v, 2 * width_q + width_v + heads_here)
    grad_q, grad_k, grad_v, grad_decay, grad_beta = jnp.split(grad_mix, ends, axis=1)
    pairs = (
        (d_q_low, q_weight),
        (d_k_low, k_weight),
        (d_v_low, v_weight),
        (d_gate_low_mix, gate_weight),
        (d_decay_low, decay_weight),
        (d_beta_low, beta_weight),
    )
    d_normed = heads_sum(
        lambda pick: sum(rows_back(pick(rows), weight) for rows, weight in pairs),
        span,
        jnp.bfloat16,
    )
    _, in_norm_pull = jax.vjp(rms_scale, resid, norm_gain)
    d_in_norm, d_norm_gain = in_norm_pull(d_normed)
    input_grad = d_mid + d_in_norm
    shared = (d_norm_gain, d_ffn_gain, d_out_gain[0])
    owned = (d_log, d_bias) + tuple(part.reshape(-1) for part in conv_grads)
    flat = sum_all(jnp.concatenate(shared + owned))
    everyone = heads_gather(flat[None])
    marks = np.cumsum([part.size for part in shared + owned])
    pieces = jnp.split(everyone, marks[:-1], axis=1)
    small = [piece.sum(0) for piece in pieces[:3]] + [pieces[3].reshape(-1), pieces[4].reshape(-1)]
    for piece in pieces[5:]:
        small.append(
            jnp.swapaxes(piece.reshape(piece.shape[0], taps, -1), 0, 1).reshape(taps, -1)
        )
    return (
        output[None],
        input_grad[None],
        small[0],
        grad_q,
        grad_k,
        grad_v,
        grad_gate_mix,
        grad_decay,
        grad_beta,
        small[5],
        small[6],
        small[7],
        small[3],
        small[4],
        small[2],
        grad_out,
        small[1],
        grad_gate,
        grad_up,
        grad_down,
    )


def solution(mesh):
    in_specs = (
        P("dp", ("seq", "heads"), None),
        P("dp", ("seq", "heads"), None),
        P("dp", None),
        P(),
        P(None, "heads"),
        P(None, "heads"),
        P(None, "heads"),
        P(None, "heads"),
        P(None, "heads"),
        P(None, "heads"),
        P(None, "heads"),
        P(None, "heads"),
        P(None, "heads"),
        P("heads"),
        P("heads"),
        P(),
        P("heads", None),
        P(),
        P(None, "heads"),
        P(None, "heads"),
        P("heads", None),
    )
    out_specs = (
        P("dp", ("seq", "heads"), None),
        P("dp", ("seq", "heads"), None),
        P(),
        P(("dp", "seq"), "heads"),
        P(("dp", "seq"), "heads"),
        P(("dp", "seq"), "heads"),
        P(("dp", "seq"), "heads"),
        P(("dp", "seq"), "heads"),
        P(("dp", "seq"), "heads"),
        P(),
        P(),
        P(),
        P(),
        P(),
        P(),
        P("heads", ("dp", "seq")),
        P(),
        P(("dp", "seq"), "heads"),
        P(("dp", "seq"), "heads"),
        P("heads", ("dp", "seq")),
    )
    return jax.shard_map(body, mesh=mesh, in_specs=in_specs, out_specs=out_specs, check_vma=False)
```

time: 2660 us -> 1380 us (0.52)
  other arithmetic: 724 us -> 56.3 us
  matrix products: 978 us -> 364 us
  local copies, waits for them, and re-layouts: 420 us -> 63.2 us
  Pallas kernels: 0 us -> 260 us
  waiting for transfers between devices: 425 us -> 555 us
    dot_general x266 -> x0, matrix products: 547 us -> none  [the longest x84 176 us: group_state(): jnp.einsum('lwo,loq->lwq', w_part, memory_state, precision=PRECISE_MODE)]
    another operation x18 -> x1, other arithmetic: 486 us -> 0.62 us  [body(): spot = jnp.stack([lengths[0, 0], seq_index * span]).astype(jnp.int32)]
    pallas_call x0 -> x4, Pallas kernels: none -> 260 us  [the longest x1 120 us: state_forward(): pl.pallas_call(functools.partial(state_kernel, taps, n), grid=(heads // n...]
    squeeze x132 -> x0, local copies, waits for them, and re-layouts: 134 us -> none  [run_span(): final, outs = lax.scan(advance, memory_state, local + (keep,))]
    ppermute x40, waiting for transfers between devices: 378 us -> 495 us  [trade(): lax.ppermute(value, axis, [(place, place ^ 1 << bit) for place in range(c...]
    unnamed x786 -> x437, local copies, waits for them, and re-layouts: 104 us -> 33.6 us
    reduce_sum x25 -> x0, other arithmetic: 57 us -> none  [the longest x3 22.1 us: short_conv(): padded[tap:tap + count] * weight[tap] * valid[:, tap:tap + 1]]
    ppermute x6 -> x12, waiting for transfers between devices: 0.02 us -> 56.1 us  [shifted(): lax.ppermute(value, axis, [(source, source + steps) for source in range(l...]
  transfers between devices with their start and end apart: 59 -> 61, of which waited for: 17 -> 20; matrix products, arithmetic and copies ran while one was open for 78% -> 33% of each run, Pallas kernels for 0% -> 19%
where the time goes in v2:
time: 1380 us
  waiting for transfers between devices  555 us (40%)
  matrix products  364 us (26%)
  Pallas kernels  260 us (19%)
  starting transfers between devices  74.3 us (5%)
  local copies, waits for them, and re-layouts  63.2 us (5%)
  other arithmetic  56.3 us (4%)
    ppermute x40, waiting for transfers between devices, trade(): lax.ppermute(value, axis, [(place, place ^ 1 << bit) for place in range(c...  495 us
    dot_general x27, matrix products, weight_grad(): jnp.einsum('td,tc->dc', rows, grads, preferred_element_type=jnp.float32)  137 us
    pallas_call x1, Pallas kernels, state_forward(): pl.pallas_call(functools.partial(state_kernel, taps, n), grid=(heads // n...  120 us
    pallas_call x1, Pallas kernels, state_backward(): pl.pallas_call(functools.partial(state_back_kernel, taps, n), grid=(heads...  118 us
    dot_general x16, matrix products, rows_back(): jnp.einsum('tc,dc->td', left, weight, preferred_element_type=jnp.float32)  105 us
    ppermute x12, waiting for transfers between devices, shifted(): lax.ppermute(value, axis, [(source, source + steps) for source in range(l...  56.1 us
    dot_general x7, matrix products, project(): return jnp.dot(rows, weight, preferred_element_type=jnp.float32)  56 us
    ppermute x40, starting transfers between devices, trade(): lax.ppermute(value, axis, [(place, place ^ 1 << bit) for place in range(c...  44.1 us
  transfers between devices with their start and end apart: 61, of which 20 were waited for; matrix products, arithmetic and copies ran while one was open for 33% of the time, Pallas kernels for 19%

profile of v2, /device:TPU:0, one launch (start us, length us, event | category | flops | bytes accessed | tf_op | source)
XLA Modules:
  0.0 1376.7 jit_solution(17928617541074975238)
XLA Ops:
  12.1 11.0 fusion.209.v_ref
  45.7 120.1 %shard_map.356 = (f32[768,2048]{1,0:T(8,128)}, bf16[768,1024]{1,0:T(8,128)(2,1)}, bf16[8,128,128]{2,1,0:T(8,128)(2,1)}, bf16[8,128,256]{2,1,0:T(8,128)(2,1)}, bf...) custom-call(s32[2]{0:T(128)} %pad_add_fusion.spot, f32[768,1024]{1,0:T(8,128)} %copy-done.149, ...), custom_call_target="tpu_custom_call" | custom-call | flops 4089446400 | bytes 24576000 | tf_op jit(solution)/shard_map/pallas_call | solution.py:273
  173.6 10.6 fusion.210.gate_ref
  185.2 11.9 collective-permute-done.6.far_ref
  197.8 10.1 shard_map.357
  244.9 11.6 fusion.211
  256.4 14.9 %fusion.212 = f32[768,2816]{1,0:T(8,128)} fusion(bf16[768,2048]{1,0:T(8,128)(2,1)S(1)} %constant_dynamic-update-slice_fusion.32, bf16[2048,2816]{1,0:T(8,128)(2,1)} %param.40), kind=kOutput, calls=%fused_computation.422 | convolution fusion | flops 8858370048 | bytes 23330816 | tf_op jit(solution)/shard_map/dot_general | solution.py:874
  271.3 23.4 %multiply_convert_fusion = (bf16[768,2816]{1,0:T(8,128)(2,1)}, bf16[768,2816]{1,0:T(8,128)(2,1)}, bf16[768,2816]{1,0:T(8,128)(2,1)}) fusion(f32[768,2816]{1,0:T(8,128)} %fusion.211, f32[768,2816]{1,0:T(8,128)} %fusion.212, bf16[768,2048]{1,0:T(8,128)(2,1)} %copy-done.14, bf16[2816,2048]{1,0:T(8,128)(2,1)} %param.41), kind=kOutput, calls=%fused_computation.4 | convolution fusion | flops 8892973056 | bytes 44957696 | tf_op jit(solution)/shard_map/td,fd->tf/dot_general | solution.py:1024
  294.8 10.0 convolution_convert_fusion
  306.4 10.0 fusion.20
  316.4 12.3 convolution_add_fusion.6
  335.3 10.4 convolution_convert_fusion.1
  354.4 9.8 fusion.23
  364.3 13.9 %multiply_reduce_fusion = (f32[2048]{0:T(1024)}, f32[384]{0:T(512)S(1)}, f32[384,2048]{1,0:T(8,128)}) fusion(f32[384,2048]{1,0:T(8,128)S(1)} %get-tuple-element.230, f32[384]{0:T(512)S(1)} %fusion.180, f32[2048]{0:T(1024)S(1)} %copy-done.123, f32[384,2048]{1,0:T(8,128)} %collective-permute-done.11, f32[384,2048]{1,0:T(8,128)} %fusion.23, ...), kind=kOutput, calls=%fused_computation.45 | convolution fusion | flops 4435473920 | bytes 26299396 | tf_op jit(solution)/shard_map/tc,dc->td/dot_general | solution.py:882
  390.0 10.6 fusion.30
  409.9 11.5 shard_map.358
  424.1 9.1 fusion.37
  458.9 26.0 %collective-permute-done.15.far_ref = bf16[8,128,256]{2,1,0:T(8,128)(2,1)S(1)} collective-permute-done((bf16[8,128,256]{2,1,0:T(8,128)(2,1)}, bf16[8,128,256]{2,1,0:T(8,128)(2,1)S(1)}, u32[]{:S(2)}, u32[]{:S(2)}) %collective-permute-start.15) | collective-permute-done | bytes 524320 | tf_op jit(solution)/shard_map/ppermute | solution.py:862
  485.7 118.3 %shard_map.359 = (bf16[768,1024]{1,0:T(8,128)(2,1)}, bf16[768,1024]{1,0:T(8,128)(2,1)}, bf16[768,2048]{1,0:T(8,128)(2,1)}, f32[8,1024]{1,0:T(8,128)}, f32[8,1024...) custom-call(s32[2]{0:T(128)} %pad_add_fusion.spot, ...), custom_call_target="tpu_custom_call" | custom-call | flops 7864320000 | bytes 36864000 | tf_op jit(solution)/shard_map/pallas_call | solution.py:764
  611.9 17.4 %collective-permute-done.17 = f32[8,1024]{1,0:T(8,128)S(1)} collective-permute-done((f32[8,1024]{1,0:T(8,128)S(1)}, f32[8,1024]{1,0:T(8,128)S(1)}, u32[]{:S(2)}, u32[]{:S(2)}) %collective-permute-start.17) | collective-permute-done | bytes 32800 | tf_op jit(solution)/shard_map/ppermute | solution.py:862
  756.3 66.8 %collective-permute-done.21 = f32[20752]{0:T(1024)S(1)} collective-permute-done((f32[20752]{0:T(1024)S(1)}, f32[20752]{0:T(1024)S(1)}, u32[]{:S(2)}, u32[]{:S(2)}) %collective-permute-start.21) | collective-permute-done | bytes 83040 | tf_op jit(solution)/shard_map/ppermute | solution.py:895
  851.8 15.5 %collective-permute-done.42 = bf16[512,1024]{1,0:T(8,128)(2,1)S(1)} collective-permute-done((bf16[512,1024]{1,0:T(8,128)(2,1)}, bf16[512,1024]{1,0:T(8,128)(2,1)S(1)}, u32[]{:S(2)}, u32[]{:S(2)}) %collective-permute-start.42) | collective-permute-done | bytes 1048608 | tf_op jit(solution)/shard_map/ppermute | solution.py:895
  890.8 139.0 %collective-permute-done.39 = bf16[256,1024]{1,0:T(8,128)(2,1)S(1)} collective-permute-done((bf16[256,1024]{1,0:T(8,128)(2,1)S(1)}, bf16[256,1024]{1,0:T(8,128)(2,1)S(1)}, u32[]{:S(2)}, u32[]{:S(2)}) %collective-permute-start.39) | collective-permute-done | bytes 524320 | tf_op jit(solution)/shard_map/ppermute | solution.py:895
  1045.5 13.8 %collective-permute-done.44 = bf16[128,1024]{1,0:T(8,128)(2,1)S(1)} collective-permute-done((bf16[128,1024]{1,0:T(8,128)(2,1)S(1)}, bf16[128,1024]{1,0:T(8,128)(2,1)S(1)}, u32[]{:S(2)}, u32[]{:S(2)}) %collective-permute-start.44) | collective-permute-done | bytes 262176 | tf_op jit(solution)/shard_map/ppermute | solution.py:895
  1065.0 30.5 %collective-permute-done.50 = bf16[512,2816]{1,0:T(8,128)(2,1)} collective-permute-done((bf16[512,2816]{1,0:T(8,128)(2,1)}, bf16[512,2816]{1,0:T(8,128)(2,1)}, u32[]{:S(2)}, u32[]{:S(2)}) %collective-permute-start.50) | collective-permute-done | bytes 2883616 | tf_op jit(solution)/shard_map/ppermute | solution.py:895
  1110.8 12.8 collective-permute-done.26
  1129.5 39.1 %collective-permute-done.27 = bf16[256,1280]{1,0:T(8,128)(2,1)S(1)} collective-permute-done((bf16[256,1280]{1,0:T(8,128)(2,1)S(1)}, bf16[256,1280]{1,0:T(8,128)(2,1)S(1)}, u32[]{:S(2)}, u32[]{:S(2)}) %collective-permute-start.27) | collective-permute-done | bytes 655392 | tf_op jit(solution)/shard_map/ppermute | solution.py:895
  1175.3 25.2 %collective-permute-done.28 = bf16[128,1280]{1,0:T(8,128)(2,1)S(1)} collective-permute-done((bf16[128,1280]{1,0:T(8,128)(2,1)S(1)}, bf16[128,1280]{1,0:T(8,128)(2,1)S(1)}, u32[]{:S(2)}, u32[]{:S(2)}) %collective-permute-start.28) | collective-permute-done | bytes 327712 | tf_op jit(solution)/shard_map/ppermute | solution.py:895
  1204.7 87.7 %collective-permute-done.32 = bf16[128,1408]{1,0:T(8,128)(2,1)S(1)} collective-permute-done((bf16[128,1408]{1,0:T(8,128)(2,1)S(1)}, bf16[128,1408]{1,0:T(8,128)(2,1)S(1)}, u32[]{:S(2)}, u32[]{:S(2)}) %collective-permute-start.32) | collective-permute-done | bytes 360480 | tf_op jit(solution)/shard_map/ppermute | solution.py:895
  1297.9 13.3 collective-permute-done.36
  1332.6 15.7 %collective-permute-done.47 = bf16[256,2048]{1,0:T(8,128)(2,1)} collective-permute-done((bf16[256,2048]{1,0:T(8,128)(2,1)}, bf16[256,2048]{1,0:T(8,128)(2,1)}, u32[]{:S(2)}, u32[]{:S(2)}) %collective-permute-start.47) | collective-permute-done | bytes 1048608 | tf_op jit(solution)/shard_map/ppermute | solution.py:895
  1352.6 21.4 %collective-permute-done.48 = bf16[128,2048]{1,0:T(8,128)(2,1)S(1)} collective-permute-done((bf16[128,2048]{1,0:T(8,128)(2,1)S(1)}, bf16[128,2048]{1,0:T(8,128)(2,1)S(1)}, u32[]{:S(2)}, u32[]{:S(2)}) %collective-permute-start.48) | collective-permute-done | bytes 524320 | tf_op jit(solution)/shard_map/ppermute | solution.py:895
  (683 shorter events, 419.4 us)
Async XLA Ops:
  6.2 212.7 %collective-permute-start.10 = (bf16[384,2048]{1,0:T(8,128)(2,1)}, bf16[384,2048]{1,0:T(8,128)(2,1)}, u32[]{:S(2)}, u32[]{:S(2)}) collective-permute-start(bf16[384,2048]{1,0:T(8,128)(2,1)} %bitcast.8), channel_id=1, source_target_pairs={{0,1},{1,0},{2,3},{3,2},{4,5},{5,4},{6,7},{7,6},{8,9},{9,8},{10,11... | collective-permute-start | bytes 4718600 | tf_op jit(solution)/shard_map/ppermute | solution.py:932
  242.2 213.5 %collective-permute-start.14 = (bf16[8,128,128]{2,1,0:T(8,128)(2,1)}, bf16[8,128,128]{2,1,0:T(8,128)(2,1)}, u32[]{:S(2)}, u32[]{:S(2)}) collective-permute-start(bf16[8,128,128]{2,1,0:T(8,128)(2,1)} %get-tuple-element.52), channel_id=1, source_target_pairs={{2,0},{4,2},{6,4},{3,1},{5,3},{7,5},{10,8},{12,10},{14,12},{11,9},... | collective-permute-start | bytes 786440 | tf_op jit(solution)/shard_map/ppermute | solution.py:862
  304.8 402.9 %collective-permute-start.57 = (bf16[1024,2816]{1,0:T(8,128)(2,1)}, bf16[1024,2816]{1,0:T(8,128)(2,1)}, u32[]{:S(2)}, u32[]{:S(2)}) collective-permute-start(bf16[1024,2816]{1,0:T(8,128)(2,1)} %convolution_convert_fusion), channel_id=1, source_target_pairs={{0,8},{8,0},{16,24},{24,16},{1,9},{9,1},{17,25},{25,17},{2,10},{10... | collective-permute-start | bytes 17301512 | tf_op jit(solution)/shard_map/ppermute | solution.py:895
  345.6 355.6 %collective-permute-start.53 = (bf16[1024,2816]{1,0:T(8,128)(2,1)}, bf16[1024,2816]{1,0:T(8,128)(2,1)}, u32[]{:S(2)}, u32[]{:S(2)}) collective-permute-start(bf16[1024,2816]{1,0:T(8,128)(2,1)} %convolution_convert_fusion.1), channel_id=1, source_target_pairs={{0,4},{2,6},{4,0},{6,2},{1,5},{3,7},{5,1},{7,3},{8,12},{10,14},{12... | collective-permute-start | bytes 17301512 | tf_op jit(solution)/shard_map/ppermute | solution.py:895
  421.4 37.4 %collective-permute-start.13 = (bf16[8,128,256]{2,1,0:T(8,128)(2,1)}, bf16[8,128,256]{2,1,0:T(8,128)(2,1)S(1)}, u32[]{:S(2)}, u32[]{:S(2)}) collective-permute-start(bf16[8,128,256]{2,1,0:T(8,128)(2,1)} %get-tuple-element.61), channel_id=1, source_target_pairs={{2,0},{4,2},{6,4},{3,1},{5,3},{7,5},{10,8},{12,10},{14,12},{11,9},... | collective-permute-start | bytes 1572872 | tf_op jit(solution)/shard_map/ppermute | solution.py:862
  422.7 62.1 %collective-permute-start.15 = (bf16[8,128,256]{2,1,0:T(8,128)(2,1)}, bf16[8,128,256]{2,1,0:T(8,128)(2,1)S(1)}, u32[]{:S(2)}, u32[]{:S(2)}) collective-permute-start(bf16[8,128,256]{2,1,0:T(8,128)(2,1)} %get-tuple-element.61), channel_id=1, source_target_pairs={{4,0},{6,2},{5,1},{7,3},{12,8},{14,10},{13,9},{15,11},{20,16},{22,... | collective-permute-start | bytes 1572872 | tf_op jit(solution)/shard_map/ppermute | solution.py:862
  455.7 236.6 %collective-permute-start.49 = (bf16[1024,2816]{1,0:T(8,128)(2,1)}, bf16[1024,2816]{1,0:T(8,128)(2,1)}, u32[]{:S(2)}, u32[]{:S(2)}) collective-permute-start(bf16[1024,2816]{1,0:T(8,128)(2,1)} %convolution_convert_fusion.2), channel_id=1, source_target_pairs={{0,2},{2,0},{4,6},{6,4},{1,3},{3,1},{5,7},{7,5},{8,10},{10,8},{12,... | collective-permute-start | bytes 17301512 | tf_op jit(solution)/shard_map/ppermute | solution.py:895
  458.8 274.9 %collective-permute-start.37 = (bf16[1024,1024]{1,0:T(8,128)(2,1)}, bf16[1024,1024]{1,0:T(8,128)(2,1)}, u32[]{:S(2)}, u32[]{:S(2)}) collective-permute-start(bf16[1024,1024]{1,0:T(8,128)(2,1)} %convolution_convert_fusion.9), channel_id=1, source_target_pairs={{0,2},{2,0},{4,6},{6,4},{1,3},{3,1},{5,7},{7,5},{8,10},{10,8},{12,... | collective-permute-start | bytes 6291464 | tf_op jit(solution)/shard_map/ppermute | solution.py:895
  650.0 95.0 %collective-permute-start.41 = (bf16[1024,1024]{1,0:T(8,128)(2,1)}, bf16[1024,1024]{1,0:T(8,128)(2,1)}, u32[]{:S(2)}, u32[]{:S(2)}) collective-permute-start(bf16[1024,1024]{1,0:T(8,128)(2,1)} %convolution_convert_fusion.8), channel_id=1, source_target_pairs={{0,4},{2,6},{4,0},{6,2},{1,5},{3,7},{5,1},{7,3},{8,12},{10,14},{12... | collective-permute-start | bytes 6291464 | tf_op jit(solution)/shard_map/ppermute | solution.py:895
  692.3 175.5 %collective-permute-start.25 = (bf16[1024,1280]{1,0:T(8,128)(2,1)}, bf16[1024,1280]{1,0:T(8,128)(2,1)}, u32[]{:S(2)}, u32[]{:S(2)}) collective-permute-start(bf16[1024,1280]{1,0:T(8,128)(2,1)} %convolution_convert_fusion.5), channel_id=1, source_target_pairs={{0,2},{2,0},{4,6},{6,4},{1,3},{3,1},{5,7},{7,5},{8,10},{10,8},{12,... | collective-permute-start | bytes 7864328 | tf_op jit(solution)/shard_map/ppermute | solution.py:895
  701.2 183.6 %collective-permute-start.33 = (bf16[1024,1424]{0,1:T(8,128)(2,1)}, bf16[1024,1424]{0,1:T(8,128)(2,1)}, u32[]{:S(2)}, u32[]{:S(2)}) collective-permute-start(bf16[1024,1424]{0,1:T(8,128)(2,1)} %convolution_convert_fusion.3), channel_id=1, source_target_pairs={{0,8},{8,0},{16,24},{24,16},{1,9},{9,1},{17,25},{25,17},{2,10},{10... | collective-permute-start | bytes 8749064 | tf_op jit(solution)/shard_map/ppermute | solution.py:895
  733.7 142.3 %collective-permute-start.29 = (bf16[1024,1408]{1,0:T(8,128)(2,1)}, bf16[1024,1408]{1,0:T(8,128)(2,1)}, u32[]{:S(2)}, u32[]{:S(2)}) collective-permute-start(bf16[1024,1408]{1,0:T(8,128)(2,1)} %convolution_convert_fusion.4), channel_id=1, source_target_pairs={{0,4},{2,6},{4,0},{6,2},{1,5},{3,7},{5,1},{7,3},{8,12},{10,14},{12... | collective-permute-start | bytes 8650760 | tf_op jit(solution)/shard_map/ppermute | solution.py:895
  737.2 110.5 %collective-permute-start.38 = (bf16[512,1024]{1,0:T(8,128)(2,1)}, bf16[512,1024]{1,0:T(8,128)(2,1)}, u32[]{:S(2)}, u32[]{:S(2)}) collective-permute-start(bf16[512,1024]{1,0:T(8,128)(2,1)} %add_convert_fusion.7), channel_id=1, source_target_pairs={{0,4},{2,6},{4,0},{6,2},{1,5},{3,7},{5,1},{7,3},{8,12},{10,14},{12... | collective-permute-start | bytes 3145736 | tf_op jit(solution)/shard_map/ppermute | solution.py:895
  752.3 70.8 %collective-permute-start.21 = (f32[20752]{0:T(1024)S(1)}, f32[20752]{0:T(1024)S(1)}, u32[]{:S(2)}, u32[]{:S(2)}) collective-permute-start(f32[20752]{0:T(1024)S(1)} %add.523), channel_id=1, source_target_pairs={{0,4},{2,6},{4,0},{6,2},{1,5},{3,7},{5,1},{7,3},{8,12},{10,14},{12... | collective-permute-start | bytes 249032 | tf_op jit(solution)/shard_map/ppermute | solution.py:895
  847.6 252.4 %collective-permute-start.45 = (bf16[1024,2048]{1,0:T(8,128)(2,1)}, bf16[1024,2048]{1,0:T(8,128)(2,1)}, u32[]{:S(2)}, u32[]{:S(2)}) collective-permute-start(bf16[1024,2048]{1,0:T(8,128)(2,1)} %convolution_convert_fusion.6), channel_id=1, source_target_pairs={{0,8},{8,0},{16,24},{24,16},{1,9},{9,1},{17,25},{25,17},{2,10},{10... | collective-permute-start | bytes 12582920 | tf_op jit(solution)/shard_map/ppermute | solution.py:895
  867.3 194.3 %collective-permute-start.58 = (bf16[512,2816]{1,0:T(8,128)(2,1)S(1)}, bf16[512,2816]{1,0:T(8,128)(2,1)S(1)}, u32[]{:S(2)}, u32[]{:S(2)}) collective-permute-start(bf16[512,2816]{1,0:T(8,128)(2,1)S(1)} %copy-done.158), channel_id=1, source_target_pairs={{0,2},{2,0},{4,6},{6,4},{1,3},{3,1},{5,7},{7,5},{8,10},{10,8},{12,... | collective-permute-start | bytes 8650760 | tf_op jit(solution)/shard_map/ppermute | solution.py:895
  867.8 195.5 %collective-permute-start.54 = (bf16[512,2816]{1,0:T(8,128)(2,1)}, bf16[512,2816]{1,0:T(8,128)(2,1)S(1)}, u32[]{:S(2)}, u32[]{:S(2)}) collective-permute-start(bf16[512,2816]{1,0:T(8,128)(2,1)} %add_convert_fusion.1), channel_id=1, source_target_pairs={{0,8},{8,0},{16,24},{24,16},{1,9},{9,1},{17,25},{25,17},{2,10},{10... | collective-permute-start | bytes 8650760 | tf_op jit(solution)/shard_map/ppermute | solution.py:895
  876.0 153.8 %collective-permute-start.39 = (bf16[256,1024]{1,0:T(8,128)(2,1)S(1)}, bf16[256,1024]{1,0:T(8,128)(2,1)S(1)}, u32[]{:S(2)}, u32[]{:S(2)}) collective-permute-start(bf16[256,1024]{1,0:T(8,128)(2,1)S(1)} %get-tuple-element.203), channel_id=1, source_target_pairs={{0,8},{8,0},{16,24},{24,16},{1,9},{9,1},{17,25},{25,17},{2,10},{10... | collective-permute-start | bytes 1572872 | tf_op jit(solution)/shard_map/ppermute | solution.py:895
  884.8 145.5 %collective-permute-start.43 = (bf16[256,1024]{1,0:T(8,128)(2,1)S(1)}, bf16[256,1024]{1,0:T(8,128)(2,1)S(1)}, u32[]{:S(2)}, u32[]{:S(2)}) collective-permute-start(bf16[256,1024]{1,0:T(8,128)(2,1)S(1)} %get-tuple-element.205), channel_id=1, source_target_pairs={{0,2},{2,0},{4,6},{6,4},{1,3},{3,1},{5,7},{7,5},{8,10},{10,8},{12,... | collective-permute-start | bytes 1572872 | tf_op jit(solution)/shard_map/ppermute | solution.py:895
  1029.8 65.7 %collective-permute-start.50 = (bf16[512,2816]{1,0:T(8,128)(2,1)}, bf16[512,2816]{1,0:T(8,128)(2,1)}, u32[]{:S(2)}, u32[]{:S(2)}) collective-permute-start(bf16[512,2816]{1,0:T(8,128)(2,1)} %add_convert_fusion.2), channel_id=1, source_target_pairs={{0,4},{2,6},{4,0},{6,2},{1,5},{3,7},{5,1},{7,3},{8,12},{10,14},{12... | collective-permute-start | bytes 8650760 | tf_op jit(solution)/shard_map/ppermute | solution.py:895
  1059.2 64.4 %collective-permute-start.26 = (bf16[512,1280]{1,0:T(8,128)(2,1)}, bf16[512,1280]{1,0:T(8,128)(2,1)}, u32[]{:S(2)}, u32[]{:S(2)}) collective-permute-start(bf16[512,1280]{1,0:T(8,128)(2,1)} %fusion.15), channel_id=1, source_target_pairs={{0,4},{2,6},{4,0},{6,2},{1,5},{3,7},{5,1},{7,3},{8,12},{10,14},{12... | collective-permute-start | bytes 3932168 | tf_op jit(solution)/shard_map/ppermute | solution.py:895
  1061.6 63.9 %collective-permute-start.30 = (bf16[512,1408]{1,0:T(8,128)(2,1)}, bf16[512,1408]{1,0:T(8,128)(2,1)}, u32[]{:S(2)}, u32[]{:S(2)}) collective-permute-start(bf16[512,1408]{1,0:T(8,128)(2,1)} %fusion.14), channel_id=1, source_target_pairs={{0,8},{8,0},{16,24},{24,16},{1,9},{9,1},{17,25},{25,17},{2,10},{10... | collective-permute-start | bytes 4325384 | tf_op jit(solution)/shard_map/ppermute | solution.py:895
  1063.3 65.7 %collective-permute-start.34 = (bf16[512,1424]{0,1:T(8,128)(2,1)}, bf16[512,1424]{0,1:T(8,128)(2,1)S(1)}, u32[]{:S(2)}, u32[]{:S(2)}) collective-permute-start(bf16[512,1424]{0,1:T(8,128)(2,1)} %fusion.13), channel_id=1, source_target_pairs={{0,2},{2,0},{4,6},{6,4},{1,3},{3,1},{5,7},{7,5},{8,10},{10,8},{12,... | collective-permute-start | bytes 4374536 | tf_op jit(solution)/shard_map/ppermute | solution.py:895
  1095.6 73.1 %collective-permute-start.59 = (bf16[256,2816]{1,0:T(8,128)(2,1)}, bf16[256,2816]{1,0:T(8,128)(2,1)S(1)}, u32[]{:S(2)}, u32[]{:S(2)}) collective-permute-start(bf16[256,2816]{1,0:T(8,128)(2,1)} %get-tuple-element.155), channel_id=1, source_target_pairs={{0,4},{2,6},{4,0},{6,2},{1,5},{3,7},{5,1},{7,3},{8,12},{10,14},{12... | collective-permute-start | bytes 4325384 | tf_op jit(solution)/shard_map/ppermute | solution.py:895
  1100.0 70.3 %collective-permute-start.55 = (bf16[256,2816]{1,0:T(8,128)(2,1)S(1)}, bf16[256,2816]{1,0:T(8,128)(2,1)S(1)}, u32[]{:S(2)}, u32[]{:S(2)}) collective-permute-start(bf16[256,2816]{1,0:T(8,128)(2,1)S(1)} %copy-done.48), channel_id=1, source_target_pairs={{0,2},{2,0},{4,6},{6,4},{1,3},{3,1},{5,7},{7,5},{8,10},{10,8},{12,... | collective-permute-start | bytes 4325384 | tf_op jit(solution)/shard_map/ppermute | solution.py:895
  1123.6 49.5 %collective-permute-start.51 = (bf16[256,2816]{1,0:T(8,128)(2,1)S(1)}, bf16[256,2816]{1,0:T(8,128)(2,1)S(1)}, u32[]{:S(2)}, u32[]{:S(2)}) collective-permute-start(bf16[256,2816]{1,0:T(8,128)(2,1)S(1)} %get-tuple-element.159), channel_id=1, source_target_pairs={{0,8},{8,0},{16,24},{24,16},{1,9},{9,1},{17,25},{25,17},{2,10},{10... | collective-permute-start | bytes 4325384 | tf_op jit(solution)/shard_map/ppermute | solution.py:895
  1125.5 43.1 %collective-permute-start.27 = (bf16[256,1280]{1,0:T(8,128)(2,1)S(1)}, bf16[256,1280]{1,0:T(8,128)(2,1)S(1)}, u32[]{:S(2)}, u32[]{:S(2)}) collective-permute-start(bf16[256,1280]{1,0:T(8,128)(2,1)S(1)} %get-tuple-element.167), channel_id=1, source_target_pairs={{0,8},{8,0},{16,24},{24,16},{1,9},{9,1},{17,25},{25,17},{2,10},{10... | collective-permute-start | bytes 1966088 | tf_op jit(solution)/shard_map/ppermute | solution.py:895
  1129.0 188.9 %collective-permute-start.46 = (bf16[512,2048]{1,0:T(8,128)(2,1)}, bf16[512,2048]{1,0:T(8,128)(2,1)}, u32[]{:S(2)}, u32[]{:S(2)}) collective-permute-start(bf16[512,2048]{1,0:T(8,128)(2,1)} %add_convert_fusion.3), channel_id=1, source_target_pairs={{0,2},{2,0},{4,6},{6,4},{1,3},{3,1},{5,7},{7,5},{8,10},{10,8},{12,... | collective-permute-start | bytes 6291464 | tf_op jit(solution)/shard_map/ppermute | solution.py:895
  1173.1 151.7 %collective-permute-start.60 = (bf16[128,2816]{1,0:T(8,128)(2,1)}, bf16[128,2816]{1,0:T(8,128)(2,1)}, u32[]{:S(2)}, u32[]{:S(2)}) collective-permute-start(bf16[128,2816]{1,0:T(8,128)(2,1)} %fusion.49), channel_id=1, source_target_pairs={{0,16},{8,24},{16,0},{24,8},{1,17},{9,25},{17,1},{25,9},{2,18},{10... | collective-permute-start | bytes 2162696 | tf_op jit(solution)/shard_map/ppermute | solution.py:895
  1200.5 126.8 %collective-permute-start.56 = (bf16[128,2816]{1,0:T(8,128)(2,1)}, bf16[128,2816]{1,0:T(8,128)(2,1)}, u32[]{:S(2)}, u32[]{:S(2)}) collective-permute-start(bf16[128,2816]{1,0:T(8,128)(2,1)} %fusion.52), channel_id=1, source_target_pairs={{0,16},{8,24},{16,0},{24,8},{1,17},{9,25},{17,1},{25,9},{2,18},{10... | collective-permute-start | bytes 2162696 | tf_op jit(solution)/shard_map/ppermute | solution.py:895
  1200.6 149.3 %collective-permute-start.52 = (bf16[128,2816]{1,0:T(8,128)(2,1)}, bf16[128,2816]{1,0:T(8,128)(2,1)}, u32[]{:S(2)}, u32[]{:S(2)}) collective-permute-start(bf16[128,2816]{1,0:T(8,128)(2,1)} %fusion.54), channel_id=1, source_target_pairs={{0,16},{8,24},{16,0},{24,8},{1,17},{9,25},{17,1},{25,9},{2,18},{10... | collective-permute-start | bytes 2162696 | tf_op jit(solution)/shard_map/ppermute | solution.py:895
  1203.7 88.7 %collective-permute-start.32 = (bf16[128,1408]{1,0:T(8,128)(2,1)S(1)}, bf16[128,1408]{1,0:T(8,128)(2,1)S(1)}, u32[]{:S(2)}, u32[]{:S(2)}) collective-permute-start(bf16[128,1408]{1,0:T(8,128)(2,1)S(1)} %fusion.140), channel_id=1, source_target_pairs={{0,16},{8,24},{16,0},{24,8},{1,17},{9,25},{17,1},{25,9},{2,18},{10... | collective-permute-start | bytes 1081352 | tf_op jit(solution)/shard_map/ppermute | solution.py:895
  (226 other events, 2962.2 us)

commit v3 on v2

v3 whole, which is shorter than its diff:
```python
import functools

import jax
import jax.numpy as jnp
import numpy as np
from jax import lax
from jax.experimental import pallas as pl
from jax.experimental.pallas import tpu as pltpu
from jax.sharding import PartitionSpec as P

HEADS = 16
DK = 128
DV = 256
GROUP = 64
EPS = 1e-06
PAIR = 2 * GROUP
RIM = 8
VMEM_BYTES = 56 * 1024 * 1024


def mm(left, right):
    return lax.dot_general(
        left, right, (((1,), (0,)), ((), ())), preferred_element_type=jnp.float32
    )


def mm_nt(left, right):
    return lax.dot_general(
        left, right, (((1,), (1,)), ((), ())), preferred_element_type=jnp.float32
    )


def mm_tn(left, right):
    return lax.dot_general(
        left, right, (((0,), (0,)), ((), ())), preferred_element_type=jnp.float32
    )


def low(value):
    return value.astype(jnp.bfloat16)


def high(value):
    return value.astype(jnp.float32)


def grid_masks():
    row = lax.broadcasted_iota(jnp.int32, (PAIR, PAIR), 0)
    col = lax.broadcasted_iota(jnp.int32, (PAIR, PAIR), 1)
    same = (row // GROUP) == (col // GROUP)
    return row, col, same & (row >= col), same & (row > col)


def masks_low(row, col):
    sizes, masks = [], []
    size = 1
    while size < GROUP:
        here = ((row // (2 * size)) == (col // (2 * size))) & ((row // size) > (col // size))
        masks.append(low(jnp.where(here, 1.0, 0.0)))
        sizes.append(size)
        size *= 2
    return masks


def sigmoid(value):
    return 0.5 * jnp.tanh(0.5 * value) + 0.5


def unit_scale(value):
    return lax.rsqrt(jnp.sum(value * value, axis=-1, keepdims=True) + EPS)


def column(table, head):
    lane = lax.broadcasted_iota(jnp.int32, table.shape, 1)
    return jnp.sum(jnp.where(lane == head, table, 0.0), axis=1, keepdims=True)


def reset_row(first, base, count):
    inside = (first > base) & (first < base + count)
    return pl.multiple_of(jnp.where(inside, first - base, 0), GROUP)


def reset_places(first, base, reset):
    token = base + reset + lax.broadcasted_iota(jnp.int32, (RIM, 1), 0)
    return token - jnp.where(token >= first, first, 0)


def conv_total(ext, total, weight, reset, places):
    count, taps = total.shape[0], weight.shape[0]
    lead = RIM - taps + 1
    whole = ext[lead : lead + count, :] * weight[0:1, :]
    for tap in range(1, taps):
        whole = whole + ext[lead + tap : lead + tap + count, :] * weight[tap : tap + 1, :]
    total[...] = whole
    near = ext[pl.ds(reset, 2 * RIM), :]
    fixed = near[RIM : 2 * RIM] * weight[taps - 1 : taps, :]
    for tap in range(taps - 1):
        rows = jnp.where(places >= taps - 1 - tap, near[lead + tap : lead + tap + RIM], 0.0)
        fixed = fixed + rows * weight[tap : tap + 1, :]
    total[pl.ds(reset, RIM), :] = fixed


def load_ext(ext, rim, body):
    ext[0:RIM, :] = rim
    ext[RIM : RIM + body.shape[0], :] = body


def load_features(taps, j, refs, ext, total, reset, places):
    q_ref, k_ref, v_ref, q_rim, k_rim, v_rim, conv_q, conv_k, conv_v = refs
    cols = slice(j * DK, (j + 1) * DK)
    sources = [(q_ref, q_rim, conv_q, cols), (k_ref, k_rim, conv_k, cols)]
    for half in range(DV // DK):
        begin = j * DV + half * DK
        sources.append((v_ref, v_rim, conv_v, slice(begin, begin + DK)))
    for piece, (body, rim, weight, cut) in enumerate(sources):
        load_ext(ext.at[j, piece], rim[:, cut], body[:, cut])
        conv_total(ext.at[j, piece], total.at[j, piece], weight[:, cut], reset, places)


def block_ends(g):
    return jnp.concatenate(
        [
            jnp.broadcast_to(g[GROUP - 1 : GROUP], (GROUP, DK)),
            jnp.broadcast_to(g[PAIR - 1 : PAIR], (GROUP, DK)),
        ],
        axis=0,
    )


def decay_tables(decay_ref, beta_ref, log_ref, bias_ref, cum_ref, rate_ref):
    count = decay_ref.shape[0]
    shifted_in = decay_ref[...] + bias_ref[...]
    soft = jnp.maximum(shifted_in, 0.0) + jnp.log1p(jnp.exp(-jnp.abs(shifted_in)))
    log_decay = -jnp.exp(log_ref[...]) * soft
    _, _, within, _ = grid_masks()
    ones = jnp.where(within, 1.0, 0.0)
    for pair in range(count // PAIR):
        rows = slice(pair * PAIR, (pair + 1) * PAIR)
        cum_ref[rows, :] = lax.dot_general(
            ones,
            log_decay[rows, :],
            (((1,), (0,)), ((), ())),
            precision=lax.Precision.HIGHEST,
            preferred_element_type=jnp.float32,
        )
    rate_ref[...] = jax.nn.sigmoid(beta_ref[...])


def state_kernel(
    taps,
    per_step,
    spot,
    q_ref,
    k_ref,
    v_ref,
    q_rim,
    k_rim,
    v_rim,
    conv_q,
    conv_k,
    conv_v,
    decay_ref,
    beta_ref,
    log_ref,
    bias_ref,
    mixed_ref,
    reach_ref,
    map_ref,
    add_ref,
    inverse_ref,
    pass_ref,
    turn_ref,
    gain_ref,
    cum_ref,
    rate_ref,
    ext,
    total,
    cum,
    lower,
    halfway,
    score,
    grown_q,
    grown_k,
    scaled_v,
    tail,
    states,
    starts,
):
    step = pl.program_id(0)
    count = q_ref.shape[0]
    pairs = count // PAIR
    blocks = count // GROUP
    first, base = spot[0], spot[1]
    reset = reset_row(first, base, count)
    places = reset_places(first, base, reset)

    @pl.when(step == 0)
    def _():
        decay_tables(decay_ref, beta_ref, log_ref, bias_ref, cum_ref, rate_ref)

    row, col, within, below = grid_masks()
    refs = (q_ref, k_ref, v_ref, q_rim, k_rim, v_rim, conv_q, conv_k, conv_v)
    for j in range(per_step):
        load_features(taps, j, refs, ext, total, reset, places)
        head = step * per_step + j
        cum[j] = jnp.broadcast_to(column(cum_ref[...], head), (count, DK))
        halfway[j] = jnp.broadcast_to(column(rate_ref[...], head), (count, DK))

    def local(pair, carry):
        at = pl.ds(pl.multiple_of(pair * PAIR, PAIR), PAIR)
        for j in range(per_step):
            g = cum[j, at, :]
            b = halfway[j, at, :]
            u = total[j, 0, at, :]
            c = u * sigmoid(u)
            q = c * (unit_scale(c) * DK**-0.5)
            u = total[j, 1, at, :]
            c = u * sigmoid(u)
            k = c * unit_scale(c)
            k_low = low(k)
            spread = jnp.where(within, jnp.exp(jnp.where(within, g - g.T, 0.0)), 0.0)
            keys = mm_nt(k_low, k_low)
            lower[j, at, :] = low(jnp.where(below, b * keys * spread, 0.0))
            score[j, at, :] = low(mm_nt(low(q), k_low) * spread)
            grown = jnp.exp(g)
            for half in range(DV // DK):
                u = total[j, 2 + half, at, :]
                scaled_v[j, at, half * DK : (half + 1) * DK] = low(b * (u * sigmoid(u)))
            grown_k[j, at, :] = low(b * grown * k)
            tail[j, at, :] = low(jnp.exp(block_ends(g) - g) * k)
            grown_q[j, at, :] = grown * q
        return carry

    lax.fori_loop(0, pairs, local, 0, unroll=2)

    masks = masks_low(row, col)
    spots = [
        (j, slice(pair * PAIR, (pair + 1) * PAIR))
        for pair in range(pairs)
        for j in range(per_step)
    ]
    eye = low(jnp.where(row == col, 1.0, 0.0))
    for j, at in spots:
        inverse_ref[j, at, :] = eye - lower[j, at, :] * masks[0]
    for mask in masks[1:]:
        for j, at in spots:
            halfway[j, at, :] = mm(lower[j, at, :] * mask, inverse_ref[j, at, :])
        for j, at in spots:
            inverse = inverse_ref[j, at, :]
            inverse_ref[j, at, :] = inverse - low(mm(inverse, low(halfway[j, at, :])))

    def combine(pair, carry):
        at = pl.ds(pl.multiple_of(pair * PAIR, PAIR), PAIR)
        for j in range(per_step):
            cols = slice(j * DK, (j + 1) * DK)
            wide = slice(j * DV, (j + 1) * DV)
            inverse = inverse_ref[j, at, :]
            scored = score[j, at, :]
            u_low = low(mm(inverse, scaled_v[j, at, :]))
            w_low = low(mm(inverse, grown_k[j, at, :]))
            mixed_ref[at, wide] = mm(scored, u_low)
            pass_ref[at, cols] = low(grown_q[j, at, :] - mm(scored, w_low))
            falls = tail[j, at, :]
            for half in range(2):
                part = slice(half * GROUP, (half + 1) * GROUP)
                turn_ref[j, 2 * pair + half] = low(mm_tn(falls[part], w_low[part]))
                gain_ref[j, 2 * pair + half] = low(mm_tn(falls[part], u_low[part]))
        return carry

    lax.fori_loop(0, pairs, combine, 0, unroll=2)

    for j in range(per_step):
        states[j] = jnp.concatenate(
            [jnp.where(row == col, 1.0, 0.0), jnp.zeros((DK, DV), jnp.float32)], axis=1
        )

    def advance(block, carry):
        begin = base + block * GROUP
        keep = jnp.where((begin != 0) & (begin != first), 1.0, 0.0)
        for j in range(per_step):
            state = states[j] * keep
            state_low = low(state)
            starts[j, block] = state_low
            last = jnp.exp(cum[j, pl.ds(block * GROUP + GROUP - 1, 1), :])
            last = jnp.concatenate([last] * 3, axis=1)
            moved = last * state - mm(turn_ref[j, block], state_low)
            states[j, :, :DK] = moved[:, :DK]
            states[j, :, DK:] = moved[:, DK:] + high(gain_ref[j, block])
        return carry

    lax.fori_loop(0, blocks, advance, 0, unroll=2)

    def close(block, carry):
        at = pl.ds(pl.multiple_of(block * GROUP, GROUP), GROUP)
        for j in range(per_step):
            cols = slice(j * DK, (j + 1) * DK)
            wide = slice(j * DV, (j + 1) * DV)
            out = mm(pass_ref[at, cols], starts[j, block])
            reach_ref[at, cols] = low(out[:, :DK])
            mixed_ref[at, wide] = mixed_ref[at, wide] + out[:, DK:]
        return carry

    lax.fori_loop(0, blocks, close, 0, unroll=4)
    for j in range(per_step):
        map_ref[j] = low(states[j, :, :DK])
        add_ref[j] = low(states[j, :, DK:])


def spec(shape, index):
    return pl.BlockSpec(shape, index)


def state_forward(q, k, v, rims, convs, decay, beta, decay_log, decay_bias, spot, per_step):
    count = q.shape[0]
    heads = decay.shape[1]
    taps = convs[0].shape[0]
    n = per_step
    blocks = count // GROUP
    along = lambda i: (0, i)
    fixed = lambda i: (0, 0)
    lead = lambda i: (i, 0, 0)
    lead4 = lambda i: (i, 0, 0, 0)
    f32, bf16 = jnp.float32, jnp.bfloat16
    shape = jax.ShapeDtypeStruct
    vm = pltpu.VMEM
    return pl.pallas_call(
        functools.partial(state_kernel, taps, n),
        grid=(heads // n,),
        in_specs=[
            pl.BlockSpec(memory_space=pltpu.SMEM),
            spec((count, n * DK), along),
            spec((count, n * DK), along),
            spec((count, n * DV), along),
            spec((RIM, n * DK), along),
            spec((RIM, n * DK), along),
            spec((RIM, n * DV), along),
            spec((taps, n * DK), along),
            spec((taps, n * DK), along),
            spec((taps, n * DV), along),
            spec((count, heads), fixed),
            spec((count, heads), fixed),
            spec((1, heads), fixed),
            spec((1, heads), fixed),
        ],
        out_specs=[
            spec((count, n * DV), along),
            spec((count, n * DK), along),
            spec((n, DK, DK), lead),
            spec((n, DK, DV), lead),
            spec((n, count, PAIR), lead),
            spec((count, n * DK), along),
            spec((n, blocks, DK, DK), lead4),
            spec((n, blocks, DK, DV), lead4),
            spec((count, heads), fixed),
            spec((count, heads), fixed),
        ],
        out_shape=[
            shape((count, heads * DV), f32),
            shape((count, heads * DK), bf16),
            shape((heads, DK, DK), bf16),
            shape((heads, DK, DV), bf16),
            shape((heads, count, PAIR), bf16),
            shape((count, heads * DK), bf16),
            shape((heads, blocks, DK, DK), bf16),
            shape((heads, blocks, DK, DV), bf16),
            shape((count, heads), f32),
            shape((count, heads), f32),
        ],
        scratch_shapes=[
            vm((n, 4, count + RIM, DK), f32),
            vm((n, 4, count, DK), f32),
            vm((n, count, DK), f32),
            vm((n, count, PAIR), bf16),
            vm((n, count, PAIR), f32),
            vm((n, count, PAIR), bf16),
            vm((n, count, DK), f32),
            vm((n, count, DK), bf16),
            vm((n, count, DV), bf16),
            vm((n, count, DK), bf16),
            vm((n, DK, DK + DV), f32),
            vm((n, blocks, DK, DK + DV), bf16),
        ],
        compiler_params=pltpu.CompilerParams(
            dimension_semantics=("arbitrary",), vmem_limit_bytes=VMEM_BYTES
        ),
        cost_estimate=pl.CostEstimate(
            flops=heads * count * 10_000_000, bytes_accessed=count * heads * 4000, transcendentals=0
        ),
    )(spot, q, k, v, *rims, *convs, decay, beta, decay_log, decay_bias)


def silu(value):
    return value * sigmoid(value)


def gate_kernel(per_step, mixed_ref, reach_ref, map_ref, add_ref, far_ref, gate_ref, gain_ref, gated_ref, kept_ref, start_ref):
    for j in range(per_step):
        cols = slice(j * DK, (j + 1) * DK)
        wide = slice(j * DV, (j + 1) * DV)
        start = low(high(add_ref[j]) + mm(map_ref[j], far_ref[j]))
        start_ref[j] = start
        mixed = mixed_ref[:, wide] + mm(reach_ref[:, cols], start)
        kept_ref[:, wide] = low(mixed)
        scale = lax.rsqrt(jnp.mean(mixed * mixed, axis=-1, keepdims=True) + EPS)
        gated_ref[:, wide] = low(mixed * scale * gain_ref[...] * silu(gate_ref[:, wide]))


def gate_forward(mixed, reach, near_map, near_add, far_add, gate, gain, per_step):
    count = mixed.shape[0]
    heads = near_map.shape[0]
    n = per_step
    along = lambda i: (0, i)
    lead = lambda i: (i, 0, 0)
    bf16 = jnp.bfloat16
    return pl.pallas_call(
        functools.partial(gate_kernel, n),
        grid=(heads // n,),
        in_specs=[
            spec((count, n * DV), along),
            spec((count, n * DK), along),
            spec((n, DK, DK), lead),
            spec((n, DK, DV), lead),
            spec((n, DK, DV), lead),
            spec((count, n * DV), along),
            spec((1, DV), lambda i: (0, 0)),
        ],
        out_specs=[
            spec((count, n * DV), along),
            spec((count, n * DV), along),
            spec((n, DK, DV), lead),
        ],
        out_shape=[
            jax.ShapeDtypeStruct((count, heads * DV), bf16),
            jax.ShapeDtypeStruct((count, heads * DV), bf16),
            jax.ShapeDtypeStruct((heads, DK, DV), bf16),
        ],
        compiler_params=pltpu.CompilerParams(
            dimension_semantics=("arbitrary",), vmem_limit_bytes=VMEM_BYTES
        ),
    )(mixed, reach, near_map, near_add, far_add, gate, gain)


def gate_back_kernel(per_step, d_gated_ref, kept_ref, reach_ref, gate_ref, gain_ref, d_mixed_ref, d_gate_ref, d_start_ref, d_gain_ref):
    @pl.when(pl.program_id(0) == 0)
    def _():
        d_gain_ref[...] = jnp.zeros_like(d_gain_ref)

    for j in range(per_step):
        cols = slice(j * DK, (j + 1) * DK)
        wide = slice(j * DV, (j + 1) * DV)
        mixed = high(kept_ref[:, wide])
        scale = lax.rsqrt(jnp.mean(mixed * mixed, axis=-1, keepdims=True) + EPS)
        normal = mixed * scale
        gate = gate_ref[:, wide]
        sig = sigmoid(gate)
        d_gated = d_gated_ref[:, wide]
        d_scaled = d_gated * (gate * sig)
        d_gain_ref[...] += jnp.sum(d_scaled * normal, axis=0, keepdims=True)
        d_gate_ref[:, wide] = low(
            d_gated * (normal * gain_ref[...]) * (sig * (1.0 + gate * (1.0 - sig)))
        )
        d_normal = d_scaled * gain_ref[...]
        d_mixed = low(scale * (d_normal - normal * jnp.mean(d_normal * normal, axis=-1, keepdims=True)))
        d_mixed_ref[:, wide] = d_mixed
        d_start_ref[j] = low(mm_tn(reach_ref[:, cols], d_mixed))


def gate_backward(d_gated, kept, reach, gate, gain, per_step):
    count = kept.shape[0]
    heads = kept.shape[1] // DV
    n = per_step
    along = lambda i: (0, i)
    lead = lambda i: (i, 0, 0)
    bf16 = jnp.bfloat16
    return pl.pallas_call(
        functools.partial(gate_back_kernel, n),
        grid=(heads // n,),
        in_specs=[
            spec((count, n * DV), along),
            spec((count, n * DV), along),
            spec((count, n * DK), along),
            spec((count, n * DV), along),
            spec((1, DV), lambda i: (0, 0)),
        ],
        out_specs=[
            spec((count, n * DV), along),
            spec((count, n * DV), along),
            spec((n, DK, DV), lead),
            spec((1, DV), lambda i: (0, 0)),
        ],
        out_shape=[
            jax.ShapeDtypeStruct((count, heads * DV), bf16),
            jax.ShapeDtypeStruct((count, heads * DV), bf16),
            jax.ShapeDtypeStruct((heads, DK, DV), bf16),
            jax.ShapeDtypeStruct((1, DV), jnp.float32),
        ],
        compiler_params=pltpu.CompilerParams(
            dimension_semantics=("arbitrary",), vmem_limit_bytes=VMEM_BYTES
        ),
    )(d_gated, kept, reach, gate, gain)


def state_back_kernel(
    taps,
    per_step,
    offset,
    extra,
    spot,
    q_ref,
    k_ref,
    v_ref,
    q_rim,
    k_rim,
    v_rim,
    conv_q,
    conv_k,
    conv_v,
    decay_ref,
    log_ref,
    bias_ref,
    cum_ref,
    rate_ref,
    inverse_ref,
    pass_ref,
    turn_ref,
    gain_ref,
    start_ref,
    d_mixed_ref,
    near_ref,
    map_ref,
    far_ref,
    *rest,
):
    (
        dq_ref,
        dk_ref,
        dv_ref,
        dq_rim,
        dk_rim,
        dv_rim,
        dq_end,
        dk_end,
        dv_end,
        d_conv_q,
        d_conv_k,
        d_conv_v,
        d_decay_ref,
        d_beta_ref,
        d_log_ref,
        d_bias_ref,
        ext,
        total,
        query,
        key,
        d_value,
        cum,
        rate,
        starts,
        ends,
        states,
        d_states,
        d_total,
        d_ext,
        d_cum,
        d_rate,
    ) = rest[extra:]
    step = pl.program_id(0)
    count = q_ref.shape[0]
    pairs = count // PAIR
    blocks = count // GROUP
    first, base = spot[0], spot[1]
    reset = reset_row(first, base, count)
    places = reset_places(first, base, reset)

    @pl.when(step == 0)
    def _():
        d_cum[...] = jnp.zeros_like(d_cum)
        d_rate[...] = jnp.zeros_like(d_rate)

    refs = (q_ref, k_ref, v_ref, q_rim, k_rim, v_rim, conv_q, conv_k, conv_v)
    for j in range(per_step):
        load_features(taps, j, refs, ext, total, reset, places)
        head = offset + step * per_step + j
        cum[j] = jnp.broadcast_to(column(cum_ref[...], head), (count, DK))
        rate[j] = jnp.broadcast_to(column(rate_ref[...], head), (count, DK))
        u = total[j, 0]
        c = u * sigmoid(u)
        query[j] = c * (unit_scale(c) * DK**-0.5)
        u = total[j, 1]
        c = u * sigmoid(u)
        key[j] = c * unit_scale(c)
        states[j] = high(start_ref[j])
        d_states[j] = high(near_ref[j]) + mm_tn(map_ref[j], far_ref[j])

    row, col, within, below = grid_masks()

    def keep_of(block):
        begin = base + block * GROUP
        return jnp.where((begin != 0) & (begin != first), 1.0, 0.0)

    def last_of(j, block):
        last = jnp.exp(cum[j, pl.ds(block * GROUP + GROUP - 1, 1), :])
        return jnp.concatenate([last, last], axis=1)

    def chain(block, carry):
        back = blocks - 1 - block
        at = pl.ds(pl.multiple_of(back * GROUP, GROUP), GROUP)
        for j in range(per_step):
            state = states[j] * keep_of(block)
            state_low = low(state)
            starts[j, block] = state_low
            states[j] = (
                last_of(j, block) * state
                - mm(turn_ref[j, block], state_low)
                + high(gain_ref[j, block])
            )
            d_state = d_states[j]
            d_low = low(d_state)
            ends[j, back] = d_low
            d_out = d_mixed_ref[at, j * DV : (j + 1) * DV]
            d_states[j] = keep_of(back) * (
                last_of(j, back) * d_state
                - mm_tn(turn_ref[j, back], d_low)
                + mm_tn(pass_ref[at, j * DK : (j + 1) * DK], d_out)
            )
        return carry

    lax.fori_loop(0, blocks, chain, 0, unroll=2)

    lane = lax.broadcasted_iota(jnp.int32, (PAIR, d_cum.shape[1]), 1)
    tall = lax.broadcasted_iota(jnp.int32, (PAIR, 1), 0)

    def assemble(pair, carry):
        at = pl.ds(pl.multiple_of(pair * PAIR, PAIR), PAIR)
        halves = [slice(half * GROUP, (half + 1) * GROUP) for half in range(2)]
        for j in range(per_step):
            g = cum[j, at, :]
            b = rate[j, at, :]
            k = key[j, at, :]
            q = query[j, at, :]
            v = []
            for half in range(DV // DK):
                u = total[j, 2 + half, at, :]
                v.append(u * sigmoid(u))
            v = jnp.concatenate(v, axis=1)
            bb = jnp.concatenate([b, b], axis=1)
            k_low, q_low = low(k), low(q)
            inverse = inverse_ref[j, at, :]
            spread = jnp.where(within, jnp.exp(jnp.where(within, g - g.T, 0.0)), 0.0)
            grown = jnp.exp(g)
            fall = jnp.exp(block_ends(g) - g)
            scores = mm_nt(q_low, k_low)
            d_out = d_mixed_ref[at, j * DV : (j + 1) * DV]
            grown_k = low(b * grown * k)
            falls = low(fall * k)
            begin = [starts[j, 2 * pair + half] for half in range(2)]
            end = [ends[j, 2 * pair + half] for half in range(2)]
            known = jnp.concatenate(
                [mm(grown_k[part], begin[half]) for half, part in enumerate(halves)], axis=0
            )
            change = low(mm(inverse, low(bb * v - known)))
            pulled = jnp.concatenate(
                [mm(falls[part], end[half]) for half, part in enumerate(halves)], axis=0
            )
            rhs = mm_tn(inverse, low(mm_tn(low(scores * spread), d_out) + pulled))
            rhs_low = low(rhs)
            d_lower = jnp.where(below, -mm_nt(rhs_low, change), 0.0)
            d_score = mm_nt(d_out, change) * spread
            d_gk = jnp.concatenate(
                [-mm_nt(rhs_low[part], begin[half]) for half, part in enumerate(halves)], axis=0
            )
            d_gq = jnp.concatenate(
                [mm_nt(d_out[part], begin[half]) for half, part in enumerate(halves)], axis=0
            )
            d_tail = jnp.concatenate(
                [mm_nt(change[part], end[half]) for half, part in enumerate(halves)], axis=0
            )
            bonus = [jnp.sum(high(begin[half]) * high(end[half])) for half in range(2)]
            d_a = d_lower * mm_nt(k_low, k_low) * spread
            cross = d_a * b + d_score * scores
            gk_k = d_gk * k
            rate_col = jnp.sum(d_a + grown * gk_k, axis=-1, keepdims=True) + jnp.sum(
                rhs * v, axis=-1, keepdims=True
            )
            tail_sum = jnp.sum(d_tail * (fall * k), axis=-1, keepdims=True)
            cum_col = (
                jnp.sum(
                    cross - cross.T + b * grown * gk_k + d_gq * (grown * q), axis=-1, keepdims=True
                )
                - tail_sum
            )
            for half, part in enumerate(halves):
                at_end = half * GROUP + GROUP - 1
                more = jnp.sum(tail_sum[part], axis=0, keepdims=True) + bonus[half] * grown[
                    at_end : at_end + 1, :1
                ]
                cum_col = cum_col + jnp.where(tall == at_end, more, 0.0)
            head = offset + step * per_step + j
            d_cum[at, :] = d_cum[at, :] + jnp.where(lane == head, cum_col, 0.0)
            d_rate[at, :] = d_rate[at, :] + jnp.where(lane == head, rate_col, 0.0)
            d_keys = d_lower * spread * b
            d_keys = low(d_keys + d_keys.T)
            d_score_low = low(d_score)
            d_query = grown * d_gq + mm(d_score_low, k_low)
            d_key = b * grown * d_gk + fall * d_tail + mm(d_keys, k_low) + mm_tn(d_score_low, q_low)
            query[j, at, :] = d_query
            key[j, at, :] = d_key
            d_value[j, at, :] = bb * rhs
        return carry

    lax.fori_loop(0, pairs, assemble, 0, unroll=2)

    d_total[0:RIM, :] = jnp.zeros((RIM, DK), jnp.float32)
    d_total[RIM + count : 2 * RIM + count, :] = jnp.zeros((RIM, DK), jnp.float32)

    def conv_back(rows, weight, out_ref, rim_ref, end_ref, d_weight_ref, cols):
        size = count + RIM
        spread_rows = None
        grads = []
        for tap in range(taps):
            moved = d_total[taps - 1 - tap : taps - 1 - tap + size, :]
            term = moved * weight[tap : tap + 1, :]
            spread_rows = term if spread_rows is None else spread_rows + term
            grads.append(jnp.sum(moved * rows[...], axis=0, keepdims=True))
        d_ext[...] = spread_rows
        near = d_total[pl.ds(reset + RIM, RIM), :]
        around = rows[pl.ds(reset, 2 * RIM), :]
        wrong_rows = jnp.zeros((2 * RIM, DK), jnp.float32)
        for tap in range(taps - 1):
            lead = RIM - taps + 1 + tap
            wrong = jnp.where(places >= taps - 1 - tap, 0.0, near)
            grads[tap] = grads[tap] - jnp.sum(
                wrong * around[lead : lead + RIM], axis=0, keepdims=True
            )
            wrong_rows = wrong_rows + jnp.concatenate(
                [
                    jnp.zeros((lead, DK), jnp.float32),
                    wrong * weight[tap : tap + 1, :],
                    jnp.zeros((RIM - lead, DK), jnp.float32),
                ],
                axis=0,
            )
        d_ext[pl.ds(reset, 2 * RIM), :] = d_ext[pl.ds(reset, 2 * RIM), :] - wrong_rows
        d_weight_ref[:, cols] = jnp.concatenate(grads, axis=0)
        rim_ref[:, cols] = d_ext[0:RIM, :]
        out_ref[:, cols] = low(d_ext[RIM : RIM + count, :])
        end_ref[:, cols] = d_ext[count : count + RIM, :]

    for j in range(per_step):
        cols = slice(j * DK, (j + 1) * DK)

        def unit_back(piece, d_unit, factor):
            u = total[j, piece]
            sig = sigmoid(u)
            c = u * sig
            scale = unit_scale(c)
            unit = c * scale
            d_unit = d_unit * factor
            d_c = scale * (d_unit - unit * jnp.sum(d_unit * unit, axis=-1, keepdims=True))
            d_total[RIM : RIM + count, :] = d_c * (sig * (1.0 + u * (1.0 - sig)))

        unit_back(0, query[j], DK**-0.5)
        conv_back(ext.at[j, 0], conv_q[:, cols], dq_ref, dq_rim, dq_end, d_conv_q, cols)
        unit_back(1, key[j], 1.0)
        conv_back(ext.at[j, 1], conv_k[:, cols], dk_ref, dk_rim, dk_end, d_conv_k, cols)
        for half in range(DV // DK):
            begin = j * DV + half * DK
            cut = slice(begin, begin + DK)
            u = total[j, 2 + half]
            sig = sigmoid(u)
            d_total[RIM : RIM + count, :] = d_value[j, :, half * DK : (half + 1) * DK] * (
                sig * (1.0 + u * (1.0 - sig))
            )
            conv_back(ext.at[j, 2 + half], conv_v[:, cut], dv_ref, dv_rim, dv_end, d_conv_v, cut)

    @pl.when(step == pl.num_programs(0) - 1)
    def _():
        shifted_in = decay_ref[...] + bias_ref[...]
        soft = jnp.maximum(shifted_in, 0.0) + jnp.log1p(jnp.exp(-jnp.abs(shifted_in)))
        speed = -jnp.exp(log_ref[...])
        after = jnp.where(within, 1.0, 0.0)
        d_log = jnp.zeros_like(d_log_ref)
        d_bias = jnp.zeros_like(d_bias_ref)
        for pair in range(pairs):
            rows = slice(pair * PAIR, (pair + 1) * PAIR)
            d_decay = lax.dot_general(
                after,
                d_cum[rows, :],
                (((0,), (0,)), ((), ())),
                precision=lax.Precision.HIGHEST,
                preferred_element_type=jnp.float32,
            )
            d_log = d_log + jnp.sum(d_decay * (speed * soft[rows]), axis=0, keepdims=True)
            d_in = d_decay * speed * jax.nn.sigmoid(shifted_in[rows])
            d_bias = d_bias + jnp.sum(d_in, axis=0, keepdims=True)
            d_decay_ref[rows, :] = d_in
        d_log_ref[...] = d_log
        d_bias_ref[...] = d_bias
        rates = rate_ref[...]
        d_beta_ref[...] = d_rate[...] * rates * (1.0 - rates)


def state_backward(
    q, k, v, rims, convs, decay, decay_log, decay_bias, cum, rate, saved, start, d_mixed, near, near_map, far, spot, per_step, offset, held, after
):
    count = q.shape[0]
    heads = decay.shape[1]
    taps = convs[0].shape[0]
    n = per_step
    blocks = count // GROUP
    skip = offset // n
    along = lambda i: (0, i + skip)
    fixed = lambda i: (0, 0)
    lead = lambda i: (i + skip, 0, 0)
    lead4 = lambda i: (i + skip, 0, 0, 0)
    out_along = lambda i: (0, i)
    f32, bf16 = jnp.float32, jnp.bfloat16
    shape = jax.ShapeDtypeStruct
    vm = pltpu.VMEM
    thin = [(RIM, DK), (RIM, DK), (RIM, DV)]
    out_blocks = [(count, DK), (count, DK), (count, DV)] + thin + thin
    out_blocks += [(taps, DK), (taps, DK), (taps, DV)]
    tables = [(count, heads), (count, heads), (1, heads), (1, heads)]
    return pl.pallas_call(
        functools.partial(state_back_kernel, taps, n, offset, len(after)),
        grid=(held // n,),
        in_specs=[
            pl.BlockSpec(memory_space=pltpu.SMEM),
            spec((count, n * DK), along),
            spec((count, n * DK), along),
            spec((count, n * DV), along),
            spec((RIM, n * DK), along),
            spec((RIM, n * DK), along),
            spec((RIM, n * DV), along),
            spec((taps, n * DK), along),
            spec((taps, n * DK), along),
            spec((taps, n * DV), along),
            spec((count, heads), fixed),
            spec((1, heads), fixed),
            spec((1, heads), fixed),
            spec((count, heads), fixed),
            spec((count, heads), fixed),
            spec((n, count, PAIR), lead),
            spec((count, n * DK), along),
            spec((n, blocks, DK, DK), lead4),
            spec((n, blocks, DK, DV), lead4),
            spec((n, DK, DV), lead),
            spec((count, n * DV), along),
            spec((n, DK, DV), lead),
            spec((n, DK, DK), lead),
            spec((n, DK, DV), lead),
        ]
        + [pl.BlockSpec(memory_space=pl.ANY) for _ in after],
        out_specs=[spec((rows, n * width), out_along) for rows, width in out_blocks]
        + [spec(block, fixed) for block in tables],
        out_shape=[
            shape((rows, held * width), bf16 if i < 3 else f32)
            for i, (rows, width) in enumerate(out_blocks)
        ]
        + [shape(block, f32) for block in tables],
        scratch_shapes=[
            vm((n, 4, count + RIM, DK), f32),
            vm((n, 4, count, DK), f32),
            vm((n, count, DK), f32),
            vm((n, count, DK), f32),
            vm((n, count, DV), f32),
            vm((n, count, DK), f32),
            vm((n, count, DK), f32),
            vm((n, blocks, DK, DV), bf16),
            vm((n, blocks, DK, DV), bf16),
            vm((n, DK, DV), f32),
            vm((n, DK, DV), f32),
            vm((count + 2 * RIM, DK), f32),
            vm((count + RIM, DK), f32),
            vm((count, heads), f32),
            vm((count, heads), f32),
        ],
        compiler_params=pltpu.CompilerParams(
            dimension_semantics=("arbitrary",), vmem_limit_bytes=VMEM_BYTES
        ),
        cost_estimate=pl.CostEstimate(
            flops=held * count * 14_000_000, bytes_accessed=count * held * 6000, transcendentals=0
        ),
    )(
        spot,
        q,
        k,
        v,
        *rims,
        *convs,
        decay,
        decay_log,
        decay_bias,
        cum,
        rate,
        *saved,
        start,
        d_mixed,
        near,
        near_map,
        far,
        *after,
    )


def shifted(value, axis, steps):
    count = lax.axis_size(axis)
    leading, last = (max(0, -steps), min(count, count - steps))
    return lax.ppermute(value, axis, [(source, source + steps) for source in range(leading, last)])


def rms_scale(values, gain):
    return values * lax.rsqrt(jnp.mean(values * values, axis=-1, keepdims=True) + EPS) * gain


def swish_product(gate_ffn, up_ffn):
    return jax.nn.silu(gate_ffn) * up_ffn


def project(rows, weight):
    return jnp.dot(rows, weight, preferred_element_type=jnp.float32)


def rows_product(left, right):
    return jnp.dot(left, right, preferred_element_type=jnp.float32)


def rows_back(left, weight):
    return jnp.einsum("tc,dc->td", left, weight, preferred_element_type=jnp.float32)


def weight_grad(rows, grads):
    return jnp.einsum("td,tc->dc", rows, grads, preferred_element_type=jnp.float32)


STAGES = {"x": ("seq", 0, 1), "y": ("seq", 1, 2), "l": ("dp", 0, 4), "h": ("dp", 1, 8)}


def trade(value, stage):
    axis, bit, _ = STAGES[stage]
    count = lax.axis_size(axis)
    return lax.ppermute(value, axis, [(place, place ^ (1 << bit)) for place in range(count)])


def arrange_kernel(picks, left_ref, right_ref, *rest):
    left_out, right_out = rest[-2:]
    width = left_ref.shape[1] // 16
    for place in range(16):
        source = pl.ds(pl.multiple_of(picks[place] * width, width), width)
        target = slice(place * width, (place + 1) * width)
        left_out[:, target] = left_ref[:, source]
        right_out[:, target] = right_ref[:, source]


def relative_order(rows, more, order, after):
    own = lax.axis_index("dp") * lax.axis_size("seq") + lax.axis_index("seq")
    masks = [
        sum(STAGES[stage][2] for k, stage in enumerate(order) if place >> (3 - k) & 1)
        for place in range(16)
    ]
    picks = own ^ jnp.array(masks, jnp.int32)
    count, width = rows.shape
    size = 96
    piece = pl.BlockSpec((size, width), lambda i: (i, 0))
    return pl.pallas_call(
        arrange_kernel,
        grid=(count // size,),
        in_specs=[pl.BlockSpec(memory_space=pltpu.SMEM), piece, piece]
        + [pl.BlockSpec(memory_space=pl.ANY) for _ in after],
        out_specs=[piece, piece],
        out_shape=[jax.ShapeDtypeStruct((count, width), rows.dtype)] * 2,
        compiler_params=pltpu.CompilerParams(
            dimension_semantics=("arbitrary",), vmem_limit_bytes=VMEM_BYTES
        ),
        cost_estimate=pl.CostEstimate(
            flops=0, bytes_accessed=12 * count * width, transcendentals=0
        ),
    )(picks, rows, more, *after)


def own_side(stage):
    axis, bit, _ = STAGES[stage]
    return lax.rem(lax.axis_index(axis) // (1 << bit), 2)


def paired_rows(own_rows, got_rows, order, *after):
    both = relative_order(own_rows, got_rows, order[1:] + order[:1], after)
    return tuple(heads_gather(rows) for rows in both)


def trade_halves(grads, order):
    half = grads.shape[1] // 2
    side = own_side(order[0])
    mine = lax.dynamic_slice_in_dim(grads, side * half, half, 1)
    theirs = lax.dynamic_slice_in_dim(grads, (1 - side) * half, half, 1)
    return mine, trade(theirs, order[0])


def pair_grad(rows, halves, begin, end):
    width = rows[0].shape[1] // 16
    cut = slice(begin * width, end * width)
    return sum(weight_grad(part[:, cut], grads) for part, grads in zip(rows, halves))


def grad_open(rows, halves, order):
    sent = low(pair_grad(rows, halves, 8, 16))
    return rows, halves, sent, trade(sent, order[1])


def grad_next(opened, order):
    rows, halves, _, first = opened
    width = rows[0].shape[1] // 16
    sent = low(pair_grad(rows, halves, 4, 8) + high(first[4 * width :]))
    rest = pair_grad(rows, halves, 0, 4) + high(first[: 4 * width])
    return rest, sent, trade(sent, order[2])


def grad_close(moved, order):
    rest, _, second = moved
    width = rest.shape[0] // 4
    half = rest.shape[1]
    side = own_side(order[0])
    third = trade(low(rest[2 * width :] + high(second[2 * width :])), order[3])
    final = rest[: 2 * width] + high(second[: 2 * width]) + high(third)
    other = high(trade(low(final[width:]), order[0]))
    left = jnp.where(side == 0, final[:width], other)
    right = jnp.where(side == 0, other, final[:width])
    return jnp.concatenate([left, right], axis=1)


def finish_kernel(plan, head_steps, *refs):
    groups = len(plan)
    grads, small_ref = refs[:groups], refs[groups]
    outs, small_out = refs[groups + 1 : 2 * groups + 1], refs[2 * groups + 1]
    scratch = refs[2 * groups + 2 :]
    buffers = [scratch[7 * g : 7 * g + 7] for g in range(groups)]
    small_sum, small_got, send_sem, recv_sem, small_send, small_recv = scratch[7 * groups :]
    width = grads[0].shape[0] // 16

    def side(stage):
        axis, bit, _ = STAGES[stage]
        return lax.rem(lax.axis_index(axis) // (1 << bit), 2)

    def partner(stage):
        axis, bit, _ = STAGES[stage]
        return {axis: lax.axis_index(axis) + (1 - 2 * side(stage)) * (1 << bit)}

    def head_partner(step):
        me = lax.axis_index("heads")
        return {"heads": me + (1 - 2 * lax.rem(me // step, 2)) * step}

    barrier = pltpu.get_barrier_semaphore()
    targets = [partner(stage) for stage in "xylh"] + [head_partner(step) for step in head_steps]
    for target in targets:
        pl.semaphore_signal(
            barrier, inc=1, device_id=target, device_id_type=pl.DeviceIdType.MESH
        )
    pl.semaphore_wait(barrier, len(targets))

    started = []

    def send(source, target, sems, device):
        copy = pltpu.make_async_remote_copy(
            src_ref=source,
            dst_ref=target,
            send_sem=sems[0],
            recv_sem=sems[1],
            device_id=device,
            device_id_type=pl.DeviceIdType.MESH,
        )
        copy.start()
        started.append(copy)
        return copy

    most = max(len(cuts) for _, cuts in plan)
    chunks, number = [], 0
    rounds = [[] for _ in range(most)]
    for g, (order, cuts) in enumerate(plan):
        for k, cut in enumerate(cuts):
            chunks.append((g, order, slice(*cut)))
            rounds[k].append(number)
            number += 1
    copies = {}

    def launch(stage, index, source, target, name):
        sems = (send_sem.at[4 * index + stage], recv_sem.at[4 * index + stage])
        copies[stage, index] = send(source, target, sems, partner(name))

    def open_chunk(index):
        g, order, cut = chunks[index]
        launch(0, index, grads[g].at[8 * width :, cut], buffers[g][0].at[:, cut], order[1])

    def second_chunk(index):
        g, order, cut = chunks[index]
        copies[0, index].wait_recv()
        got, sent, got_next = buffers[g][0], buffers[g][4], buffers[g][1]
        rows = slice(4 * width, 8 * width)
        sent[:, cut] = low(high(grads[g][rows, cut]) + high(got[rows, cut]))
        launch(1, index, sent.at[:, cut], got_next.at[:, cut], order[2])

    def third_chunk(index):
        g, order, cut = chunks[index]
        copies[1, index].wait_recv()
        rows = slice(2 * width, 4 * width)
        first, second, sent = buffers[g][0], buffers[g][1], buffers[g][5]
        sent[:, cut] = low(
            high(grads[g][rows, cut]) + high(first[rows, cut]) + high(second[rows, cut])
        )
        launch(2, index, sent.at[:, cut], buffers[g][2].at[:, cut], order[3])

    def fourth_chunk(index):
        g, order, cut = chunks[index]
        copies[2, index].wait_recv()
        first, second, third, sent = (buffers[g][k] for k in (0, 1, 2, 6))
        half = grads[g].shape[1]
        rows = slice(0, 2 * width)
        final = high(grads[g][rows, cut]) + high(first[rows, cut])
        final = final + high(second[rows, cut]) + high(third[:, cut])
        sent[:, cut] = low(final[width:])
        launch(3, index, sent.at[:, cut], buffers[g][3].at[:, cut], order[0])
        place = pl.multiple_of(side(order[0]) * half + cut.start, 128)
        outs[g][:, pl.ds(place, cut.stop - cut.start)] = final[:width]

    def last_chunk(index):
        g, order, cut = chunks[index]
        copies[3, index].wait_recv()
        half = grads[g].shape[1]
        place = pl.multiple_of((1 - side(order[0])) * half + cut.start, 128)
        outs[g][:, pl.ds(place, cut.stop - cut.start)] = high(buffers[g][3][:, cut])

    small_copies = []
    names = "xylh"

    def small_step(step):
        if step >= 1 and step <= 4:
            small_copies[step - 1].wait_recv()
            small_sum[step] = small_sum[step - 1] + small_got[step - 1]
        if step == 4:
            small_out[pl.ds(lax.axis_index("heads"), 1)] = small_sum[4:5]
        if step < 4:
            if step == 0:
                small_sum[0] = small_ref[...]
            sems = (small_send.at[step], small_recv.at[step])
            small_copies.append(
                send(small_sum.at[step], small_got.at[step], sems, partner(names[step]))
            )
        elif step - 4 <= len(head_steps):
            k = step - 4
            if k >= 1:
                small_copies[step - 1].wait_recv()
            if k < len(head_steps):
                size = head_steps[k]
                begin = lax.axis_index("heads") // size * size
                block = small_out.at[pl.ds(begin, size)]
                sems = (small_send.at[step], small_recv.at[step])
                small_copies.append(send(block, block, sems, head_partner(size)))

    total_small = 5 + len(head_steps)
    for index in rounds[0]:
        open_chunk(index)
    small_step(0)
    if most > 1:
        for index in rounds[1]:
            open_chunk(index)
    for t in range(max(most + 3, total_small - 1)):
        if t < most:
            for index in rounds[t]:
                second_chunk(index)
        if t + 2 < most:
            for index in rounds[t + 2]:
                open_chunk(index)
        for lag, work in ((1, third_chunk), (2, fourth_chunk), (3, last_chunk)):
            if 0 <= t - lag < most:
                for index in rounds[t - lag]:
                    work(index)
        if t + 1 < total_small:
            small_step(t + 1)
    for copy in started:
        copy.wait_send()


def finish(grads, orders, small):
    count = lax.axis_size("heads")
    head_steps = []
    while 1 << len(head_steps) < count:
        head_steps.append(1 << len(head_steps))
    plan, scratch = [], []
    for array, order in zip(grads, orders):
        full, half = array.shape
        step = min(256, half)
        plan.append((order, [(at, at + step) for at in range(0, half, step)]))
        for rows in (8, 4, 2, 1, 4, 2, 1):
            scratch.append(pltpu.VMEM((full // 16 * rows, half), jnp.bfloat16))
    pieces = sum(len(cuts) for _, cuts in plan)
    inside = pl.BlockSpec(memory_space=pltpu.VMEM)
    rows = small.shape[0]
    f32 = jnp.float32
    return pl.pallas_call(
        functools.partial(finish_kernel, tuple(plan), tuple(head_steps)),
        in_specs=[inside] * (len(grads) + 1),
        out_specs=[inside] * (len(grads) + 1),
        out_shape=[
            jax.ShapeDtypeStruct((array.shape[0] // 16, 2 * array.shape[1]), f32)
            for array in grads
        ]
        + [jax.ShapeDtypeStruct((count, rows, 128), f32)],
        scratch_shapes=scratch
        + [
            pltpu.VMEM((5, rows, 128), f32),
            pltpu.VMEM((4, rows, 128), f32),
            pltpu.SemaphoreType.DMA((4 * pieces,)),
            pltpu.SemaphoreType.DMA((4 * pieces,)),
            pltpu.SemaphoreType.DMA((8,)),
            pltpu.SemaphoreType.DMA((8,)),
        ],
        compiler_params=pltpu.CompilerParams(
            collective_id=0, has_side_effects=True, vmem_limit_bytes=VMEM_BYTES
        ),
        cost_estimate=pl.CostEstimate(
            flops=100_000_000_000, bytes_accessed=20_000_000, transcendentals=0
        ),
    )(*grads, small)


def heads_gather(rows):
    count = lax.axis_size("heads")
    own = lax.axis_index("heads")
    step = 1
    while step < count:
        other = lax.ppermute(rows, "heads", [(place, place ^ step) for place in range(count)])
        upper = lax.rem(own // step, 2) == 1
        rows = jnp.concatenate(
            [jnp.where(upper, other, rows), jnp.where(upper, rows, other)], axis=0
        )
        step *= 2
    return rows


def heads_sum(compute, count, kind):
    if lax.axis_size("heads") != 2:
        whole = compute(lambda rows: rows).astype(kind)
        return high(lax.psum_scatter(whole, "heads", scatter_dimension=0, tiled=True))
    own = lax.axis_index("heads")
    half = count // 2

    def part(which):
        return compute(lambda rows: lax.dynamic_slice_in_dim(rows, which * half, half, 0))

    got = lax.ppermute(part(1 - own).astype(kind), "heads", [(0, 1), (1, 0)])
    return part(own) + high(got)


ORDERS = ("xylh", "ylxh", "lxyh")


def body(
    hidden_in,
    out_cotangent,
    lengths,
    norm_gain,
    q_weight,
    k_weight,
    v_weight,
    gate_weight,
    decay_weight,
    beta_weight,
    conv_q,
    conv_k,
    conv_v,
    decay_log,
    decay_bias,
    out_gain,
    out_weight,
    ffn_gain,
    ffn_gate,
    ffn_up,
    ffn_down,
):
    resid = hidden_in[0].astype(jnp.float32)
    normed_own = rms_scale(resid, norm_gain).astype(jnp.bfloat16)
    normed, cotangent = (
        heads_gather(normed_own),
        heads_gather(out_cotangent[0]),
    )
    span = normed.shape[0]
    normed_got = {order: trade(normed_own, order[0]) for order in ORDERS}
    cotangent_got = trade(out_cotangent[0], ORDERS[2][0])
    taps = conv_q.shape[0]
    q_proj = project(normed, q_weight)
    k_proj = project(normed, k_weight)
    v_proj = project(normed, v_weight)
    gate_proj = project(normed, gate_weight)
    heads = decay_weight.shape[1]
    per_step = min(2, heads)
    narrow = project(normed, jnp.concatenate([decay_weight, beta_weight], axis=1))
    decay_proj, beta_proj = narrow[:, :heads], narrow[:, heads:]
    seq_index = lax.axis_index("seq")
    spot = jnp.stack([lengths[0, 0], seq_index * span]).astype(jnp.int32)
    rims = shifted((q_proj[span - RIM :], k_proj[span - RIM :], v_proj[span - RIM :]), "seq", 1)
    convs = (conv_q, conv_k, conv_v)
    log_row, bias_row, gain_row = decay_log[None], decay_bias[None], out_gain[None]
    mixed_local, reach, span_map, span_add, *saved, cum, rate = state_forward(
        q_proj, k_proj, v_proj, rims, convs, decay_proj, beta_proj, log_row, bias_row, spot, per_step
    )
    near_map, near_add = shifted((span_map, span_add), "seq", 1)
    far_add = shifted(span_add, "seq", 2)
    next_map = shifted(span_map, "seq", -1)
    gated_low, mixed_low, start_state = gate_forward(
        mixed_local, reach, near_map, near_add, far_add, gate_proj, gain_row, per_step
    )
    mixer = heads_sum(
        lambda pick: rows_product(pick(gated_low), out_weight), span, jnp.float32
    )
    resid_mid = resid + mixer
    ffn_own = rms_scale(resid_mid, ffn_gain).astype(jnp.bfloat16)
    ffn_in = heads_gather(ffn_own)
    ffn_got = {order: trade(ffn_own, order[0]) for order in ORDERS[:2]}
    out_halves = trade_halves(gated_low, ORDERS[0])
    gate_ffn = project(ffn_in, ffn_gate)
    up_ffn = project(ffn_in, ffn_up)
    act, act_pull = jax.vjp(swish_product, gate_ffn, up_ffn)
    act_low = act.astype(jnp.bfloat16)
    down_halves = trade_halves(act_low, ORDERS[2])
    ffn_out = heads_sum(lambda pick: rows_product(pick(act_low), ffn_down), span, jnp.bfloat16)
    output = (resid_mid + ffn_out).astype(jnp.bfloat16)
    d_act = jnp.einsum("td,fd->tf", cotangent, ffn_down, preferred_element_type=jnp.float32)
    d_gate_ffn, d_up_ffn = act_pull(d_act)
    d_gate_low = d_gate_ffn.astype(jnp.bfloat16)
    d_up_low = d_up_ffn.astype(jnp.bfloat16)
    cotangent_rel = paired_rows(out_cotangent[0], cotangent_got, ORDERS[2], act_low)
    gate_halves = trade_halves(d_gate_low, ORDERS[0])
    up_halves = trade_halves(d_up_low, ORDERS[1])
    ffn_rel = {
        order: paired_rows(ffn_own, ffn_got[order], order, d_gate_low) for order in ORDERS[:2]
    }
    down_open = grad_open(cotangent_rel, down_halves, ORDERS[2])
    gate_open = grad_open(ffn_rel[ORDERS[0]], gate_halves, ORDERS[0])
    up_open = grad_open(ffn_rel[ORDERS[1]], up_halves, ORDERS[1])
    d_ffn = heads_sum(
        lambda pick: rows_back(pick(d_gate_low), ffn_gate) + rows_back(pick(d_up_low), ffn_up),
        span,
        jnp.float32,
    )
    _, ffn_norm_pull = jax.vjp(rms_scale, resid_mid, ffn_gain)
    d_mid_norm, d_ffn_gain = ffn_norm_pull(d_ffn)
    d_mid = out_cotangent[0].astype(jnp.float32) + d_mid_norm
    d_mid_low = low(d_mid)
    d_mid_all = heads_gather(d_mid_low)
    d_mid_got = trade(d_mid_low, ORDERS[0][0])
    d_gated = jnp.einsum("td,cd->tc", d_mid_all, out_weight, preferred_element_type=jnp.float32)
    d_mixed, d_gate_low_mix, d_start, d_out_gain = gate_backward(
        d_gated, mixed_low, reach, gate_proj, gain_row, per_step
    )
    next_start = shifted(d_start, "seq", -1)
    beyond_start = shifted(d_start, "seq", -2)
    mix_halves = trade_halves(d_gate_low_mix, ORDERS[2])
    parts = 2 if heads > 1 else 1
    held = heads // parts
    per_step = min(per_step, held)
    backs, grads_low, mix_halves_part = [], [], []
    for part in range(parts):
        if part == 0:
            after = (down_open[2], gate_open[2], up_open[2])
        else:
            down_next = grad_next(down_open, ORDERS[2])
            gate_next = grad_next(gate_open, ORDERS[0])
            up_next = grad_next(up_open, ORDERS[1])
            gate_mix_rel = paired_rows(normed_own, normed_got[ORDERS[2]], ORDERS[2], up_next[1])
            gate_mix_grad = low(pair_grad(gate_mix_rel, mix_halves, 0, 16))
            d_mid_rel = paired_rows(d_mid_low, d_mid_got, ORDERS[0], up_next[1])
            out_grad = low(pair_grad(d_mid_rel, out_halves, 0, 16))
            after = (down_next[1], gate_next[1], up_next[1], gate_mix_grad, out_grad)
        back = state_backward(
            q_proj,
            k_proj,
            v_proj,
            rims,
            convs,
            decay_proj,
            log_row,
            bias_row,
            cum,
            rate,
            saved,
            start_state,
            d_mixed,
            next_start,
            next_map,
            beyond_start,
            spot,
            per_step,
            part * held,
            held,
            after,
        )
        rim = shifted(jnp.concatenate(back[3:6], axis=1), "seq", -1)
        passed = jnp.split(rim, (held * DK, 2 * held * DK), axis=1)
        lows = [
            lax.dynamic_update_slice_in_dim(whole, low(end + more), span - RIM, 0)
            for whole, end, more in zip(back[0:3], back[6:9], passed)
        ]
        backs.append(back)
        grads_low.append(lows)
    d_q_low, d_k_low, d_v_low = (jnp.concatenate(part, axis=1) for part in zip(*grads_low))
    conv_grads = [jnp.concatenate(part, axis=1) for part in zip(*(back[9:12] for back in backs))]
    d_decay_low, d_beta_low, d_log, d_bias = (
        sum(part) for part in zip(*(back[12:16] for back in backs))
    )
    d_decay_low, d_beta_low = low(d_decay_low), low(d_beta_low)
    d_log, d_bias = d_log[0], d_bias[0]
    grad_down = grad_close(down_next, ORDERS[2]).T
    grad_gate = grad_close(gate_next, ORDERS[0])
    grad_up = grad_close(up_next, ORDERS[1])
    tails, tail_orders = [gate_mix_grad, out_grad], [ORDERS[2], ORDERS[0]]
    for part, lows in enumerate(grads_low):
        flat_low = jnp.concatenate(lows, axis=1)
        pieces = 2 if part == parts - 1 and parts > 1 else 1
        size = flat_low.shape[1] // pieces
        for piece in range(pieces):
            order = ORDERS[(1, 0, 2)[part + piece]]
            if order == ORDERS[2]:
                rows = gate_mix_rel
            else:
                rows = paired_rows(normed_own, normed_got[order], order, backs[0][0])
            halves = trade_halves(flat_low[:, piece * size : (piece + 1) * size], order)
            tails.append(low(pair_grad(rows, halves, 0, 16)))
            tail_orders.append(order)
    narrow_grad = weight_grad(jnp.concatenate([d_decay_low, d_beta_low], axis=1), normed)
    pairs = (
        (d_q_low, q_weight),
        (d_k_low, k_weight),
        (d_v_low, v_weight),
        (d_gate_low_mix, gate_weight),
        (d_decay_low, decay_weight),
        (d_beta_low, beta_weight),
    )
    d_normed = heads_sum(
        lambda pick: sum(rows_back(pick(rows), weight) for rows, weight in pairs),
        span,
        jnp.bfloat16,
    )
    _, in_norm_pull = jax.vjp(rms_scale, resid, norm_gain)
    d_in_norm, d_norm_gain = in_norm_pull(d_normed)
    input_grad = d_mid + d_in_norm
    owned = (d_log, d_bias) + tuple(part.reshape(-1) for part in conv_grads)
    shared = (d_norm_gain, d_ffn_gain, d_out_gain[0], narrow_grad.reshape(-1))
    marks = [int(mark) for mark in np.cumsum([part.size for part in shared + owned])]
    rows = -(-marks[-1] // 1024) * 8
    blank = jnp.zeros((rows * 128 - marks[-1],), jnp.float32)
    flat = jnp.concatenate(shared + owned + (blank,)).reshape(rows, 128)
    grad_gate_mix, grad_out, *mixes, everyone = finish(tails, tail_orders, flat)
    grad_out = grad_out.T
    everyone = everyone.reshape(everyone.shape[0], -1)
    own_head = lax.axis_index("heads")
    narrow_own = lax.dynamic_slice(
        everyone, (own_head, marks[2]), (1, narrow_grad.size)
    ).reshape(narrow_grad.shape)
    shard = lax.axis_index("dp") * lax.axis_size("seq") + lax.axis_index("seq")
    size = narrow_grad.shape[1] // 16
    narrow_sum = lax.dynamic_slice_in_dim(narrow_own, shard * size, size, 1).T
    grad_decay, grad_beta = narrow_sum[:, :heads], narrow_sum[:, heads:]
    pieces = jnp.split(everyone, marks, axis=1)[:-1]
    small = [piece.sum(0) for piece in pieces[:3]]
    small += [pieces[4].reshape(-1), pieces[5].reshape(-1)]
    for piece in pieces[6:]:
        small.append(
            jnp.swapaxes(piece.reshape(piece.shape[0], taps, -1), 0, 1).reshape(taps, -1)
        )
    wide = held * DK
    by_part = [mixes[0]] if parts == 1 else [mixes[0], jnp.concatenate(mixes[1:], axis=1)]
    grad_q, grad_k, grad_v = (
        jnp.concatenate(part, axis=1)
        for part in zip(*(jnp.split(mix, (wide, 2 * wide), axis=1) for mix in by_part))
    )
    return (
        output[None],
        input_grad[None],
        small[0],
        grad_q,
        grad_k,
        grad_v,
        grad_gate_mix,
        grad_decay,
        grad_beta,
        small[5],
        small[6],
        small[7],
        small[3],
        small[4],
        small[2],
        grad_out,
        small[1],
        grad_gate,
        grad_up,
        grad_down,
    )


def solution(mesh):
    in_specs = (
        P("dp", ("seq", "heads"), None),
        P("dp", ("seq", "heads"), None),
        P("dp", None),
        P(),
        P(None, "heads"),
        P(None, "heads"),
        P(None, "heads"),
        P(None, "heads"),
        P(None, "heads"),
        P(None, "heads"),
        P(None, "heads"),
        P(None, "heads"),
        P(None, "heads"),
        P("heads"),
        P("heads"),
        P(),
        P("heads", None),
        P(),
        P(None, "heads"),
        P(None, "heads"),
        P("heads", None),
    )
    out_specs = (
        P("dp", ("seq", "heads"), None),
        P("dp", ("seq", "heads"), None),
        P(),
        P(("dp", "seq"), "heads"),
        P(("dp", "seq"), "heads"),
        P(("dp", "seq"), "heads"),
        P(("dp", "seq"), "heads"),
        P(("dp", "seq"), "heads"),
        P(("dp", "seq"), "heads"),
        P(),
        P(),
        P(),
        P(),
        P(),
        P(),
        P("heads", ("dp", "seq")),
        P(),
        P(("dp", "seq"), "heads"),
        P(("dp", "seq"), "heads"),
        P("heads", ("dp", "seq")),
    )
    return jax.shard_map(body, mesh=mesh, in_specs=in_specs, out_specs=out_specs, check_vma=False)
```

time: 1380 us -> 1160 us (0.84)
  waiting for transfers between devices: 555 us -> 193 us
  Pallas kernels: 260 us -> 368 us
  other arithmetic: 56.3 us -> 75.8 us
    ppermute x40 -> x27, waiting for transfers between devices: 495 us -> 165 us  [trade(): lax.ppermute(value, axis, [(place, place ^ 1 << bit) for place in range(c...]
    pallas_call x1 -> x10, Pallas kernels: 118 us -> 293 us  [the longest x1 170 us: finish(): pl.pallas_call(functools.partial(finish_kernel, tuple(plan), tuple(head_s...]
    pallas_call x1, Pallas kernels: 120 us -> 53.8 us  [state_forward(): pl.pallas_call(functools.partial(state_kernel, taps, n), grid=(heads // n...]
    ppermute x12 -> x11, waiting for transfers between devices: 56.1 us -> 13.1 us  [shifted(): lax.ppermute(value, axis, [(source, source + steps) for source in range(l...]
    select_n x0 -> x21, other arithmetic: none -> 29.3 us  [the longest x12 17 us: heads_gather(): jnp.where(upper, other, rows)]
    unnamed x437 -> x361, local copies, waits for them, and re-layouts: 33.6 us -> 23 us
    ppermute x40 -> x27, starting transfers between devices: 44.1 us -> 52.6 us  [trade(): lax.ppermute(value, axis, [(place, place ^ 1 << bit) for place in range(c...]
    dot_general x27 -> x29, matrix products: 137 us -> 135 us  [weight_grad(): jnp.einsum('td,tc->dc', rows, grads, preferred_element_type=jnp.float32)]
  transfers between devices with their start and end apart: 61 -> 60, of which waited for: 20 -> 16; matrix products, arithmetic and copies ran while one was open for 33% -> 36% of each run, Pallas kernels for 19% -> 12%
where the time goes in v3:
time: 1160 us; the launch traced here: 1150 us
  Pallas kernels  368 us (32%)
  matrix products  363 us (31%)
  waiting for transfers between devices  193 us (17%)
  starting transfers between devices  85.2 us (7%)
  other arithmetic  75.8 us (7%)
  local copies, waits for them, and re-layouts  65.2 us (6%)
    pallas_call x1, Pallas kernels, finish(): pl.pallas_call(functools.partial(finish_kernel, tuple(plan), tuple(head_s...  170 us
    ppermute x27, waiting for transfers between devices, trade(): lax.ppermute(value, axis, [(place, place ^ 1 << bit) for place in range(c...  165 us
    dot_general x29, matrix products, weight_grad(): jnp.einsum('td,tc->dc', rows, grads, preferred_element_type=jnp.float32)  135 us
    dot_general x16, matrix products, rows_back(): jnp.einsum('tc,dc->td', left, weight, preferred_element_type=jnp.float32)  105 us
    pallas_call x2, Pallas kernels, state_backward(): pl.pallas_call(functools.partial(state_back_kernel, taps, n, offset, len(...  90.2 us
    dot_general x7, matrix products, project(): return jnp.dot(rows, weight, preferred_element_type=jnp.float32)  56.4 us
    pallas_call x1, Pallas kernels, state_forward(): pl.pallas_call(functools.partial(state_kernel, taps, n), grid=(heads // n...  53.8 us
    ppermute x27, starting transfers between devices, trade(): lax.ppermute(value, axis, [(place, place ^ 1 << bit) for place in range(c...  52.6 us
  transfers between devices with their start and end apart: 60, of which 16 were waited for; matrix products, arithmetic and copies ran while one was open for 36% of the time, Pallas kernels for 12%

profile of v3, /device:TPU:0, one launch (start us, length us, event | category | flops | bytes accessed | tf_op | source)
XLA Modules:
  0.0 1153.9 jit_solution(896184993038922659)
XLA Ops:
  11.0 10.2 fusion.258.v_ref
  43.3 53.8 %shard_map.419 = (f32[768,2048]{1,0:T(8,128)}, bf16[768,1024]{1,0:T(8,128)(2,1)}, bf16[8,128,128]{2,1,0:T(8,128)(2,1)}, bf16[8,128,256]{2,1,0:T(8,128)(2,1)}, bf...) custom-call(s32[2]{0:T(128)} %pad_add_fusion.spot, ...), custom_call_target="tpu_custom_call" | custom-call | flops 61440000000 | bytes 24576000 | tf_op jit(solution)/shard_map/pallas_call | solution.py:326
  105.3 10.8 fusion.257.gate_ref
  116.3 11.9 %collective-permute-done.6.far_ref = bf16[8,128,256]{2,1,0:T(8,128)(2,1)S(1)} collective-permute-done((bf16[8,128,256]{2,1,0:T(8,128)(2,1)}, bf16[8,128,256]{2,1,0:T(8,128)(2,1)S(1)}, u32[]{:S(2)}, u32[]{:S(2)}) %collective-permute-start.6) | collective-permute-done | bytes 524320 | tf_op jit(solution)/shard_map/ppermute | solution.py:909
  129.0 9.9 shard_map.420
  153.3 8.8 multiply_reduce_fusion.2
  178.3 15.1 %fusion.70 = f32[768,2816]{1,0:T(8,128)} fusion(bf16[2048,2816]{1,0:T(8,128)(2,1)} %param.47, bf16[384,2048]{1,0:T(8,128)(2,1)S(1)} %get-tuple-element.240, bf16[384,2048]{1,0:T(8,128)(2,1)S(1)} %get-tuple-element.239), kind=kOutput, calls=%fused_computation.136 | convolution fusion | flops 8864661504 | bytes 23330816 | tf_op jit(solution)/shard_map/dot_general | solution.py:921
  193.5 12.4 %fusion.71 = f32[768,2816]{1,0:T(8,128)} fusion(bf16[2048,2816]{1,0:T(8,128)(2,1)S(1)} %bitcast.153, bf16[384,2048]{1,0:T(8,128)(2,1)S(1)} %get-tuple-element.240, bf16[384,2048]{1,0:T(8,128)(2,1)S(1)} %get-tuple-element.239), kind=kOutput, calls=%fused_computation.137 | convolution fusion | flops 8864661504 | bytes 23330816 | tf_op jit(solution)/shard_map/dot_general | solution.py:921
  205.9 22.1 %multiply_convert_fusion = (bf16[768,2816]{1,0:T(8,128)(2,1)}, bf16[768,2816]{1,0:T(8,128)(2,1)}, bf16[768,2816]{1,0:T(8,128)(2,1)}) fusion(f32[768,2816]{1,0:T(8,128)} %fusion.71, f32[768,2816]{1,0:T(8,128)} %fusion.70, bf16[2816,2048]{1,0:T(8,128)(2,1)} %param.48, bf16[384,2048]{1,0:T(8,128)(2,1)S(1)} %copy-done.71, bf16[384,2048]{1,0:T(8,128)(2,1)S(1)} %copy-done.70), kind=kOutput, calls=%fused_computation.4 | convolution fusion | flops 8899264512 | bytes 44957696 | tf_op jit(solution)/shard_map/td,fd->tf/dot_general | solution.py:1326
  228.0 11.4 fusion.55
  239.4 12.2 %convolution_add_fusion.6 = f32[384,2048]{1,0:T(8,128)} fusion(f32[384,2048]{1,0:T(8,128)} %fusion.55, bf16[2048,2816]{1,0:T(8,128)(2,1)} %param.47, bf16[768,2816]{1,0:T(8,128)(2,1)} %get-tuple-element.204, s32[]{:T(128)S(6)} %select_n.295), kind=kOutput, calls=%fused_computation.118 | convolution fusion | flops 4429971456 | bytes 19988484 | tf_op jit(solution)/shard_map/tc,dc->td/dot_general | solution.py:929
  251.6 9.6 fusion.58
  266.4 10.2 convolution_convert_fusion
  307.2 10.6 fusion.65
  323.1 26.5 %collective-permute-done.19 = bf16[768,1408]{1,0:T(8,128)(2,1)S(1)} collective-permute-done((bf16[768,1408]{1,0:T(8,128)(2,1)}, bf16[768,1408]{1,0:T(8,128)(2,1)S(1)}, u32[]{:S(2)}, u32[]{:S(2)}) %collective-permute-start.19) | collective-permute-done | bytes 2162720 | tf_op jit(solution)/shard_map/ppermute | solution.py:942
  393.1 14.7 %multiply_reduce_fusion = (f32[2048]{0:T(1024)}, f32[384]{0:T(512)S(1)}, f32[384,2048]{1,0:T(8,128)}) fusion(f32[384,2048]{1,0:T(8,128)} %copy-done, f32[384]{0:T(512)S(1)} %copy-done.113, f32[2048]{0:T(1024)S(1)} %copy-done.107, f32[384,2048]{1,0:T(8,128)} %collective-permute-done.11, f32[384,2048]{1,0:T(8,128)} %fusion.58, ...), kind=kOutput, calls=%fused_computation.107 | convolution fusion | flops 4435473920 | bytes 26299396 | tf_op jit(solution)/shard_map/tc,dc->td/dot_general | solution.py:929
  431.2 8.9 fusion.23.d_gated_ref
  440.1 11.6 %shard_map.421 = (bf16[768,2048]{1,0:T(8,128)(2,1)}, bf16[768,2048]{1,0:T(8,128)(2,1)}, bf16[8,128,256]{2,1,0:T(8,128)(2,1)}, f32[1,256]{1,0:T(1,128)}) custom-call(f32[768,2048]{1,0:T(8,128)} %fusion.23.d_gated_ref, bf16[768,2048]{1,0:T(8,128)(2,1)} %get-tuple-element.101.kept_ref, bf16[768,1024]{1,0:T(8,128)(2,1)} %get-tuple-element.90.reach_ref, ...), custom_call_target="tpu_custom_call" | custom-call | tf_op jit(solution)/shard_map/pallas_call | solution.py:475
  454.6 8.7 fusion.103
  463.3 8.6 fusion.105
  484.0 11.4 collective-permute-done.30
  509.9 16.9 %collective-permute-start.46 = (bf16[384,2048]{1,0:T(8,128)(2,1)}, bf16[384,2048]{1,0:T(8,128)(2,1)}, u32[]{:S(2)}, u32[]{:S(2)}) collective-permute-start(bf16[384,2048]{1,0:T(8,128)(2,1)} %fusion.12.left_ref), channel_id=1, source_target_pairs={{0,2},{2,0},{4,6},{6,4},{1,3},{3,1},{5,7},{7,5},{8,10},{10,8},{12,... | collective-permute-start | bytes 4718600 | tf_op jit(solution)/shard_map/ppermute | solution.py:942
  530.4 45.1 %shard_map.425 = (bf16[768,512]{1,0:T(8,128)(2,1)}, bf16[768,512]{1,0:T(8,128)(2,1)}, bf16[768,1024]{1,0:T(8,128)(2,1)}, f32[8,512]{1,0:T(8,128)}, f32[8,512]{1,...) custom-call(s32[2]{0:T(128)} %pad_add_fusion.spot, ...), custom_call_target="tpu_custom_call" | custom-call | flops 43008000000 | bytes 18432000 | tf_op jit(solution)/shard_map/pallas_call | solution.py:824
  576.3 18.3 %collective-permute-done.36.right_ref = bf16[384,2048]{1,0:T(8,128)(2,1)} collective-permute-done((bf16[384,2048]{1,0:T(8,128)(2,1)S(1)}, bf16[384,2048]{1,0:T(8,128)(2,1)}, u32[]{:S(2)}, u32[]{:S(2)}) %collective-permute-start.36) | collective-permute-done | bytes 1572896 | tf_op jit(solution)/shard_map/ppermute | solution.py:942
  633.2 39.6 %collective-permute-done.54 = bf16[512,1408]{1,0:T(8,128)(2,1)} collective-permute-done((bf16[512,1408]{1,0:T(8,128)(2,1)S(1)}, bf16[512,1408]{1,0:T(8,128)(2,1)}, u32[]{:S(2)}, u32[]{:S(2)}) %collective-permute-start.54) | collective-permute-done | bytes 1441824 | tf_op jit(solution)/shard_map/ppermute | solution.py:942
  713.1 45.1 %shard_map.428 = (bf16[768,512]{1,0:T(8,128)(2,1)}, bf16[768,512]{1,0:T(8,128)(2,1)}, bf16[768,1024]{1,0:T(8,128)(2,1)}, f32[8,512]{1,0:T(8,128)}, f32[8,512]{1,...) custom-call(s32[2]{0:T(128)} %pad_add_fusion.spot, ...), custom_call_target="tpu_custom_call" | custom-call | flops 43008000000 | bytes 18432000 | tf_op jit(solution)/shard_map/pallas_call | solution.py:824
  775.4 9.1 fusion.85
  835.9 36.0 %collective-permute-done.58 = bf16[256,1408]{1,0:T(8,128)(2,1)} collective-permute-done((bf16[256,1408]{1,0:T(8,128)(2,1)}, bf16[256,1408]{1,0:T(8,128)(2,1)}, u32[]{:S(2)}, u32[]{:S(2)}) %collective-permute-start.58) | collective-permute-done | bytes 720928 | tf_op jit(solution)/shard_map/ppermute | solution.py:942
  875.4 12.1 %collective-permute-done.55 = bf16[256,1408]{1,0:T(8,128)(2,1)} collective-permute-done((bf16[256,1408]{1,0:T(8,128)(2,1)}, bf16[256,1408]{1,0:T(8,128)(2,1)}, u32[]{:S(2)}, u32[]{:S(2)}) %collective-permute-start.55) | collective-permute-done | bytes 720928 | tf_op jit(solution)/shard_map/ppermute | solution.py:942
  890.6 12.3 %collective-permute-done.52 = bf16[256,1408]{1,0:T(8,128)(2,1)} collective-permute-done((bf16[256,1408]{1,0:T(8,128)(2,1)}, bf16[256,1408]{1,0:T(8,128)(2,1)}, u32[]{:S(2)}, u32[]{:S(2)}) %collective-permute-start.52) | collective-permute-done | bytes 720928 | tf_op jit(solution)/shard_map/ppermute | solution.py:942
  937.9 11.8 %concatenate.141 = f32[54272]{0:T(1024)} concatenate(f32[2048]{0:T(1024)S(1)} %get-tuple-element.200, f32[2048]{0:T(1024)} %get-tuple-element.198, f32[256]{0:T(256)} %bitcast.151, f32[32768]{0:T(1024)S(1)} %bitcast.137, f32[8]{0:T(128)} %get-tuple-element.274, f32[8]{0:T(128)} %get-tuple-element.273, f32[4096]{0:T(1024)} %bitcast.146, f32[4096]{0:T(1024)} %bitcast.145, ...), dimensions={0} | concatenate | bytes 434176 | tf_op jit(solution)/shard_map/concatenate | solution.py:1450
  949.7 170.0 %shard_map.431 = (f32[128,2048]{1,0:T(8,128)}, f32[128,2048]{1,0:T(8,128)}, f32[128,2048]{1,0:T(8,128)}, f32[128,1024]{1,0:T(8,128)}, f32[128,1024]{1,0:T(8,128)}, /*index=5*/f32[2,424,128]{2,1,0:T(8,128)}) custom-call(bf16[2048,1024]{1,0:T(8,128)(2,1)} %add_convert_fusion.2.rest_3_.refs_0_, bf16[2048,1024]{1,0:T(8,128)(2,1)} %add_convert_fusion.1.rest_4_.refs_1_, ...), custom_call_target="tpu_custom_call" | custom-call | flops 99999997952 | bytes 20000000 | tf_op jit(solution)/shard_map/pallas_call | solution.py:1198
  (620 shorter events, 435.1 us)
Async XLA Ops:
  164.4 96.8 %collective-permute-start.16 = (bf16[384,2048]{1,0:T(8,128)(2,1)}, bf16[384,2048]{1,0:T(8,128)(2,1)}, u32[]{:S(2)}, u32[]{:S(2)}) collective-permute-start(bf16[384,2048]{1,0:T(8,128)(2,1)} %bitcast.8.left_ref), channel_id=1, source_target_pairs={{0,8},{8,0},{16,24},{24,16},{1,9},{9,1},{17,25},{25,17},{2,10},{10... | collective-permute-start | bytes 4718600 | tf_op jit(solution)/shard_map/ppermute | solution.py:942
  166.0 440.3 %collective-permute-start.32 = (bf16[384,2048]{1,0:T(8,128)(2,1)}, bf16[384,2048]{1,0:T(8,128)(2,1)}, u32[]{:S(2)}, u32[]{:S(2)}) collective-permute-start(bf16[384,2048]{1,0:T(8,128)(2,1)} %fusion.12.left_ref), channel_id=1, source_target_pairs={{0,8},{8,0},{16,24},{24,16},{1,9},{9,1},{17,25},{25,17},{2,10},{10... | collective-permute-start | bytes 4718600 | tf_op jit(solution)/shard_map/ppermute | solution.py:942
  173.3 103.3 %collective-permute-start.24 = (bf16[384,2048]{1,0:T(8,128)(2,1)}, bf16[384,2048]{1,0:T(8,128)(2,1)}, u32[]{:S(2)}, u32[]{:S(2)}) collective-permute-start(bf16[384,2048]{1,0:T(8,128)(2,1)} %multiply_convert_fusion.2.left_ref), channel_id=1, source_target_pairs={{0,4},{2,6},{4,0},{6,2},{1,5},{3,7},{5,1},{7,3},{8,12},{10,14},{12... | collective-permute-start | bytes 4718600 | tf_op jit(solution)/shard_map/ppermute | solution.py:942
  175.7 111.9 %collective-permute-start.20 = (bf16[384,2048]{1,0:T(8,128)(2,1)}, bf16[384,2048]{1,0:T(8,128)(2,1)}, u32[]{:S(2)}, u32[]{:S(2)}) collective-permute-start(bf16[384,2048]{1,0:T(8,128)(2,1)} %multiply_convert_fusion.2.left_ref), channel_id=1, source_target_pairs={{0,2},{2,0},{4,6},{6,4},{1,3},{3,1},{5,7},{7,5},{8,10},{10,8},{12,... | collective-permute-start | bytes 4718600 | tf_op jit(solution)/shard_map/ppermute | solution.py:942
  287.6 325.9 %collective-permute-start.42 = (bf16[384,2048]{1,0:T(8,128)(2,1)}, bf16[384,2048]{1,0:T(8,128)(2,1)}, u32[]{:S(2)}, u32[]{:S(2)}) collective-permute-start(bf16[384,2048]{1,0:T(8,128)(2,1)} %fusion.12.left_ref), channel_id=1, source_target_pairs={{0,4},{2,6},{4,0},{6,2},{1,5},{3,7},{5,1},{7,3},{8,12},{10,14},{12... | collective-permute-start | bytes 4718600 | tf_op jit(solution)/shard_map/ppermute | solution.py:942
  299.9 49.7 %collective-permute-start.19 = (bf16[768,1408]{1,0:T(8,128)(2,1)}, bf16[768,1408]{1,0:T(8,128)(2,1)S(1)}, u32[]{:S(2)}, u32[]{:S(2)}) collective-permute-start(bf16[768,1408]{1,0:T(8,128)(2,1)} %constant_dynamic-slice_fusion.7), channel_id=1, source_target_pairs={{0,8},{8,0},{16,24},{24,16},{1,9},{9,1},{17,25},{25,17},{2,10},{10... | collective-permute-start | bytes 6488072 | tf_op jit(solution)/shard_map/ppermute | solution.py:942
  305.4 65.6 %collective-permute-start.27 = (bf16[768,1408]{1,0:T(8,128)(2,1)}, bf16[768,1408]{1,0:T(8,128)(2,1)}, u32[]{:S(2)}, u32[]{:S(2)}) collective-permute-start(bf16[768,1408]{1,0:T(8,128)(2,1)} %constant_dynamic-slice_fusion.5), channel_id=1, source_target_pairs={{0,4},{2,6},{4,0},{6,2},{1,5},{3,7},{5,1},{7,3},{8,12},{10,14},{12... | collective-permute-start | bytes 6488072 | tf_op jit(solution)/shard_map/ppermute | solution.py:942
  317.8 94.4 %collective-permute-start.23 = (bf16[768,1408]{1,0:T(8,128)(2,1)}, bf16[768,1408]{1,0:T(8,128)(2,1)}, u32[]{:S(2)}, u32[]{:S(2)}) collective-permute-start(bf16[768,1408]{1,0:T(8,128)(2,1)} %constant_dynamic-slice_fusion.6), channel_id=1, source_target_pairs={{0,2},{2,0},{4,6},{6,4},{1,3},{3,1},{5,7},{7,5},{8,10},{10,8},{12,... | collective-permute-start | bytes 6488072 | tf_op jit(solution)/shard_map/ppermute | solution.py:942
  349.5 41.8 %collective-permute-start.11 = (f32[384,2048]{1,0:T(8,128)S(1)}, f32[384,2048]{1,0:T(8,128)}, u32[]{:S(2)}, u32[]{:S(2)}) collective-permute-start(f32[384,2048]{1,0:T(8,128)S(1)} %copy-done.140), channel_id=1, source_target_pairs={{0,1},{1,0},{2,3},{3,2},{4,5},{5,4},{6,7},{7,6},{8,9},{9,8},{10,11... | collective-permute-start | bytes 9437192 | tf_op jit(solution)/shard_map/ppermute | solution.py:1249
  371.0 100.9 %collective-permute-start.29 = (bf16[1024,1408]{1,0:T(8,128)(2,1)}, bf16[1024,1408]{1,0:T(8,128)(2,1)}, u32[]{:S(2)}, u32[]{:S(2)}) collective-permute-start(bf16[1024,1408]{1,0:T(8,128)(2,1)} %add_convert_fusion.5.rest_0_), channel_id=1, source_target_pairs={{0,2},{2,0},{4,6},{6,4},{1,3},{3,1},{5,7},{7,5},{8,10},{10,8},{12,... | collective-permute-start | bytes 8650760 | tf_op jit(solution)/shard_map/ppermute | solution.py:942
  391.4 86.4 %collective-permute-start.31 = (bf16[1024,1408]{1,0:T(8,128)(2,1)}, bf16[1024,1408]{1,0:T(8,128)(2,1)}, u32[]{:S(2)}, u32[]{:S(2)}) collective-permute-start(bf16[1024,1408]{1,0:T(8,128)(2,1)} %add_convert_fusion.3.rest_2_), channel_id=1, source_target_pairs={{0,8},{8,0},{16,24},{24,16},{1,9},{9,1},{17,25},{25,17},{2,10},{10... | collective-permute-start | bytes 8650760 | tf_op jit(solution)/shard_map/ppermute | solution.py:942
  430.7 64.7 %collective-permute-start.30 = (bf16[1024,1408]{1,0:T(8,128)(2,1)}, bf16[1024,1408]{1,0:T(8,128)(2,1)}, u32[]{:S(2)}, u32[]{:S(2)}) collective-permute-start(bf16[1024,1408]{1,0:T(8,128)(2,1)} %add_convert_fusion.4.rest_1_), channel_id=1, source_target_pairs={{0,4},{2,6},{4,0},{6,2},{1,5},{3,7},{5,1},{7,3},{8,12},{10,14},{12... | collective-permute-start | bytes 8650760 | tf_op jit(solution)/shard_map/ppermute | solution.py:942
  471.9 38.0 %collective-permute-start.14 = (bf16[8,128,128]{2,1,0:T(8,128)(2,1)S(1)}, bf16[8,128,128]{2,1,0:T(8,128)(2,1)S(1)}, u32[]{:S(2)}, u32[]{:S(2)}) collective-permute-start(bf16[8,128,128]{2,1,0:T(8,128)(2,1)S(1)} %copy-done.145), channel_id=1, source_target_pairs={{2,0},{4,2},{6,4},{3,1},{5,3},{7,5},{10,8},{12,10},{14,12},{11,9},... | collective-permute-start | bytes 786440 | tf_op jit(solution)/shard_map/ppermute | solution.py:909
  477.8 49.1 %collective-permute-start.13 = (bf16[8,128,256]{2,1,0:T(8,128)(2,1)S(1)}, bf16[8,128,256]{2,1,0:T(8,128)(2,1)S(1)}, u32[]{:S(2)}, u32[]{:S(2)}) collective-permute-start(bf16[8,128,256]{2,1,0:T(8,128)(2,1)S(1)} %copy-done.144), channel_id=1, source_target_pairs={{2,0},{4,2},{6,4},{3,1},{5,3},{7,5},{10,8},{12,10},{14,12},{11,9},... | collective-permute-start | bytes 1572872 | tf_op jit(solution)/shard_map/ppermute | solution.py:909
  509.9 108.8 %collective-permute-start.46 = (bf16[384,2048]{1,0:T(8,128)(2,1)}, bf16[384,2048]{1,0:T(8,128)(2,1)}, u32[]{:S(2)}, u32[]{:S(2)}) collective-permute-start(bf16[384,2048]{1,0:T(8,128)(2,1)} %fusion.12.left_ref), channel_id=1, source_target_pairs={{0,2},{2,0},{4,6},{6,4},{1,3},{3,1},{5,7},{7,5},{8,10},{10,8},{12,... | collective-permute-start | bytes 4718600 | tf_op jit(solution)/shard_map/ppermute | solution.py:942
  526.8 67.7 %collective-permute-start.36 = (bf16[384,2048]{1,0:T(8,128)(2,1)S(1)}, bf16[384,2048]{1,0:T(8,128)(2,1)}, u32[]{:S(2)}, u32[]{:S(2)}) collective-permute-start(bf16[384,2048]{1,0:T(8,128)(2,1)S(1)} %fusion.256.left_ref), channel_id=1, source_target_pairs={{0,2},{2,0},{4,6},{6,4},{1,3},{3,1},{5,7},{7,5},{8,10},{10,8},{12,... | collective-permute-start | bytes 4718600 | tf_op jit(solution)/shard_map/ppermute | solution.py:942
  526.9 101.2 %collective-permute-start.57 = (bf16[512,1408]{1,0:T(8,128)(2,1)}, bf16[512,1408]{1,0:T(8,128)(2,1)}, u32[]{:S(2)}, u32[]{:S(2)}) collective-permute-start(bf16[512,1408]{1,0:T(8,128)(2,1)} %fusion.51.rest_0_), channel_id=1, source_target_pairs={{0,4},{2,6},{4,0},{6,2},{1,5},{3,7},{5,1},{7,3},{8,12},{10,14},{12... | collective-permute-start | bytes 4325384 | tf_op jit(solution)/shard_map/ppermute | solution.py:942
  606.3 80.9 %collective-permute-start.39 = (bf16[768,1024]{1,0:T(8,128)(2,1)S(1)}, bf16[768,1024]{1,0:T(8,128)(2,1)}, u32[]{:S(2)}, u32[]{:S(2)}) collective-permute-start(bf16[768,1024]{1,0:T(8,128)(2,1)S(1)} %copy-done.46), channel_id=1, source_target_pairs={{0,2},{2,0},{4,6},{6,4},{1,3},{3,1},{5,7},{7,5},{8,10},{10,8},{12,... | collective-permute-start | bytes 4718600 | tf_op jit(solution)/shard_map/ppermute | solution.py:942
  613.5 89.2 %collective-permute-start.35 = (bf16[768,1024]{1,0:T(8,128)(2,1)S(1)}, bf16[768,1024]{1,0:T(8,128)(2,1)}, u32[]{:S(2)}, u32[]{:S(2)}) collective-permute-start(bf16[768,1024]{1,0:T(8,128)(2,1)S(1)} %copy-done.56), channel_id=1, source_target_pairs={{0,8},{8,0},{16,24},{24,16},{1,9},{9,1},{17,25},{25,17},{2,10},{10... | collective-permute-start | bytes 4718600 | tf_op jit(solution)/shard_map/ppermute | solution.py:942
  618.7 54.1 %collective-permute-start.54 = (bf16[512,1408]{1,0:T(8,128)(2,1)S(1)}, bf16[512,1408]{1,0:T(8,128)(2,1)}, u32[]{:S(2)}, u32[]{:S(2)}) collective-permute-start(bf16[512,1408]{1,0:T(8,128)(2,1)S(1)} %copy-done.20), channel_id=1, source_target_pairs={{0,2},{2,0},{4,6},{6,4},{1,3},{3,1},{5,7},{7,5},{8,10},{10,8},{12,... | collective-permute-start | bytes 4325384 | tf_op jit(solution)/shard_map/ppermute | solution.py:942
  623.6 55.1 %collective-permute-start.51 = (bf16[512,1408]{1,0:T(8,128)(2,1)}, bf16[512,1408]{1,0:T(8,128)(2,1)S(1)}, u32[]{:S(2)}, u32[]{:S(2)}) collective-permute-start(bf16[512,1408]{1,0:T(8,128)(2,1)} %fusion.50.rest_1_), channel_id=1, source_target_pairs={{0,8},{8,0},{16,24},{24,16},{1,9},{9,1},{17,25},{25,17},{2,10},{10... | collective-permute-start | bytes 4325384 | tf_op jit(solution)/shard_map/ppermute | solution.py:942
  628.1 51.8 %collective-permute-start.37 = (bf16[384,2048]{1,0:T(8,128)(2,1)S(1)}, bf16[384,2048]{1,0:T(8,128)(2,1)S(1)}, u32[]{:S(2)}, u32[]{:S(2)}) collective-permute-start(bf16[384,2048]{1,0:T(8,128)(2,1)S(1)} %copy-done.60), channel_id=1, source_target_pairs={{0,1},{1,0},{2,3},{3,2},{4,5},{5,4},{6,7},{7,6},{8,9},{9,8},{10,11... | collective-permute-start | bytes 4718600 | tf_op jit(solution)/shard_map/ppermute | solution.py:1230
  680.5 125.9 %collective-permute-start.47 = (bf16[384,2048]{1,0:T(8,128)(2,1)}, bf16[384,2048]{1,0:T(8,128)(2,1)}, u32[]{:S(2)}, u32[]{:S(2)}) collective-permute-start(bf16[384,2048]{1,0:T(8,128)(2,1)} %get-tuple-element.139), channel_id=1, source_target_pairs={{0,1},{1,0},{2,3},{3,2},{4,5},{5,4},{6,7},{7,6},{8,9},{9,8},{10,11... | collective-permute-start | bytes 4718600 | tf_op jit(solution)/shard_map/ppermute | solution.py:1230
  682.2 129.0 %collective-permute-start.48 = (bf16[384,2048]{1,0:T(8,128)(2,1)}, bf16[384,2048]{1,0:T(8,128)(2,1)}, u32[]{:S(2)}, u32[]{:S(2)}) collective-permute-start(bf16[384,2048]{1,0:T(8,128)(2,1)} %get-tuple-element.140), channel_id=1, source_target_pairs={{0,1},{1,0},{2,3},{3,2},{4,5},{5,4},{6,7},{7,6},{8,9},{9,8},{10,11... | collective-permute-start | bytes 4718600 | tf_op jit(solution)/shard_map/ppermute | solution.py:1230
  686.7 127.0 %collective-permute-start.43 = (bf16[384,2048]{1,0:T(8,128)(2,1)}, bf16[384,2048]{1,0:T(8,128)(2,1)}, u32[]{:S(2)}, u32[]{:S(2)}) collective-permute-start(bf16[384,2048]{1,0:T(8,128)(2,1)} %get-tuple-element.137), channel_id=1, source_target_pairs={{0,1},{1,0},{2,3},{3,2},{4,5},{5,4},{6,7},{7,6},{8,9},{9,8},{10,11... | collective-permute-start | bytes 4718600 | tf_op jit(solution)/shard_map/ppermute | solution.py:1230
  687.2 131.2 %collective-permute-start.44 = (bf16[384,2048]{1,0:T(8,128)(2,1)}, bf16[384,2048]{1,0:T(8,128)(2,1)}, u32[]{:S(2)}, u32[]{:S(2)}) collective-permute-start(bf16[384,2048]{1,0:T(8,128)(2,1)} %get-tuple-element.138), channel_id=1, source_target_pairs={{0,1},{1,0},{2,3},{3,2},{4,5},{5,4},{6,7},{7,6},{8,9},{9,8},{10,11... | collective-permute-start | bytes 4718600 | tf_op jit(solution)/shard_map/ppermute | solution.py:1230
  772.5 48.1 %collective-permute-start.45 = (bf16[768,1024]{1,0:T(8,128)(2,1)S(1)}, bf16[768,1024]{1,0:T(8,128)(2,1)}, u32[]{:S(2)}, u32[]{:S(2)}) collective-permute-start(bf16[768,1024]{1,0:T(8,128)(2,1)S(1)} %copy-done.55), channel_id=1, source_target_pairs={{0,4},{2,6},{4,0},{6,2},{1,5},{3,7},{5,1},{7,3},{8,12},{10,14},{12... | collective-permute-start | bytes 4718600 | tf_op jit(solution)/shard_map/ppermute | solution.py:942
  806.5 65.5 %collective-permute-start.58 = (bf16[256,1408]{1,0:T(8,128)(2,1)}, bf16[256,1408]{1,0:T(8,128)(2,1)}, u32[]{:S(2)}, u32[]{:S(2)}) collective-permute-start(bf16[256,1408]{1,0:T(8,128)(2,1)} %fusion.112), channel_id=1, source_target_pairs={{0,16},{8,24},{16,0},{24,8},{1,17},{9,25},{17,1},{25,9},{2,18},{10... | collective-permute-start | bytes 2162696 | tf_op jit(solution)/shard_map/ppermute | solution.py:942
  811.2 76.2 %collective-permute-start.55 = (bf16[256,1408]{1,0:T(8,128)(2,1)}, bf16[256,1408]{1,0:T(8,128)(2,1)}, u32[]{:S(2)}, u32[]{:S(2)}) collective-permute-start(bf16[256,1408]{1,0:T(8,128)(2,1)} %fusion.114), channel_id=1, source_target_pairs={{0,16},{8,24},{16,0},{24,8},{1,17},{9,25},{17,1},{25,9},{2,18},{10... | collective-permute-start | bytes 2162696 | tf_op jit(solution)/shard_map/ppermute | solution.py:942
  813.7 89.2 %collective-permute-start.52 = (bf16[256,1408]{1,0:T(8,128)(2,1)}, bf16[256,1408]{1,0:T(8,128)(2,1)}, u32[]{:S(2)}, u32[]{:S(2)}) collective-permute-start(bf16[256,1408]{1,0:T(8,128)(2,1)} %fusion.116), channel_id=1, source_target_pairs={{0,16},{8,24},{16,0},{24,8},{1,17},{9,25},{17,1},{25,9},{2,18},{10... | collective-permute-start | bytes 2162696 | tf_op jit(solution)/shard_map/ppermute | solution.py:942
  818.5 111.0 %collective-permute-start.41 = (bf16[384,2048]{1,0:T(8,128)(2,1)}, bf16[384,2048]{1,0:T(8,128)(2,1)}, u32[]{:S(2)}, u32[]{:S(2)}) collective-permute-start(bf16[384,2048]{1,0:T(8,128)(2,1)} %add_convert_fusion.8), channel_id=1, source_target_pairs={{0,1},{1,0},{2,3},{3,2},{4,5},{5,4},{6,7},{7,6},{8,9},{9,8},{10,11... | collective-permute-start | bytes 4718600 | tf_op jit(solution)/shard_map/ppermute | solution.py:1249
  820.7 92.8 %collective-permute-start.50 = (bf16[768,512]{1,0:T(8,128)(2,1)}, bf16[768,512]{1,0:T(8,128)(2,1)}, u32[]{:S(2)}, u32[]{:S(2)}) collective-permute-start(bf16[768,512]{1,0:T(8,128)(2,1)} %constant_dynamic-slice_fusion.1), channel_id=1, source_target_pairs={{0,8},{8,0},{16,24},{24,16},{1,9},{9,1},{17,25},{25,17},{2,10},{10... | collective-permute-start | bytes 2359304 | tf_op jit(solution)/shard_map/ppermute | solution.py:942
  (203 other events, 2820.3 us)

commit v4 on v3

--- a/solution.py
+++ b/solution.py
@@ -2,7 +2,6 @@
 
 import jax
 import jax.numpy as jnp
-import numpy as np
 from jax import lax
 from jax.experimental import pallas as pl
 from jax.experimental.pallas import tpu as pltpu
@@ -16,6 +15,7 @@
 PAIR = 2 * GROUP
 RIM = 8
 VMEM_BYTES = 56 * 1024 * 1024
+LITTLE = pl.CostEstimate(flops=0, bytes_accessed=0, transcendentals=0)
 
 
 def mm(left, right):
@@ -383,9 +383,7 @@
         compiler_params=pltpu.CompilerParams(
             dimension_semantics=("arbitrary",), vmem_limit_bytes=VMEM_BYTES
         ),
-        cost_estimate=pl.CostEstimate(
-            flops=heads * count * 10_000_000, bytes_accessed=count * heads * 4000, transcendentals=0
-        ),
+        cost_estimate=LITTLE,
     )(spot, q, k, v, *rims, *convs, decay, beta, decay_log, decay_bias)
 
 
@@ -437,6 +435,7 @@
         compiler_params=pltpu.CompilerParams(
             dimension_semantics=("arbitrary",), vmem_limit_bytes=VMEM_BYTES
         ),
+        cost_estimate=LITTLE,
     )(mixed, reach, near_map, near_add, far_add, gate, gain)
 
 
@@ -497,6 +496,7 @@
         compiler_params=pltpu.CompilerParams(
             dimension_semantics=("arbitrary",), vmem_limit_bytes=VMEM_BYTES
         ),
+        cost_estimate=LITTLE,
     )(d_gated, kept, reach, gate, gain)
 
 
@@ -878,9 +878,7 @@
         compiler_params=pltpu.CompilerParams(
             dimension_semantics=("arbitrary",), vmem_limit_bytes=VMEM_BYTES
         ),
-        cost_estimate=pl.CostEstimate(
-            flops=held * count * 14_000_000, bytes_accessed=count * held * 6000, transcendentals=0
-        ),
+        cost_estimate=LITTLE,
     )(
         spot,
         q,
@@ -942,40 +940,49 @@
     return lax.ppermute(value, axis, [(place, place ^ (1 << bit)) for place in range(count)])
 
 
-def arrange_kernel(picks, left_ref, right_ref, *rest):
-    left_out, right_out = rest[-2:]
-    width = left_ref.shape[1] // 16
+def arrange_kernel(per_head, picks, full_ref, mine_ref, other_ref, *rest):
+    out_ref = rest[-1]
+    width = full_ref.shape[1] // 16
+    mine = (pl.program_id(0) // per_head) == picks[16]
     for place in range(16):
         source = pl.ds(pl.multiple_of(picks[place] * width, width), width)
         target = slice(place * width, (place + 1) * width)
-        left_out[:, target] = left_ref[:, source]
-        right_out[:, target] = right_ref[:, source]
-
-
-def relative_order(rows, more, order, after):
+        out_ref[0, :, target] = full_ref[:, source]
+        out_ref[1, :, target] = jnp.where(mine, mine_ref[:, source], other_ref[:, source])
+
+
+def paired_rows(full, got, order, *after):
+    order = order[1:] + order[:1]
     own = lax.axis_index("dp") * lax.axis_size("seq") + lax.axis_index("seq")
     masks = [
         sum(STAGES[stage][2] for k, stage in enumerate(order) if place >> (3 - k) & 1)
         for place in range(16)
     ]
-    picks = own ^ jnp.array(masks, jnp.int32)
-    count, width = rows.shape
+    picks = jnp.concatenate(
+        [own ^ jnp.array(masks, jnp.int32), lax.axis_index("heads").astype(jnp.int32)[None]]
+    )
+    if lax.axis_size("heads") == 2:
+        other = lax.ppermute(got, "heads", [(0, 1), (1, 0)])
+    else:
+        got = other = heads_gather(got)
+    count, width = full.shape
     size = 96
+    blocks = got.shape[0] // size
     piece = pl.BlockSpec((size, width), lambda i: (i, 0))
-    return pl.pallas_call(
-        arrange_kernel,
+    part = pl.BlockSpec((size, width), lambda i: (lax.rem(i, blocks), 0))
+    both = pl.pallas_call(
+        functools.partial(arrange_kernel, blocks),
         grid=(count // size,),
-        in_specs=[pl.BlockSpec(memory_space=pltpu.SMEM), piece, piece]
+        in_specs=[pl.BlockSpec(memory_space=pltpu.SMEM), piece, part, part]
         + [pl.BlockSpec(memory_space=pl.ANY) for _ in after],
-        out_specs=[piece, piece],
-        out_shape=[jax.ShapeDtypeStruct((count, width), rows.dtype)] * 2,
+        out_specs=pl.BlockSpec((2, size, width), lambda i: (0, i, 0)),
+        out_shape=jax.ShapeDtypeStruct((2, count, width), full.dtype),
         compiler_params=pltpu.CompilerParams(
             dimension_semantics=("arbitrary",), vmem_limit_bytes=VMEM_BYTES
         ),
-        cost_estimate=pl.CostEstimate(
-            flops=0, bytes_accessed=12 * count * width, transcendentals=0
-        ),
-    )(picks, rows, more, *after)
+        cost_estimate=LITTLE,
+    )(picks, full, got, other, *after)
+    return both.reshape(-1, width)
 
 
 def own_side(stage):
@@ -983,49 +990,41 @@
     return lax.rem(lax.axis_index(axis) // (1 << bit), 2)
 
 
-def paired_rows(own_rows, got_rows, order, *after):
-    both = relative_order(own_rows, got_rows, order[1:] + order[:1], after)
-    return tuple(heads_gather(rows) for rows in both)
-
-
-def trade_halves(grads, order):
+def pick_half(grads, order, which):
     half = grads.shape[1] // 2
     side = own_side(order[0])
-    mine = lax.dynamic_slice_in_dim(grads, side * half, half, 1)
-    theirs = lax.dynamic_slice_in_dim(grads, (1 - side) * half, half, 1)
-    return mine, trade(theirs, order[0])
-
-
-def pair_grad(rows, halves, begin, end):
-    width = rows[0].shape[1] // 16
-    cut = slice(begin * width, end * width)
-    return sum(weight_grad(part[:, cut], grads) for part, grads in zip(rows, halves))
-
-
-def grad_open(rows, halves, order):
-    sent = low(pair_grad(rows, halves, 8, 16))
-    return rows, halves, sent, trade(sent, order[1])
+    return lax.dynamic_slice_in_dim(grads, (side if which else 1 - side) * half, half, 1)
+
+
+def join_halves(grads, got, order):
+    return jnp.concatenate([pick_half(grads, order, 1), got], axis=0)
+
+
+def trade_halves(grads, order):
+    return join_halves(grads, trade(pick_half(grads, order, 0), order[0]), order)
+
+
+def pair_grad(rows, grads, begin, end):
+    width = rows.shape[1] // 16
+    return weight_grad(rows[:, begin * width : end * width], grads)
+
+
+def grad_open(rows, grads, order):
+    sent = low(pair_grad(rows, grads, 8, 16))
+    return rows, grads, sent, trade(sent, order[1])
 
 
 def grad_next(opened, order):
-    rows, halves, _, first = opened
-    width = rows[0].shape[1] // 16
-    sent = low(pair_grad(rows, halves, 4, 8) + high(first[4 * width :]))
-    rest = pair_grad(rows, halves, 0, 4) + high(first[: 4 * width])
+    rows, grads, _, first = opened
+    middle = first.shape[0] // 2
+    sent = low(pair_grad(rows, grads, 4, 8) + high(first[middle:]))
+    rest = pair_grad(rows, grads, 0, 4) + high(first[:middle])
     return rest, sent, trade(sent, order[2])
 
 
-def grad_close(moved, order):
+def grad_last(moved):
     rest, _, second = moved
-    width = rest.shape[0] // 4
-    half = rest.shape[1]
-    side = own_side(order[0])
-    third = trade(low(rest[2 * width :] + high(second[2 * width :])), order[3])
-    final = rest[: 2 * width] + high(second[: 2 * width]) + high(third)
-    other = high(trade(low(final[width:]), order[0]))
-    left = jnp.where(side == 0, final[:width], other)
-    right = jnp.where(side == 0, other, final[:width])
-    return jnp.concatenate([left, right], axis=1)
+    return low(rest + high(second))
 
 
 def finish_kernel(plan, head_steps, *refs):
@@ -1033,9 +1032,11 @@
     grads, small_ref = refs[:groups], refs[groups]
     outs, small_out = refs[groups + 1 : 2 * groups + 1], refs[2 * groups + 1]
     scratch = refs[2 * groups + 2 :]
-    buffers = [scratch[7 * g : 7 * g + 7] for g in range(groups)]
-    small_sum, small_got, send_sem, recv_sem, small_send, small_recv = scratch[7 * groups :]
-    width = grads[0].shape[0] // 16
+    buffers = []
+    for stages, _ in plan:
+        buffers.append(scratch[: len(stages)])
+        scratch = scratch[len(stages) :]
+    small_sum, small_got, send_sem, recv_sem, small_send, small_recv = scratch
 
     def side(stage):
         axis, bit, _ = STAGES[stage]
@@ -1073,60 +1074,51 @@
         return copy
 
     most = max(len(cuts) for _, cuts in plan)
+    longest = max(len(stages) for stages, _ in plan)
     chunks, number = [], 0
     rounds = [[] for _ in range(most)]
-    for g, (order, cuts) in enumerate(plan):
+    for g, (stages, cuts) in enumerate(plan):
         for k, cut in enumerate(cuts):
-            chunks.append((g, order, slice(*cut)))
+            chunks.append((g, stages, slice(*cut)))
             rounds[k].append(number)
             number += 1
     copies = {}
 
-    def launch(stage, index, source, target, name):
-        sems = (send_sem.at[4 * index + stage], recv_sem.at[4 * index + stage])
-        copies[stage, index] = send(source, target, sems, partner(name))
-
-    def open_chunk(index):
-        g, order, cut = chunks[index]
-        launch(0, index, grads[g].at[8 * width :, cut], buffers[g][0].at[:, cut], order[1])
-
-    def second_chunk(index):
-        g, order, cut = chunks[index]
-        copies[0, index].wait_recv()
-        got, sent, got_next = buffers[g][0], buffers[g][4], buffers[g][1]
-        rows = slice(4 * width, 8 * width)
-        sent[:, cut] = low(high(grads[g][rows, cut]) + high(got[rows, cut]))
-        launch(1, index, sent.at[:, cut], got_next.at[:, cut], order[2])
-
-    def third_chunk(index):
-        g, order, cut = chunks[index]
-        copies[1, index].wait_recv()
-        rows = slice(2 * width, 4 * width)
-        first, second, sent = buffers[g][0], buffers[g][1], buffers[g][5]
-        sent[:, cut] = low(
-            high(grads[g][rows, cut]) + high(first[rows, cut]) + high(second[rows, cut])
+    def advance(index, step):
+        g, stages, cut = chunks[index]
+        if step > len(stages):
+            return
+        if step > 0:
+            copies[index, step - 1].wait_recv()
+        full = grads[g].shape[0]
+        here = buffers[g]
+        if step == len(stages):
+            there = 1 - side(stages[-1])
+            outs[g][pl.ds(there, 1), :, cut] = here[-1][:, cut][None]
+            return
+        rows = slice(full >> (step + 1), full >> step)
+        if step == 0:
+            source = grads[g].at[rows, cut]
+            if len(stages) == 1:
+                outs[g][pl.ds(side(stages[0]), 1), :, cut] = grads[g][: rows.start, cut][None]
+        else:
+            last = step == len(stages) - 1
+            begin = 0 if last else rows.start
+            value = high(grads[g][begin : rows.stop, cut])
+            for got in here[:step]:
+                value = value + high(got[begin : rows.stop, cut])
+            if last:
+                outs[g][pl.ds(side(stages[-1]), 1), :, cut] = low(value[: rows.start])[None]
+                value = value[rows.start :]
+            here[0][rows, cut] = low(value)
+            source = here[0].at[rows, cut]
+        place = 4 * index + step
+        copies[index, step] = send(
+            source,
+            here[step].at[:, cut],
+            (send_sem.at[place], recv_sem.at[place]),
+            partner(stages[step]),
         )
-        launch(2, index, sent.at[:, cut], buffers[g][2].at[:, cut], order[3])
-
-    def fourth_chunk(index):
-        g, order, cut = chunks[index]
-        copies[2, index].wait_recv()
-        first, second, third, sent = (buffers[g][k] for k in (0, 1, 2, 6))
-        half = grads[g].shape[1]
-        rows = slice(0, 2 * width)
-        final = high(grads[g][rows, cut]) + high(first[rows, cut])
-        final = final + high(second[rows, cut]) + high(third[:, cut])
-        sent[:, cut] = low(final[width:])
-        launch(3, index, sent.at[:, cut], buffers[g][3].at[:, cut], order[0])
-        place = pl.multiple_of(side(order[0]) * half + cut.start, 128)
-        outs[g][:, pl.ds(place, cut.stop - cut.start)] = final[:width]
-
-    def last_chunk(index):
-        g, order, cut = chunks[index]
-        copies[3, index].wait_recv()
-        half = grads[g].shape[1]
-        place = pl.multiple_of((1 - side(order[0])) * half + cut.start, 128)
-        outs[g][:, pl.ds(place, cut.stop - cut.start)] = high(buffers[g][3][:, cut])
 
     small_copies = []
     names = "xylh"
@@ -1156,23 +1148,18 @@
                 small_copies.append(send(block, block, sems, head_partner(size)))
 
     total_small = 5 + len(head_steps)
-    for index in rounds[0]:
-        open_chunk(index)
     small_step(0)
-    if most > 1:
-        for index in rounds[1]:
-            open_chunk(index)
-    for t in range(max(most + 3, total_small - 1)):
-        if t < most:
-            for index in rounds[t]:
-                second_chunk(index)
-        if t + 2 < most:
-            for index in rounds[t + 2]:
-                open_chunk(index)
-        for lag, work in ((1, third_chunk), (2, fourth_chunk), (3, last_chunk)):
+    for ahead in range(min(2, most)):
+        for index in rounds[ahead]:
+            advance(index, 0)
+    for t in range(max(most + longest, total_small - 1)):
+        for lag in range(longest):
+            if lag == 1 and t + 2 < most:
+                for index in rounds[t + 2]:
+                    advance(index, 0)
             if 0 <= t - lag < most:
                 for index in rounds[t - lag]:
-                    work(index)
+                    advance(index, lag + 1)
         if t + 1 < total_small:
             small_step(t + 1)
     for copy in started:
@@ -1184,45 +1171,68 @@
     head_steps = []
     while 1 << len(head_steps) < count:
         head_steps.append(1 << len(head_steps))
-    plan, scratch = [], []
+    plan, scratch, outs = [], [], []
     for array, order in zip(grads, orders):
         full, half = array.shape
-        step = min(256, half)
-        plan.append((order, [(at, at + step) for at in range(0, half, step)]))
-        for rows in (8, 4, 2, 1, 4, 2, 1):
-            scratch.append(pltpu.VMEM((full // 16 * rows, half), jnp.bfloat16))
+        step = min(256 if len(order) == 4 else 512, half) if half % 128 == 0 else half
+        cuts = [(at, min(at + step, half)) for at in range(0, half, step)]
+        plan.append((order[1:] + order[:1], cuts))
+        for level in range(len(order)):
+            scratch.append(pltpu.VMEM((full >> (level + 1), half), jnp.bfloat16))
+        outs.append(jax.ShapeDtypeStruct((2, full >> len(order), half), jnp.bfloat16))
     pieces = sum(len(cuts) for _, cuts in plan)
     inside = pl.BlockSpec(memory_space=pltpu.VMEM)
-    rows = small.shape[0]
     f32 = jnp.float32
     return pl.pallas_call(
         functools.partial(finish_kernel, tuple(plan), tuple(head_steps)),
         in_specs=[inside] * (len(grads) + 1),
         out_specs=[inside] * (len(grads) + 1),
-        out_shape=[
-            jax.ShapeDtypeStruct((array.shape[0] // 16, 2 * array.shape[1]), f32)
-            for array in grads
-        ]
-        + [jax.ShapeDtypeStruct((count, rows, 128), f32)],
+        out_shape=outs + [jax.ShapeDtypeStruct((count,) + small.shape, f32)],
         scratch_shapes=scratch
         + [
-            pltpu.VMEM((5, rows, 128), f32),
-            pltpu.VMEM((4, rows, 128), f32),
+            pltpu.VMEM((5,) + small.shape, f32),
+            pltpu.VMEM((4,) + small.shape, f32),
             pltpu.SemaphoreType.DMA((4 * pieces,)),
             pltpu.SemaphoreType.DMA((4 * pieces,)),
             pltpu.SemaphoreType.DMA((8,)),
             pltpu.SemaphoreType.DMA((8,)),
         ],
         compiler_params=pltpu.CompilerParams(
-            collective_id=0, has_side_effects=True, vmem_limit_bytes=VMEM_BYTES
+            collective_id=0, has_side_effects=True, vmem_limit_bytes=60 * 1024 * 1024
         ),
-        cost_estimate=pl.CostEstimate(
-            flops=100_000_000_000, bytes_accessed=20_000_000, transcendentals=0
-        ),
+        cost_estimate=LITTLE,
     )(*grads, small)
 
 
-def heads_gather(rows):
+def fence(one, *after):
+    return pl.pallas_call(
+        lambda one_ref, *rest: rest[-1].__setitem__(..., one_ref[...]),
+        in_specs=[pl.BlockSpec(memory_space=pltpu.VMEM)]
+        + [pl.BlockSpec(memory_space=pl.ANY) for _ in after],
+        out_specs=pl.BlockSpec(memory_space=pltpu.VMEM),
+        out_shape=jax.ShapeDtypeStruct(one.shape, one.dtype),
+        compiler_params=pltpu.CompilerParams(vmem_limit_bytes=VMEM_BYTES),
+        cost_estimate=LITTLE,
+    )(one, *after)
+
+
+def order_kernel(*refs):
+    pass
+
+
+def ordered(values, *after):
+    anywhere = pl.BlockSpec(memory_space=pl.ANY)
+    return pl.pallas_call(
+        order_kernel,
+        in_specs=[anywhere] * (len(values) + len(after)),
+        out_specs=[anywhere] * len(values),
+        out_shape=[jax.ShapeDtypeStruct(part.shape, part.dtype) for part in values],
+        input_output_aliases={k: k for k in range(len(values))},
+        cost_estimate=LITTLE,
+    )(*values, *after)
+
+
+def heads_gather(rows, axis=0):
     count = lax.axis_size("heads")
     own = lax.axis_index("heads")
     step = 1
@@ -1230,7 +1240,7 @@
         other = lax.ppermute(rows, "heads", [(place, place ^ step) for place in range(count)])
         upper = lax.rem(own // step, 2) == 1
         rows = jnp.concatenate(
-            [jnp.where(upper, other, rows), jnp.where(upper, rows, other)], axis=0
+            [jnp.where(upper, other, rows), jnp.where(upper, rows, other)], axis=axis
         )
         step *= 2
     return rows
@@ -1250,7 +1260,8 @@
     return part(own) + high(got)
 
 
-ORDERS = ("xylh", "ylxh", "lxyh")
+ORDERS = ("xylh", "yxlh", "lxyh")
+FFN_ORDERS = ("xlyh", "yxlh", "lyhx")
 
 
 def body(
@@ -1283,8 +1294,8 @@
         heads_gather(out_cotangent[0]),
     )
     span = normed.shape[0]
-    normed_got = {order: trade(normed_own, order[0]) for order in ORDERS}
-    cotangent_got = trade(out_cotangent[0], ORDERS[2][0])
+    normed_got = {order: trade(normed_own, order[0]) for order in ORDERS[:2]}
+    cotangent_got = trade(out_cotangent[0], FFN_ORDERS[2][0])
     taps = conv_q.shape[0]
     q_proj = project(normed, q_weight)
     k_proj = project(normed, k_weight)
@@ -1302,129 +1313,124 @@
     mixed_local, reach, span_map, span_add, *saved, cum, rate = state_forward(
         q_proj, k_proj, v_proj, rims, convs, decay_proj, beta_proj, log_row, bias_row, spot, per_step
     )
+    span_map, span_add = ordered((span_map, span_add), cotangent_got, *normed_got.values())
     near_map, near_add = shifted((span_map, span_add), "seq", 1)
     far_add = shifted(span_add, "seq", 2)
     next_map = shifted(span_map, "seq", -1)
+    (mixed_local,) = ordered((mixed_local,), next_map)
     gated_low, mixed_low, start_state = gate_forward(
         mixed_local, reach, near_map, near_add, far_add, gate_proj, gain_row, per_step
     )
     mixer = heads_sum(
-        lambda pick: rows_product(pick(gated_low), out_weight), span, jnp.float32
+        lambda pick: rows_product(pick(gated_low), out_weight), span, jnp.bfloat16
     )
     resid_mid = resid + mixer
     ffn_own = rms_scale(resid_mid, ffn_gain).astype(jnp.bfloat16)
     ffn_in = heads_gather(ffn_own)
-    ffn_got = {order: trade(ffn_own, order[0]) for order in ORDERS[:2]}
-    out_halves = trade_halves(gated_low, ORDERS[0])
+    ffn_got = {order: trade(ffn_own, order[0]) for order in FFN_ORDERS[:2]}
     gate_ffn = project(ffn_in, ffn_gate)
     up_ffn = project(ffn_in, ffn_up)
     act, act_pull = jax.vjp(swish_product, gate_ffn, up_ffn)
     act_low = act.astype(jnp.bfloat16)
-    down_halves = trade_halves(act_low, ORDERS[2])
-    ffn_out = heads_sum(lambda pick: rows_product(pick(act_low), ffn_down), span, jnp.bfloat16)
-    output = (resid_mid + ffn_out).astype(jnp.bfloat16)
     d_act = jnp.einsum("td,fd->tf", cotangent, ffn_down, preferred_element_type=jnp.float32)
     d_gate_ffn, d_up_ffn = act_pull(d_act)
     d_gate_low = d_gate_ffn.astype(jnp.bfloat16)
     d_up_low = d_up_ffn.astype(jnp.bfloat16)
-    cotangent_rel = paired_rows(out_cotangent[0], cotangent_got, ORDERS[2], act_low)
-    gate_halves = trade_halves(d_gate_low, ORDERS[0])
-    up_halves = trade_halves(d_up_low, ORDERS[1])
-    ffn_rel = {
-        order: paired_rows(ffn_own, ffn_got[order], order, d_gate_low) for order in ORDERS[:2]
-    }
-    down_open = grad_open(cotangent_rel, down_halves, ORDERS[2])
-    gate_open = grad_open(ffn_rel[ORDERS[0]], gate_halves, ORDERS[0])
-    up_open = grad_open(ffn_rel[ORDERS[1]], up_halves, ORDERS[1])
+    ffn_low = (d_gate_low, d_up_low, act_low)
+    theirs = [pick_half(part, order, 0) for part, order in zip(ffn_low, FFN_ORDERS)]
+    ffn_traded = [trade(part, order[0]) for part, order in zip(theirs, FFN_ORDERS)]
+    ffn_low = ordered(ffn_low, *ffn_got.values(), *theirs)
+    d_gate_low, d_up_low, act_low = ffn_low
+    gate_halves, up_halves, down_halves = (
+        join_halves(part, got, order)
+        for part, got, order in zip(ffn_low, ffn_traded, FFN_ORDERS)
+    )
+    ffn_out = heads_sum(lambda pick: rows_product(pick(act_low), ffn_down), span, jnp.bfloat16)
+    output = (resid_mid + ffn_out).astype(jnp.bfloat16)
+    cotangent_rel = paired_rows(cotangent, cotangent_got, FFN_ORDERS[2], act_low)
+    ffn_rel = [
+        paired_rows(ffn_in, ffn_got[order], order, d_gate_low) for order in FFN_ORDERS[:2]
+    ]
+    gate_open = grad_open(ffn_rel[0], gate_halves, FFN_ORDERS[0])
+    up_open = grad_open(ffn_rel[1], up_halves, FFN_ORDERS[1])
+    down_open = grad_open(cotangent_rel, down_halves, FFN_ORDERS[2])
     d_ffn = heads_sum(
         lambda pick: rows_back(pick(d_gate_low), ffn_gate) + rows_back(pick(d_up_low), ffn_up),
         span,
-        jnp.float32,
+        jnp.bfloat16,
     )
     _, ffn_norm_pull = jax.vjp(rms_scale, resid_mid, ffn_gain)
     d_mid_norm, d_ffn_gain = ffn_norm_pull(d_ffn)
     d_mid = out_cotangent[0].astype(jnp.float32) + d_mid_norm
     d_mid_low = low(d_mid)
     d_mid_all = heads_gather(d_mid_low)
-    d_mid_got = trade(d_mid_low, ORDERS[0][0])
+    d_mid_got = trade(d_mid_low, ORDERS[2][0])
     d_gated = jnp.einsum("td,cd->tc", d_mid_all, out_weight, preferred_element_type=jnp.float32)
     d_mixed, d_gate_low_mix, d_start, d_out_gain = gate_backward(
         d_gated, mixed_low, reach, gate_proj, gain_row, per_step
     )
     next_start = shifted(d_start, "seq", -1)
     beyond_start = shifted(d_start, "seq", -2)
-    mix_halves = trade_halves(d_gate_low_mix, ORDERS[2])
-    parts = 2 if heads > 1 else 1
-    held = heads // parts
-    per_step = min(per_step, held)
-    backs, grads_low, mix_halves_part = [], [], []
-    for part in range(parts):
-        if part == 0:
-            after = (down_open[2], gate_open[2], up_open[2])
-        else:
-            down_next = grad_next(down_open, ORDERS[2])
-            gate_next = grad_next(gate_open, ORDERS[0])
-            up_next = grad_next(up_open, ORDERS[1])
-            gate_mix_rel = paired_rows(normed_own, normed_got[ORDERS[2]], ORDERS[2], up_next[1])
-            gate_mix_grad = low(pair_grad(gate_mix_rel, mix_halves, 0, 16))
-            d_mid_rel = paired_rows(d_mid_low, d_mid_got, ORDERS[0], up_next[1])
-            out_grad = low(pair_grad(d_mid_rel, out_halves, 0, 16))
-            after = (down_next[1], gate_next[1], up_next[1], gate_mix_grad, out_grad)
-        back = state_backward(
-            q_proj,
-            k_proj,
-            v_proj,
-            rims,
-            convs,
-            decay_proj,
-            log_row,
-            bias_row,
-            cum,
-            rate,
-            saved,
-            start_state,
-            d_mixed,
-            next_start,
-            next_map,
-            beyond_start,
-            spot,
-            per_step,
-            part * held,
-            held,
-            after,
-        )
-        rim = shifted(jnp.concatenate(back[3:6], axis=1), "seq", -1)
-        passed = jnp.split(rim, (held * DK, 2 * held * DK), axis=1)
-        lows = [
-            lax.dynamic_update_slice_in_dim(whole, low(end + more), span - RIM, 0)
-            for whole, end, more in zip(back[0:3], back[6:9], passed)
-        ]
-        backs.append(back)
-        grads_low.append(lows)
-    d_q_low, d_k_low, d_v_low = (jnp.concatenate(part, axis=1) for part in zip(*grads_low))
-    conv_grads = [jnp.concatenate(part, axis=1) for part in zip(*(back[9:12] for back in backs))]
-    d_decay_low, d_beta_low, d_log, d_bias = (
-        sum(part) for part in zip(*(back[12:16] for back in backs))
-    )
-    d_decay_low, d_beta_low = low(d_decay_low), low(d_beta_low)
-    d_log, d_bias = d_log[0], d_bias[0]
-    grad_down = grad_close(down_next, ORDERS[2]).T
-    grad_gate = grad_close(gate_next, ORDERS[0])
-    grad_up = grad_close(up_next, ORDERS[1])
-    tails, tail_orders = [gate_mix_grad, out_grad], [ORDERS[2], ORDERS[0]]
-    for part, lows in enumerate(grads_low):
-        flat_low = jnp.concatenate(lows, axis=1)
-        pieces = 2 if part == parts - 1 and parts > 1 else 1
-        size = flat_low.shape[1] // pieces
-        for piece in range(pieces):
-            order = ORDERS[(1, 0, 2)[part + piece]]
-            if order == ORDERS[2]:
-                rows = gate_mix_rel
-            else:
-                rows = paired_rows(normed_own, normed_got[order], order, backs[0][0])
-            halves = trade_halves(flat_low[:, piece * size : (piece + 1) * size], order)
-            tails.append(low(pair_grad(rows, halves, 0, 16)))
-            tail_orders.append(order)
+    mix_halves = trade_halves(d_gate_low_mix, ORDERS[0])
+    (gated_low,) = ordered((gated_low,), d_gate_low_mix)
+    out_halves = trade_halves(gated_low, ORDERS[2])
+    normed_rel = [
+        paired_rows(normed, normed_got[order], order, up_open[2]) for order in ORDERS[:2]
+    ]
+    d_mid_rel = paired_rows(d_mid_all, d_mid_got, ORDERS[2], up_open[2])
+    moved = [
+        grad_next(opened, order)
+        for opened, order in zip((gate_open, up_open, down_open), FFN_ORDERS)
+    ]
+    back = state_backward(
+        q_proj,
+        k_proj,
+        v_proj,
+        rims,
+        convs,
+        decay_proj,
+        log_row,
+        bias_row,
+        cum,
+        rate,
+        saved,
+        start_state,
+        d_mixed,
+        next_start,
+        next_map,
+        beyond_start,
+        spot,
+        per_step,
+        0,
+        heads,
+        [part[1] for part in moved] + [d_mid_rel, *normed_rel],
+    )
+    rim = jnp.concatenate(back[3:6], axis=1)
+    (rim,) = ordered((rim,), *(part[2] for part in moved))
+    rim = shifted(rim, "seq", -1)
+    passed = jnp.split(rim, (heads * DK, 2 * heads * DK), axis=1)
+    d_q_low, d_k_low, d_v_low = (
+        lax.dynamic_update_slice_in_dim(whole, low(end + more), span - RIM, 0)
+        for whole, end, more in zip(back[0:3], back[6:9], passed)
+    )
+    d_decay_low, d_beta_low = low(back[12]), low(back[13])
+    flat_lows = (jnp.concatenate([d_q_low, d_k_low], axis=1), d_v_low)
+    late = [pick_half(part, order, 0) for part, order in zip(flat_lows, ORDERS)]
+    late_got = [trade(part, order[0]) for part, order in zip(late, ORDERS)]
+    d_gate_low_mix, d_mid_rel, *normed_rel = ordered(
+        (d_gate_low_mix, d_mid_rel, *normed_rel), *late
+    )
+    tails = [
+        grad_last(moved[0]),
+        grad_last(moved[1]),
+        grad_last(moved[2]),
+        low(pair_grad(normed_rel[0], mix_halves, 0, 16)),
+        low(pair_grad(d_mid_rel, out_halves, 0, 16)),
+    ]
+    tail_orders = [order[:1] + order[3:] for order in FFN_ORDERS] + [ORDERS[0], ORDERS[2]]
+    for flat_low, got, rows, order in zip(flat_lows, late_got, normed_rel, ORDERS):
+        tails.append(low(pair_grad(rows, join_halves(flat_low, got, order), 0, 16)))
+        tail_orders.append(order)
     narrow_grad = weight_grad(jnp.concatenate([d_decay_low, d_beta_low], axis=1), normed)
     pairs = (
         (d_q_low, q_weight),
@@ -1442,36 +1448,50 @@
     _, in_norm_pull = jax.vjp(rms_scale, resid, norm_gain)
     d_in_norm, d_norm_gain = in_norm_pull(d_normed)
     input_grad = d_mid + d_in_norm
-    owned = (d_log, d_bias) + tuple(part.reshape(-1) for part in conv_grads)
-    shared = (d_norm_gain, d_ffn_gain, d_out_gain[0], narrow_grad.reshape(-1))
-    marks = [int(mark) for mark in np.cumsum([part.size for part in shared + owned])]
-    rows = -(-marks[-1] // 1024) * 8
-    blank = jnp.zeros((rows * 128 - marks[-1],), jnp.float32)
-    flat = jnp.concatenate(shared + owned + (blank,)).reshape(rows, 128)
-    grad_gate_mix, grad_out, *mixes, everyone = finish(tails, tail_orders, flat)
-    grad_out = grad_out.T
-    everyone = everyone.reshape(everyone.shape[0], -1)
-    own_head = lax.axis_index("heads")
-    narrow_own = lax.dynamic_slice(
-        everyone, (own_head, marks[2]), (1, narrow_grad.size)
-    ).reshape(narrow_grad.shape)
+    wide = normed.shape[1]
+    conv_all = jnp.concatenate(back[9:12], axis=1)
+
+    def full_rows(part):
+        return jnp.pad(part, ((0, 0), (0, wide - part.shape[1])))
+
+    conv_rows = [full_rows(conv_all[:, at : at + wide]) for at in range(0, conv_all.shape[1], wide)]
+    last_row = full_rows(jnp.concatenate([d_out_gain, back[14], back[15]], axis=1))
+    stacked = [narrow_grad] + conv_rows + [d_norm_gain[None], d_ffn_gain[None], last_row]
+    flat = jnp.concatenate(stacked, axis=0)
+    flat = jnp.pad(flat, ((0, -flat.shape[0] % 8), (0, 0)))
+    *sums, everyone = finish(tails, tail_orders, flat)
+    grad_gate, grad_up, grad_down, grad_gate_mix, grad_out, grad_qk, grad_v = (
+        high(jnp.concatenate([part[0], part[1]], axis=1)) for part in sums
+    )
+    grad_down, grad_out = grad_down.T, grad_out.T
+    grad_q, grad_k = jnp.split(grad_qk, 2, axis=1)
     shard = lax.axis_index("dp") * lax.axis_size("seq") + lax.axis_index("seq")
-    size = narrow_grad.shape[1] // 16
-    narrow_sum = lax.dynamic_slice_in_dim(narrow_own, shard * size, size, 1).T
+    size = wide // 16
+    narrow_sum = lax.dynamic_slice(
+        everyone, (lax.axis_index("heads"), 0, shard * size), (1, 2 * heads, size)
+    )[0].T
     grad_decay, grad_beta = narrow_sum[:, :heads], narrow_sum[:, heads:]
-    pieces = jnp.split(everyone, marks, axis=1)[:-1]
-    small = [piece.sum(0) for piece in pieces[:3]]
-    small += [pieces[4].reshape(-1), pieces[5].reshape(-1)]
-    for piece in pieces[6:]:
-        small.append(
-            jnp.swapaxes(piece.reshape(piece.shape[0], taps, -1), 0, 1).reshape(taps, -1)
-        )
-    wide = held * DK
-    by_part = [mixes[0]] if parts == 1 else [mixes[0], jnp.concatenate(mixes[1:], axis=1)]
-    grad_q, grad_k, grad_v = (
-        jnp.concatenate(part, axis=1)
-        for part in zip(*(jnp.split(mix, (wide, 2 * wide), axis=1) for mix in by_part))
-    )
+    at = 2 * heads
+    conv_sum = jnp.concatenate(
+        [everyone[:, at + taps * k : at + taps * (k + 1)] for k in range(len(conv_rows))], axis=2
+    )
+    at += taps * len(conv_rows)
+    width_k = heads * DK
+
+    def by_head(part):
+        return jnp.swapaxes(part, 0, 1).reshape(part.shape[1], -1)
+
+    width_v = out_gain.shape[0]
+    small = [
+        everyone[:, at].sum(0),
+        everyone[:, at + 1].sum(0),
+        everyone[:, at + 2, :width_v].sum(0),
+        everyone[:, at + 2, width_v : width_v + heads].reshape(-1),
+        everyone[:, at + 2, width_v + heads : width_v + 2 * heads].reshape(-1),
+        by_head(conv_sum[:, :, :width_k]),
+        by_head(conv_sum[:, :, width_k : 2 * width_k]),
+        by_head(conv_sum[:, :, 2 * width_k : 2 * width_k + heads * DV]),
+    ]
     return (
         output[None],
         input_grad[None],

time: 1160 us -> 947 us (0.82)
  waiting for transfers between devices: 193 us -> 34.6 us
  Pallas kernels: 368 us -> 417 us
  matrix products: 363 us -> 319 us
  starting transfers between devices: 85.2 us -> 60.4 us
  other arithmetic: 75.8 us -> 53.7 us
  local copies, waits for them, and re-layouts: 65.2 us -> 51.6 us
    ppermute x27 -> x19, waiting for transfers between devices: 165 us -> 22.4 us  [trade(): lax.ppermute(value, axis, [(place, place ^ 1 << bit) for place in range(c...]
    pallas_call x1, Pallas kernels: 170 us -> 200 us  [finish(): pl.pallas_call(functools.partial(finish_kernel, tuple(plan), tuple(head_s...]
    dot_general x29 -> x14, matrix products: 135 us -> 106 us  [weight_grad(): jnp.einsum('td,tc->dc', rows, grads, preferred_element_type=jnp.float32)]
    ppermute x27 -> x19, starting transfers between devices: 52.6 us -> 26.8 us  [trade(): lax.ppermute(value, axis, [(place, place ^ 1 << bit) for place in range(c...]
    pallas_call x7 -> x12, Pallas kernels: 32.6 us -> 57 us  [the longest x6 56.9 us: paired_rows(): pl.pallas_call(functools.partial(arrange_kernel, blocks), grid=(count //...]
    dot_general x16, matrix products: 105 us -> 88.2 us  [rows_back(): jnp.einsum('tc,dc->td', left, weight, preferred_element_type=jnp.float32)]
    select_n x9 -> x0, other arithmetic: 12.3 us -> none  [the longest x6 9.4 us: heads_gather(): jnp.where(upper, rows, other)]
    concatenate x1, local copies, waits for them, and re-layouts: 11.8 us -> 0.1 us  [body(): flat = jnp.concatenate(stacked, axis=0)]
  transfers between devices with their start and end apart: 60 -> 43, of which waited for: 16 -> 7; matrix products, arithmetic and copies ran while one was open for 36% -> 38% of each run, Pallas kernels for 12% -> 23%
where the time goes in v4:
time: 947 us; the launch traced here: 939 us
  Pallas kernels  417 us (44%)
  matrix products  319 us (34%)
  starting transfers between devices  60.4 us (6%)
  other arithmetic  53.7 us (6%)
  local copies, waits for them, and re-layouts  51.6 us (5%)
  waiting for transfers between devices  34.6 us (4%)
    pallas_call x1, Pallas kernels, finish(): pl.pallas_call(functools.partial(finish_kernel, tuple(plan), tuple(head_s...  200 us
    dot_general x14, matrix products, weight_grad(): jnp.einsum('td,tc->dc', rows, grads, preferred_element_type=jnp.float32)  106 us
    dot_general x16, matrix products, rows_back(): jnp.einsum('tc,dc->td', left, weight, preferred_element_type=jnp.float32)  88.2 us
    pallas_call x1, Pallas kernels, state_backward(): pl.pallas_call(functools.partial(state_back_kernel, taps, n, offset, len(...  84.5 us
    dot_general x7, matrix products, project(): return jnp.dot(rows, weight, preferred_element_type=jnp.float32)  62.4 us
    pallas_call x6, Pallas kernels, paired_rows(): pl.pallas_call(functools.partial(arrange_kernel, blocks), grid=(count //...  56.9 us
    pallas_call x1, Pallas kernels, state_forward(): pl.pallas_call(functools.partial(state_kernel, taps, n), grid=(heads // n...  53.8 us
    dot_general x4, matrix products, rows_product(): return jnp.dot(left, right, preferred_element_type=jnp.float32)  34.6 us
  transfers between devices with their start and end apart: 43, of which 7 were waited for; matrix products, arithmetic and copies ran while one was open for 38% of the time, Pallas kernels for 23%

profile of v4, /device:TPU:0, one launch (start us, length us, event | category | flops | bytes accessed | tf_op | source)
XLA Modules:
  0.0 939.2 jit_solution(4938240607102213737)
XLA Ops:
  52.9 53.8 %shard_map.410 = (f32[768,2048]{1,0:T(8,128)}, bf16[768,1024]{1,0:T(8,128)(2,1)}, bf16[8,128,128]{2,1,0:T(8,128)(2,1)}, bf16[8,128,256]{2,1,0:T(8,128)(2,1)}, bf...) custom-call(s32[2]{0:T(128)} %pad_add_fusion.spot, ...), custom_call_target="tpu_custom_call" | custom-call | tf_op jit(solution)/shard_map/pallas_call | solution.py:326
  122.0 11.2 %fusion.136.gate_ref = f32[768,2048]{1,0:T(8,128)} fusion(bf16[2048,2048]{1,0:T(8,128)(2,1)} %param.34, bf16[384,2048]{1,0:T(8,128)(2,1)} %copy-done.25, bf16[384,2048]{1,0:T(8,128)(2,1)S(1)} %copy-done.22), kind=kOutput, calls=%fused_computation.252 | convolution fusion | flops 6448742400 | bytes 17825792 | tf_op jit(solution)/shard_map/dot_general | solution.py:919
  140.6 9.9 %shard_map.413 = (bf16[768,2048]{1,0:T(8,128)(2,1)}, bf16[768,2048]{1,0:T(8,128)(2,1)}, bf16[8,128,256]{2,1,0:T(8,128)(2,1)}) custom-call(f32[768,2048]{1,0:T(8,128)} %shard_map.412.mixed_ref, bf16[768,1024]{1,0:T(8,128)(2,1)} %get-tuple-element.74.reach_ref, bf16[8,128,128]{2,1,0:T(8,128)(2,1)} %collective-permute-done.8.map_ref, ...), custom_call_target="tpu_custom_call" | custom-call | tf_op jit(solution)/shard_map/pallas_call | solution.py:413
  150.5 7.3 convolution_convert_fusion.8
  171.0 15.7 %fusion.132 = f32[768,2816]{1,0:T(8,128)} fusion(bf16[2816,2048]{1,0:T(8,128)(2,1)} %param.47, bf16[384,2048]{1,0:T(8,128)(2,1)S(1)} %get-tuple-element.183, bf16[384,2048]{1,0:T(8,128)(2,1)S(1)} %get-tuple-element.182), kind=kOutput, calls=%fused_computation.248 | convolution fusion | flops 8864661504 | bytes 23330816 | tf_op jit(solution)/shard_map/td,fd->tf/dot_general | solution.py:1335
  196.3 14.8 %fusion.134 = f32[768,2816]{1,0:T(8,128)} fusion(bf16[2048,2816]{1,0:T(8,128)(2,1)} %param.45, bf16[384,2048]{1,0:T(8,128)(2,1)S(1)} %get-tuple-element.185, bf16[384,2048]{1,0:T(8,128)(2,1)S(1)} %get-tuple-element.184), kind=kOutput, calls=%fused_computation.250 | convolution fusion | flops 8864661504 | bytes 23330816 | tf_op jit(solution)/shard_map/dot_general | solution.py:919
  211.1 21.9 %multiply_convert_fusion = (bf16[768,2816]{1,0:T(8,128)(2,1)}, bf16[768,2816]{1,0:T(8,128)(2,1)}, bf16[768,2816]{1,0:T(8,128)(2,1)}) fusion(f32[768,2816]{1,0:T(8,128)} %fusion.134, f32[768,2816]{1,0:T(8,128)} %fusion.132, bf16[2048,2816]{1,0:T(8,128)(2,1)} %param.46, bf16[384,2048]{1,0:T(8,128)(2,1)} %copy-done.33, bf16[384,2048]{1,0:T(8,128)(2,1)} %copy-done.32), kind=kOutput, calls=%fused_computation.4 | convolution fusion | flops 8899264512 | bytes 44957696 | tf_op jit(solution)/shard_map/dot_general | solution.py:919
  243.4 10.8 %convolution_convert_fusion.7 = bf16[384,2048]{1,0:T(8,128)(2,1)} fusion(bf16[2816,2048]{1,0:T(8,128)(2,1)} %param.47, bf16[768,2816]{1,0:T(8,128)(2,1)} %get-tuple-element.77.rest_0_, s32[]{:T(128)S(6)} %select_n.130), kind=kOutput, calls=%fused_computation.81 | convolution fusion | flops 4429971456 | bytes 15269892 | tf_op jit(solution)/shard_map/dot_general | solution.py:923
  254.2 9.8 %fusion.38 = f32[384,2048]{1,0:T(8,128)} fusion(bf16[2048,2816]{1,0:T(8,128)(2,1)} %param.46, bf16[768,2816]{1,0:T(8,128)(2,1)S(1)} %copy-done.13, s32[]{:T(128)S(6)} %select_n.130), kind=kOutput, calls=%fused_computation.84 | convolution fusion | flops 4429185024 | bytes 16842756 | tf_op jit(solution)/shard_map/tc,dc->td/dot_general | solution.py:927
  264.0 13.4 %add_convert_fusion.1 = bf16[384,2048]{1,0:T(8,128)(2,1)} fusion(f32[384,2048]{1,0:T(8,128)} %fusion.38, bf16[2048,2816]{1,0:T(8,128)(2,1)} %param.45, bf16[768,2816]{1,0:T(8,128)(2,1)S(1)} %copy-done.3, s32[]{:T(128)S(6)} %select_n.130), kind=kOutput, calls=%fused_computation.71 | convolution fusion | flops 4430757888 | bytes 18415620 | tf_op jit(solution)/shard_map/tc,dc->td/dot_general | solution.py:927
  281.2 9.6 %fusion.43 = f32[384,2048]{1,0:T(8,128)} fusion(bf16[2048,2816]{1,0:T(8,128)(2,1)} %param.45, bf16[768,2816]{1,0:T(8,128)(2,1)S(1)} %copy-done.3, s32[]{:T(128)S(6)} %select_n.129), kind=kOutput, calls=%fused_computation.89 | convolution fusion | flops 4429185024 | bytes 16842756 | tf_op jit(solution)/shard_map/tc,dc->td/dot_general | solution.py:927
  292.8 9.4 shard_map.418
  303.7 8.7 fusion.41
  318.8 9.7 %shard_map.416 = bf16[2,768,2048]{2,1,0:T(8,128)(2,1)} custom-call(s32[17]{0:T(128)} %pad_add_fusion.1.picks, bf16[768,2048]{1,0:T(8,128)(2,1)} %pad_maximum_fusion.5.full_ref, bf16[384,2048]{1,0:T(8,128)(2,1)} %collective-permute-done.14.refs_3_.mine_ref, bf16[384,2048]{1,0:T(8,128)(2,1)} %collective-permute-done.21.other_ref, ...), custom_call_target="tpu_custom_call" | custom-call | tf_op jit(solution)/shard_map/pallas_call | solution.py:973
  328.6 9.4 %shard_map.417 = bf16[2,768,2048]{2,1,0:T(8,128)(2,1)} custom-call(s32[17]{0:T(128)} %pad_add_fusion.2.picks, bf16[768,2048]{1,0:T(8,128)(2,1)} %pad_maximum_fusion.5.full_ref, bf16[384,2048]{1,0:T(8,128)(2,1)} %collective-permute-done.15.refs_4_.mine_ref, bf16[384,2048]{1,0:T(8,128)(2,1)} %collective-permute-done.24.other_ref, ...), custom_call_target="tpu_custom_call" | custom-call | tf_op jit(solution)/shard_map/pallas_call | solution.py:973
  340.0 10.3 %fusion.37 = bf16[1,384,2048]{2,1,0:T(8,128)(2,1)} fusion(f32[384,2048]{1,0:T(8,128)S(1)} %get-tuple-element.213, bf16[384,2048]{1,0:T(8,128)(2,1)} %collective-permute-done.16, bf16[2816,2048]{1,0:T(8,128)(2,1)} %param.47, bf16[768,2816]{1,0:T(8,128)(2,1)S(1)} %bitcast.127, s32[]{:T(128)S(6)} %select_n.129), kind=kOutput, calls=%fused_computation.83 | convolution fusion | flops 4432330752 | bytes 19988484 | tf_op jit(solution)/shard_map/dot_general | solution.py:923
  351.3 10.5 %collective-permute-done.28 = bf16[768,1408]{1,0:T(8,128)(2,1)} collective-permute-done((bf16[768,1408]{1,0:T(8,128)(2,1)}, bf16[768,1408]{1,0:T(8,128)(2,1)}, u32[]{:S(2)}, u32[]{:S(2)}) %collective-permute-start.28) | collective-permute-done | bytes 2162720 | tf_op jit(solution)/shard_map/ppermute | solution.py:940
  363.3 8.7 convolution_convert_fusion.4
  378.4 8.4 convolution_convert_fusion.5.rest_0_
  398.1 9.6 %shard_map.421 = bf16[2,768,2048]{2,1,0:T(8,128)(2,1)} custom-call(s32[17]{0:T(128)} %pad_add_fusion.2.picks, bf16[768,2048]{1,0:T(8,128)(2,1)} %pad_maximum_fusion.3.full_ref, bf16[384,2048]{1,0:T(8,128)(2,1)} %collective-permute-done.6.refs_4_.mine_ref, bf16[384,2048]{1,0:T(8,128)(2,1)} %collective-permute-done.33.other_ref, ...), custom_call_target="tpu_custom_call" | custom-call | tf_op jit(solution)/shard_map/pallas_call | solution.py:973
  407.9 9.5 %shard_map.420 = bf16[2,768,2048]{2,1,0:T(8,128)(2,1)} custom-call(s32[17]{0:T(128)} %pad_add_fusion.5.picks, bf16[768,2048]{1,0:T(8,128)(2,1)} %pad_maximum_fusion.3.full_ref, bf16[384,2048]{1,0:T(8,128)(2,1)} %collective-permute-done.5.refs_3_.mine_ref, bf16[384,2048]{1,0:T(8,128)(2,1)} %collective-permute-done.32.other_ref, ...), custom_call_target="tpu_custom_call" | custom-call | tf_op jit(solution)/shard_map/pallas_call | solution.py:973
  417.7 11.9 %fusion.131.d_gated_ref = f32[768,2048]{1,0:T(8,128)} fusion(bf16[2048,2048]{1,0:T(8,128)(2,1)} %param.43, bf16[384,2048]{1,0:T(8,128)(2,1)S(1)} %get-tuple-element.181, bf16[384,2048]{1,0:T(8,128)(2,1)S(1)} %get-tuple-element.180), kind=kOutput, calls=%fused_computation.247 | convolution fusion | flops 6448742400 | bytes 17825792 | tf_op jit(solution)/shard_map/td,cd->tc/dot_general | solution.py:1368
  429.5 11.7 %shard_map.415 = (bf16[768,2048]{1,0:T(8,128)(2,1)}, bf16[768,2048]{1,0:T(8,128)(2,1)}, bf16[8,128,256]{2,1,0:T(8,128)(2,1)}, f32[1,256]{1,0:T(1,128)}) custom-call(f32[768,2048]{1,0:T(8,128)} %fusion.131.d_gated_ref, bf16[768,2048]{1,0:T(8,128)(2,1)} %get-tuple-element.87.kept_ref, bf16[768,1024]{1,0:T(8,128)(2,1)} %get-tuple-element.74.reach_ref, ...), custom_call_target="tpu_custom_call" | custom-call | tf_op jit(solution)/shard_map/pallas_call | solution.py:474
  451.7 9.3 shard_map.419
  489.3 84.5 %shard_map.422 = (bf16[768,1024]{1,0:T(8,128)(2,1)}, bf16[768,1024]{1,0:T(8,128)(2,1)}, bf16[768,2048]{1,0:T(8,128)(2,1)}, f32[8,1024]{1,0:T(8,128)}, f32[8,1024...) custom-call(s32[2]{0:T(128)} %pad_add_fusion.spot, ...), custom_call_target="tpu_custom_call" | custom-call | tf_op jit(solution)/shard_map/pallas_call | solution.py:824
  585.8 7.4 fusion.31.refs_2_
  599.7 7.0 fusion.32.refs_1_
  647.4 9.9 %convolution_convert_fusion.2.refs_4_ = bf16[2048,1024]{1,0:T(8,128)(2,1)} fusion(bf16[1536,2048]{1,0:T(8,128)(2,1)S(1)} %bitcast.125, bf16[768,1024]{1,0:T(8,128)(2,1)} %collective-permute-done.40, bf16[768,1024]{1,0:T(8,128)(2,1)S(1)} %copy-done.49), kind=kOutput, calls=%fused_computation.20 | convolution fusion | flops 6450839552 | bytes 13631488 | tf_op jit(solution)/shard_map/td,tc->dc/dot_general | solution.py:931
  657.4 10.4 %convolution_convert_fusion.3.refs_3_ = bf16[2048,1024]{1,0:T(8,128)(2,1)} fusion(bf16[1536,2048]{1,0:T(8,128)(2,1)S(1)} %bitcast.121, bf16[768,1024]{1,0:T(8,128)(2,1)} %collective-permute-done.39, bf16[768,1024]{1,0:T(8,128)(2,1)S(1)} %copy-done.48), kind=kOutput, calls=%fused_computation.21 | convolution fusion | flops 6450839552 | bytes 13631488 | tf_op jit(solution)/shard_map/td,tc->dc/dot_general | solution.py:931
  684.3 11.5 %convolution_convert_fusion.1.refs_5_ = bf16[2048,1024]{1,0:T(8,128)(2,1)} fusion(bf16[1536,2048]{1,0:T(8,128)(2,1)} %get-tuple-element.103, bf16[768,1024]{1,0:T(8,128)(2,1)} %collective-permute-done.41, bf16[768,1024]{1,0:T(8,128)(2,1)} %get-tuple-element.174), kind=kOutput, calls=%fused_computation.19 | convolution fusion | flops 6450839552 | bytes 13631488 | tf_op jit(solution)/shard_map/td,tc->dc/dot_general | solution.py:931
  695.9 10.0 %convolution_convert_fusion.refs_6_ = bf16[2048,1024]{1,0:T(8,128)(2,1)} fusion(bf16[1536,2048]{1,0:T(8,128)(2,1)S(1)} %bitcast.117, bf16[768,1024]{1,0:T(8,128)(2,1)} %collective-permute-done.42, bf16[768,1024]{1,0:T(8,128)(2,1)S(1)} %copy-done.50), kind=kOutput, calls=%fused_computation.18 | convolution fusion | flops 6450839552 | bytes 13631488 | tf_op jit(solution)/shard_map/td,tc->dc/dot_general | solution.py:931
  705.8 200.3 %shard_map.426 = (bf16[2,128,1408]{2,1,0:T(8,128)(2,1)}, bf16[2,128,1408]{2,1,0:T(8,128)(2,1)}, bf16[2,128,1408]{2,1,0:T(8,128)(2,1)}, bf16[2,128,1024]{2,1,0:T(...) custom-call(bf16[512,1408]{1,0:T(8,128)(2,1)} %fusion.33.refs_0_, ...), custom_call_target="tpu_custom_call" | custom-call | tf_op jit(solution)/shard_map/pallas_call | solution.py:1186
  (472 shorter events, 290.6 us)
Async XLA Ops:
  6.7 100.1 %collective-permute-start.6 = (bf16[384,2048]{1,0:T(8,128)(2,1)}, bf16[384,2048]{1,0:T(8,128)(2,1)}, u32[]{:S(2)}, u32[]{:S(2)}) collective-permute-start(bf16[384,2048]{1,0:T(8,128)(2,1)} %fusion.9), channel_id=1, source_target_pairs={{0,4},{2,6},{4,0},{6,2},{1,5},{3,7},{5,1},{7,3},{8,12},{10,14},{12... | collective-permute-start | bytes 4718600 | tf_op jit(solution)/shard_map/ppermute | solution.py:940
  9.2 97.5 %collective-permute-start.5 = (bf16[384,2048]{1,0:T(8,128)(2,1)}, bf16[384,2048]{1,0:T(8,128)(2,1)}, u32[]{:S(2)}, u32[]{:S(2)}) collective-permute-start(bf16[384,2048]{1,0:T(8,128)(2,1)} %fusion.9), channel_id=1, source_target_pairs={{0,2},{2,0},{4,6},{6,4},{1,3},{3,1},{5,7},{7,5},{8,10},{10,8},{12,... | collective-permute-start | bytes 4718600 | tf_op jit(solution)/shard_map/ppermute | solution.py:940
  10.7 96.1 %collective-permute-start.4 = (bf16[384,2048]{1,0:T(8,128)(2,1)S(1)}, bf16[384,2048]{1,0:T(8,128)(2,1)}, u32[]{:S(2)}, u32[]{:S(2)}) collective-permute-start(bf16[384,2048]{1,0:T(8,128)(2,1)S(1)} %bitcast.130), channel_id=1, source_target_pairs={{0,8},{8,0},{16,24},{24,16},{1,9},{9,1},{17,25},{25,17},{2,10},{10... | collective-permute-start | bytes 4718600 | tf_op jit(solution)/shard_map/ppermute | solution.py:940
  51.6 108.1 %collective-permute-start.12 = (bf16[384,2048]{1,0:T(8,128)(2,1)S(1)}, bf16[384,2048]{1,0:T(8,128)(2,1)}, u32[]{:S(2)}, u32[]{:S(2)}) collective-permute-start(bf16[384,2048]{1,0:T(8,128)(2,1)S(1)} %bitcast.131), channel_id=1, source_target_pairs={{0,1},{1,0},{2,3},{3,2},{4,5},{5,4},{6,7},{7,6},{8,9},{9,8},{10,11... | collective-permute-start | bytes 4718600 | tf_op jit(solution)/shard_map/ppermute | solution.py:1240
  113.2 27.4 %collective-permute-start.10 = (bf16[8,128,256]{2,1,0:T(8,128)(2,1)}, bf16[8,128,256]{2,1,0:T(8,128)(2,1)}, u32[]{:S(2)}, u32[]{:S(2)}) collective-permute-start(bf16[8,128,256]{2,1,0:T(8,128)(2,1)} %get-tuple-element.75), channel_id=1, source_target_pairs={{0,4},{2,6},{1,5},{3,7},{8,12},{10,14},{9,13},{11,15},{16,20},{18,... | collective-permute-start | bytes 1572872 | tf_op jit(solution)/shard_map/ppermute | solution.py:907
  186.7 209.6 %collective-permute-start.33 = (bf16[384,2048]{1,0:T(8,128)(2,1)}, bf16[384,2048]{1,0:T(8,128)(2,1)}, u32[]{:S(2)}, u32[]{:S(2)}) collective-permute-start(bf16[384,2048]{1,0:T(8,128)(2,1)} %collective-permute-done.6.refs_4_.mine_ref), channel_id=1, source_target_pairs={{0,1},{1,0},{2,3},{3,2},{4,5},{5,4},{6,7},{7,6},{8,9},{9,8},{10,11... | collective-permute-start | bytes 4718600 | tf_op jit(solution)/shard_map/ppermute | solution.py:965
  186.8 105.5 %collective-permute-start.27 = (bf16[384,2048]{1,0:T(8,128)(2,1)}, bf16[384,2048]{1,0:T(8,128)(2,1)}, u32[]{:S(2)}, u32[]{:S(2)}) collective-permute-start(bf16[384,2048]{1,0:T(8,128)(2,1)} %collective-permute-done.4.refs_2_.mine_ref), channel_id=1, source_target_pairs={{0,1},{1,0},{2,3},{3,2},{4,5},{5,4},{6,7},{7,6},{8,9},{9,8},{10,11... | collective-permute-start | bytes 4718600 | tf_op jit(solution)/shard_map/ppermute | solution.py:965
  191.1 52.3 %collective-permute-start.15 = (bf16[384,2048]{1,0:T(8,128)(2,1)}, bf16[384,2048]{1,0:T(8,128)(2,1)}, u32[]{:S(2)}, u32[]{:S(2)}) collective-permute-start(bf16[384,2048]{1,0:T(8,128)(2,1)} %multiply_convert_fusion.2), channel_id=1, source_target_pairs={{0,4},{2,6},{4,0},{6,2},{1,5},{3,7},{5,1},{7,3},{8,12},{10,14},{12... | collective-permute-start | bytes 4718600 | tf_op jit(solution)/shard_map/ppermute | solution.py:940
  193.6 49.8 %collective-permute-start.14 = (bf16[384,2048]{1,0:T(8,128)(2,1)}, bf16[384,2048]{1,0:T(8,128)(2,1)}, u32[]{:S(2)}, u32[]{:S(2)}) collective-permute-start(bf16[384,2048]{1,0:T(8,128)(2,1)} %multiply_convert_fusion.2), channel_id=1, source_target_pairs={{0,2},{2,0},{4,6},{6,4},{1,3},{3,1},{5,7},{7,5},{8,10},{10,8},{12,... | collective-permute-start | bytes 4718600 | tf_op jit(solution)/shard_map/ppermute | solution.py:940
  254.2 83.8 %collective-permute-start.16 = (bf16[384,2048]{1,0:T(8,128)(2,1)}, bf16[384,2048]{1,0:T(8,128)(2,1)}, u32[]{:S(2)}, u32[]{:S(2)}) collective-permute-start(bf16[384,2048]{1,0:T(8,128)(2,1)} %convolution_convert_fusion.7), channel_id=1, source_target_pairs={{0,1},{1,0},{2,3},{3,2},{4,5},{5,4},{6,7},{7,6},{8,9},{9,8},{10,11... | collective-permute-start | bytes 4718600 | tf_op jit(solution)/shard_map/ppermute | solution.py:1259
  280.7 31.7 %collective-permute-start.17 = (bf16[384,2048]{1,0:T(8,128)(2,1)}, bf16[384,2048]{1,0:T(8,128)(2,1)}, u32[]{:S(2)}, u32[]{:S(2)}) collective-permute-start(bf16[384,2048]{1,0:T(8,128)(2,1)} %add_convert_fusion.1), channel_id=1, source_target_pairs={{0,1},{1,0},{2,3},{3,2},{4,5},{5,4},{6,7},{7,6},{8,9},{9,8},{10,11... | collective-permute-start | bytes 4718600 | tf_op jit(solution)/shard_map/ppermute | solution.py:1259
  292.3 36.2 %collective-permute-start.24 = (bf16[384,2048]{1,0:T(8,128)(2,1)}, bf16[384,2048]{1,0:T(8,128)(2,1)}, u32[]{:S(2)}, u32[]{:S(2)}) collective-permute-start(bf16[384,2048]{1,0:T(8,128)(2,1)} %collective-permute-done.15.refs_4_.mine_ref), channel_id=1, source_target_pairs={{0,1},{1,0},{2,3},{3,2},{4,5},{5,4},{6,7},{7,6},{8,9},{9,8},{10,11... | collective-permute-start | bytes 4718600 | tf_op jit(solution)/shard_map/ppermute | solution.py:965
  312.4 49.4 %collective-permute-start.28 = (bf16[768,1408]{1,0:T(8,128)(2,1)}, bf16[768,1408]{1,0:T(8,128)(2,1)}, u32[]{:S(2)}, u32[]{:S(2)}) collective-permute-start(bf16[768,1408]{1,0:T(8,128)(2,1)} %constant_dynamic-slice_fusion.10.refs_7_), channel_id=1, source_target_pairs={{0,8},{8,0},{16,24},{24,16},{1,9},{9,1},{17,25},{25,17},{2,10},{10... | collective-permute-start | bytes 6488072 | tf_op jit(solution)/shard_map/ppermute | solution.py:940
  318.7 89.0 %collective-permute-start.32 = (bf16[384,2048]{1,0:T(8,128)(2,1)}, bf16[384,2048]{1,0:T(8,128)(2,1)}, u32[]{:S(2)}, u32[]{:S(2)}) collective-permute-start(bf16[384,2048]{1,0:T(8,128)(2,1)} %collective-permute-done.5.refs_3_.mine_ref), channel_id=1, source_target_pairs={{0,1},{1,0},{2,3},{3,2},{4,5},{5,4},{6,7},{7,6},{8,9},{9,8},{10,11... | collective-permute-start | bytes 4718600 | tf_op jit(solution)/shard_map/ppermute | solution.py:965
  328.5 49.8 %collective-permute-start.25 = (bf16[768,1408]{1,0:T(8,128)(2,1)}, bf16[768,1408]{1,0:T(8,128)(2,1)}, u32[]{:S(2)}, u32[]{:S(2)}) collective-permute-start(bf16[768,1408]{1,0:T(8,128)(2,1)} %constant_dynamic-slice_fusion.11.refs_6_), channel_id=1, source_target_pairs={{0,4},{2,6},{4,0},{6,2},{1,5},{3,7},{5,1},{7,3},{8,12},{10,14},{12... | collective-permute-start | bytes 6488072 | tf_op jit(solution)/shard_map/ppermute | solution.py:940
  338.0 49.9 %collective-permute-start.22 = (bf16[768,1408]{1,0:T(8,128)(2,1)}, bf16[768,1408]{1,0:T(8,128)(2,1)S(1)}, u32[]{:S(2)}, u32[]{:S(2)}) collective-permute-start(bf16[768,1408]{1,0:T(8,128)(2,1)} %constant_dynamic-slice_fusion.12.refs_5_), channel_id=1, source_target_pairs={{0,2},{2,0},{4,6},{6,4},{1,3},{3,1},{5,7},{7,5},{8,10},{10,8},{12,... | collective-permute-start | bytes 6488072 | tf_op jit(solution)/shard_map/ppermute | solution.py:940
  361.8 55.6 %collective-permute-start.30 = (bf16[384,2048]{1,0:T(8,128)(2,1)S(1)}, bf16[384,2048]{1,0:T(8,128)(2,1)}, u32[]{:S(2)}, u32[]{:S(2)}) collective-permute-start(bf16[384,2048]{1,0:T(8,128)(2,1)S(1)} %fusion.133), channel_id=1, source_target_pairs={{0,8},{8,0},{16,24},{24,16},{1,9},{9,1},{17,25},{25,17},{2,10},{10... | collective-permute-start | bytes 4718600 | tf_op jit(solution)/shard_map/ppermute | solution.py:940
  378.3 39.1 %collective-permute-start.18 = (bf16[384,2048]{1,0:T(8,128)(2,1)S(1)}, bf16[384,2048]{1,0:T(8,128)(2,1)S(1)}, u32[]{:S(2)}, u32[]{:S(2)}) collective-permute-start(bf16[384,2048]{1,0:T(8,128)(2,1)S(1)} %fusion.133), channel_id=1, source_target_pairs={{0,1},{1,0},{2,3},{3,2},{4,5},{5,4},{6,7},{7,6},{8,9},{9,8},{10,11... | collective-permute-start | bytes 4718600 | tf_op jit(solution)/shard_map/ppermute | solution.py:1240
  387.9 73.1 %collective-permute-start.29 = (bf16[1024,1408]{1,0:T(8,128)(2,1)}, bf16[1024,1408]{1,0:T(8,128)(2,1)}, u32[]{:S(2)}, u32[]{:S(2)}) collective-permute-start(bf16[1024,1408]{1,0:T(8,128)(2,1)} %convolution_convert_fusion.4), channel_id=1, source_target_pairs={{0,4},{2,6},{4,0},{6,2},{1,5},{3,7},{5,1},{7,3},{8,12},{10,14},{12... | collective-permute-start | bytes 8650760 | tf_op jit(solution)/shard_map/ppermute | solution.py:940
  396.3 83.1 %collective-permute-start.26 = (bf16[1024,1408]{1,0:T(8,128)(2,1)}, bf16[1024,1408]{1,0:T(8,128)(2,1)}, u32[]{:S(2)}, u32[]{:S(2)}) collective-permute-start(bf16[1024,1408]{1,0:T(8,128)(2,1)} %convolution_convert_fusion.5.rest_0_), channel_id=1, source_target_pairs={{0,2},{2,0},{4,6},{6,4},{1,3},{3,1},{5,7},{7,5},{8,10},{10,8},{12,... | collective-permute-start | bytes 8650760 | tf_op jit(solution)/shard_map/ppermute | solution.py:940
  407.6 65.7 %collective-permute-start.23 = (bf16[1024,1408]{1,0:T(8,128)(2,1)}, bf16[1024,1408]{1,0:T(8,128)(2,1)}, u32[]{:S(2)}, u32[]{:S(2)}) collective-permute-start(bf16[1024,1408]{1,0:T(8,128)(2,1)} %convolution_convert_fusion.6), channel_id=1, source_target_pairs={{0,8},{8,0},{16,24},{24,16},{1,9},{9,1},{17,25},{25,17},{2,10},{10... | collective-permute-start | bytes 8650760 | tf_op jit(solution)/shard_map/ppermute | solution.py:940
  417.4 32.9 %collective-permute-start.31 = (bf16[384,2048]{1,0:T(8,128)(2,1)}, bf16[384,2048]{1,0:T(8,128)(2,1)}, u32[]{:S(2)}, u32[]{:S(2)}) collective-permute-start(bf16[384,2048]{1,0:T(8,128)(2,1)} %collective-permute-done.30.mine_ref), channel_id=1, source_target_pairs={{0,1},{1,0},{2,3},{3,2},{4,5},{5,4},{6,7},{7,6},{8,9},{9,8},{10,11... | collective-permute-start | bytes 4718600 | tf_op jit(solution)/shard_map/ppermute | solution.py:965
  441.2 47.1 %collective-permute-start.20 = (bf16[8,128,256]{2,1,0:T(8,128)(2,1)}, bf16[8,128,256]{2,1,0:T(8,128)(2,1)S(1)}, u32[]{:S(2)}, u32[]{:S(2)}) collective-permute-start(bf16[8,128,256]{2,1,0:T(8,128)(2,1)} %get-tuple-element.89), channel_id=1, source_target_pairs={{4,0},{6,2},{5,1},{7,3},{12,8},{14,10},{13,9},{15,11},{20,16},{22,... | collective-permute-start | bytes 1572872 | tf_op jit(solution)/shard_map/ppermute | solution.py:907
  450.3 38.3 %collective-permute-start.19 = (bf16[8,128,256]{2,1,0:T(8,128)(2,1)S(1)}, bf16[8,128,256]{2,1,0:T(8,128)(2,1)S(1)}, u32[]{:S(2)}, u32[]{:S(2)}) collective-permute-start(bf16[8,128,256]{2,1,0:T(8,128)(2,1)S(1)} %copy-done.111), channel_id=1, source_target_pairs={{2,0},{4,2},{6,4},{3,1},{5,3},{7,5},{10,8},{12,10},{14,12},{11,9},... | collective-permute-start | bytes 1572872 | tf_op jit(solution)/shard_map/ppermute | solution.py:907
  461.0 186.3 %collective-permute-start.40 = (bf16[768,1024]{1,0:T(8,128)(2,1)}, bf16[768,1024]{1,0:T(8,128)(2,1)}, u32[]{:S(2)}, u32[]{:S(2)}) collective-permute-start(bf16[768,1024]{1,0:T(8,128)(2,1)} %get-tuple-element.177), channel_id=1, source_target_pairs={{0,8},{8,0},{16,24},{24,16},{1,9},{9,1},{17,25},{25,17},{2,10},{10... | collective-permute-start | bytes 4718600 | tf_op jit(solution)/shard_map/ppermute | solution.py:940
  473.4 184.0 %collective-permute-start.39 = (bf16[768,1024]{1,0:T(8,128)(2,1)}, bf16[768,1024]{1,0:T(8,128)(2,1)}, u32[]{:S(2)}, u32[]{:S(2)}) collective-permute-start(bf16[768,1024]{1,0:T(8,128)(2,1)} %get-tuple-element.179), channel_id=1, source_target_pairs={{0,2},{2,0},{4,6},{6,4},{1,3},{3,1},{5,7},{7,5},{8,10},{10,8},{12,... | collective-permute-start | bytes 4718600 | tf_op jit(solution)/shard_map/ppermute | solution.py:940
  479.4 104.7 %collective-permute-start.36 = (bf16[512,1408]{1,0:T(8,128)(2,1)}, bf16[512,1408]{1,0:T(8,128)(2,1)}, u32[]{:S(2)}, u32[]{:S(2)}) collective-permute-start(bf16[512,1408]{1,0:T(8,128)(2,1)} %fusion.36.rest_2_), channel_id=1, source_target_pairs={{0,16},{8,24},{16,0},{24,8},{1,17},{9,25},{17,1},{25,9},{2,18},{10... | collective-permute-start | bytes 4325384 | tf_op jit(solution)/shard_map/ppermute | solution.py:940
  488.3 95.8 %collective-permute-start.34 = (bf16[512,1408]{1,0:T(8,128)(2,1)}, bf16[512,1408]{1,0:T(8,128)(2,1)}, u32[]{:S(2)}, u32[]{:S(2)}) collective-permute-start(bf16[512,1408]{1,0:T(8,128)(2,1)} %fusion.34.rest_0_), channel_id=1, source_target_pairs={{0,4},{2,6},{4,0},{6,2},{1,5},{3,7},{5,1},{7,3},{8,12},{10,14},{12... | collective-permute-start | bytes 4325384 | tf_op jit(solution)/shard_map/ppermute | solution.py:940
  488.5 95.5 %collective-permute-start.35 = (bf16[512,1408]{1,0:T(8,128)(2,1)}, bf16[512,1408]{1,0:T(8,128)(2,1)}, u32[]{:S(2)}, u32[]{:S(2)}) collective-permute-start(bf16[512,1408]{1,0:T(8,128)(2,1)} %fusion.35.rest_1_), channel_id=1, source_target_pairs={{0,8},{8,0},{16,24},{24,16},{1,9},{9,1},{17,25},{25,17},{2,10},{10... | collective-permute-start | bytes 4325384 | tf_op jit(solution)/shard_map/ppermute | solution.py:940
  609.8 86.0 %collective-permute-start.42 = (bf16[768,1024]{1,0:T(8,128)(2,1)}, bf16[768,1024]{1,0:T(8,128)(2,1)}, u32[]{:S(2)}, u32[]{:S(2)}) collective-permute-start(bf16[768,1024]{1,0:T(8,128)(2,1)} %get-tuple-element.173.refs_5_), channel_id=1, source_target_pairs={{0,4},{2,6},{4,0},{6,2},{1,5},{3,7},{5,1},{7,3},{8,12},{10,14},{12... | collective-permute-start | bytes 4718600 | tf_op jit(solution)/shard_map/ppermute | solution.py:940
  620.7 63.6 %collective-permute-start.41 = (bf16[768,1024]{1,0:T(8,128)(2,1)}, bf16[768,1024]{1,0:T(8,128)(2,1)}, u32[]{:S(2)}, u32[]{:S(2)}) collective-permute-start(bf16[768,1024]{1,0:T(8,128)(2,1)} %get-tuple-element.175.refs_4_), channel_id=1, source_target_pairs={{0,2},{2,0},{4,6},{6,4},{1,3},{3,1},{5,7},{7,5},{8,10},{10,8},{12,... | collective-permute-start | bytes 4718600 | tf_op jit(solution)/shard_map/ppermute | solution.py:940
  641.3 37.1 %collective-permute-start.38 = (bf16[384,2048]{1,0:T(8,128)(2,1)}, bf16[384,2048]{1,0:T(8,128)(2,1)}, u32[]{:S(2)}, u32[]{:S(2)}) collective-permute-start(bf16[384,2048]{1,0:T(8,128)(2,1)} %add_convert_fusion), channel_id=1, source_target_pairs={{0,1},{1,0},{2,3},{3,2},{4,5},{5,4},{6,7},{7,6},{8,9},{9,8},{10,11... | collective-permute-start | bytes 4718600 | tf_op jit(solution)/shard_map/ppermute | solution.py:1259
  (147 other events, 2069.9 us)

commit v5 on v4

--- a/solution.py
+++ b/solution.py
@@ -948,7 +948,26 @@
         source = pl.ds(pl.multiple_of(picks[place] * width, width), width)
         target = slice(place * width, (place + 1) * width)
         out_ref[0, :, target] = full_ref[:, source]
-        out_ref[1, :, target] = jnp.where(mine, mine_ref[:, source], other_ref[:, source])
+
+    def fill(part_ref):
+        for place in range(16):
+            source = pl.ds(pl.multiple_of(picks[place] * width, width), width)
+            out_ref[1, :, place * width : (place + 1) * width] = part_ref[:, source]
+
+    @pl.when(mine)
+    def _():
+        fill(mine_ref)
+
+    @pl.when(jnp.logical_not(mine))
+    def _():
+        fill(other_ref)
+
+
+def with_other(got):
+    if lax.axis_size("heads") == 2:
+        return got, lax.ppermute(got, "heads", [(0, 1), (1, 0)])
+    whole = heads_gather(got)
+    return whole, whole
 
 
 def paired_rows(full, got, order, *after):
@@ -961,12 +980,9 @@
     picks = jnp.concatenate(
         [own ^ jnp.array(masks, jnp.int32), lax.axis_index("heads").astype(jnp.int32)[None]]
     )
-    if lax.axis_size("heads") == 2:
-        other = lax.ppermute(got, "heads", [(0, 1), (1, 0)])
-    else:
-        got = other = heads_gather(got)
+    got, other = got
     count, width = full.shape
-    size = 96
+    size = 192 if got.shape[0] % 192 == 0 else 96
     blocks = got.shape[0] // size
     piece = pl.BlockSpec((size, width), lambda i: (i, 0))
     part = pl.BlockSpec((size, width), lambda i: (lax.rem(i, blocks), 0))
@@ -1307,19 +1323,27 @@
     decay_proj, beta_proj = narrow[:, :heads], narrow[:, heads:]
     seq_index = lax.axis_index("seq")
     spot = jnp.stack([lengths[0, 0], seq_index * span]).astype(jnp.int32)
-    rims = shifted((q_proj[span - RIM :], k_proj[span - RIM :], v_proj[span - RIM :]), "seq", 1)
+    ends = [part[span - RIM :] for part in (q_proj, k_proj, v_proj)]
+    rims = jnp.split(
+        shifted(jnp.concatenate(ends, axis=1), "seq", 1), (heads * DK, 2 * heads * DK), axis=1
+    )
     convs = (conv_q, conv_k, conv_v)
     log_row, bias_row, gain_row = decay_log[None], decay_bias[None], out_gain[None]
     mixed_local, reach, span_map, span_add, *saved, cum, rate = state_forward(
         q_proj, k_proj, v_proj, rims, convs, decay_proj, beta_proj, log_row, bias_row, spot, per_step
     )
     span_map, span_add = ordered((span_map, span_add), cotangent_got, *normed_got.values())
+    normed_got = {order: with_other(got) for order, got in normed_got.items()}
+    cotangent_got = with_other(cotangent_got)
     near_map, near_add = shifted((span_map, span_add), "seq", 1)
     far_add = shifted(span_add, "seq", 2)
     next_map = shifted(span_map, "seq", -1)
     (mixed_local,) = ordered((mixed_local,), next_map)
     gated_low, mixed_low, start_state = gate_forward(
         mixed_local, reach, near_map, near_add, far_add, gate_proj, gain_row, per_step
+    )
+    (gated_low,) = ordered(
+        (gated_low,), cotangent_got[1], *(got[1] for got in normed_got.values())
     )
     mixer = heads_sum(
         lambda pick: rows_product(pick(gated_low), out_weight), span, jnp.bfloat16
@@ -1341,6 +1365,7 @@
     ffn_traded = [trade(part, order[0]) for part, order in zip(theirs, FFN_ORDERS)]
     ffn_low = ordered(ffn_low, *ffn_got.values(), *theirs)
     d_gate_low, d_up_low, act_low = ffn_low
+    ffn_got = {order: with_other(got) for order, got in ffn_got.items()}
     gate_halves, up_halves, down_halves = (
         join_halves(part, got, order)
         for part, got, order in zip(ffn_low, ffn_traded, FFN_ORDERS)
@@ -1364,7 +1389,7 @@
     d_mid = out_cotangent[0].astype(jnp.float32) + d_mid_norm
     d_mid_low = low(d_mid)
     d_mid_all = heads_gather(d_mid_low)
-    d_mid_got = trade(d_mid_low, ORDERS[2][0])
+    d_mid_got = with_other(trade(d_mid_low, ORDERS[2][0]))
     d_gated = jnp.einsum("td,cd->tc", d_mid_all, out_weight, preferred_element_type=jnp.float32)
     d_mixed, d_gate_low_mix, d_start, d_out_gain = gate_backward(
         d_gated, mixed_low, reach, gate_proj, gain_row, per_step

time: 947 us -> 923 us (0.975)
  waiting for transfers between devices: 34.6 us -> 19.2 us
  Pallas kernels: 417 us -> 404 us
    ppermute x19, waiting for transfers between devices: 22.4 us -> 0.05 us  [trade(): lax.ppermute(value, axis, [(place, place ^ 1 << bit) for place in range(c...]
    pallas_call x6, Pallas kernels: 56.9 us -> 44 us  [paired_rows(): pl.pallas_call(functools.partial(arrange_kernel, blocks), grid=(count //...]
    ppermute x10 -> x8, starting transfers between devices: 30.9 us -> 24.9 us  [shifted(): lax.ppermute(value, axis, [(source, source + steps) for source in range(l...]
  transfers between devices with their start and end apart: 43 -> 41, of which waited for: 7 -> 4; matrix products, arithmetic and copies ran while one was open for 38% -> 40% of each run, Pallas kernels for 23% -> 22%
where the time goes in v5:
time: 923 us; the launch traced here: 913 us
  Pallas kernels  404 us (44%)
  matrix products  327 us (35%)
  starting transfers between devices  55.7 us (6%)
  local copies, waits for them, and re-layouts  52.3 us (6%)
  other arithmetic  52 us (6%)
  waiting for transfers between devices  19.2 us (2%)
    pallas_call x1, Pallas kernels, finish(): pl.pallas_call(functools.partial(finish_kernel, tuple(plan), tuple(head_s...  200 us
    dot_general x14, matrix products, weight_grad(): jnp.einsum('td,tc->dc', rows, grads, preferred_element_type=jnp.float32)  109 us
    dot_general x16, matrix products, rows_back(): jnp.einsum('tc,dc->td', left, weight, preferred_element_type=jnp.float32)  92.4 us
    pallas_call x1, Pallas kernels, state_backward(): pl.pallas_call(functools.partial(state_back_kernel, taps, n, offset, len(...  84.1 us
    dot_general x7, matrix products, project(): return jnp.dot(rows, weight, preferred_element_type=jnp.float32)  62.4 us
    pallas_call x1, Pallas kernels, state_forward(): pl.pallas_call(functools.partial(state_kernel, taps, n), grid=(heads // n...  53.9 us
    pallas_call x6, Pallas kernels, paired_rows(): pl.pallas_call(functools.partial(arrange_kernel, blocks), grid=(count //...  44 us
    dot_general x4, matrix products, rows_product(): return jnp.dot(left, right, preferred_element_type=jnp.float32)  36 us
  transfers between devices with their start and end apart: 41, of which 4 were waited for; matrix products, arithmetic and copies ran while one was open for 40% of the time, Pallas kernels for 22%

profile of v5, /device:TPU:0, one launch (start us, length us, event | category | flops | bytes accessed | tf_op | source)
XLA Modules:
  0.0 913.0 jit_solution(15806130475805238105)
XLA Ops:
  35.6 12.1 %collective-permute-done.1 = f32[8,4096]{1,0:T(8,128)S(1)} collective-permute-done((f32[8,4096]{1,0:T(8,128)S(1)}, f32[8,4096]{1,0:T(8,128)S(1)}, u32[]{:S(2)}, u32[]{:S(2)}) %collective-permute-start.1) | collective-permute-done | bytes 131104 | tf_op jit(solution)/shard_map/ppermute | solution.py:907
  49.0 53.9 %shard_map.410 = (f32[768,2048]{1,0:T(8,128)}, bf16[768,1024]{1,0:T(8,128)(2,1)}, bf16[8,128,128]{2,1,0:T(8,128)(2,1)}, bf16[8,128,256]{2,1,0:T(8,128)(2,1)}, bf...) custom-call(s32[2]{0:T(128)} %pad_add_fusion.spot, ...), custom_call_target="tpu_custom_call" | custom-call | tf_op jit(solution)/shard_map/pallas_call | solution.py:326
  112.9 7.7 collective-permute-start.8
  124.0 11.2 %fusion.136.gate_ref = f32[768,2048]{1,0:T(8,128)} fusion(bf16[2048,2048]{1,0:T(8,128)(2,1)} %param.34, bf16[384,2048]{1,0:T(8,128)(2,1)} %copy-done.25, bf16[384,2048]{1,0:T(8,128)(2,1)S(1)} %copy-done.22), kind=kOutput, calls=%fused_computation.253 | convolution fusion | flops 6448742400 | bytes 17825792 | tf_op jit(solution)/shard_map/dot_general | solution.py:919
  139.5 9.9 %shard_map.413 = (bf16[768,2048]{1,0:T(8,128)(2,1)}, bf16[768,2048]{1,0:T(8,128)(2,1)}, bf16[8,128,256]{2,1,0:T(8,128)(2,1)}) custom-call(f32[768,2048]{1,0:T(8,128)} %shard_map.412.mixed_ref, bf16[768,1024]{1,0:T(8,128)(2,1)} %get-tuple-element.74.reach_ref, bf16[8,128,128]{2,1,0:T(8,128)(2,1)} %collective-permute-done.6.map_ref, ...), custom_call_target="tpu_custom_call" | custom-call | tf_op jit(solution)/shard_map/pallas_call | solution.py:413
  149.6 7.3 convolution_convert_fusion.8
  169.6 15.4 %fusion.132 = f32[768,2816]{1,0:T(8,128)} fusion(bf16[2816,2048]{1,0:T(8,128)(2,1)} %param.47, bf16[384,2048]{1,0:T(8,128)(2,1)S(1)} %get-tuple-element.183, bf16[384,2048]{1,0:T(8,128)(2,1)S(1)} %get-tuple-element.182), kind=kOutput, calls=%fused_computation.249 | convolution fusion | flops 8864661504 | bytes 23330816 | tf_op jit(solution)/shard_map/td,fd->tf/dot_general | solution.py:1359
  193.9 14.8 %fusion.134 = f32[768,2816]{1,0:T(8,128)} fusion(bf16[2048,2816]{1,0:T(8,128)(2,1)} %param.45, bf16[384,2048]{1,0:T(8,128)(2,1)S(1)} %get-tuple-element.185, bf16[384,2048]{1,0:T(8,128)(2,1)S(1)} %get-tuple-element.184), kind=kOutput, calls=%fused_computation.251 | convolution fusion | flops 8864661504 | bytes 23330816 | tf_op jit(solution)/shard_map/dot_general | solution.py:919
  208.7 21.9 %multiply_convert_fusion = (bf16[768,2816]{1,0:T(8,128)(2,1)}, bf16[768,2816]{1,0:T(8,128)(2,1)}, bf16[768,2816]{1,0:T(8,128)(2,1)}) fusion(f32[768,2816]{1,0:T(8,128)} %fusion.134, f32[768,2816]{1,0:T(8,128)} %fusion.132, bf16[2048,2816]{1,0:T(8,128)(2,1)} %param.46, bf16[384,2048]{1,0:T(8,128)(2,1)} %copy-done.34, bf16[384,2048]{1,0:T(8,128)(2,1)} %copy-done.32), kind=kOutput, calls=%fused_computation.4 | convolution fusion | flops 8899264512 | bytes 44957696 | tf_op jit(solution)/shard_map/dot_general | solution.py:919
  242.6 10.8 %convolution_convert_fusion.7 = bf16[384,2048]{1,0:T(8,128)(2,1)} fusion(bf16[2816,2048]{1,0:T(8,128)(2,1)} %param.47, bf16[768,2816]{1,0:T(8,128)(2,1)} %get-tuple-element.77.rest_0_, s32[]{:T(128)S(6)} %select_n.130), kind=kOutput, calls=%fused_computation.81 | convolution fusion | flops 4429971456 | bytes 15269892 | tf_op jit(solution)/shard_map/dot_general | solution.py:923
  256.5 9.9 %fusion.38 = f32[384,2048]{1,0:T(8,128)} fusion(bf16[2048,2816]{1,0:T(8,128)(2,1)} %param.46, bf16[768,2816]{1,0:T(8,128)(2,1)S(1)} %copy-done.14, s32[]{:T(128)S(6)} %select_n.130), kind=kOutput, calls=%fused_computation.84 | convolution fusion | flops 4429185024 | bytes 16842756 | tf_op jit(solution)/shard_map/tc,dc->td/dot_general | solution.py:927
  266.4 10.0 %fusion.43 = f32[384,2048]{1,0:T(8,128)} fusion(bf16[2048,2816]{1,0:T(8,128)(2,1)} %param.45, bf16[768,2816]{1,0:T(8,128)(2,1)S(1)} %bitcast.115, s32[]{:T(128)S(6)} %select_n.129), kind=kOutput, calls=%fused_computation.89 | convolution fusion | flops 4429185024 | bytes 16842756 | tf_op jit(solution)/shard_map/tc,dc->td/dot_general | solution.py:927
  276.4 13.4 %add_convert_fusion.1 = bf16[384,2048]{1,0:T(8,128)(2,1)} fusion(f32[384,2048]{1,0:T(8,128)} %fusion.38, bf16[2048,2816]{1,0:T(8,128)(2,1)} %param.45, bf16[768,2816]{1,0:T(8,128)(2,1)S(1)} %bitcast.115, s32[]{:T(128)S(6)} %select_n.130), kind=kOutput, calls=%fused_computation.71 | convolution fusion | flops 4430757888 | bytes 18415620 | tf_op jit(solution)/shard_map/tc,dc->td/dot_general | solution.py:927
  292.9 7.3 shard_map.419
  301.7 12.1 %fusion.41 = f32[384,2048]{1,0:T(8,128)} fusion(bf16[2048,2816]{1,0:T(8,128)(2,1)} %param.46, bf16[768,2816]{1,0:T(8,128)(2,1)} %get-tuple-element.79, s32[]{:T(128)S(6)} %select_n.129), kind=kOutput, calls=%fused_computation.87 | convolution fusion | flops 4429185024 | bytes 16842756 | tf_op jit(solution)/shard_map/tc,dc->td/dot_general | solution.py:927
  318.5 11.6 %fusion.37 = bf16[1,384,2048]{2,1,0:T(8,128)(2,1)} fusion(f32[384,2048]{1,0:T(8,128)S(1)} %get-tuple-element.215, bf16[384,2048]{1,0:T(8,128)(2,1)} %collective-permute-done.17, bf16[2816,2048]{1,0:T(8,128)(2,1)} %param.47, bf16[768,2816]{1,0:T(8,128)(2,1)S(1)} %bitcast.129, s32[]{:T(128)S(6)} %select_n.129), kind=kOutput, calls=%fused_computation.83 | convolution fusion | flops 4432330752 | bytes 19988484 | tf_op jit(solution)/shard_map/dot_general | solution.py:923
  333.8 7.5 shard_map.417
  341.5 7.4 shard_map.418
  348.9 9.0 convolution_convert_fusion.4
  359.8 8.3 convolution_convert_fusion.6
  369.8 8.2 convolution_convert_fusion.5.rest_0_
  377.9 7.3 shard_map.422
  385.2 7.4 shard_map.421
  394.3 11.9 %fusion.131.d_gated_ref = f32[768,2048]{1,0:T(8,128)} fusion(bf16[2048,2048]{1,0:T(8,128)(2,1)} %param.43, bf16[384,2048]{1,0:T(8,128)(2,1)S(1)} %get-tuple-element.181, bf16[384,2048]{1,0:T(8,128)(2,1)S(1)} %get-tuple-element.180), kind=kOutput, calls=%fused_computation.248 | convolution fusion | flops 6448742400 | bytes 17825792 | tf_op jit(solution)/shard_map/td,cd->tc/dot_general | solution.py:1393
  406.2 11.6 %shard_map.416 = (bf16[768,2048]{1,0:T(8,128)(2,1)}, bf16[768,2048]{1,0:T(8,128)(2,1)}, bf16[8,128,256]{2,1,0:T(8,128)(2,1)}, f32[1,256]{1,0:T(1,128)}) custom-call(f32[768,2048]{1,0:T(8,128)} %fusion.131.d_gated_ref, bf16[768,2048]{1,0:T(8,128)(2,1)} %get-tuple-element.87.kept_ref, bf16[768,1024]{1,0:T(8,128)(2,1)} %get-tuple-element.74.reach_ref, ...), custom_call_target="tpu_custom_call" | custom-call | tf_op jit(solution)/shard_map/pallas_call | solution.py:474
  463.6 84.1 %shard_map.423 = (bf16[768,1024]{1,0:T(8,128)(2,1)}, bf16[768,1024]{1,0:T(8,128)(2,1)}, bf16[768,2048]{1,0:T(8,128)(2,1)}, f32[8,1024]{1,0:T(8,128)}, f32[8,1024...) custom-call(s32[2]{0:T(128)} %pad_add_fusion.spot, ...), custom_call_target="tpu_custom_call" | custom-call | tf_op jit(solution)/shard_map/pallas_call | solution.py:824
  559.7 7.4 fusion.31.refs_2_
  621.2 9.9 %convolution_convert_fusion.2.refs_4_ = bf16[2048,1024]{1,0:T(8,128)(2,1)} fusion(bf16[1536,2048]{1,0:T(8,128)(2,1)S(1)} %bitcast.127, bf16[768,1024]{1,0:T(8,128)(2,1)} %collective-permute-done.38, bf16[768,1024]{1,0:T(8,128)(2,1)S(1)} %copy-done.51), kind=kOutput, calls=%fused_computation.20 | convolution fusion | flops 6450839552 | bytes 13631488 | tf_op jit(solution)/shard_map/td,tc->dc/dot_general | solution.py:931
  631.2 10.1 %convolution_convert_fusion.3.refs_3_ = bf16[2048,1024]{1,0:T(8,128)(2,1)} fusion(bf16[1536,2048]{1,0:T(8,128)(2,1)S(1)} %bitcast.123, bf16[768,1024]{1,0:T(8,128)(2,1)} %collective-permute-done.37, bf16[768,1024]{1,0:T(8,128)(2,1)S(1)} %copy-done.50), kind=kOutput, calls=%fused_computation.21 | convolution fusion | flops 6450839552 | bytes 13631488 | tf_op jit(solution)/shard_map/td,tc->dc/dot_general | solution.py:931
  657.9 11.6 %convolution_convert_fusion.1.refs_5_ = bf16[2048,1024]{1,0:T(8,128)(2,1)} fusion(bf16[1536,2048]{1,0:T(8,128)(2,1)} %get-tuple-element.103, bf16[768,1024]{1,0:T(8,128)(2,1)} %collective-permute-done.39, bf16[768,1024]{1,0:T(8,128)(2,1)} %get-tuple-element.174), kind=kOutput, calls=%fused_computation.19 | convolution fusion | flops 6450839552 | bytes 13631488 | tf_op jit(solution)/shard_map/td,tc->dc/dot_general | solution.py:931
  669.5 10.0 %convolution_convert_fusion.refs_6_ = bf16[2048,1024]{1,0:T(8,128)(2,1)} fusion(bf16[1536,2048]{1,0:T(8,128)(2,1)S(1)} %bitcast.119, bf16[768,1024]{1,0:T(8,128)(2,1)} %collective-permute-done.40, bf16[768,1024]{1,0:T(8,128)(2,1)S(1)} %copy-done.52), kind=kOutput, calls=%fused_computation.18 | convolution fusion | flops 6450839552 | bytes 13631488 | tf_op jit(solution)/shard_map/td,tc->dc/dot_general | solution.py:931
  679.5 200.3 %shard_map.427 = (bf16[2,128,1408]{2,1,0:T(8,128)(2,1)}, bf16[2,128,1408]{2,1,0:T(8,128)(2,1)}, bf16[2,128,1408]{2,1,0:T(8,128)(2,1)}, bf16[2,128,1024]{2,1,0:T(...) custom-call(bf16[512,1408]{1,0:T(8,128)(2,1)} %fusion.33.refs_0_, ...), custom_call_target="tpu_custom_call" | custom-call | tf_op jit(solution)/shard_map/pallas_call | solution.py:1202
  (464 shorter events, 269.0 us)
Async XLA Ops:
  6.7 96.2 %collective-permute-start.4 = (bf16[384,2048]{1,0:T(8,128)(2,1)}, bf16[384,2048]{1,0:T(8,128)(2,1)}, u32[]{:S(2)}, u32[]{:S(2)}) collective-permute-start(bf16[384,2048]{1,0:T(8,128)(2,1)} %fusion.9), channel_id=1, source_target_pairs={{0,4},{2,6},{4,0},{6,2},{1,5},{3,7},{5,1},{7,3},{8,12},{10,14},{12... | collective-permute-start | bytes 4718600 | tf_op jit(solution)/shard_map/ppermute | solution.py:940
  9.2 93.7 %collective-permute-start.3 = (bf16[384,2048]{1,0:T(8,128)(2,1)}, bf16[384,2048]{1,0:T(8,128)(2,1)}, u32[]{:S(2)}, u32[]{:S(2)}) collective-permute-start(bf16[384,2048]{1,0:T(8,128)(2,1)} %fusion.9), channel_id=1, source_target_pairs={{0,2},{2,0},{4,6},{6,4},{1,3},{3,1},{5,7},{7,5},{8,10},{10,8},{12,... | collective-permute-start | bytes 4718600 | tf_op jit(solution)/shard_map/ppermute | solution.py:940
  10.7 92.2 %collective-permute-start.2 = (bf16[384,2048]{1,0:T(8,128)(2,1)S(1)}, bf16[384,2048]{1,0:T(8,128)(2,1)}, u32[]{:S(2)}, u32[]{:S(2)}) collective-permute-start(bf16[384,2048]{1,0:T(8,128)(2,1)S(1)} %bitcast.130), channel_id=1, source_target_pairs={{0,8},{8,0},{16,24},{24,16},{1,9},{9,1},{17,25},{25,17},{2,10},{10... | collective-permute-start | bytes 4718600 | tf_op jit(solution)/shard_map/ppermute | solution.py:940
  110.1 39.4 %collective-permute-start.11 = (bf16[384,2048]{1,0:T(8,128)(2,1)}, bf16[384,2048]{1,0:T(8,128)(2,1)}, u32[]{:S(2)}, u32[]{:S(2)}) collective-permute-start(bf16[384,2048]{1,0:T(8,128)(2,1)} %collective-permute-done.4.refs_4_.mine_ref), channel_id=1, source_target_pairs={{0,1},{1,0},{2,3},{3,2},{4,5},{5,4},{6,7},{7,6},{8,9},{9,8},{10,11... | collective-permute-start | bytes 4718600 | tf_op jit(solution)/shard_map/ppermute | solution.py:968
  110.1 39.4 %collective-permute-start.10 = (bf16[384,2048]{1,0:T(8,128)(2,1)}, bf16[384,2048]{1,0:T(8,128)(2,1)}, u32[]{:S(2)}, u32[]{:S(2)}) collective-permute-start(bf16[384,2048]{1,0:T(8,128)(2,1)} %collective-permute-done.3.refs_3_.mine_ref), channel_id=1, source_target_pairs={{0,1},{1,0},{2,3},{3,2},{4,5},{5,4},{6,7},{7,6},{8,9},{9,8},{10,11... | collective-permute-start | bytes 4718600 | tf_op jit(solution)/shard_map/ppermute | solution.py:968
  110.6 38.9 %collective-permute-start.9 = (bf16[384,2048]{1,0:T(8,128)(2,1)}, bf16[384,2048]{1,0:T(8,128)(2,1)}, u32[]{:S(2)}, u32[]{:S(2)}) collective-permute-start(bf16[384,2048]{1,0:T(8,128)(2,1)} %collective-permute-done.2.refs_2_.mine_ref), channel_id=1, source_target_pairs={{0,1},{1,0},{2,3},{3,2},{4,5},{5,4},{6,7},{7,6},{8,9},{9,8},{10,11... | collective-permute-start | bytes 4718600 | tf_op jit(solution)/shard_map/ppermute | solution.py:968
  112.9 26.6 %collective-permute-start.8 = (bf16[8,128,256]{2,1,0:T(8,128)(2,1)}, bf16[8,128,256]{2,1,0:T(8,128)(2,1)}, u32[]{:S(2)}, u32[]{:S(2)}) collective-permute-start(bf16[8,128,256]{2,1,0:T(8,128)(2,1)} %get-tuple-element.75), channel_id=1, source_target_pairs={{0,4},{2,6},{1,5},{3,7},{8,12},{10,14},{9,13},{11,15},{16,20},{18,... | collective-permute-start | bytes 1572872 | tf_op jit(solution)/shard_map/ppermute | solution.py:907
  188.8 53.9 %collective-permute-start.16 = (bf16[384,2048]{1,0:T(8,128)(2,1)}, bf16[384,2048]{1,0:T(8,128)(2,1)}, u32[]{:S(2)}, u32[]{:S(2)}) collective-permute-start(bf16[384,2048]{1,0:T(8,128)(2,1)} %multiply_convert_fusion.2), channel_id=1, source_target_pairs={{0,4},{2,6},{4,0},{6,2},{1,5},{3,7},{5,1},{7,3},{8,12},{10,14},{12... | collective-permute-start | bytes 4718600 | tf_op jit(solution)/shard_map/ppermute | solution.py:940
  191.2 51.4 %collective-permute-start.15 = (bf16[384,2048]{1,0:T(8,128)(2,1)}, bf16[384,2048]{1,0:T(8,128)(2,1)}, u32[]{:S(2)}, u32[]{:S(2)}) collective-permute-start(bf16[384,2048]{1,0:T(8,128)(2,1)} %multiply_convert_fusion.2), channel_id=1, source_target_pairs={{0,2},{2,0},{4,6},{6,4},{1,3},{3,1},{5,7},{7,5},{8,10},{10,8},{12,... | collective-permute-start | bytes 4718600 | tf_op jit(solution)/shard_map/ppermute | solution.py:940
  233.9 135.9 %collective-permute-start.26 = (bf16[768,1408]{1,0:T(8,128)(2,1)}, bf16[768,1408]{1,0:T(8,128)(2,1)}, u32[]{:S(2)}, u32[]{:S(2)}) collective-permute-start(bf16[768,1408]{1,0:T(8,128)(2,1)} %constant_dynamic-slice_fusion.11.refs_6_), channel_id=1, source_target_pairs={{0,4},{2,6},{4,0},{6,2},{1,5},{3,7},{5,1},{7,3},{8,12},{10,14},{12... | collective-permute-start | bytes 6488072 | tf_op jit(solution)/shard_map/ppermute | solution.py:940
  235.4 124.4 %collective-permute-start.23 = (bf16[768,1408]{1,0:T(8,128)(2,1)}, bf16[768,1408]{1,0:T(8,128)(2,1)}, u32[]{:S(2)}, u32[]{:S(2)}) collective-permute-start(bf16[768,1408]{1,0:T(8,128)(2,1)} %constant_dynamic-slice_fusion.12.refs_5_), channel_id=1, source_target_pairs={{0,2},{2,0},{4,6},{6,4},{1,3},{3,1},{5,7},{7,5},{8,10},{10,8},{12,... | collective-permute-start | bytes 6488072 | tf_op jit(solution)/shard_map/ppermute | solution.py:940
  239.0 109.8 %collective-permute-start.28 = (bf16[768,1408]{1,0:T(8,128)(2,1)}, bf16[768,1408]{1,0:T(8,128)(2,1)}, u32[]{:S(2)}, u32[]{:S(2)}) collective-permute-start(bf16[768,1408]{1,0:T(8,128)(2,1)} %constant_dynamic-slice_fusion.10.refs_7_), channel_id=1, source_target_pairs={{0,8},{8,0},{16,24},{24,16},{1,9},{9,1},{17,25},{25,17},{2,10},{10... | collective-permute-start | bytes 6488072 | tf_op jit(solution)/shard_map/ppermute | solution.py:940
  253.5 64.9 %collective-permute-start.17 = (bf16[384,2048]{1,0:T(8,128)(2,1)}, bf16[384,2048]{1,0:T(8,128)(2,1)}, u32[]{:S(2)}, u32[]{:S(2)}) collective-permute-start(bf16[384,2048]{1,0:T(8,128)(2,1)} %convolution_convert_fusion.7), channel_id=1, source_target_pairs={{0,1},{1,0},{2,3},{3,2},{4,5},{5,4},{6,7},{7,6},{8,9},{9,8},{10,11... | collective-permute-start | bytes 4718600 | tf_op jit(solution)/shard_map/ppermute | solution.py:1275
  289.8 24.0 %collective-permute-start.18 = (bf16[384,2048]{1,0:T(8,128)(2,1)}, bf16[384,2048]{1,0:T(8,128)(2,1)}, u32[]{:S(2)}, u32[]{:S(2)}) collective-permute-start(bf16[384,2048]{1,0:T(8,128)(2,1)} %add_convert_fusion.1), channel_id=1, source_target_pairs={{0,1},{1,0},{2,3},{3,2},{4,5},{5,4},{6,7},{7,6},{8,9},{9,8},{10,11... | collective-permute-start | bytes 4718600 | tf_op jit(solution)/shard_map/ppermute | solution.py:1275
  313.8 27.6 %collective-permute-start.25 = (bf16[384,2048]{1,0:T(8,128)(2,1)}, bf16[384,2048]{1,0:T(8,128)(2,1)}, u32[]{:S(2)}, u32[]{:S(2)}) collective-permute-start(bf16[384,2048]{1,0:T(8,128)(2,1)} %collective-permute-done.16.refs_4_.mine_ref), channel_id=1, source_target_pairs={{0,1},{1,0},{2,3},{3,2},{4,5},{5,4},{6,7},{7,6},{8,9},{9,8},{10,11... | collective-permute-start | bytes 4718600 | tf_op jit(solution)/shard_map/ppermute | solution.py:968
  333.4 59.2 %collective-permute-start.30 = (bf16[384,2048]{1,0:T(8,128)(2,1)}, bf16[384,2048]{1,0:T(8,128)(2,1)}, u32[]{:S(2)}, u32[]{:S(2)}) collective-permute-start(bf16[384,2048]{1,0:T(8,128)(2,1)} %fusion.133), channel_id=1, source_target_pairs={{0,8},{8,0},{16,24},{24,16},{1,9},{9,1},{17,25},{25,17},{2,10},{10... | collective-permute-start | bytes 4718600 | tf_op jit(solution)/shard_map/ppermute | solution.py:940
  341.4 51.2 %collective-permute-start.19 = (bf16[384,2048]{1,0:T(8,128)(2,1)}, bf16[384,2048]{1,0:T(8,128)(2,1)S(1)}, u32[]{:S(2)}, u32[]{:S(2)}) collective-permute-start(bf16[384,2048]{1,0:T(8,128)(2,1)} %fusion.133), channel_id=1, source_target_pairs={{0,1},{1,0},{2,3},{3,2},{4,5},{5,4},{6,7},{7,6},{8,9},{9,8},{10,11... | collective-permute-start | bytes 4718600 | tf_op jit(solution)/shard_map/ppermute | solution.py:1256
  357.9 77.5 %collective-permute-start.29 = (bf16[1024,1408]{1,0:T(8,128)(2,1)}, bf16[1024,1408]{1,0:T(8,128)(2,1)}, u32[]{:S(2)}, u32[]{:S(2)}) collective-permute-start(bf16[1024,1408]{1,0:T(8,128)(2,1)} %convolution_convert_fusion.4), channel_id=1, source_target_pairs={{0,4},{2,6},{4,0},{6,2},{1,5},{3,7},{5,1},{7,3},{8,12},{10,14},{12... | collective-permute-start | bytes 8650760 | tf_op jit(solution)/shard_map/ppermute | solution.py:940
  368.1 74.4 %collective-permute-start.24 = (bf16[1024,1408]{1,0:T(8,128)(2,1)}, bf16[1024,1408]{1,0:T(8,128)(2,1)}, u32[]{:S(2)}, u32[]{:S(2)}) collective-permute-start(bf16[1024,1408]{1,0:T(8,128)(2,1)} %convolution_convert_fusion.6), channel_id=1, source_target_pairs={{0,8},{8,0},{16,24},{24,16},{1,9},{9,1},{17,25},{25,17},{2,10},{10... | collective-permute-start | bytes 8650760 | tf_op jit(solution)/shard_map/ppermute | solution.py:940
  377.9 73.5 %collective-permute-start.27 = (bf16[1024,1408]{1,0:T(8,128)(2,1)}, bf16[1024,1408]{1,0:T(8,128)(2,1)}, u32[]{:S(2)}, u32[]{:S(2)}) collective-permute-start(bf16[1024,1408]{1,0:T(8,128)(2,1)} %convolution_convert_fusion.5.rest_0_), channel_id=1, source_target_pairs={{0,2},{2,0},{4,6},{6,4},{1,3},{3,1},{5,7},{7,5},{8,10},{10,8},{12,... | collective-permute-start | bytes 8650760 | tf_op jit(solution)/shard_map/ppermute | solution.py:940
  392.6 34.2 %collective-permute-start.31 = (bf16[384,2048]{1,0:T(8,128)(2,1)}, bf16[384,2048]{1,0:T(8,128)(2,1)}, u32[]{:S(2)}, u32[]{:S(2)}) collective-permute-start(bf16[384,2048]{1,0:T(8,128)(2,1)} %collective-permute-done.30.mine_ref), channel_id=1, source_target_pairs={{0,1},{1,0},{2,3},{3,2},{4,5},{5,4},{6,7},{7,6},{8,9},{9,8},{10,11... | collective-permute-start | bytes 4718600 | tf_op jit(solution)/shard_map/ppermute | solution.py:968
  417.8 42.5 %collective-permute-start.21 = (bf16[8,128,256]{2,1,0:T(8,128)(2,1)}, bf16[8,128,256]{2,1,0:T(8,128)(2,1)S(1)}, u32[]{:S(2)}, u32[]{:S(2)}) collective-permute-start(bf16[8,128,256]{2,1,0:T(8,128)(2,1)} %get-tuple-element.89), channel_id=1, source_target_pairs={{4,0},{6,2},{5,1},{7,3},{12,8},{14,10},{13,9},{15,11},{20,16},{22,... | collective-permute-start | bytes 1572872 | tf_op jit(solution)/shard_map/ppermute | solution.py:907
  426.8 35.9 %collective-permute-start.20 = (bf16[8,128,256]{2,1,0:T(8,128)(2,1)S(1)}, bf16[8,128,256]{2,1,0:T(8,128)(2,1)S(1)}, u32[]{:S(2)}, u32[]{:S(2)}) collective-permute-start(bf16[8,128,256]{2,1,0:T(8,128)(2,1)S(1)} %copy-done.107), channel_id=1, source_target_pairs={{2,0},{4,2},{6,4},{3,1},{5,3},{7,5},{10,8},{12,10},{14,12},{11,9},... | collective-permute-start | bytes 1572872 | tf_op jit(solution)/shard_map/ppermute | solution.py:907
  435.4 185.8 %collective-permute-start.38 = (bf16[768,1024]{1,0:T(8,128)(2,1)}, bf16[768,1024]{1,0:T(8,128)(2,1)}, u32[]{:S(2)}, u32[]{:S(2)}) collective-permute-start(bf16[768,1024]{1,0:T(8,128)(2,1)} %get-tuple-element.177), channel_id=1, source_target_pairs={{0,8},{8,0},{16,24},{24,16},{1,9},{9,1},{17,25},{25,17},{2,10},{10... | collective-permute-start | bytes 4718600 | tf_op jit(solution)/shard_map/ppermute | solution.py:940
  442.5 188.7 %collective-permute-start.37 = (bf16[768,1024]{1,0:T(8,128)(2,1)}, bf16[768,1024]{1,0:T(8,128)(2,1)}, u32[]{:S(2)}, u32[]{:S(2)}) collective-permute-start(bf16[768,1024]{1,0:T(8,128)(2,1)} %get-tuple-element.179), channel_id=1, source_target_pairs={{0,2},{2,0},{4,6},{6,4},{1,3},{3,1},{5,7},{7,5},{8,10},{10,8},{12,... | collective-permute-start | bytes 4718600 | tf_op jit(solution)/shard_map/ppermute | solution.py:940
  451.5 106.6 %collective-permute-start.34 = (bf16[512,1408]{1,0:T(8,128)(2,1)}, bf16[512,1408]{1,0:T(8,128)(2,1)}, u32[]{:S(2)}, u32[]{:S(2)}) collective-permute-start(bf16[512,1408]{1,0:T(8,128)(2,1)} %fusion.36.rest_2_), channel_id=1, source_target_pairs={{0,16},{8,24},{16,0},{24,8},{1,17},{9,25},{17,1},{25,9},{2,18},{10... | collective-permute-start | bytes 4325384 | tf_op jit(solution)/shard_map/ppermute | solution.py:940
  460.2 97.8 %collective-permute-start.32 = (bf16[512,1408]{1,0:T(8,128)(2,1)}, bf16[512,1408]{1,0:T(8,128)(2,1)}, u32[]{:S(2)}, u32[]{:S(2)}) collective-permute-start(bf16[512,1408]{1,0:T(8,128)(2,1)} %fusion.34.rest_0_), channel_id=1, source_target_pairs={{0,4},{2,6},{4,0},{6,2},{1,5},{3,7},{5,1},{7,3},{8,12},{10,14},{12... | collective-permute-start | bytes 4325384 | tf_op jit(solution)/shard_map/ppermute | solution.py:940
  462.7 95.3 %collective-permute-start.33 = (bf16[512,1408]{1,0:T(8,128)(2,1)}, bf16[512,1408]{1,0:T(8,128)(2,1)}, u32[]{:S(2)}, u32[]{:S(2)}) collective-permute-start(bf16[512,1408]{1,0:T(8,128)(2,1)} %fusion.35.rest_1_), channel_id=1, source_target_pairs={{0,8},{8,0},{16,24},{24,16},{1,9},{9,1},{17,25},{25,17},{2,10},{10... | collective-permute-start | bytes 4325384 | tf_op jit(solution)/shard_map/ppermute | solution.py:940
  558.1 23.0 %collective-permute-start.35 = (f32[8,4096]{1,0:T(8,128)}, f32[8,4096]{1,0:T(8,128)S(1)}, u32[]{:S(2)}, u32[]{:S(2)}) collective-permute-start(f32[8,4096]{1,0:T(8,128)} %shard_map.424), channel_id=1, source_target_pairs={{2,0},{4,2},{6,4},{3,1},{5,3},{7,5},{10,8},{12,10},{14,12},{11,9},... | collective-permute-start | bytes 393224 | tf_op jit(solution)/shard_map/ppermute | solution.py:907
  584.3 85.2 %collective-permute-start.40 = (bf16[768,1024]{1,0:T(8,128)(2,1)}, bf16[768,1024]{1,0:T(8,128)(2,1)}, u32[]{:S(2)}, u32[]{:S(2)}) collective-permute-start(bf16[768,1024]{1,0:T(8,128)(2,1)} %get-tuple-element.173.refs_5_), channel_id=1, source_target_pairs={{0,4},{2,6},{4,0},{6,2},{1,5},{3,7},{5,1},{7,3},{8,12},{10,14},{12... | collective-permute-start | bytes 4718600 | tf_op jit(solution)/shard_map/ppermute | solution.py:940
  594.7 63.2 %collective-permute-start.39 = (bf16[768,1024]{1,0:T(8,128)(2,1)}, bf16[768,1024]{1,0:T(8,128)(2,1)}, u32[]{:S(2)}, u32[]{:S(2)}) collective-permute-start(bf16[768,1024]{1,0:T(8,128)(2,1)} %get-tuple-element.175.refs_4_), channel_id=1, source_target_pairs={{0,2},{2,0},{4,6},{6,4},{1,3},{3,1},{5,7},{7,5},{8,10},{10,8},{12,... | collective-permute-start | bytes 4718600 | tf_op jit(solution)/shard_map/ppermute | solution.py:940
  615.1 36.9 %collective-permute-start.36 = (bf16[384,2048]{1,0:T(8,128)(2,1)}, bf16[384,2048]{1,0:T(8,128)(2,1)}, u32[]{:S(2)}, u32[]{:S(2)}) collective-permute-start(bf16[384,2048]{1,0:T(8,128)(2,1)} %add_convert_fusion), channel_id=1, source_target_pairs={{0,1},{1,0},{2,3},{3,2},{4,5},{5,4},{6,7},{7,6},{8,9},{9,8},{10,11... | collective-permute-start | bytes 4718600 | tf_op jit(solution)/shard_map/ppermute | solution.py:1275
  (141 other events, 1839.7 us)

commit v6 on v5

--- a/solution.py
+++ b/solution.py
@@ -231,7 +231,7 @@
             grown_q[j, at, :] = grown * q
         return carry
 
-    lax.fori_loop(0, pairs, local, 0, unroll=2)
+    lax.fori_loop(0, pairs, local, 0, unroll=3)
 
     masks = masks_low(row, col)
     spots = [
@@ -267,7 +267,7 @@
                 gain_ref[j, 2 * pair + half] = low(mm_tn(falls[part], u_low[part]))
         return carry
 
-    lax.fori_loop(0, pairs, combine, 0, unroll=2)
+    lax.fori_loop(0, pairs, combine, 0, unroll=3)
 
     for j in range(per_step):
         states[j] = jnp.concatenate(
@@ -288,7 +288,7 @@
             states[j, :, DK:] = moved[:, DK:] + high(gain_ref[j, block])
         return carry
 
-    lax.fori_loop(0, blocks, advance, 0, unroll=2)
+    lax.fori_loop(0, blocks, advance, 0, unroll=4)
 
     def close(block, carry):
         at = pl.ds(pl.multiple_of(block * GROUP, GROUP), GROUP)
@@ -300,7 +300,7 @@
             mixed_ref[at, wide] = mixed_ref[at, wide] + out[:, DK:]
         return carry
 
-    lax.fori_loop(0, blocks, close, 0, unroll=4)
+    lax.fori_loop(0, blocks, close, 0, unroll=6)
     for j in range(per_step):
         map_ref[j] = low(states[j, :, :DK])
         add_ref[j] = low(states[j, :, DK:])
@@ -625,7 +625,7 @@
             )
         return carry
 
-    lax.fori_loop(0, blocks, chain, 0, unroll=2)
+    lax.fori_loop(0, blocks, chain, 0, unroll=3)
 
     lane = lax.broadcasted_iota(jnp.int32, (PAIR, d_cum.shape[1]), 1)
     tall = lax.broadcasted_iota(jnp.int32, (PAIR, 1), 0)
@@ -708,7 +708,7 @@
             d_value[j, at, :] = bb * rhs
         return carry
 
-    lax.fori_loop(0, pairs, assemble, 0, unroll=2)
+    lax.fori_loop(0, pairs, assemble, 0, unroll=6)
 
     d_total[0:RIM, :] = jnp.zeros((RIM, DK), jnp.float32)
     d_total[RIM + count : 2 * RIM + count, :] = jnp.zeros((RIM, DK), jnp.float32)

time: 923 us -> 911 us (0.987)
  Pallas kernels: 404 us -> 393 us
  transfers between devices with their start and end apart: 41 -> 41, of which waited for: 4 -> 4; matrix products, arithmetic and copies ran while one was open for 40% -> 40% of each run, Pallas kernels for 22% -> 21%
where the time goes in v6:
time: 911 us; the launch traced here: 902 us
  Pallas kernels  393 us (43%)
  matrix products  327 us (36%)
  starting transfers between devices  55.5 us (6%)
  local copies, waits for them, and re-layouts  52.3 us (6%)
  other arithmetic  52 us (6%)
  waiting for transfers between devices  19.2 us (2%)
    pallas_call x1, Pallas kernels, finish(): pl.pallas_call(functools.partial(finish_kernel, tuple(plan), tuple(head_s...  200 us
    dot_general x14, matrix products, weight_grad(): jnp.einsum('td,tc->dc', rows, grads, preferred_element_type=jnp.float32)  109 us
    dot_general x16, matrix products, rows_back(): jnp.einsum('tc,dc->td', left, weight, preferred_element_type=jnp.float32)  92.2 us
    pallas_call x1, Pallas kernels, state_backward(): pl.pallas_call(functools.partial(state_back_kernel, taps, n, offset, len(...  75.4 us
    dot_general x7, matrix products, project(): return jnp.dot(rows, weight, preferred_element_type=jnp.float32)  62.4 us
    pallas_call x1, Pallas kernels, state_forward(): pl.pallas_call(functools.partial(state_kernel, taps, n), grid=(heads // n...  51.8 us
    pallas_call x6, Pallas kernels, paired_rows(): pl.pallas_call(functools.partial(arrange_kernel, blocks), grid=(count //...  44 us
    dot_general x4, matrix products, rows_product(): return jnp.dot(left, right, preferred_element_type=jnp.float32)  36 us
  transfers between devices with their start and end apart: 41, of which 4 were waited for; matrix products, arithmetic and copies ran while one was open for 40% of the time, Pallas kernels for 21%

profile of v6, /device:TPU:0, one launch (start us, length us, event | category | flops | bytes accessed | tf_op | source)
XLA Modules:
  0.0 901.9 jit_solution(4347283633195386841)
XLA Ops:
  35.6 12.1 %collective-permute-done.1 = f32[8,4096]{1,0:T(8,128)S(1)} collective-permute-done((f32[8,4096]{1,0:T(8,128)S(1)}, f32[8,4096]{1,0:T(8,128)S(1)}, u32[]{:S(2)}, u32[]{:S(2)}) %collective-permute-start.1) | collective-permute-done | bytes 131104 | tf_op jit(solution)/shard_map/ppermute | solution.py:907
  49.0 51.8 %shard_map.410 = (f32[768,2048]{1,0:T(8,128)}, bf16[768,1024]{1,0:T(8,128)(2,1)}, bf16[8,128,128]{2,1,0:T(8,128)(2,1)}, bf16[8,128,256]{2,1,0:T(8,128)(2,1)}, bf...) custom-call(s32[2]{0:T(128)} %pad_add_fusion.spot, ...), custom_call_target="tpu_custom_call" | custom-call | tf_op jit(solution)/shard_map/pallas_call | solution.py:326
  110.8 7.7 collective-permute-start.8
  121.9 11.2 %fusion.136.gate_ref = f32[768,2048]{1,0:T(8,128)} fusion(bf16[2048,2048]{1,0:T(8,128)(2,1)} %param.34, bf16[384,2048]{1,0:T(8,128)(2,1)} %copy-done.25, bf16[384,2048]{1,0:T(8,128)(2,1)S(1)} %copy-done.22), kind=kOutput, calls=%fused_computation.253 | convolution fusion | flops 6448742400 | bytes 17825792 | tf_op jit(solution)/shard_map/dot_general | solution.py:919
  137.5 9.9 %shard_map.413 = (bf16[768,2048]{1,0:T(8,128)(2,1)}, bf16[768,2048]{1,0:T(8,128)(2,1)}, bf16[8,128,256]{2,1,0:T(8,128)(2,1)}) custom-call(f32[768,2048]{1,0:T(8,128)} %shard_map.412.mixed_ref, bf16[768,1024]{1,0:T(8,128)(2,1)} %get-tuple-element.74.reach_ref, bf16[8,128,128]{2,1,0:T(8,128)(2,1)} %collective-permute-done.6.map_ref, ...), custom_call_target="tpu_custom_call" | custom-call | tf_op jit(solution)/shard_map/pallas_call | solution.py:413
  147.5 7.3 convolution_convert_fusion.8
  167.5 15.4 %fusion.132 = f32[768,2816]{1,0:T(8,128)} fusion(bf16[2816,2048]{1,0:T(8,128)(2,1)} %param.47, bf16[384,2048]{1,0:T(8,128)(2,1)S(1)} %get-tuple-element.183, bf16[384,2048]{1,0:T(8,128)(2,1)S(1)} %get-tuple-element.182), kind=kOutput, calls=%fused_computation.249 | convolution fusion | flops 8864661504 | bytes 23330816 | tf_op jit(solution)/shard_map/td,fd->tf/dot_general | solution.py:1359
  191.8 14.8 %fusion.134 = f32[768,2816]{1,0:T(8,128)} fusion(bf16[2048,2816]{1,0:T(8,128)(2,1)} %param.45, bf16[384,2048]{1,0:T(8,128)(2,1)S(1)} %get-tuple-element.185, bf16[384,2048]{1,0:T(8,128)(2,1)S(1)} %get-tuple-element.184), kind=kOutput, calls=%fused_computation.251 | convolution fusion | flops 8864661504 | bytes 23330816 | tf_op jit(solution)/shard_map/dot_general | solution.py:919
  206.6 21.9 %multiply_convert_fusion = (bf16[768,2816]{1,0:T(8,128)(2,1)}, bf16[768,2816]{1,0:T(8,128)(2,1)}, bf16[768,2816]{1,0:T(8,128)(2,1)}) fusion(f32[768,2816]{1,0:T(8,128)} %fusion.134, f32[768,2816]{1,0:T(8,128)} %fusion.132, bf16[2048,2816]{1,0:T(8,128)(2,1)} %param.46, bf16[384,2048]{1,0:T(8,128)(2,1)} %copy-done.34, bf16[384,2048]{1,0:T(8,128)(2,1)} %copy-done.32), kind=kOutput, calls=%fused_computation.4 | convolution fusion | flops 8899264512 | bytes 44957696 | tf_op jit(solution)/shard_map/dot_general | solution.py:919
  240.6 10.8 %convolution_convert_fusion.7 = bf16[384,2048]{1,0:T(8,128)(2,1)} fusion(bf16[2816,2048]{1,0:T(8,128)(2,1)} %param.47, bf16[768,2816]{1,0:T(8,128)(2,1)} %get-tuple-element.77.rest_0_, s32[]{:T(128)S(6)} %select_n.130), kind=kOutput, calls=%fused_computation.81 | convolution fusion | flops 4429971456 | bytes 15269892 | tf_op jit(solution)/shard_map/dot_general | solution.py:923
  254.4 9.9 %fusion.38 = f32[384,2048]{1,0:T(8,128)} fusion(bf16[2048,2816]{1,0:T(8,128)(2,1)} %param.46, bf16[768,2816]{1,0:T(8,128)(2,1)S(1)} %copy-done.14, s32[]{:T(128)S(6)} %select_n.130), kind=kOutput, calls=%fused_computation.84 | convolution fusion | flops 4429185024 | bytes 16842756 | tf_op jit(solution)/shard_map/tc,dc->td/dot_general | solution.py:927
  264.3 10.0 %fusion.43 = f32[384,2048]{1,0:T(8,128)} fusion(bf16[2048,2816]{1,0:T(8,128)(2,1)} %param.45, bf16[768,2816]{1,0:T(8,128)(2,1)S(1)} %bitcast.115, s32[]{:T(128)S(6)} %select_n.129), kind=kOutput, calls=%fused_computation.89 | convolution fusion | flops 4429185024 | bytes 16842756 | tf_op jit(solution)/shard_map/tc,dc->td/dot_general | solution.py:927
  274.3 13.4 %add_convert_fusion.1 = bf16[384,2048]{1,0:T(8,128)(2,1)} fusion(f32[384,2048]{1,0:T(8,128)} %fusion.38, bf16[2048,2816]{1,0:T(8,128)(2,1)} %param.45, bf16[768,2816]{1,0:T(8,128)(2,1)S(1)} %bitcast.115, s32[]{:T(128)S(6)} %select_n.130), kind=kOutput, calls=%fused_computation.71 | convolution fusion | flops 4430757888 | bytes 18415620 | tf_op jit(solution)/shard_map/tc,dc->td/dot_general | solution.py:927
  290.8 7.3 shard_map.419
  299.6 12.1 %fusion.41 = f32[384,2048]{1,0:T(8,128)} fusion(bf16[2048,2816]{1,0:T(8,128)(2,1)} %param.46, bf16[768,2816]{1,0:T(8,128)(2,1)} %get-tuple-element.79, s32[]{:T(128)S(6)} %select_n.129), kind=kOutput, calls=%fused_computation.87 | convolution fusion | flops 4429185024 | bytes 16842756 | tf_op jit(solution)/shard_map/tc,dc->td/dot_general | solution.py:927
  316.4 11.6 %fusion.37 = bf16[1,384,2048]{2,1,0:T(8,128)(2,1)} fusion(f32[384,2048]{1,0:T(8,128)S(1)} %get-tuple-element.215, bf16[384,2048]{1,0:T(8,128)(2,1)} %collective-permute-done.17, bf16[2816,2048]{1,0:T(8,128)(2,1)} %param.47, bf16[768,2816]{1,0:T(8,128)(2,1)S(1)} %bitcast.129, s32[]{:T(128)S(6)} %select_n.129), kind=kOutput, calls=%fused_computation.83 | convolution fusion | flops 4432330752 | bytes 19988484 | tf_op jit(solution)/shard_map/dot_general | solution.py:923
  331.8 7.5 shard_map.417
  339.4 7.4 shard_map.418
  346.8 9.0 convolution_convert_fusion.4
  357.7 8.3 convolution_convert_fusion.6
  367.7 8.2 convolution_convert_fusion.5.rest_0_
  375.9 7.3 shard_map.422
  383.2 7.4 shard_map.421
  392.2 11.9 %fusion.131.d_gated_ref = f32[768,2048]{1,0:T(8,128)} fusion(bf16[2048,2048]{1,0:T(8,128)(2,1)} %param.43, bf16[384,2048]{1,0:T(8,128)(2,1)S(1)} %get-tuple-element.181, bf16[384,2048]{1,0:T(8,128)(2,1)S(1)} %get-tuple-element.180), kind=kOutput, calls=%fused_computation.248 | convolution fusion | flops 6448742400 | bytes 17825792 | tf_op jit(solution)/shard_map/td,cd->tc/dot_general | solution.py:1393
  404.1 11.6 %shard_map.416 = (bf16[768,2048]{1,0:T(8,128)(2,1)}, bf16[768,2048]{1,0:T(8,128)(2,1)}, bf16[8,128,256]{2,1,0:T(8,128)(2,1)}, f32[1,256]{1,0:T(1,128)}) custom-call(f32[768,2048]{1,0:T(8,128)} %fusion.131.d_gated_ref, bf16[768,2048]{1,0:T(8,128)(2,1)} %get-tuple-element.87.kept_ref, bf16[768,1024]{1,0:T(8,128)(2,1)} %get-tuple-element.74.reach_ref, ...), custom_call_target="tpu_custom_call" | custom-call | tf_op jit(solution)/shard_map/pallas_call | solution.py:474
  461.6 75.4 %shard_map.423 = (bf16[768,1024]{1,0:T(8,128)(2,1)}, bf16[768,1024]{1,0:T(8,128)(2,1)}, bf16[768,2048]{1,0:T(8,128)(2,1)}, f32[8,1024]{1,0:T(8,128)}, f32[8,1024...) custom-call(s32[2]{0:T(128)} %pad_add_fusion.spot, ...), custom_call_target="tpu_custom_call" | custom-call | tf_op jit(solution)/shard_map/pallas_call | solution.py:824
  548.7 7.4 fusion.31.refs_2_
  610.0 9.9 %convolution_convert_fusion.2.refs_4_ = bf16[2048,1024]{1,0:T(8,128)(2,1)} fusion(bf16[1536,2048]{1,0:T(8,128)(2,1)S(1)} %bitcast.127, bf16[768,1024]{1,0:T(8,128)(2,1)} %collective-permute-done.38, bf16[768,1024]{1,0:T(8,128)(2,1)S(1)} %copy-done.51), kind=kOutput, calls=%fused_computation.20 | convolution fusion | flops 6450839552 | bytes 13631488 | tf_op jit(solution)/shard_map/td,tc->dc/dot_general | solution.py:931
  620.0 10.1 %convolution_convert_fusion.3.refs_3_ = bf16[2048,1024]{1,0:T(8,128)(2,1)} fusion(bf16[1536,2048]{1,0:T(8,128)(2,1)S(1)} %bitcast.123, bf16[768,1024]{1,0:T(8,128)(2,1)} %collective-permute-done.37, bf16[768,1024]{1,0:T(8,128)(2,1)S(1)} %copy-done.50), kind=kOutput, calls=%fused_computation.21 | convolution fusion | flops 6450839552 | bytes 13631488 | tf_op jit(solution)/shard_map/td,tc->dc/dot_general | solution.py:931
  646.7 11.6 %convolution_convert_fusion.1.refs_5_ = bf16[2048,1024]{1,0:T(8,128)(2,1)} fusion(bf16[1536,2048]{1,0:T(8,128)(2,1)} %get-tuple-element.103, bf16[768,1024]{1,0:T(8,128)(2,1)} %collective-permute-done.39, bf16[768,1024]{1,0:T(8,128)(2,1)} %get-tuple-element.174), kind=kOutput, calls=%fused_computation.19 | convolution fusion | flops 6450839552 | bytes 13631488 | tf_op jit(solution)/shard_map/td,tc->dc/dot_general | solution.py:931
  658.3 10.0 %convolution_convert_fusion.refs_6_ = bf16[2048,1024]{1,0:T(8,128)(2,1)} fusion(bf16[1536,2048]{1,0:T(8,128)(2,1)S(1)} %bitcast.119, bf16[768,1024]{1,0:T(8,128)(2,1)} %collective-permute-done.40, bf16[768,1024]{1,0:T(8,128)(2,1)S(1)} %copy-done.52), kind=kOutput, calls=%fused_computation.18 | convolution fusion | flops 6450839552 | bytes 13631488 | tf_op jit(solution)/shard_map/td,tc->dc/dot_general | solution.py:931
  668.4 200.3 %shard_map.427 = (bf16[2,128,1408]{2,1,0:T(8,128)(2,1)}, bf16[2,128,1408]{2,1,0:T(8,128)(2,1)}, bf16[2,128,1408]{2,1,0:T(8,128)(2,1)}, bf16[2,128,1024]{2,1,0:T(...) custom-call(bf16[512,1408]{1,0:T(8,128)(2,1)} %fusion.33.refs_0_, ...), custom_call_target="tpu_custom_call" | custom-call | tf_op jit(solution)/shard_map/pallas_call | solution.py:1202
  (464 shorter events, 268.6 us)
Async XLA Ops:
  6.7 94.2 %collective-permute-start.4 = (bf16[384,2048]{1,0:T(8,128)(2,1)}, bf16[384,2048]{1,0:T(8,128)(2,1)}, u32[]{:S(2)}, u32[]{:S(2)}) collective-permute-start(bf16[384,2048]{1,0:T(8,128)(2,1)} %fusion.9), channel_id=1, source_target_pairs={{0,4},{2,6},{4,0},{6,2},{1,5},{3,7},{5,1},{7,3},{8,12},{10,14},{12... | collective-permute-start | bytes 4718600 | tf_op jit(solution)/shard_map/ppermute | solution.py:940
  9.2 91.6 %collective-permute-start.3 = (bf16[384,2048]{1,0:T(8,128)(2,1)}, bf16[384,2048]{1,0:T(8,128)(2,1)}, u32[]{:S(2)}, u32[]{:S(2)}) collective-permute-start(bf16[384,2048]{1,0:T(8,128)(2,1)} %fusion.9), channel_id=1, source_target_pairs={{0,2},{2,0},{4,6},{6,4},{1,3},{3,1},{5,7},{7,5},{8,10},{10,8},{12,... | collective-permute-start | bytes 4718600 | tf_op jit(solution)/shard_map/ppermute | solution.py:940
  10.7 90.2 %collective-permute-start.2 = (bf16[384,2048]{1,0:T(8,128)(2,1)S(1)}, bf16[384,2048]{1,0:T(8,128)(2,1)}, u32[]{:S(2)}, u32[]{:S(2)}) collective-permute-start(bf16[384,2048]{1,0:T(8,128)(2,1)S(1)} %bitcast.130), channel_id=1, source_target_pairs={{0,8},{8,0},{16,24},{24,16},{1,9},{9,1},{17,25},{25,17},{2,10},{10... | collective-permute-start | bytes 4718600 | tf_op jit(solution)/shard_map/ppermute | solution.py:940
  108.0 39.4 %collective-permute-start.11 = (bf16[384,2048]{1,0:T(8,128)(2,1)}, bf16[384,2048]{1,0:T(8,128)(2,1)}, u32[]{:S(2)}, u32[]{:S(2)}) collective-permute-start(bf16[384,2048]{1,0:T(8,128)(2,1)} %collective-permute-done.4.refs_4_.mine_ref), channel_id=1, source_target_pairs={{0,1},{1,0},{2,3},{3,2},{4,5},{5,4},{6,7},{7,6},{8,9},{9,8},{10,11... | collective-permute-start | bytes 4718600 | tf_op jit(solution)/shard_map/ppermute | solution.py:968
  108.0 39.4 %collective-permute-start.10 = (bf16[384,2048]{1,0:T(8,128)(2,1)}, bf16[384,2048]{1,0:T(8,128)(2,1)}, u32[]{:S(2)}, u32[]{:S(2)}) collective-permute-start(bf16[384,2048]{1,0:T(8,128)(2,1)} %collective-permute-done.3.refs_3_.mine_ref), channel_id=1, source_target_pairs={{0,1},{1,0},{2,3},{3,2},{4,5},{5,4},{6,7},{7,6},{8,9},{9,8},{10,11... | collective-permute-start | bytes 4718600 | tf_op jit(solution)/shard_map/ppermute | solution.py:968
  108.5 38.9 %collective-permute-start.9 = (bf16[384,2048]{1,0:T(8,128)(2,1)}, bf16[384,2048]{1,0:T(8,128)(2,1)}, u32[]{:S(2)}, u32[]{:S(2)}) collective-permute-start(bf16[384,2048]{1,0:T(8,128)(2,1)} %collective-permute-done.2.refs_2_.mine_ref), channel_id=1, source_target_pairs={{0,1},{1,0},{2,3},{3,2},{4,5},{5,4},{6,7},{7,6},{8,9},{9,8},{10,11... | collective-permute-start | bytes 4718600 | tf_op jit(solution)/shard_map/ppermute | solution.py:968
  110.8 26.6 %collective-permute-start.8 = (bf16[8,128,256]{2,1,0:T(8,128)(2,1)}, bf16[8,128,256]{2,1,0:T(8,128)(2,1)}, u32[]{:S(2)}, u32[]{:S(2)}) collective-permute-start(bf16[8,128,256]{2,1,0:T(8,128)(2,1)} %get-tuple-element.75), channel_id=1, source_target_pairs={{0,4},{2,6},{1,5},{3,7},{8,12},{10,14},{9,13},{11,15},{16,20},{18,... | collective-permute-start | bytes 1572872 | tf_op jit(solution)/shard_map/ppermute | solution.py:907
  186.7 53.9 %collective-permute-start.16 = (bf16[384,2048]{1,0:T(8,128)(2,1)}, bf16[384,2048]{1,0:T(8,128)(2,1)}, u32[]{:S(2)}, u32[]{:S(2)}) collective-permute-start(bf16[384,2048]{1,0:T(8,128)(2,1)} %multiply_convert_fusion.2), channel_id=1, source_target_pairs={{0,4},{2,6},{4,0},{6,2},{1,5},{3,7},{5,1},{7,3},{8,12},{10,14},{12... | collective-permute-start | bytes 4718600 | tf_op jit(solution)/shard_map/ppermute | solution.py:940
  189.2 51.4 %collective-permute-start.15 = (bf16[384,2048]{1,0:T(8,128)(2,1)}, bf16[384,2048]{1,0:T(8,128)(2,1)}, u32[]{:S(2)}, u32[]{:S(2)}) collective-permute-start(bf16[384,2048]{1,0:T(8,128)(2,1)} %multiply_convert_fusion.2), channel_id=1, source_target_pairs={{0,2},{2,0},{4,6},{6,4},{1,3},{3,1},{5,7},{7,5},{8,10},{10,8},{12,... | collective-permute-start | bytes 4718600 | tf_op jit(solution)/shard_map/ppermute | solution.py:940
  231.8 135.9 %collective-permute-start.26 = (bf16[768,1408]{1,0:T(8,128)(2,1)}, bf16[768,1408]{1,0:T(8,128)(2,1)}, u32[]{:S(2)}, u32[]{:S(2)}) collective-permute-start(bf16[768,1408]{1,0:T(8,128)(2,1)} %constant_dynamic-slice_fusion.11.refs_6_), channel_id=1, source_target_pairs={{0,4},{2,6},{4,0},{6,2},{1,5},{3,7},{5,1},{7,3},{8,12},{10,14},{12... | collective-permute-start | bytes 6488072 | tf_op jit(solution)/shard_map/ppermute | solution.py:940
  233.4 124.3 %collective-permute-start.23 = (bf16[768,1408]{1,0:T(8,128)(2,1)}, bf16[768,1408]{1,0:T(8,128)(2,1)}, u32[]{:S(2)}, u32[]{:S(2)}) collective-permute-start(bf16[768,1408]{1,0:T(8,128)(2,1)} %constant_dynamic-slice_fusion.12.refs_5_), channel_id=1, source_target_pairs={{0,2},{2,0},{4,6},{6,4},{1,3},{3,1},{5,7},{7,5},{8,10},{10,8},{12,... | collective-permute-start | bytes 6488072 | tf_op jit(solution)/shard_map/ppermute | solution.py:940
  236.9 109.8 %collective-permute-start.28 = (bf16[768,1408]{1,0:T(8,128)(2,1)}, bf16[768,1408]{1,0:T(8,128)(2,1)}, u32[]{:S(2)}, u32[]{:S(2)}) collective-permute-start(bf16[768,1408]{1,0:T(8,128)(2,1)} %constant_dynamic-slice_fusion.10.refs_7_), channel_id=1, source_target_pairs={{0,8},{8,0},{16,24},{24,16},{1,9},{9,1},{17,25},{25,17},{2,10},{10... | collective-permute-start | bytes 6488072 | tf_op jit(solution)/shard_map/ppermute | solution.py:940
  251.4 64.9 %collective-permute-start.17 = (bf16[384,2048]{1,0:T(8,128)(2,1)}, bf16[384,2048]{1,0:T(8,128)(2,1)}, u32[]{:S(2)}, u32[]{:S(2)}) collective-permute-start(bf16[384,2048]{1,0:T(8,128)(2,1)} %convolution_convert_fusion.7), channel_id=1, source_target_pairs={{0,1},{1,0},{2,3},{3,2},{4,5},{5,4},{6,7},{7,6},{8,9},{9,8},{10,11... | collective-permute-start | bytes 4718600 | tf_op jit(solution)/shard_map/ppermute | solution.py:1275
  287.7 24.0 %collective-permute-start.18 = (bf16[384,2048]{1,0:T(8,128)(2,1)}, bf16[384,2048]{1,0:T(8,128)(2,1)}, u32[]{:S(2)}, u32[]{:S(2)}) collective-permute-start(bf16[384,2048]{1,0:T(8,128)(2,1)} %add_convert_fusion.1), channel_id=1, source_target_pairs={{0,1},{1,0},{2,3},{3,2},{4,5},{5,4},{6,7},{7,6},{8,9},{9,8},{10,11... | collective-permute-start | bytes 4718600 | tf_op jit(solution)/shard_map/ppermute | solution.py:1275
  311.7 27.6 %collective-permute-start.25 = (bf16[384,2048]{1,0:T(8,128)(2,1)}, bf16[384,2048]{1,0:T(8,128)(2,1)}, u32[]{:S(2)}, u32[]{:S(2)}) collective-permute-start(bf16[384,2048]{1,0:T(8,128)(2,1)} %collective-permute-done.16.refs_4_.mine_ref), channel_id=1, source_target_pairs={{0,1},{1,0},{2,3},{3,2},{4,5},{5,4},{6,7},{7,6},{8,9},{9,8},{10,11... | collective-permute-start | bytes 4718600 | tf_op jit(solution)/shard_map/ppermute | solution.py:968
  331.4 59.2 %collective-permute-start.30 = (bf16[384,2048]{1,0:T(8,128)(2,1)}, bf16[384,2048]{1,0:T(8,128)(2,1)}, u32[]{:S(2)}, u32[]{:S(2)}) collective-permute-start(bf16[384,2048]{1,0:T(8,128)(2,1)} %fusion.133), channel_id=1, source_target_pairs={{0,8},{8,0},{16,24},{24,16},{1,9},{9,1},{17,25},{25,17},{2,10},{10... | collective-permute-start | bytes 4718600 | tf_op jit(solution)/shard_map/ppermute | solution.py:940
  339.3 51.2 %collective-permute-start.19 = (bf16[384,2048]{1,0:T(8,128)(2,1)}, bf16[384,2048]{1,0:T(8,128)(2,1)S(1)}, u32[]{:S(2)}, u32[]{:S(2)}) collective-permute-start(bf16[384,2048]{1,0:T(8,128)(2,1)} %fusion.133), channel_id=1, source_target_pairs={{0,1},{1,0},{2,3},{3,2},{4,5},{5,4},{6,7},{7,6},{8,9},{9,8},{10,11... | collective-permute-start | bytes 4718600 | tf_op jit(solution)/shard_map/ppermute | solution.py:1256
  355.8 77.5 %collective-permute-start.29 = (bf16[1024,1408]{1,0:T(8,128)(2,1)}, bf16[1024,1408]{1,0:T(8,128)(2,1)}, u32[]{:S(2)}, u32[]{:S(2)}) collective-permute-start(bf16[1024,1408]{1,0:T(8,128)(2,1)} %convolution_convert_fusion.4), channel_id=1, source_target_pairs={{0,4},{2,6},{4,0},{6,2},{1,5},{3,7},{5,1},{7,3},{8,12},{10,14},{12... | collective-permute-start | bytes 8650760 | tf_op jit(solution)/shard_map/ppermute | solution.py:940
  366.0 74.4 %collective-permute-start.24 = (bf16[1024,1408]{1,0:T(8,128)(2,1)}, bf16[1024,1408]{1,0:T(8,128)(2,1)}, u32[]{:S(2)}, u32[]{:S(2)}) collective-permute-start(bf16[1024,1408]{1,0:T(8,128)(2,1)} %convolution_convert_fusion.6), channel_id=1, source_target_pairs={{0,8},{8,0},{16,24},{24,16},{1,9},{9,1},{17,25},{25,17},{2,10},{10... | collective-permute-start | bytes 8650760 | tf_op jit(solution)/shard_map/ppermute | solution.py:940
  375.9 73.5 %collective-permute-start.27 = (bf16[1024,1408]{1,0:T(8,128)(2,1)}, bf16[1024,1408]{1,0:T(8,128)(2,1)}, u32[]{:S(2)}, u32[]{:S(2)}) collective-permute-start(bf16[1024,1408]{1,0:T(8,128)(2,1)} %convolution_convert_fusion.5.rest_0_), channel_id=1, source_target_pairs={{0,2},{2,0},{4,6},{6,4},{1,3},{3,1},{5,7},{7,5},{8,10},{10,8},{12,... | collective-permute-start | bytes 8650760 | tf_op jit(solution)/shard_map/ppermute | solution.py:940
  390.5 34.2 %collective-permute-start.31 = (bf16[384,2048]{1,0:T(8,128)(2,1)}, bf16[384,2048]{1,0:T(8,128)(2,1)}, u32[]{:S(2)}, u32[]{:S(2)}) collective-permute-start(bf16[384,2048]{1,0:T(8,128)(2,1)} %collective-permute-done.30.mine_ref), channel_id=1, source_target_pairs={{0,1},{1,0},{2,3},{3,2},{4,5},{5,4},{6,7},{7,6},{8,9},{9,8},{10,11... | collective-permute-start | bytes 4718600 | tf_op jit(solution)/shard_map/ppermute | solution.py:968
  415.7 42.5 %collective-permute-start.21 = (bf16[8,128,256]{2,1,0:T(8,128)(2,1)}, bf16[8,128,256]{2,1,0:T(8,128)(2,1)S(1)}, u32[]{:S(2)}, u32[]{:S(2)}) collective-permute-start(bf16[8,128,256]{2,1,0:T(8,128)(2,1)} %get-tuple-element.89), channel_id=1, source_target_pairs={{4,0},{6,2},{5,1},{7,3},{12,8},{14,10},{13,9},{15,11},{20,16},{22,... | collective-permute-start | bytes 1572872 | tf_op jit(solution)/shard_map/ppermute | solution.py:907
  424.7 36.0 %collective-permute-start.20 = (bf16[8,128,256]{2,1,0:T(8,128)(2,1)S(1)}, bf16[8,128,256]{2,1,0:T(8,128)(2,1)S(1)}, u32[]{:S(2)}, u32[]{:S(2)}) collective-permute-start(bf16[8,128,256]{2,1,0:T(8,128)(2,1)S(1)} %copy-done.107), channel_id=1, source_target_pairs={{2,0},{4,2},{6,4},{3,1},{5,3},{7,5},{10,8},{12,10},{14,12},{11,9},... | collective-permute-start | bytes 1572872 | tf_op jit(solution)/shard_map/ppermute | solution.py:907
  433.3 176.6 %collective-permute-start.38 = (bf16[768,1024]{1,0:T(8,128)(2,1)}, bf16[768,1024]{1,0:T(8,128)(2,1)}, u32[]{:S(2)}, u32[]{:S(2)}) collective-permute-start(bf16[768,1024]{1,0:T(8,128)(2,1)} %get-tuple-element.177), channel_id=1, source_target_pairs={{0,8},{8,0},{16,24},{24,16},{1,9},{9,1},{17,25},{25,17},{2,10},{10... | collective-permute-start | bytes 4718600 | tf_op jit(solution)/shard_map/ppermute | solution.py:940
  440.4 179.5 %collective-permute-start.37 = (bf16[768,1024]{1,0:T(8,128)(2,1)}, bf16[768,1024]{1,0:T(8,128)(2,1)}, u32[]{:S(2)}, u32[]{:S(2)}) collective-permute-start(bf16[768,1024]{1,0:T(8,128)(2,1)} %get-tuple-element.179), channel_id=1, source_target_pairs={{0,2},{2,0},{4,6},{6,4},{1,3},{3,1},{5,7},{7,5},{8,10},{10,8},{12,... | collective-permute-start | bytes 4718600 | tf_op jit(solution)/shard_map/ppermute | solution.py:940
  449.4 97.8 %collective-permute-start.34 = (bf16[512,1408]{1,0:T(8,128)(2,1)}, bf16[512,1408]{1,0:T(8,128)(2,1)}, u32[]{:S(2)}, u32[]{:S(2)}) collective-permute-start(bf16[512,1408]{1,0:T(8,128)(2,1)} %fusion.36.rest_2_), channel_id=1, source_target_pairs={{0,16},{8,24},{16,0},{24,8},{1,17},{9,25},{17,1},{25,9},{2,18},{10... | collective-permute-start | bytes 4325384 | tf_op jit(solution)/shard_map/ppermute | solution.py:940
  458.2 89.0 %collective-permute-start.32 = (bf16[512,1408]{1,0:T(8,128)(2,1)}, bf16[512,1408]{1,0:T(8,128)(2,1)}, u32[]{:S(2)}, u32[]{:S(2)}) collective-permute-start(bf16[512,1408]{1,0:T(8,128)(2,1)} %fusion.34.rest_0_), channel_id=1, source_target_pairs={{0,4},{2,6},{4,0},{6,2},{1,5},{3,7},{5,1},{7,3},{8,12},{10,14},{12... | collective-permute-start | bytes 4325384 | tf_op jit(solution)/shard_map/ppermute | solution.py:940
  460.7 86.6 %collective-permute-start.33 = (bf16[512,1408]{1,0:T(8,128)(2,1)}, bf16[512,1408]{1,0:T(8,128)(2,1)}, u32[]{:S(2)}, u32[]{:S(2)}) collective-permute-start(bf16[512,1408]{1,0:T(8,128)(2,1)} %fusion.35.rest_1_), channel_id=1, source_target_pairs={{0,8},{8,0},{16,24},{24,16},{1,9},{9,1},{17,25},{25,17},{2,10},{10... | collective-permute-start | bytes 4325384 | tf_op jit(solution)/shard_map/ppermute | solution.py:940
  547.3 22.8 %collective-permute-start.35 = (f32[8,4096]{1,0:T(8,128)}, f32[8,4096]{1,0:T(8,128)S(1)}, u32[]{:S(2)}, u32[]{:S(2)}) collective-permute-start(f32[8,4096]{1,0:T(8,128)} %shard_map.424), channel_id=1, source_target_pairs={{2,0},{4,2},{6,4},{3,1},{5,3},{7,5},{10,8},{12,10},{14,12},{11,9},... | collective-permute-start | bytes 393224 | tf_op jit(solution)/shard_map/ppermute | solution.py:907
  573.2 85.0 %collective-permute-start.40 = (bf16[768,1024]{1,0:T(8,128)(2,1)}, bf16[768,1024]{1,0:T(8,128)(2,1)}, u32[]{:S(2)}, u32[]{:S(2)}) collective-permute-start(bf16[768,1024]{1,0:T(8,128)(2,1)} %get-tuple-element.173.refs_5_), channel_id=1, source_target_pairs={{0,4},{2,6},{4,0},{6,2},{1,5},{3,7},{5,1},{7,3},{8,12},{10,14},{12... | collective-permute-start | bytes 4718600 | tf_op jit(solution)/shard_map/ppermute | solution.py:940
  583.6 63.0 %collective-permute-start.39 = (bf16[768,1024]{1,0:T(8,128)(2,1)}, bf16[768,1024]{1,0:T(8,128)(2,1)}, u32[]{:S(2)}, u32[]{:S(2)}) collective-permute-start(bf16[768,1024]{1,0:T(8,128)(2,1)} %get-tuple-element.175.refs_4_), channel_id=1, source_target_pairs={{0,2},{2,0},{4,6},{6,4},{1,3},{3,1},{5,7},{7,5},{8,10},{10,8},{12,... | collective-permute-start | bytes 4718600 | tf_op jit(solution)/shard_map/ppermute | solution.py:940
  603.9 36.9 %collective-permute-start.36 = (bf16[384,2048]{1,0:T(8,128)(2,1)}, bf16[384,2048]{1,0:T(8,128)(2,1)}, u32[]{:S(2)}, u32[]{:S(2)}) collective-permute-start(bf16[384,2048]{1,0:T(8,128)(2,1)} %add_convert_fusion), channel_id=1, source_target_pairs={{0,1},{1,0},{2,3},{3,2},{4,5},{5,4},{6,7},{7,6},{8,9},{9,8},{10,11... | collective-permute-start | bytes 4718600 | tf_op jit(solution)/shard_map/ppermute | solution.py:1275
  (141 other events, 1812.9 us)
